TPU v7x, 512 devices: a whole 4x4x16 slice. The times are simulated.
512 devices in a mesh: noise: 32 (over y, x, core), dp: 16 (over z).
Axes of the slice: x: 4, y: 4, z: 16, core: 2. Of those that a mesh axis runs over, the one named last changes fastest.
Arguments:
- noise_rows: bfloat16 [4096, 16384], P('noise', 'dp'), may hold values from -10 to 10
- data_rows: bfloat16 [4096, 16384], P('noise', 'dp'), may hold values from -6 to 6
Outputs:
- targets: bfloat16 [4096, 16384], P('noise', 'dp')
- noise_potential: float32 [4096], P('noise')
- data_potential: float32 [4096], P('dp')
All inputs are finite; a program needn't handle non-finite values.
Results may differ from a plain program's by a relative error of at most 0.0045.
Values may be sent and summed in bfloat16 or wider, within the bound.
No kernel may reach another device: no remote copies, remote signals or barrier semaphores. Data moves between devices by JAX's collectives and lax.ppermute only.
A program may use at most 64 MiB of HBM per device.

v0:
```python
import math

import jax
import jax.numpy as jnp
from jax import lax
from jax.sharding import PartitionSpec as P

D = 16384
ITERS = 4


def row_lse(values):
    peak = jnp.max(values, axis=1)
    total = jnp.sum(jnp.exp(values - peak[:, None]), axis=1)
    whole_peak = lax.pmax(peak, "dp")
    whole_total = lax.psum(total * jnp.exp(peak - whole_peak), "dp")
    return whole_peak + jnp.log(whole_total)


def col_lse(values):
    peak = jnp.max(values, axis=0)
    total = jnp.sum(jnp.exp(values - peak[None, :]), axis=0)
    whole_peak = lax.pmax(peak, "noise")
    whole_total = lax.psum(total * jnp.exp(peak - whole_peak), "noise")
    return whole_peak + jnp.log(whole_total)


def on_device(noise_rows, data_rows):
    tokens = noise_rows.shape[0] * lax.axis_size("noise")
    noise_wide = noise_rows.astype(jnp.float32)
    noise_square = jnp.sum(noise_wide * noise_wide, axis=1)
    everything = lax.all_gather(data_rows, "noise", axis=0, tiled=True)
    every_wide = everything.astype(jnp.float32)
    every_square = jnp.sum(every_wide * every_wide, axis=1)
    cross = lax.dot_general(
        noise_rows, everything, (((1,), (1,)), ((), ())), preferred_element_type=jnp.float32
    )
    partial_value = noise_square[:, None] + every_square[None, :] - 2.0 * cross
    cost = lax.psum_scatter(partial_value, "dp", scatter_dimension=1, tiled=True) / D
    epsilon = 0.7 / math.sqrt(D)
    log_weight = -math.log(tokens)
    noise_potential = jnp.zeros((cost.shape[0],), jnp.float32)
    data_potential = jnp.zeros((cost.shape[1],), jnp.float32)
    for step in range(ITERS):
        noise_potential = epsilon * log_weight - epsilon * row_lse(
            (data_potential[None, :] - cost) / epsilon
        )
        data_potential = epsilon * log_weight - epsilon * col_lse(
            (noise_potential[:, None] - cost) / epsilon
        )
    plan = jnp.exp(
        (noise_potential[:, None] + data_potential[None, :] - cost) / epsilon + math.log(tokens)
    ).astype(jnp.bfloat16)
    wide_plan = lax.all_gather(plan, "dp", axis=1, tiled=True)
    mass = jnp.sum(wide_plan.astype(jnp.float32), axis=1)
    weighted = jnp.dot(wide_plan, everything, preferred_element_type=jnp.float32)
    targets = (weighted / mass[:, None]).astype(jnp.bfloat16)
    return (targets, noise_potential, data_potential)


def solution(mesh):
    return jax.shard_map(
        on_device,
        mesh=mesh,
        in_specs=(P("noise", "dp"), P("noise", "dp")),
        out_specs=(P("noise", "dp"), P("noise"), P("dp")),
        check_vma=False,
    )
```

profile of v0, /device:TPU:1, one launch (start us, length us, event | category | flops | bytes accessed | tf_op | source)
XLA Modules:
  0.0 980.9 jit_solution(10615627279020475105)
XLA Ops:
  7.2 0.0 copy-start.1
  7.2 0.0 all-gather.3.cloned.1.call-start
  7.2 0.7 all-gather.3.cloned.1.call-update
  7.9 0.0 reduce-scatter.2.cloned.1.call-start
  8.0 1.1 multiply_reduce_fusion.1
  9.0 76.1 %all-gather.3.cloned.1.call-done = bf16[4096,1024]{1,0:T(8,128)(2,1)} async-done(((bf16[128,1024]{1,0:T(8,128)(2,1)}), bf16[4096,1024]{1,0:T(8,128)(2,1)}) %all-gather.3.cloned.1.call-update) | async-done | bytes 8388624 | tf_op jit(solution)/shard_map/all_gather | solution.py:32
  85.1 0.0 copy-start
  85.1 5.2 multiply_reduce_fusion
  90.4 0.0 copy-done.1
  90.4 0.5 copy-done
  90.9 4.3 fusion
  95.2 0.0 reduce-scatter.2.cloned.1.call-update
  95.2 0.0 all-gather.5.cloned.1.call-start
  95.3 62.5 %reduce-scatter.2.cloned.1.call-done = f32[128,256]{1,0:T(8,128)} async-done(((f32[128,4096]{1,0:T(8,128)}), f32[128,256]{1,0:T(8,128)}) %reduce-scatter.2.cloned.1.call-update) | async-done | bytes 131088 | tf_op jit(solution)/shard_map/reduce_scatter | solution.py:39
  157.8 1.0 fusion.2
  158.8 22.1 %pmax.56 = f32[128]{0:T(128)S(1)} all-reduce(f32[128]{0:T(128)S(1)} %fusion.2), channel_id=1, replica_groups=mesh['noise'=32,'dp'=16] {'dp'}, use_global_device_ids=true, to_apply=%region_4.0 | all-reduce | flops 128 | bytes 1024 | tf_op jit(solution)/shard_map/pmax | solution.py:15
  180.9 1.1 exponential_reduce_fusion.7
  182.0 21.0 %psum.56 = f32[128]{0:T(128)S(1)} all-reduce(f32[128]{0:T(128)S(1)} %exponential_multiply_fusion.7), channel_id=1, replica_groups=mesh['noise'=32,'dp'=16] {'dp'}, use_global_device_ids=true, to_apply=%region_6.0 | all-reduce | flops 128 | bytes 1024 | tf_op jit(solution)/shard_map/psum | solution.py:16
  203.0 1.0 fusion.3
  204.1 86.9 %pmax.57 = f32[256]{0:T(256)S(1)} all-reduce(f32[256]{0:T(256)S(1)} %fusion.3), channel_id=1, replica_groups=mesh['noise'=32,'dp'=16] {'noise'}, use_global_device_ids=true, to_apply=%region_8.0 | all-reduce | flops 256 | bytes 2048 | tf_op jit(solution)/shard_map/pmax | solution.py:23
  290.9 1.0 exponential_reduce_fusion.6
  291.9 62.7 %psum.57 = f32[256]{0:T(256)S(1)} all-reduce(f32[256]{0:T(256)S(1)} %exponential_multiply_fusion.3), channel_id=1, replica_groups=mesh['noise'=32,'dp'=16] {'noise'}, use_global_device_ids=true, to_apply=%region_10.0 | all-reduce | flops 256 | bytes 2048 | tf_op jit(solution)/shard_map/psum | solution.py:24
  354.6 1.0 fusion.4
  355.6 21.5 %pmax.58 = f32[128]{0:T(128)S(1)} all-reduce(f32[128]{0:T(128)S(1)} %fusion.4), channel_id=1, replica_groups=mesh['noise'=32,'dp'=16] {'dp'}, use_global_device_ids=true, to_apply=%region_12.0 | all-reduce | flops 128 | bytes 1024 | tf_op jit(solution)/shard_map/pmax | solution.py:15
  377.1 1.1 exponential_reduce_fusion.5
  378.2 20.3 %psum.58 = f32[128]{0:T(128)S(1)} all-reduce(f32[128]{0:T(128)S(1)} %exponential_multiply_fusion.6), channel_id=1, replica_groups=mesh['noise'=32,'dp'=16] {'dp'}, use_global_device_ids=true, to_apply=%region_14.0 | all-reduce | flops 128 | bytes 1024 | tf_op jit(solution)/shard_map/psum | solution.py:16
  398.6 1.0 fusion.5
  399.6 76.9 %pmax.59 = f32[256]{0:T(256)S(1)} all-reduce(f32[256]{0:T(256)S(1)} %fusion.5), channel_id=1, replica_groups=mesh['noise'=32,'dp'=16] {'noise'}, use_global_device_ids=true, to_apply=%region_16.0 | all-reduce | flops 256 | bytes 2048 | tf_op jit(solution)/shard_map/pmax | solution.py:23
  476.5 1.0 exponential_reduce_fusion.4
  477.5 62.7 %psum.59 = f32[256]{0:T(256)S(1)} all-reduce(f32[256]{0:T(256)S(1)} %exponential_multiply_fusion.2), channel_id=1, replica_groups=mesh['noise'=32,'dp'=16] {'noise'}, use_global_device_ids=true, to_apply=%region_18.0 | all-reduce | flops 256 | bytes 2048 | tf_op jit(solution)/shard_map/psum | solution.py:24
  540.2 1.0 fusion.6
  541.2 22.3 %pmax.60 = f32[128]{0:T(128)S(1)} all-reduce(f32[128]{0:T(128)S(1)} %fusion.6), channel_id=1, replica_groups=mesh['noise'=32,'dp'=16] {'dp'}, use_global_device_ids=true, to_apply=%region_20.0 | all-reduce | flops 128 | bytes 1024 | tf_op jit(solution)/shard_map/pmax | solution.py:15
  563.5 1.1 exponential_reduce_fusion.3
  564.6 20.2 %psum.60 = f32[128]{0:T(128)S(1)} all-reduce(f32[128]{0:T(128)S(1)} %exponential_multiply_fusion.5), channel_id=1, replica_groups=mesh['noise'=32,'dp'=16] {'dp'}, use_global_device_ids=true, to_apply=%region_22.0 | all-reduce | flops 128 | bytes 1024 | tf_op jit(solution)/shard_map/psum | solution.py:16
  584.8 1.0 fusion.7
  585.8 76.6 %pmax.61 = f32[256]{0:T(256)S(1)} all-reduce(f32[256]{0:T(256)S(1)} %fusion.7), channel_id=1, replica_groups=mesh['noise'=32,'dp'=16] {'noise'}, use_global_device_ids=true, to_apply=%region_24.0 | all-reduce | flops 256 | bytes 2048 | tf_op jit(solution)/shard_map/pmax | solution.py:23
  662.3 1.0 exponential_reduce_fusion.2
  663.4 62.7 %psum.61 = f32[256]{0:T(256)S(1)} all-reduce(f32[256]{0:T(256)S(1)} %exponential_multiply_fusion.1), channel_id=1, replica_groups=mesh['noise'=32,'dp'=16] {'noise'}, use_global_device_ids=true, to_apply=%region_26.0 | all-reduce | flops 256 | bytes 2048 | tf_op jit(solution)/shard_map/psum | solution.py:24
  726.1 1.0 fusion.8
  727.1 22.0 %pmax.62 = f32[128]{0:T(128)S(1)} all-reduce(f32[128]{0:T(128)S(1)} %fusion.8), channel_id=1, replica_groups=mesh['noise'=32,'dp'=16] {'dp'}, use_global_device_ids=true, to_apply=%region_28.0 | all-reduce | flops 128 | bytes 1024 | tf_op jit(solution)/shard_map/pmax | solution.py:15
  749.1 1.1 exponential_reduce_fusion.1
  750.2 20.2 %psum.62 = f32[128]{0:T(128)S(1)} all-reduce(f32[128]{0:T(128)S(1)} %exponential_multiply_fusion.4), channel_id=1, replica_groups=mesh['noise'=32,'dp'=16] {'dp'}, use_global_device_ids=true, to_apply=%region_30.0 | all-reduce | flops 128 | bytes 1024 | tf_op jit(solution)/shard_map/psum | solution.py:16
  770.3 0.0 copy-start.2
  770.4 1.0 fusion.9
  771.4 76.6 %pmax.63 = f32[256]{0:T(256)S(1)} all-reduce(f32[256]{0:T(256)S(1)} %fusion.9), channel_id=1, replica_groups=mesh['noise'=32,'dp'=16] {'noise'}, use_global_device_ids=true, to_apply=%region_32.0 | all-reduce | flops 256 | bytes 2048 | tf_op jit(solution)/shard_map/pmax | solution.py:23
  847.9 1.0 exponential_reduce_fusion
  849.0 62.7 %psum.63 = f32[256]{0:T(256)S(1)} all-reduce(f32[256]{0:T(256)S(1)} %exponential_multiply_fusion), channel_id=1, replica_groups=mesh['noise'=32,'dp'=16] {'noise'}, use_global_device_ids=true, to_apply=%region_34.0 | all-reduce | flops 256 | bytes 2048 | tf_op jit(solution)/shard_map/psum | solution.py:24
  911.6 0.0 copy-start.3
  911.7 1.6 exponential_convert_fusion
  913.3 0.0 all-gather.5.cloned.1.call-update
  913.3 53.9 %all-gather.5.cloned.1.call-done = bf16[128,4096]{1,0:T(8,128)(2,1)} async-done(((bf16[128,256]{1,0:T(8,128)(2,1)}), bf16[128,4096]{1,0:T(8,128)(2,1)}) %all-gather.5.cloned.1.call-update) | async-done | bytes 1048592 | tf_op jit(solution)/shard_map/all_gather | solution.py:54
  967.2 1.5 convert_reduce_fusion
  968.7 5.7 fusion.1
  974.4 0.0 copy-done.2
  974.4 0.0 copy-done.3
  (16 shorter events, 0.1 us)
Async XLA Ops:
  7.2 83.2 %copy-start.1 = (bf16[128,1024]{1,0:T(8,128)(2,1)S(1)}, bf16[128,1024]{1,0:T(8,128)(2,1)}, u32[]{:S(2)}) copy-start(bf16[128,1024]{1,0:T(8,128)(2,1)} %param.2) | copy-start | bytes 786436
  7.2 77.9 %all-gather.3.cloned.1.call-start = ((), (), s32[]{:S(2)}) async-start(), calls=%async_computation.1 | async-start | bytes 8650752 | tf_op jit(solution)/shard_map/all_gather | solution.py:32
  7.9 149.9 %reduce-scatter.2.cloned.1.call-start = ((), (), s32[]{:S(2)}) async-start(), calls=%async_computation.2 | async-start | bytes 2228224 | tf_op jit(solution)/shard_map/reduce_scatter | solution.py:39
  85.1 5.8 copy-start
  95.2 872.0 %all-gather.5.cloned.1.call-start = ((), (), s32[]{:S(2)}) async-start(), calls=%async_computation.3 | async-start | bytes 1114112 | tf_op jit(solution)/shard_map/all_gather | solution.py:54
  770.3 204.0 %copy-start.2 = (f32[128]{0:T(128)}, f32[128]{0:T(128)S(1)}, u32[]{:S(2)}) copy-start(f32[128]{0:T(128)S(1)} %multiply_subtract_fusion.4) | copy-start | bytes 1540
  911.6 62.7 %copy-start.3 = (f32[256]{0:T(256)}, f32[256]{0:T(256)S(1)}, u32[]{:S(2)}) copy-start(f32[256]{0:T(256)S(1)} %multiply_subtract_fusion) | copy-start | bytes 3076
Sparse Core Ops, SparseCore 0:
  11.1 73.9 all-gather.2
  95.3 62.3 reduce-scatter.1
  913.4 53.7 all-gather.4
where the time goes:
time: 992 us; the launch traced here: 981 us
  blocking collectives  737 us (74%)
  waiting for transfers between devices  193 us (19%)
  other arithmetic  26 us (3%)
  between operations  13.9 us (1%)
  matrix products  9.99 us (1%)
    pmax x4, blocking collectives, col_lse(): whole_peak = lax.pmax(peak, 'noise')  317 us
    psum x4, blocking collectives, col_lse(): whole_total = lax.psum(total * jnp.exp(peak - whole_peak), 'noise')  251 us
    pmax x4, blocking collectives, row_lse(): whole_peak = lax.pmax(peak, 'dp')  87.9 us
    psum x4, blocking collectives, row_lse(): whole_total = lax.psum(total * jnp.exp(peak - whole_peak), 'dp')  81.7 us
    all_gather x1, waiting for transfers between devices, on_device(): everything = lax.all_gather(data_rows, 'noise', axis=0, tiled=True)  76.1 us
    reduce_scatter x1, waiting for transfers between devices, on_device(): lax.psum_scatter(partial_value, 'dp', scatter_dimension=1, tiled=True) / D  62.5 us
    all_gather x1, waiting for transfers between devices, on_device(): wide_plan = lax.all_gather(plan, 'dp', axis=1, tiled=True)  53.9 us
  transfers between devices with their start and end apart: 3, of which 3 were waited for; matrix products, arithmetic and copies ran while one was open for 0% of the time, Pallas kernels for 0%

commit v1 on v0

v1 whole, which is shorter than its diff:
```python
import functools
import math

import jax
import jax.numpy as jnp
from jax import lax
from jax.experimental import pallas as pl
from jax.experimental.pallas import tpu as pltpu
from jax.sharding import PartitionSpec as P

D = 16384
ITERS = 4
YS, XS, CORES = 4, 4, 2
LOG2E = math.log2(math.e)
VMEM = pl.BlockSpec(memory_space=pltpu.VMEM)
SMEM = pl.BlockSpec(memory_space=pltpu.SMEM)
PARAMS = pltpu.CompilerParams(vmem_limit_bytes=48 * 1024 * 1024)


def send(value, dy=0, dx=0, dc=0):
    pairs = []
    for y in range(YS):
        for x in range(XS):
            for c in range(CORES):
                source = (y * XS + x) * CORES + c
                target = ((y + dy) % YS * XS + (x + dx) % XS) * CORES + (c + dc) % CORES
                pairs.append((source, target))
    return lax.ppermute(value, "noise", pairs)


def send_z(value, dz):
    size = lax.axis_size("dp")
    return lax.ppermute(value, "dp", [(z, (z + dz) % size) for z in range(size)])


def gather4(block, **axis):
    (name,) = axis
    before, after = send(block, **{name: 1}), send(block, **{name: -1})
    return jnp.concatenate([block, before, send(block, **{name: 2}), after], axis=0)


def squares_row(block):
    wide = block.astype(jnp.float32)
    column = jnp.sum(wide * wide, axis=1, keepdims=True)
    n = block.shape[0]
    row_at = lax.broadcasted_iota(jnp.int32, (n, n), 0)
    column_at = lax.broadcasted_iota(jnp.int32, (n, n), 1)
    return jnp.sum(jnp.where(row_at == column_at, column, 0.0), axis=0, keepdims=True)


def partial_kernel(scale, place_ref, x_here, x_there, y_ref, *refs):
    outs, (x_all, y_squares) = refs[:-2], refs[-2:]
    rows = x_here.shape[0] // XS
    high = outs[0].shape[0]
    x, c = place_ref[2], place_ref[3]
    for k in range(XS):
        at = lax.rem(x + XS - k, XS) * CORES
        block = slice(k * rows, (k + 1) * rows)
        x_all[at + c] = x_here[block, :]
        x_all[at + 1 - c] = x_there[block, :]
    for k in range(YS):
        block = slice(k * rows, (k + 1) * rows)
        y_squares[:, block] = scale * squares_row(y_ref[block, :])
    for k in range(XS * CORES):
        value = x_all[k]
        wide = value.astype(jnp.float32)
        x_squares = scale * jnp.sum(wide * wide, axis=1, keepdims=True)
        cross = lax.dot_general(
            value, y_ref[...], (((1,), (1,)), ((), ())), preferred_element_type=jnp.float32
        )
        value = (2.0 * scale) * cross - x_squares - y_squares[...]
        for t in range(rows // high):
            outs[k * (rows // high) + t][...] = value[t * high : (t + 1) * high]


def joined(parts):
    peak = jnp.max(parts, axis=0)
    return peak + jnp.log(jnp.sum(jnp.exp2(parts - peak), axis=0)) * LOG2E


def on_diagonal(n):
    rows = lax.broadcasted_iota(jnp.int32, (n, n), 0)
    return rows == lax.broadcasted_iota(jnp.int32, (n, n), 1)


def column_of(u, k):
    n = u.shape[1]
    return jnp.sum(jnp.where(on_diagonal(n), u[k : k + 1], 0.0), axis=1, keepdims=True)


def row_of(parts_ref, log_weight):
    v = log_weight - joined(parts_ref[...])
    return jnp.concatenate([v[k : k + 1] for k in range(YS)], axis=1)


def copy_out(out_ref):
    whole = out_ref[0]
    for k in range(1, out_ref.shape[0]):
        out_ref[k] = whole


def row_sums(a_ref, v, out_ref):
    n = out_ref.shape[2]
    for k in range(out_ref.shape[1]):
        value = a_ref[k * n : (k + 1) * n, :]
        if v is not None:
            value = value + v
        peak = jnp.max(value, axis=1, keepdims=True)
        total = jnp.sum(jnp.exp2(value - peak), axis=1, keepdims=True)
        part = peak + jnp.log(total) * LOG2E
        out_ref[0, k : k + 1, :] = jnp.sum(jnp.where(on_diagonal(n), part, 0.0), axis=0, keepdims=True)
    copy_out(out_ref)


def first_rows_kernel(*refs):
    pieces, (a_ref, out_ref) = refs[:-2], refs[-2:]
    high = pieces[0].shape[0]
    for k, piece in enumerate(pieces):
        a_ref[k * high : (k + 1) * high, :] = piece[...]
    row_sums(a_ref, None, out_ref)


def rows_kernel(log_weight, a_ref, parts_ref, out_ref):
    row_sums(a_ref, row_of(parts_ref, log_weight), out_ref)


def columns_kernel(log_weight, a_ref, parts_ref, u_ref, out_ref, shifted):
    u = log_weight - joined(parts_ref[...])
    u_ref[...] = u
    blocks, n = u.shape
    width = a_ref.shape[1]
    peak = None
    for k in range(blocks):
        value = a_ref[k * n : (k + 1) * n, :] + column_of(u, k)
        shifted[k * n : (k + 1) * n, :] = value
        block_peak = jnp.max(value.reshape(n // 8, 8, width), axis=0)
        peak = block_peak if peak is None else jnp.maximum(peak, block_peak)
    peak = jnp.max(peak, axis=0, keepdims=True)
    total = jnp.zeros((8, width), jnp.float32)
    for k in range(blocks):
        value = jnp.exp2(shifted[k * n : (k + 1) * n, :] - peak)
        total = total + jnp.sum(value.reshape(n // 8, 8, width), axis=0)
    part = peak + jnp.log(jnp.sum(total, axis=0, keepdims=True)) * LOG2E
    for k in range(2 * YS):
        at = k % YS * n
        out_ref[0, k : k + 1, :] = part[:, at : at + n]
    copy_out(out_ref)


def plan_kernel(log_weight, a_ref, u_ref, parts_ref, out_ref):
    v = row_of(parts_ref, log_weight)
    u = u_ref[...] - log_weight
    blocks, n = u.shape
    top = v.astype(jnp.bfloat16).astype(jnp.float32)
    rest = v - top
    middle = rest.astype(jnp.bfloat16).astype(jnp.float32)
    extra = out_ref.shape[1] - n
    row = lax.broadcasted_iota(jnp.int32, (extra, v.shape[1]), 0)
    under = jnp.where(row == 0, top, jnp.where(row == 1, middle, jnp.where(row == 2, rest - middle, 0.0)))
    under = under.astype(jnp.bfloat16)
    for k in range(blocks):
        value = a_ref[k * n : (k + 1) * n, :] + (column_of(u, k) + v)
        out_ref[k, :n, :] = jnp.exp2(value).astype(jnp.bfloat16)
        out_ref[k, n:, :] = under


def target_kernel(unit, place_ref, plan_ref, u_ref, y_ref, out_ref, f_ref, g_ref, total, mass):
    step = pl.program_id(0)
    z, x, c = place_ref[0], place_ref[2], place_ref[3]
    blocks = plan_ref.shape[0]
    n = out_ref.shape[0]

    @pl.when(step == 0)
    def _():
        total[...] = jnp.zeros_like(total)
        mass[...] = jnp.zeros_like(mass)
        f_ref[...] = unit * u_ref[pl.ds(x * CORES + c, 1), :]

    plan = jnp.concatenate([plan_ref[k, :n, :] for k in range(blocks)], axis=1)
    mass[...] += jnp.sum(plan.astype(jnp.float32), axis=1, keepdims=True)
    total[...] += jnp.dot(plan, y_ref[...], preferred_element_type=jnp.float32)

    @pl.when(step == z // XS)
    def _():
        for k in range(CORES):
            v = plan_ref[lax.rem(z, XS) * CORES + k, n:, :].astype(jnp.float32)
            g_ref[:, k * n : (k + 1) * n] = unit * (v[0:1] + v[1:2] + v[2:3])

    @pl.when(step == YS - 1)
    def _():
        out_ref[...] = (total[...] / mass[...]).astype(out_ref.dtype)


def on_device(noise_rows, data_rows):
    rows, features = noise_rows.shape
    tokens = rows * lax.axis_size("noise")
    depth = lax.axis_size("dp")
    me, z = lax.axis_index("noise"), lax.axis_index("dp")
    place = jnp.stack([z, me // (XS * CORES), me // CORES % XS, me % CORES]).astype(jnp.int32)
    epsilon = 0.7 / math.sqrt(D)
    log_weight = -math.log2(tokens)
    f32 = jnp.float32

    x_here = gather4(noise_rows, dx=1)
    x_there = send(x_here, dc=1)
    group = XS * CORES
    y_groups = [[y * group + k for y in range(YS)] for k in range(group)]
    x_groups = [[y * group + k for k in range(group)] for y in range(YS)]

    def swap(value, groups):
        return lax.all_to_all(value, "noise", 0, 0, axis_index_groups=groups, tiled=True)

    y_near = lax.all_gather(data_rows, "noise", axis_index_groups=y_groups, tiled=True)
    tall, wide = group * rows, YS * rows
    high = 16
    partial_value = pl.pallas_call(
        functools.partial(partial_kernel, LOG2E / (epsilon * D)),
        out_shape=[jax.ShapeDtypeStruct((high, wide), f32)] * (tall // high),
        in_specs=[SMEM] + [VMEM] * 3,
        out_specs=[VMEM] * (tall // high),
        scratch_shapes=[
            pltpu.VMEM((group, rows, features), jnp.bfloat16),
            pltpu.VMEM((1, wide), f32),
        ],
        compiler_params=PARAMS,
    )(place, x_here, x_there, y_near)
    late_rows, partial_value = lax.optimization_barrier((data_rows, partial_value))

    pieces = lax.psum(partial_value, "dp")
    row_shape = jax.ShapeDtypeStruct((group, group, rows), f32)
    column_shape = jax.ShapeDtypeStruct((YS, 2 * YS, rows), f32)
    u_shape = jax.ShapeDtypeStruct((group, rows), f32)
    a, part = pl.pallas_call(
        first_rows_kernel,
        out_shape=[jax.ShapeDtypeStruct((tall, wide), f32), row_shape],
        in_specs=[VMEM] * (tall // high),
        out_specs=[VMEM] * 2,
        compiler_params=PARAMS,
    )(*pieces)
    for step in range(ITERS):
        if step > 0:
            part = pl.pallas_call(
                functools.partial(rows_kernel, log_weight),
                out_shape=row_shape,
                in_specs=[VMEM] * 2,
                out_specs=VMEM,
                compiler_params=PARAMS,
            )(a, part)
        part = swap(part, x_groups)
        u, part = pl.pallas_call(
            functools.partial(columns_kernel, log_weight),
            out_shape=[u_shape, column_shape],
            in_specs=[VMEM] * 2,
            out_specs=[VMEM] * 2,
            scratch_shapes=[pltpu.VMEM((tall, wide), f32)],
            compiler_params=PARAMS,
        )(a, part)
        part = swap(part, y_groups)
    plan = pl.pallas_call(
        functools.partial(plan_kernel, log_weight),
        out_shape=jax.ShapeDtypeStruct((group, rows + 16, wide), jnp.bfloat16),
        in_specs=[VMEM] * 3,
        out_specs=VMEM,
        compiler_params=PARAMS,
    )(a, u, part)
    plan = swap(plan, x_groups)

    everything = lax.all_gather(late_rows, "noise", axis=0, tiled=True)
    targets, noise_potential, data_potential = pl.pallas_call(
        functools.partial(target_kernel, epsilon / LOG2E),
        grid=(YS,),
        out_shape=[
            jax.ShapeDtypeStruct((rows, features), jnp.bfloat16),
            jax.ShapeDtypeStruct((1, rows), f32),
            jax.ShapeDtypeStruct((1, CORES * rows), f32),
        ],
        in_specs=[
            SMEM,
            pl.BlockSpec((group, rows + 16, rows), lambda k: (0, 0, k)),
            pl.BlockSpec((group, rows), lambda k: (0, 0)),
            pl.BlockSpec((group * rows, features), lambda k: (k, 0)),
        ],
        out_specs=[
            pl.BlockSpec((rows, features), lambda k: (0, 0)),
            pl.BlockSpec((1, rows), lambda k: (0, 0)),
            pl.BlockSpec((1, CORES * rows), lambda k: (0, 0)),
        ],
        scratch_shapes=[
            pltpu.VMEM((rows, features), f32),
            pltpu.VMEM((rows, 1), f32),
        ],
        compiler_params=PARAMS,
    )(place, plan, u, everything)
    return targets, noise_potential.reshape(rows), data_potential.reshape(CORES * rows)


def solution(mesh):
    return jax.shard_map(
        on_device,
        mesh=mesh,
        in_specs=(P("noise", "dp"), P("noise", "dp")),
        out_specs=(P("noise", "dp"), P("noise"), P("dp")),
        check_vma=False,
    )
```

time: 992 us -> 393 us (0.40)
  blocking collectives: 737 us -> 86.3 us
  local copies, waits for them, and re-layouts: 0.53 us -> 50.7 us
  other arithmetic: 26 us -> 0.08 us
  starting transfers between devices: 0.12 us -> 18.7 us
  Pallas kernels: 0 us -> 16.5 us
  matrix products: 9.99 us -> 0 us
    pmax x8 -> x0, blocking collectives: 405 us -> none  [the longest x4 317 us: col_lse(): whole_peak = lax.pmax(peak, 'noise')]
    psum x8 -> x0, blocking collectives: 332 us -> none  [the longest x4 251 us: col_lse(): whole_total = lax.psum(total * jnp.exp(peak - whole_peak), 'noise')]
    psum x0 -> x1, waiting for transfers between devices: none -> 181 us  [on_device(): pieces = lax.psum(partial_value, 'dp')]
    all_gather x2, waiting for transfers between devices: 130 us -> 12.9 us  [the longest x1 12.9 us: on_device(): lax.all_gather(data_rows, 'noise', axis_index_groups=y_groups, tiled=True)]
    all_to_all x0 -> x9, blocking collectives: none -> 86.3 us  [swap(): lax.all_to_all(value, 'noise', 0, 0, axis_index_groups=groups, tiled=True)]
    reduce_scatter x1 -> x0, waiting for transfers between devices: 62.5 us -> none  [on_device(): lax.psum_scatter(partial_value, 'dp', scatter_dimension=1, tiled=True) / D]
    unnamed x8 -> x133, local copies, waits for them, and re-layouts: 0.53 us -> 50.7 us
    ppermute x0 -> x4, starting transfers between devices: none -> 18.6 us  [send(): return lax.ppermute(value, 'noise', pairs)]
  transfers between devices with their start and end apart: 3 -> 7, of which waited for: 3 -> 4; matrix products, arithmetic and copies ran while one was open for 0% -> 0% of each run, Pallas kernels for 0% -> 2%
where the time goes in v1:
time: 393 us; the launch traced here: 388 us
  waiting for transfers between devices  202 us (51%)
  blocking collectives  86.3 us (22%)
  local copies, waits for them, and re-layouts  50.7 us (13%)
  starting transfers between devices  18.7 us (5%)
  Pallas kernels  16.5 us (4%)
  between operations  13.9 us (4%)
    psum x1, waiting for transfers between devices, on_device(): pieces = lax.psum(partial_value, 'dp')  181 us
    all_to_all x9, blocking collectives, swap(): lax.all_to_all(value, 'noise', 0, 0, axis_index_groups=groups, tiled=True)  86.3 us
    unnamed x133, local copies, waits for them, and re-layouts  50.7 us
    ppermute x4, starting transfers between devices, send(): return lax.ppermute(value, 'noise', pairs)  18.6 us
    all_gather x1, waiting for transfers between devices, on_device(): lax.all_gather(data_rows, 'noise', axis_index_groups=y_groups, tiled=True)  12.9 us
  transfers between devices with their start and end apart: 7, of which 4 were waited for; matrix products, arithmetic and copies ran while one was open for 0% of the time, Pallas kernels for 2%

profile of v1, /device:TPU:1, one launch (start us, length us, event | category | flops | bytes accessed | tf_op | source)
XLA Modules:
  0.0 387.9 jit_solution(7708679965791819604)
XLA Ops:
  7.2 3.9 %collective-permute-start = (bf16[128,1024]{1,0:T(8,128)(2,1)}, bf16[128,1024]{1,0:T(8,128)(2,1)S(1)}, u32[]{:S(2)}, u32[]{:S(2)}) collective-permute-start(bf16[128,1024]{1,0:T(8,128)(2,1)} %param.2), channel_id=1, source_target_pairs={{0,32},{16,48},{32,64},{48,80},{64,96},{80,112},{96,0},{112,16},{1... | collective-permute-start | bytes 786440 | tf_op jit(solution)/shard_map/ppermute | solution.py:28
  11.2 4.4 %collective-permute-start.1 = (bf16[128,1024]{1,0:T(8,128)(2,1)}, bf16[128,1024]{1,0:T(8,128)(2,1)S(1)}, u32[]{:S(2)}, u32[]{:S(2)}) collective-permute-start(bf16[128,1024]{1,0:T(8,128)(2,1)} %param.2), channel_id=1, source_target_pairs={{0,64},{16,80},{32,96},{48,112},{64,0},{80,16},{96,32},{112,48},{1... | collective-permute-start | bytes 786440 | tf_op jit(solution)/shard_map/ppermute | solution.py:28
  15.6 3.1 collective-permute-start.2
  18.7 1.0 constant_dynamic-update-slice_fusion.3
  19.7 4.4 %collective-permute-done.1 = bf16[128,1024]{1,0:T(8,128)(2,1)S(1)} collective-permute-done((bf16[128,1024]{1,0:T(8,128)(2,1)}, bf16[128,1024]{1,0:T(8,128)(2,1)S(1)}, u32[]{:S(2)}, u32[]{:S(2)}) %collective-permute-start.1) | collective-permute-done | bytes 262176 | tf_op jit(solution)/shard_map/ppermute | solution.py:28
  24.2 7.2 %collective-permute-start.3 = (bf16[512,1024]{1,0:T(8,128)(2,1)S(1)}, bf16[512,1024]{1,0:T(8,128)(2,1)S(1)}, u32[]{:S(2)}, u32[]{:S(2)}) collective-permute-start(bf16[512,1024]{1,0:T(8,128)(2,1)S(1)} %constant_dynamic-update-slice_fusion.x_here), channel_id=1, source_target_pairs={{0,16},{16,0},{32,48},{48,32},{64,80},{80,64},{96,112},{112,96},{1... | collective-permute-start | bytes 3145736 | tf_op jit(solution)/shard_map/ppermute | solution.py:28
  31.5 2.1 collective-permute-done.3.x_there
  33.6 12.9 %all-gather.3.cloned.1.call-done.y_ref = bf16[512,1024]{1,0:T(8,128)(2,1)} async-done(((bf16[128,1024]{1,0:T(8,128)(2,1)}), bf16[512,1024]{1,0:T(8,128)(2,1)}) %all-gather.3.cloned.1.call-update) | async-done | bytes 1048592 | tf_op jit(solution)/shard_map/all_gather | solution.py:213
  46.6 1.2 copy-done
  47.8 4.6 %shard_map.49 = (f32[16,512]{1,0:T(8,128)}, f32[16,512]{1,0:T(8,128)}, f32[16,512]{1,0:T(8,128)}, f32[16,512]{1,0:T(8,128)}, f32[16,512]{1,0:T(8,128)}, /*index=...) custom-call(s32[4]{0:T(128)S(1)} %pad_add_fusion.place_ref, ...), custom_call_target="tpu_custom_call" | custom-call | tf_op jit(solution)/shard_map/pallas_call | solution.py:216
  53.2 181.4 %all-reduce.3.cloned.1.call-done = (f32[16,512]{1,0:T(8,128)}, f32[16,512]{1,0:T(8,128)}, f32[16,512]{1,0:T(8,128)}, f32[16,512]{1,0:T(8,128)}, f32[16,512]{1,0:...) async-done(((f32[16,512]{1,0:T(8,128)}, f32[16,512]{1,0:T(8,128)}, ...) | async-done | bytes 2097168 | tf_op jit(solution)/shard_map/psum | solution.py:229
  234.6 0.8 copy-done.1
  237.6 0.8 copy-done.5
  238.3 0.8 copy-done.6
  239.1 0.8 copy-done.7
  239.9 0.8 copy-done.8
  240.6 0.8 copy-done.9
  241.4 0.8 copy-done.10
  242.1 0.8 copy-done.11
  242.9 0.8 copy-done.12
  243.7 0.8 copy-done.13
  252.0 0.8 copy-done.24
  252.8 0.8 copy-done.25
  253.5 0.8 copy-done.26
  254.3 0.8 copy-done.27
  255.0 0.8 copy-done.28
  255.8 0.8 copy-done.29
  256.6 0.8 copy-done.30
  257.3 0.8 copy-done.31
  258.1 0.8 copy-done.32
  258.8 0.8 copy-done.33
  259.6 0.8 copy-done.34
  260.3 0.8 copy-done.35
  261.1 0.8 copy-done.36
  261.9 0.8 copy-done.37
  262.6 0.8 copy-done.38
  263.4 0.8 copy-done.39
  264.9 0.8 copy-done.41
  265.7 0.8 copy-done.42
  266.4 0.8 copy-done.43
  267.2 0.8 copy-done.44
  267.9 0.8 copy-done.45
  268.7 0.8 copy-done.46
  269.5 0.8 copy-done.47
  270.2 0.8 copy-done.48
  271.0 0.8 copy-done.49
  271.7 0.8 copy-done.50
  280.1 0.8 copy-done.61
  280.8 0.8 copy-done.62
  281.6 0.8 copy-done.63
  282.3 0.8 copy-done.64
  283.7 10.2 %all_to_all.45.parts_ref = f32[8,8,128]{2,1,0:T(8,128)S(1)} all-to-all(f32[8,8,128]{2,1,0:T(8,128)S(1)} %get-tuple-element.271), channel_id=1, replica_groups={{0,16,32,48,64,80,96,112},{128,144,160,176,192,208,224,240},{256,272,28..., dimensions={0} | all-to-all | bytes 65536 | tf_op jit(solution)/shard_map/all_to_all | solution.py:211
  294.0 0.9 shard_map.51
  294.8 8.5 %all_to_all.46.parts_ref = f32[4,8,128]{2,1,0:T(8,128)S(1)} all-to-all(f32[4,8,128]{2,1,0:T(8,128)S(1)} %get-tuple-element.272), channel_id=1, replica_groups={{0,128,256,384},{16,144,272,400},{32,160,288,416},{48,176,304,432},{64,..., dimensions={0} | all-to-all | bytes 32768 | tf_op jit(solution)/shard_map/all_to_all | solution.py:211
  303.9 9.1 %all_to_all.47.parts_ref = f32[8,8,128]{2,1,0:T(8,128)S(1)} all-to-all(f32[8,8,128]{2,1,0:T(8,128)S(1)} %shard_map.52), channel_id=1, replica_groups={{0,16,32,48,64,80,96,112},{128,144,160,176,192,208,224,240},{256,272,28..., dimensions={0} | all-to-all | bytes 65536 | tf_op jit(solution)/shard_map/all_to_all | solution.py:211
  313.0 0.9 shard_map.53
  313.9 6.5 %all_to_all.48.parts_ref = f32[4,8,128]{2,1,0:T(8,128)S(1)} all-to-all(f32[4,8,128]{2,1,0:T(8,128)S(1)} %get-tuple-element.273), channel_id=1, replica_groups={{0,128,256,384},{16,144,272,400},{32,160,288,416},{48,176,304,432},{64,..., dimensions={0} | all-to-all | bytes 32768 | tf_op jit(solution)/shard_map/all_to_all | solution.py:211
  321.1 9.0 %all_to_all.49.parts_ref = f32[8,8,128]{2,1,0:T(8,128)S(1)} all-to-all(f32[8,8,128]{2,1,0:T(8,128)S(1)} %shard_map.54), channel_id=1, replica_groups={{0,16,32,48,64,80,96,112},{128,144,160,176,192,208,224,240},{256,272,28..., dimensions={0} | all-to-all | bytes 65536 | tf_op jit(solution)/shard_map/all_to_all | solution.py:211
  330.0 0.9 shard_map.55
  330.9 6.5 %all_to_all.50.parts_ref = f32[4,8,128]{2,1,0:T(8,128)S(1)} all-to-all(f32[4,8,128]{2,1,0:T(8,128)S(1)} %get-tuple-element.274), channel_id=1, replica_groups={{0,128,256,384},{16,144,272,400},{32,160,288,416},{48,176,304,432},{64,..., dimensions={0} | all-to-all | bytes 32768 | tf_op jit(solution)/shard_map/all_to_all | solution.py:211
  338.1 9.0 %all_to_all.51.parts_ref = f32[8,8,128]{2,1,0:T(8,128)S(1)} all-to-all(f32[8,8,128]{2,1,0:T(8,128)S(1)} %shard_map.56), channel_id=1, replica_groups={{0,16,32,48,64,80,96,112},{128,144,160,176,192,208,224,240},{256,272,28..., dimensions={0} | all-to-all | bytes 65536 | tf_op jit(solution)/shard_map/all_to_all | solution.py:211
  347.6 6.6 %all_to_all.52.parts_ref = f32[4,8,128]{2,1,0:T(8,128)S(1)} all-to-all(f32[4,8,128]{2,1,0:T(8,128)S(1)} %get-tuple-element.276), channel_id=1, replica_groups={{0,128,256,384},{16,144,272,400},{32,160,288,416},{48,176,304,432},{64,..., dimensions={0} | all-to-all | bytes 32768 | tf_op jit(solution)/shard_map/all_to_all | solution.py:211
  354.5 20.9 %all_to_all.53.plan_ref = bf16[8,144,512]{2,1,0:T(8,128)(2,1)S(1)} all-to-all(bf16[8,144,512]{2,1,0:T(8,128)(2,1)S(1)} %shard_map.58), channel_id=1, replica_groups={{0,16,32,48,64,80,96,112},{128,144,160,176,192,208,224,240},{256,272,28..., dimensions={0} | all-to-all | bytes 2359296 | tf_op jit(solution)/shard_map/all_to_all | solution.py:211
  375.5 5.9 %shard_map.59 = (bf16[128,1024]{1,0:T(8,128)(2,1)}, f32[1,128]{1,0:T(1,128)}, f32[1,256]{1,0:T(1,128)}) custom-call(s32[4]{0:T(128)S(1)} %pad_add_fusion.place_ref, bf16[8,144,512]{2,1,0:T(8,128)(2,1)S(1)} %all_to_all.53.plan_ref, f32[8,128]{1,0:T(8,128)S(1)} %get-tuple-element.275.u_ref, bf16[4096,1024]{1,0:T(8,128)(2,1)} %all-gather.5.cloned.1.call-done.y_ref), custom_call_target="tpu_custom_call" | custom-call | tf_op jit(solution)/shard_map/pallas_call | solution.py:269
  (108 shorter events, 22.6 us)
Async XLA Ops:
  7.2 39.4 %all-gather.3.cloned.1.call-start = ((), (), s32[]{:S(2)}) async-start(), calls=%async_computation.9 | async-start | bytes 1310720 | tf_op jit(solution)/shard_map/all_gather | solution.py:213
  7.2 12.4 %collective-permute-start = (bf16[128,1024]{1,0:T(8,128)(2,1)}, bf16[128,1024]{1,0:T(8,128)(2,1)S(1)}, u32[]{:S(2)}, u32[]{:S(2)}) collective-permute-start(bf16[128,1024]{1,0:T(8,128)(2,1)} %param.2), channel_id=1, source_target_pairs={{0,32},{16,48},{32,64},{48,80},{64,96},{80,112},{96,0},{112,16},{1... | collective-permute-start | bytes 786440 | tf_op jit(solution)/shard_map/ppermute | solution.py:28
  11.2 223.4 %all-reduce.3.cloned.1.call-start = ((), (), s32[]{:S(2)}) async-start(), calls=%async_computation.11 | async-start | bytes 4194304 | tf_op jit(solution)/shard_map/psum | solution.py:229
  11.2 12.9 %collective-permute-start.1 = (bf16[128,1024]{1,0:T(8,128)(2,1)}, bf16[128,1024]{1,0:T(8,128)(2,1)S(1)}, u32[]{:S(2)}, u32[]{:S(2)}) collective-permute-start(bf16[128,1024]{1,0:T(8,128)(2,1)} %param.2), channel_id=1, source_target_pairs={{0,64},{16,80},{32,96},{48,112},{64,0},{80,16},{96,32},{112,48},{1... | collective-permute-start | bytes 786440 | tf_op jit(solution)/shard_map/ppermute | solution.py:28
  15.6 8.5 %collective-permute-start.2 = (bf16[128,1024]{1,0:T(8,128)(2,1)}, bf16[128,1024]{1,0:T(8,128)(2,1)S(1)}, u32[]{:S(2)}, u32[]{:S(2)}) collective-permute-start(bf16[128,1024]{1,0:T(8,128)(2,1)} %param.2), channel_id=1, source_target_pairs={{0,96},{16,112},{32,0},{48,16},{64,32},{80,48},{96,64},{112,80},{1... | collective-permute-start | bytes 786440 | tf_op jit(solution)/shard_map/ppermute | solution.py:28
  24.2 9.5 %collective-permute-start.3 = (bf16[512,1024]{1,0:T(8,128)(2,1)S(1)}, bf16[512,1024]{1,0:T(8,128)(2,1)S(1)}, u32[]{:S(2)}, u32[]{:S(2)}) collective-permute-start(bf16[512,1024]{1,0:T(8,128)(2,1)S(1)} %constant_dynamic-update-slice_fusion.x_here), channel_id=1, source_target_pairs={{0,16},{16,0},{32,48},{48,32},{64,80},{80,64},{96,112},{112,96},{1... | collective-permute-start | bytes 3145736 | tf_op jit(solution)/shard_map/ppermute | solution.py:28
  46.6 1.2 copy-start
  52.5 323.0 %all-gather.5.cloned.1.call-start = ((), (), s32[]{:S(2)}) async-start(), calls=%async_computation.10 | async-start | bytes 8650752 | tf_op jit(solution)/shard_map/all_gather | solution.py:268
  234.6 0.8 copy-start.1
  235.3 0.8 copy-start.2
  236.1 0.8 copy-start.3
  236.8 0.8 copy-start.4
  237.6 0.8 copy-start.5
  238.3 0.8 copy-start.6
  239.1 0.8 copy-start.7
  239.9 0.8 copy-start.8
  240.6 0.8 copy-start.9
  241.4 0.8 copy-start.10
  242.1 0.8 copy-start.11
  242.9 0.8 copy-start.12
  243.7 0.8 copy-start.13
  244.4 0.8 copy-start.14
  245.2 0.8 copy-start.15
  245.9 0.8 copy-start.16
  246.7 0.8 copy-start.17
  247.4 0.8 copy-start.18
  248.2 0.8 copy-start.19
  249.0 0.8 copy-start.20
  252.0 0.8 copy-start.24
  252.8 0.8 copy-start.25
  253.5 0.8 copy-start.26
  254.3 0.8 copy-start.27
  255.0 0.8 copy-start.28
  255.8 0.8 copy-start.29
  256.6 0.8 copy-start.30
  257.3 0.8 copy-start.31
  258.1 0.8 copy-start.32
  258.8 0.8 copy-start.33
  259.6 0.8 copy-start.34
  260.3 0.8 copy-start.35
  261.1 0.8 copy-start.36
  261.9 0.8 copy-start.37
  262.6 0.8 copy-start.38
  263.4 0.8 copy-start.39
  264.1 0.8 copy-start.40
  264.9 0.8 copy-start.41
  265.7 0.8 copy-start.42
  266.4 0.8 copy-start.43
  267.2 0.8 copy-start.44
  267.9 0.8 copy-start.45
  268.7 0.8 copy-start.46
  269.4 0.8 copy-start.47
  270.2 0.8 copy-start.48
  271.0 0.8 copy-start.49
  271.7 0.8 copy-start.50
  272.5 0.8 copy-start.51
  273.2 0.8 copy-start.52
  274.0 0.8 copy-start.53
  274.8 0.8 copy-start.54
  275.5 0.8 copy-start.55
  280.1 0.8 copy-start.61
  280.8 0.8 copy-start.62
  281.6 0.8 copy-start.63
  282.3 0.8 copy-start.64
  (8 other events, 6.1 us)
Sparse Core Ops, SparseCore 0:
  11.3 35.2 all-gather.2
  53.6 180.9 all-reduce.2
  238.2 67.6 all-gather.4

commit v2 on v1

--- a/solution.py
+++ b/solution.py
@@ -28,15 +28,19 @@
     return lax.ppermute(value, "noise", pairs)
 
 
-def send_z(value, dz):
+def send_z(value, ahead):
     size = lax.axis_size("dp")
-    return lax.ppermute(value, "dp", [(z, (z + dz) % size) for z in range(size)])
+    pairs = []
+    for n in range(YS * XS * CORES):
+        step = ahead if n % CORES == 0 else -ahead
+        pairs += [(n * size + z, n * size + (z + step) % size) for z in range(size)]
+    return lax.ppermute(value, ("noise", "dp"), pairs)
 
 
 def gather4(block, **axis):
     (name,) = axis
     before, after = send(block, **{name: 1}), send(block, **{name: -1})
-    return jnp.concatenate([block, before, send(block, **{name: 2}), after], axis=0)
+    return [block, before, send(block, **{name: 2}), after]
 
 
 def squares_row(block):
@@ -48,29 +52,42 @@
     return jnp.sum(jnp.where(row_at == column_at, column, 0.0), axis=0, keepdims=True)
 
 
-def partial_kernel(scale, place_ref, x_here, x_there, y_ref, *refs):
-    outs, (x_all, y_squares) = refs[:-2], refs[-2:]
-    rows = x_here.shape[0] // XS
-    high = outs[0].shape[0]
-    x, c = place_ref[2], place_ref[3]
+def partial_kernel(scale, place_ref, x_here, x_there, *refs):
+    ys, (own, ahead, back, ahead_rest, back_rest, x_all, y_all, y_squares, chunks) = refs[:YS], refs[YS:]
+    rows = ys[0].shape[0]
+    depth = chunks.shape[0]
+    high = rows // depth
+    z, y, x, c = place_ref[0], place_ref[1], place_ref[2], place_ref[3]
     for k in range(XS):
         at = lax.rem(x + XS - k, XS) * CORES
         block = slice(k * rows, (k + 1) * rows)
         x_all[at + c] = x_here[block, :]
         x_all[at + 1 - c] = x_there[block, :]
     for k in range(YS):
+        at = pl.multiple_of(lax.rem(y + YS - k, YS) * rows, rows)
+        y_all[pl.ds(at, rows), :] = ys[k][...]
+    for k in range(YS):
         block = slice(k * rows, (k + 1) * rows)
-        y_squares[:, block] = scale * squares_row(y_ref[block, :])
+        y_squares[:, block] = scale * squares_row(y_all[block, :])
     for k in range(XS * CORES):
         value = x_all[k]
         wide = value.astype(jnp.float32)
         x_squares = scale * jnp.sum(wide * wide, axis=1, keepdims=True)
         cross = lax.dot_general(
-            value, y_ref[...], (((1,), (1,)), ((), ())), preferred_element_type=jnp.float32
+            value, y_all[...], (((1,), (1,)), ((), ())), preferred_element_type=jnp.float32
         )
         value = (2.0 * scale) * cross - x_squares - y_squares[...]
-        for t in range(rows // high):
-            outs[k * (rows // high) + t][...] = value[t * high : (t + 1) * high]
+        for t in range(depth):
+            at = jnp.where(c == 0, lax.rem(t + depth - z, depth), lax.rem(z + depth - t, depth))
+            chunks[at, k * high : (k + 1) * high, :] = value[t * high : (t + 1) * high]
+    middle = depth // 2
+    own[...] = chunks[0]
+    ahead[...] = chunks[middle]
+    back[...] = chunks[middle + 1]
+    for k in range(1, middle):
+        ahead_rest[middle - 1 - k] = chunks[k]
+    for k in range(middle + 2, depth):
+        back_rest[k - middle - 2] = chunks[k]
 
 
 def joined(parts):
@@ -112,11 +129,17 @@
     copy_out(out_ref)
 
 
-def first_rows_kernel(*refs):
-    pieces, (a_ref, out_ref) = refs[:-2], refs[-2:]
-    high = pieces[0].shape[0]
-    for k, piece in enumerate(pieces):
-        a_ref[k * high : (k + 1) * high, :] = piece[...]
+def first_rows_kernel(place_ref, *refs):
+    chunks, (a_ref, out_ref) = refs[:-2], refs[-2:]
+    blocks, n = out_ref.shape[1:]
+    depth = len(chunks)
+    high = n // depth
+    z, c = place_ref[0], place_ref[3]
+    for k, chunk in enumerate(chunks):
+        at = jnp.where(c == 0, lax.rem(z + k, depth), lax.rem(z + depth - k, depth)) * high
+        for block in range(blocks):
+            to = pl.ds(pl.multiple_of(block * n + at, high), high)
+            a_ref[to, :] = chunk[block * high : (block + 1) * high, :]
     row_sums(a_ref, None, out_ref)
 
 
@@ -201,8 +224,6 @@
     log_weight = -math.log2(tokens)
     f32 = jnp.float32
 
-    x_here = gather4(noise_rows, dx=1)
-    x_there = send(x_here, dc=1)
     group = XS * CORES
     y_groups = [[y * group + k for y in range(YS)] for k in range(group)]
     x_groups = [[y * group + k for k in range(group)] for y in range(YS)]
@@ -210,33 +231,60 @@
     def swap(value, groups):
         return lax.all_to_all(value, "noise", 0, 0, axis_index_groups=groups, tiled=True)
 
-    y_near = lax.all_gather(data_rows, "noise", axis_index_groups=y_groups, tiled=True)
+    xs, ys = lax.optimization_barrier((gather4(noise_rows, dx=1), gather4(data_rows, dy=1)))
+    x_here = jnp.concatenate(xs, axis=0)
+    x_there = send(x_here, dc=1)
     tall, wide = group * rows, YS * rows
-    high = 16
-    partial_value = pl.pallas_call(
+    middle = depth // 2
+    chunk = (tall // depth, wide)
+    own, ahead, back, ahead_rest, back_rest = pl.pallas_call(
         functools.partial(partial_kernel, LOG2E / (epsilon * D)),
-        out_shape=[jax.ShapeDtypeStruct((high, wide), f32)] * (tall // high),
-        in_specs=[SMEM] + [VMEM] * 3,
-        out_specs=[VMEM] * (tall // high),
+        out_shape=[
+            jax.ShapeDtypeStruct(chunk, f32),
+            jax.ShapeDtypeStruct(chunk, f32),
+            jax.ShapeDtypeStruct(chunk, f32),
+            jax.ShapeDtypeStruct((middle - 1,) + chunk, f32),
+            jax.ShapeDtypeStruct((middle - 2,) + chunk, f32),
+        ],
+        in_specs=[SMEM] + [VMEM] * (2 + YS),
+        out_specs=[VMEM] * 5,
         scratch_shapes=[
             pltpu.VMEM((group, rows, features), jnp.bfloat16),
+            pltpu.VMEM((YS * rows, features), jnp.bfloat16),
             pltpu.VMEM((1, wide), f32),
+            pltpu.VMEM((depth,) + chunk, f32),
         ],
         compiler_params=PARAMS,
-    )(place, x_here, x_there, y_near)
-    late_rows, partial_value = lax.optimization_barrier((data_rows, partial_value))
-
-    pieces = lax.psum(partial_value, "dp")
+    )(place, x_here, x_there, *ys)
+    late_rows, own = lax.optimization_barrier((data_rows, own))
+
+    for step in range(middle):
+        ahead = send_z(ahead, 1)
+        if step < middle - 1:
+            ahead = ahead + ahead_rest[step]
+            back = send_z(back, -1)
+            if step < middle - 2:
+                back = back + back_rest[step]
+    own = own + ahead + back
+
+    chunks = [own] * depth
+    ahead, back = own, own
+    for step in range(1, middle + 1):
+        ahead = send_z(ahead, 1)
+        chunks[depth - step] = ahead
+        if step < middle:
+            back = send_z(back, -1)
+            chunks[step] = back
     row_shape = jax.ShapeDtypeStruct((group, group, rows), f32)
     column_shape = jax.ShapeDtypeStruct((YS, 2 * YS, rows), f32)
     u_shape = jax.ShapeDtypeStruct((group, rows), f32)
     a, part = pl.pallas_call(
         first_rows_kernel,
         out_shape=[jax.ShapeDtypeStruct((tall, wide), f32), row_shape],
-        in_specs=[VMEM] * (tall // high),
+        in_specs=[SMEM] + [VMEM] * depth,
         out_specs=[VMEM] * 2,
         compiler_params=PARAMS,
-    )(*pieces)
+    )(place, *chunks)
     for step in range(ITERS):
         if step > 0:
             part = pl.pallas_call(

time: 393 us -> 298 us (0.76)
  waiting for transfers between devices: 202 us -> 19 us
  starting transfers between devices: 18.7 us -> 139 us
  local copies, waits for them, and re-layouts: 50.7 us -> 5.87 us
  blocking collectives: 86.3 us -> 99.8 us
    psum x1 -> x0, waiting for transfers between devices: 181 us -> none  [on_device(): pieces = lax.psum(partial_value, 'dp')]
    ppermute x0 -> x30, starting transfers between devices: none -> 111 us  [send_z(): return lax.ppermute(value, ('noise', 'dp'), pairs)]
    unnamed x133 -> x25, local copies, waits for them, and re-layouts: 50.7 us -> 5.85 us
    all_to_all x9, blocking collectives: 86.3 us -> 99.8 us  [swap(): lax.all_to_all(value, 'noise', 0, 0, axis_index_groups=groups, tiled=True)]
    all_gather x1 -> x0, waiting for transfers between devices: 12.9 us -> none  [on_device(): lax.all_gather(data_rows, 'noise', axis_index_groups=y_groups, tiled=True)]
    ppermute x0 -> x30, waiting for transfers between devices: none -> 9.96 us  [send_z(): return lax.ppermute(value, ('noise', 'dp'), pairs)]
    ppermute x4 -> x7, starting transfers between devices: 18.6 us -> 27.9 us  [send(): return lax.ppermute(value, 'noise', pairs)]
    ppermute x4 -> x7, waiting for transfers between devices: 6.56 us -> 9.02 us  [send(): return lax.ppermute(value, 'noise', pairs)]
  transfers between devices with their start and end apart: 7 -> 38, of which waited for: 4 -> 18; matrix products, arithmetic and copies ran while one was open for 0% -> 1% of each run, Pallas kernels for 2% -> 2%
where the time goes in v2:
time: 298 us; the launch traced here: 296 us
  starting transfers between devices  139 us (47%)
  blocking collectives  99.8 us (33%)
  waiting for transfers between devices  19 us (6%)
  Pallas kernels  16.4 us (6%)
  between operations  14.6 us (5%)
  local copies, waits for them, and re-layouts  5.87 us (2%)
    ppermute x30, starting transfers between devices, send_z(): return lax.ppermute(value, ('noise', 'dp'), pairs)  111 us
    all_to_all x9, blocking collectives, swap(): lax.all_to_all(value, 'noise', 0, 0, axis_index_groups=groups, tiled=True)  99.8 us
    ppermute x7, starting transfers between devices, send(): return lax.ppermute(value, 'noise', pairs)  27.9 us
    ppermute x30, waiting for transfers between devices, send_z(): return lax.ppermute(value, ('noise', 'dp'), pairs)  9.96 us
    ppermute x7, waiting for transfers between devices, send(): return lax.ppermute(value, 'noise', pairs)  9.02 us
  transfers between devices with their start and end apart: 38, of which 18 were waited for; matrix products, arithmetic and copies ran while one was open for 1% of the time, Pallas kernels for 2%

profile of v2, /device:TPU:1, one launch (start us, length us, event | category | flops | bytes accessed | tf_op | source)
XLA Modules:
  0.0 296.5 jit_solution(6993491779770196426)
XLA Ops:
  7.2 4.1 %collective-permute-start = (bf16[128,1024]{1,0:T(8,128)(2,1)}, bf16[128,1024]{1,0:T(8,128)(2,1)S(1)}, u32[]{:S(2)}, u32[]{:S(2)}) collective-permute-start(bf16[128,1024]{1,0:T(8,128)(2,1)} %param.2), channel_id=1, source_target_pairs={{0,32},{16,48},{32,64},{48,80},{64,96},{80,112},{96,0},{112,16},{1... | collective-permute-start | bytes 786440 | tf_op jit(solution)/shard_map/ppermute | solution.py:28
  11.3 4.4 %collective-permute-start.1 = (bf16[128,1024]{1,0:T(8,128)(2,1)}, bf16[128,1024]{1,0:T(8,128)(2,1)S(1)}, u32[]{:S(2)}, u32[]{:S(2)}) collective-permute-start(bf16[128,1024]{1,0:T(8,128)(2,1)} %param.2), channel_id=1, source_target_pairs={{0,64},{16,80},{32,96},{48,112},{64,0},{80,16},{96,32},{112,48},{1... | collective-permute-start | bytes 786440 | tf_op jit(solution)/shard_map/ppermute | solution.py:28
  15.7 3.1 %collective-permute-start.2 = (bf16[128,1024]{1,0:T(8,128)(2,1)}, bf16[128,1024]{1,0:T(8,128)(2,1)S(1)}, u32[]{:S(2)}, u32[]{:S(2)}) collective-permute-start(bf16[128,1024]{1,0:T(8,128)(2,1)} %param.2), channel_id=1, source_target_pairs={{0,96},{16,112},{32,0},{48,16},{64,32},{80,48},{96,64},{112,80},{1... | collective-permute-start | bytes 786440 | tf_op jit(solution)/shard_map/ppermute | solution.py:28
  18.7 3.2 %collective-permute-start.3 = (bf16[128,1024]{1,0:T(8,128)(2,1)}, bf16[128,1024]{1,0:T(8,128)(2,1)S(1)}, u32[]{:S(2)}, u32[]{:S(2)}) collective-permute-start(bf16[128,1024]{1,0:T(8,128)(2,1)} %refs_0_), channel_id=1, source_target_pairs={{0,128},{16,144},{32,160},{48,176},{64,192},{80,208},{96,224},{112... | collective-permute-start | bytes 786440 | tf_op jit(solution)/shard_map/ppermute | solution.py:28
  22.0 4.5 %collective-permute-start.4 = (bf16[128,1024]{1,0:T(8,128)(2,1)}, bf16[128,1024]{1,0:T(8,128)(2,1)S(1)}, u32[]{:S(2)}, u32[]{:S(2)}) collective-permute-start(bf16[128,1024]{1,0:T(8,128)(2,1)} %refs_0_), channel_id=1, source_target_pairs={{0,256},{16,272},{32,288},{48,304},{64,320},{80,336},{96,352},{112... | collective-permute-start | bytes 786440 | tf_op jit(solution)/shard_map/ppermute | solution.py:28
  26.5 3.0 %collective-permute-start.5 = (bf16[128,1024]{1,0:T(8,128)(2,1)}, bf16[128,1024]{1,0:T(8,128)(2,1)S(1)}, u32[]{:S(2)}, u32[]{:S(2)}) collective-permute-start(bf16[128,1024]{1,0:T(8,128)(2,1)} %refs_0_), channel_id=1, source_target_pairs={{0,384},{16,400},{32,416},{48,432},{64,448},{80,464},{96,480},{112... | collective-permute-start | bytes 786440 | tf_op jit(solution)/shard_map/ppermute | solution.py:28
  29.5 5.7 %collective-permute-done.4.refs_2_ = bf16[128,1024]{1,0:T(8,128)(2,1)S(1)} collective-permute-done((bf16[128,1024]{1,0:T(8,128)(2,1)}, bf16[128,1024]{1,0:T(8,128)(2,1)S(1)}, u32[]{:S(2)}, u32[]{:S(2)}) %collective-permute-start.4) | collective-permute-done | bytes 262176 | tf_op jit(solution)/shard_map/ppermute | solution.py:28
  35.2 1.1 collective-permute-done.5.refs_3_
  36.4 1.1 constant_dynamic-update-slice_fusion.3
  37.5 5.7 %collective-permute-start.6 = (bf16[512,1024]{1,0:T(8,128)(2,1)S(1)}, bf16[512,1024]{1,0:T(8,128)(2,1)S(1)}, u32[]{:S(2)}, u32[]{:S(2)}) collective-permute-start(bf16[512,1024]{1,0:T(8,128)(2,1)S(1)} %constant_dynamic-update-slice_fusion.x_here), channel_id=1, source_target_pairs={{0,16},{16,0},{32,48},{48,32},{64,80},{80,64},{96,112},{112,96},{1... | collective-permute-start | bytes 3145736 | tf_op jit(solution)/shard_map/ppermute | solution.py:28
  43.4 2.1 collective-permute-done.6.x_there
  45.5 0.9 copy-done.4
  46.5 0.9 copy-done.6
  47.4 3.9 %shard_map.49 = (f32[64,512]{1,0:T(8,128)S(1)}, f32[64,512]{1,0:T(8,128)S(1)}, f32[64,512]{1,0:T(8,128)S(1)}, f32[7,64,512]{2,1,0:T(8,128)S(1)}, f32[6,64,512]{2,1,0:T(8,128)S(1)}) custom-call(s32[4]{0:T(128)S(1)} %pad_add_fusion.place_ref, bf16[512,1024]{1,0:T(8,128)(2,1)S(1)} %constant_dynamic-update-slice_fusion.x_here, ...), custom_call_target="tpu_custom_call" | custom-call | tf_op jit(solution)/shard_map/pallas_call | solution.py:240
  51.3 0.9 copy-done.1
  54.2 10.0 %collective-permute-start.7 = (f32[64,512]{1,0:T(8,128)}, f32[64,512]{1,0:T(8,128)S(1)}, u32[]{:S(2)}, u32[]{:S(2)}) collective-permute-start(f32[64,512]{1,0:T(8,128)} %copy-done.10), channel_id=1, source_target_pairs={{0,1},{1,2},{2,3},{3,4},{4,5},{5,6},{6,7},{7,8},{8,9},{9,10},{10,1... | collective-permute-start | bytes 393224 | tf_op jit(solution)/shard_map/ppermute | solution.py:37
  64.2 1.9 collective-permute-start.15
  66.5 4.9 %collective-permute-start.8 = (f32[64,512]{1,0:T(8,128)S(1)}, f32[64,512]{1,0:T(8,128)S(1)}, u32[]{:S(2)}, u32[]{:S(2)}) collective-permute-start(f32[64,512]{1,0:T(8,128)S(1)} %bitcast_add_fusion.12), channel_id=1, source_target_pairs={{0,1},{1,2},{2,3},{3,4},{4,5},{5,6},{6,7},{7,8},{8,9},{9,10},{10,1... | collective-permute-start | bytes 393224 | tf_op jit(solution)/shard_map/ppermute | solution.py:37
  71.4 0.9 bitcast_add_fusion.5
  72.3 2.1 collective-permute-start.16
  74.4 4.6 %collective-permute-start.9 = (f32[64,512]{1,0:T(8,128)S(1)}, f32[64,512]{1,0:T(8,128)S(1)}, u32[]{:S(2)}, u32[]{:S(2)}) collective-permute-start(f32[64,512]{1,0:T(8,128)S(1)} %bitcast_add_fusion.11), channel_id=1, source_target_pairs={{0,1},{1,2},{2,3},{3,4},{4,5},{5,6},{6,7},{7,8},{8,9},{9,10},{10,1... | collective-permute-start | bytes 393224 | tf_op jit(solution)/shard_map/ppermute | solution.py:37
  79.4 0.9 bitcast_add_fusion.4
  80.3 1.9 collective-permute-start.17
  82.3 4.6 %collective-permute-start.10 = (f32[64,512]{1,0:T(8,128)S(1)}, f32[64,512]{1,0:T(8,128)S(1)}, u32[]{:S(2)}, u32[]{:S(2)}) collective-permute-start(f32[64,512]{1,0:T(8,128)S(1)} %bitcast_add_fusion.10), channel_id=1, source_target_pairs={{0,1},{1,2},{2,3},{3,4},{4,5},{5,6},{6,7},{7,8},{8,9},{9,10},{10,1... | collective-permute-start | bytes 393224 | tf_op jit(solution)/shard_map/ppermute | solution.py:37
  87.3 1.9 collective-permute-start.18
  89.2 4.6 %collective-permute-start.11 = (f32[64,512]{1,0:T(8,128)S(1)}, f32[64,512]{1,0:T(8,128)S(1)}, u32[]{:S(2)}, u32[]{:S(2)}) collective-permute-start(f32[64,512]{1,0:T(8,128)S(1)} %bitcast_add_fusion.9), channel_id=1, source_target_pairs={{0,1},{1,2},{2,3},{3,4},{4,5},{5,6},{6,7},{7,8},{8,9},{9,10},{10,1... | collective-permute-start | bytes 393224 | tf_op jit(solution)/shard_map/ppermute | solution.py:37
  94.2 1.9 collective-permute-start.19
  96.8 5.0 %collective-permute-start.12 = (f32[64,512]{1,0:T(8,128)S(1)}, f32[64,512]{1,0:T(8,128)S(1)}, u32[]{:S(2)}, u32[]{:S(2)}) collective-permute-start(f32[64,512]{1,0:T(8,128)S(1)} %bitcast_add_fusion.8), channel_id=1, source_target_pairs={{0,1},{1,2},{2,3},{3,4},{4,5},{5,6},{6,7},{7,8},{8,9},{9,10},{10,1... | collective-permute-start | bytes 393224 | tf_op jit(solution)/shard_map/ppermute | solution.py:37
  102.2 1.9 collective-permute-start.20
  104.4 5.3 %collective-permute-start.13 = (f32[64,512]{1,0:T(8,128)S(1)}, f32[64,512]{1,0:T(8,128)S(1)}, u32[]{:S(2)}, u32[]{:S(2)}) collective-permute-start(f32[64,512]{1,0:T(8,128)S(1)} %bitcast_add_fusion.7), channel_id=1, source_target_pairs={{0,1},{1,2},{2,3},{3,4},{4,5},{5,6},{6,7},{7,8},{8,9},{9,10},{10,1... | collective-permute-start | bytes 393224 | tf_op jit(solution)/shard_map/ppermute | solution.py:37
  110.1 1.9 collective-permute-start.21
  112.1 5.0 %collective-permute-start.14 = (f32[64,512]{1,0:T(8,128)S(1)}, f32[64,512]{1,0:T(8,128)S(1)}, u32[]{:S(2)}, u32[]{:S(2)}) collective-permute-start(f32[64,512]{1,0:T(8,128)S(1)} %bitcast_add_fusion.6), channel_id=1, source_target_pairs={{0,1},{1,2},{2,3},{3,4},{4,5},{5,6},{6,7},{7,8},{8,9},{9,10},{10,1... | collective-permute-start | bytes 393224 | tf_op jit(solution)/shard_map/ppermute | solution.py:37
  117.4 1.5 collective-permute-done.14
  119.0 5.4 %collective-permute-start.29 = (f32[64,512]{1,0:T(8,128)S(1)}, f32[64,512]{1,0:T(8,128)S(1)}, u32[]{:S(2)}, u32[]{:S(2)}) collective-permute-start(f32[64,512]{1,0:T(8,128)S(1)} %add_add_fusion.refs_0_), channel_id=1, source_target_pairs={{0,1},{1,2},{2,3},{3,4},{4,5},{5,6},{6,7},{7,8},{8,9},{9,10},{10,1... | collective-permute-start | bytes 393224 | tf_op jit(solution)/shard_map/ppermute | solution.py:37
  124.4 1.9 collective-permute-start.22
  126.3 5.0 %collective-permute-start.30 = (f32[64,512]{1,0:T(8,128)S(1)}, f32[64,512]{1,0:T(8,128)S(1)}, u32[]{:S(2)}, u32[]{:S(2)}) collective-permute-start(f32[64,512]{1,0:T(8,128)S(1)} %collective-permute-done.29.refs_15_), channel_id=1, source_target_pairs={{0,1},{1,2},{2,3},{3,4},{4,5},{5,6},{6,7},{7,8},{8,9},{9,10},{10,1... | collective-permute-start | bytes 393224 | tf_op jit(solution)/shard_map/ppermute | solution.py:37
  131.3 1.9 collective-permute-start.23
  133.2 5.0 %collective-permute-start.31 = (f32[64,512]{1,0:T(8,128)S(1)}, f32[64,512]{1,0:T(8,128)S(1)}, u32[]{:S(2)}, u32[]{:S(2)}) collective-permute-start(f32[64,512]{1,0:T(8,128)S(1)} %collective-permute-done.30.refs_14_), channel_id=1, source_target_pairs={{0,1},{1,2},{2,3},{3,4},{4,5},{5,6},{6,7},{7,8},{8,9},{9,10},{10,1... | collective-permute-start | bytes 393224 | tf_op jit(solution)/shard_map/ppermute | solution.py:37
  138.2 1.9 collective-permute-start.24
  140.2 5.0 %collective-permute-start.32 = (f32[64,512]{1,0:T(8,128)S(1)}, f32[64,512]{1,0:T(8,128)S(1)}, u32[]{:S(2)}, u32[]{:S(2)}) collective-permute-start(f32[64,512]{1,0:T(8,128)S(1)} %collective-permute-done.31.refs_13_), channel_id=1, source_target_pairs={{0,1},{1,2},{2,3},{3,4},{4,5},{5,6},{6,7},{7,8},{8,9},{9,10},{10,1... | collective-permute-start | bytes 393224 | tf_op jit(solution)/shard_map/ppermute | solution.py:37
  145.1 1.9 collective-permute-start.25
  147.1 5.0 %collective-permute-start.33 = (f32[64,512]{1,0:T(8,128)S(1)}, f32[64,512]{1,0:T(8,128)S(1)}, u32[]{:S(2)}, u32[]{:S(2)}) collective-permute-start(f32[64,512]{1,0:T(8,128)S(1)} %collective-permute-done.32.refs_12_), channel_id=1, source_target_pairs={{0,1},{1,2},{2,3},{3,4},{4,5},{5,6},{6,7},{7,8},{8,9},{9,10},{10,1... | collective-permute-start | bytes 393224 | tf_op jit(solution)/shard_map/ppermute | solution.py:37
  152.3 1.9 collective-permute-start.26
  154.2 4.9 %collective-permute-start.34 = (f32[64,512]{1,0:T(8,128)S(1)}, f32[64,512]{1,0:T(8,128)S(1)}, u32[]{:S(2)}, u32[]{:S(2)}) collective-permute-start(f32[64,512]{1,0:T(8,128)S(1)} %collective-permute-done.33.refs_11_), channel_id=1, source_target_pairs={{0,1},{1,2},{2,3},{3,4},{4,5},{5,6},{6,7},{7,8},{8,9},{9,10},{10,1... | collective-permute-start | bytes 393224 | tf_op jit(solution)/shard_map/ppermute | solution.py:37
  159.1 1.7 collective-permute-done.26.refs_5_
  160.8 1.9 collective-permute-start.27
  162.8 4.9 %collective-permute-start.35 = (f32[64,512]{1,0:T(8,128)S(1)}, f32[64,512]{1,0:T(8,128)S(1)}, u32[]{:S(2)}, u32[]{:S(2)}) collective-permute-start(f32[64,512]{1,0:T(8,128)S(1)} %collective-permute-done.34.refs_10_), channel_id=1, source_target_pairs={{0,1},{1,2},{2,3},{3,4},{4,5},{5,6},{6,7},{7,8},{8,9},{9,10},{10,1... | collective-permute-start | bytes 393224 | tf_op jit(solution)/shard_map/ppermute | solution.py:37
  167.6 1.0 collective-permute-done.27.refs_6_
  168.6 1.9 collective-permute-start.28
  170.5 4.9 %collective-permute-start.36 = (f32[64,512]{1,0:T(8,128)S(1)}, f32[64,512]{1,0:T(8,128)S(1)}, u32[]{:S(2)}, u32[]{:S(2)}) collective-permute-start(f32[64,512]{1,0:T(8,128)S(1)} %collective-permute-done.35.refs_9_), channel_id=1, source_target_pairs={{0,1},{1,2},{2,3},{3,4},{4,5},{5,6},{6,7},{7,8},{8,9},{9,10},{10,1... | collective-permute-start | bytes 393224 | tf_op jit(solution)/shard_map/ppermute | solution.py:37
  175.5 1.8 collective-permute-done.36.refs_8_
  177.3 1.2 shard_map.50
  178.6 23.8 %all_to_all.45.parts_ref = f32[8,8,128]{2,1,0:T(8,128)S(1)} all-to-all(f32[8,8,128]{2,1,0:T(8,128)S(1)} %get-tuple-element.43), channel_id=1, replica_groups={{0,16,32,48,64,80,96,112},{128,144,160,176,192,208,224,240},{256,272,28..., dimensions={0} | all-to-all | bytes 65536 | tf_op jit(solution)/shard_map/all_to_all | solution.py:232
  202.4 0.9 shard_map.51
  203.2 8.2 %all_to_all.46.parts_ref = f32[4,8,128]{2,1,0:T(8,128)S(1)} all-to-all(f32[4,8,128]{2,1,0:T(8,128)S(1)} %get-tuple-element.44), channel_id=1, replica_groups={{0,128,256,384},{16,144,272,400},{32,160,288,416},{48,176,304,432},{64,..., dimensions={0} | all-to-all | bytes 32768 | tf_op jit(solution)/shard_map/all_to_all | solution.py:232
  212.1 9.2 %all_to_all.47.parts_ref = f32[8,8,128]{2,1,0:T(8,128)S(1)} all-to-all(f32[8,8,128]{2,1,0:T(8,128)S(1)} %shard_map.52), channel_id=1, replica_groups={{0,16,32,48,64,80,96,112},{128,144,160,176,192,208,224,240},{256,272,28..., dimensions={0} | all-to-all | bytes 65536 | tf_op jit(solution)/shard_map/all_to_all | solution.py:232
  221.3 0.9 shard_map.53
  222.2 6.5 %all_to_all.48.parts_ref = f32[4,8,128]{2,1,0:T(8,128)S(1)} all-to-all(f32[4,8,128]{2,1,0:T(8,128)S(1)} %get-tuple-element.45), channel_id=1, replica_groups={{0,128,256,384},{16,144,272,400},{32,160,288,416},{48,176,304,432},{64,..., dimensions={0} | all-to-all | bytes 32768 | tf_op jit(solution)/shard_map/all_to_all | solution.py:232
  229.4 9.0 %all_to_all.49.parts_ref = f32[8,8,128]{2,1,0:T(8,128)S(1)} all-to-all(f32[8,8,128]{2,1,0:T(8,128)S(1)} %shard_map.54), channel_id=1, replica_groups={{0,16,32,48,64,80,96,112},{128,144,160,176,192,208,224,240},{256,272,28..., dimensions={0} | all-to-all | bytes 65536 | tf_op jit(solution)/shard_map/all_to_all | solution.py:232
  239.2 6.5 %all_to_all.50.parts_ref = f32[4,8,128]{2,1,0:T(8,128)S(1)} all-to-all(f32[4,8,128]{2,1,0:T(8,128)S(1)} %get-tuple-element.46), channel_id=1, replica_groups={{0,128,256,384},{16,144,272,400},{32,160,288,416},{48,176,304,432},{64,..., dimensions={0} | all-to-all | bytes 32768 | tf_op jit(solution)/shard_map/all_to_all | solution.py:232
  246.4 9.0 %all_to_all.51.parts_ref = f32[8,8,128]{2,1,0:T(8,128)S(1)} all-to-all(f32[8,8,128]{2,1,0:T(8,128)S(1)} %shard_map.56), channel_id=1, replica_groups={{0,16,32,48,64,80,96,112},{128,144,160,176,192,208,224,240},{256,272,28..., dimensions={0} | all-to-all | bytes 65536 | tf_op jit(solution)/shard_map/all_to_all | solution.py:232
  255.9 6.6 %all_to_all.52.parts_ref = f32[4,8,128]{2,1,0:T(8,128)S(1)} all-to-all(f32[4,8,128]{2,1,0:T(8,128)S(1)} %get-tuple-element.48), channel_id=1, replica_groups={{0,128,256,384},{16,144,272,400},{32,160,288,416},{48,176,304,432},{64,..., dimensions={0} | all-to-all | bytes 32768 | tf_op jit(solution)/shard_map/all_to_all | solution.py:232
  262.8 20.9 %all_to_all.53.plan_ref = bf16[8,144,512]{2,1,0:T(8,128)(2,1)S(1)} all-to-all(bf16[8,144,512]{2,1,0:T(8,128)(2,1)S(1)} %shard_map.58), channel_id=1, replica_groups={{0,16,32,48,64,80,96,112},{128,144,160,176,192,208,224,240},{256,272,28..., dimensions={0} | all-to-all | bytes 2359296 | tf_op jit(solution)/shard_map/all_to_all | solution.py:232
  283.8 5.9 %shard_map.59 = (bf16[128,1024]{1,0:T(8,128)(2,1)}, f32[1,128]{1,0:T(1,128)}, f32[1,256]{1,0:T(1,128)}) custom-call(s32[4]{0:T(128)S(1)} %pad_add_fusion.place_ref, bf16[8,144,512]{2,1,0:T(8,128)(2,1)S(1)} %all_to_all.53.plan_ref, f32[8,128]{1,0:T(8,128)S(1)} %get-tuple-element.47.u_ref, bf16[4096,1024]{1,0:T(8,128)(2,1)} %all-gather.2.cloned.1.call-done.y_ref), custom_call_target="tpu_custom_call" | custom-call | tf_op jit(solution)/shard_map/pallas_call | solution.py:317
  (74 shorter events, 10.0 us)
Async XLA Ops:
  7.2 38.3 %copy-start = (bf16[128,1024]{1,0:T(8,128)(2,1)S(1)}, bf16[128,1024]{1,0:T(8,128)(2,1)}, u32[]{:S(2)}) copy-start(bf16[128,1024]{1,0:T(8,128)(2,1)} %refs_0_) | copy-start | bytes 786436
  7.2 276.6 %all-gather.2.cloned.1.call-start = ((), (), s32[]{:S(2)}) async-start(), calls=%async_computation.9 | async-start | bytes 8650752 | tf_op jit(solution)/shard_map/all_gather | solution.py:316
  7.2 19.3 %collective-permute-start = (bf16[128,1024]{1,0:T(8,128)(2,1)}, bf16[128,1024]{1,0:T(8,128)(2,1)S(1)}, u32[]{:S(2)}, u32[]{:S(2)}) collective-permute-start(bf16[128,1024]{1,0:T(8,128)(2,1)} %param.2), channel_id=1, source_target_pairs={{0,32},{16,48},{32,64},{48,80},{64,96},{80,112},{96,0},{112,16},{1... | collective-permute-start | bytes 786440 | tf_op jit(solution)/shard_map/ppermute | solution.py:28
  11.3 18.2 %collective-permute-start.1 = (bf16[128,1024]{1,0:T(8,128)(2,1)}, bf16[128,1024]{1,0:T(8,128)(2,1)S(1)}, u32[]{:S(2)}, u32[]{:S(2)}) collective-permute-start(bf16[128,1024]{1,0:T(8,128)(2,1)} %param.2), channel_id=1, source_target_pairs={{0,64},{16,80},{32,96},{48,112},{64,0},{80,16},{96,32},{112,48},{1... | collective-permute-start | bytes 786440 | tf_op jit(solution)/shard_map/ppermute | solution.py:28
  15.7 13.8 %collective-permute-start.2 = (bf16[128,1024]{1,0:T(8,128)(2,1)}, bf16[128,1024]{1,0:T(8,128)(2,1)S(1)}, u32[]{:S(2)}, u32[]{:S(2)}) collective-permute-start(bf16[128,1024]{1,0:T(8,128)(2,1)} %param.2), channel_id=1, source_target_pairs={{0,96},{16,112},{32,0},{48,16},{64,32},{80,48},{96,64},{112,80},{1... | collective-permute-start | bytes 786440 | tf_op jit(solution)/shard_map/ppermute | solution.py:28
  18.7 10.8 %collective-permute-start.3 = (bf16[128,1024]{1,0:T(8,128)(2,1)}, bf16[128,1024]{1,0:T(8,128)(2,1)S(1)}, u32[]{:S(2)}, u32[]{:S(2)}) collective-permute-start(bf16[128,1024]{1,0:T(8,128)(2,1)} %refs_0_), channel_id=1, source_target_pairs={{0,128},{16,144},{32,160},{48,176},{64,192},{80,208},{96,224},{112... | collective-permute-start | bytes 786440 | tf_op jit(solution)/shard_map/ppermute | solution.py:28
  22.0 13.3 %collective-permute-start.4 = (bf16[128,1024]{1,0:T(8,128)(2,1)}, bf16[128,1024]{1,0:T(8,128)(2,1)S(1)}, u32[]{:S(2)}, u32[]{:S(2)}) collective-permute-start(bf16[128,1024]{1,0:T(8,128)(2,1)} %refs_0_), channel_id=1, source_target_pairs={{0,256},{16,272},{32,288},{48,304},{64,320},{80,336},{96,352},{112... | collective-permute-start | bytes 786440 | tf_op jit(solution)/shard_map/ppermute | solution.py:28
  26.5 9.9 %collective-permute-start.5 = (bf16[128,1024]{1,0:T(8,128)(2,1)}, bf16[128,1024]{1,0:T(8,128)(2,1)S(1)}, u32[]{:S(2)}, u32[]{:S(2)}) collective-permute-start(bf16[128,1024]{1,0:T(8,128)(2,1)} %refs_0_), channel_id=1, source_target_pairs={{0,384},{16,400},{32,416},{48,432},{64,448},{80,464},{96,480},{112... | collective-permute-start | bytes 786440 | tf_op jit(solution)/shard_map/ppermute | solution.py:28
  35.2 8.1 %copy-start.3 = (bf16[128,1024]{1,0:T(8,128)(2,1)}, bf16[128,1024]{1,0:T(8,128)(2,1)S(1)}, u32[]{:S(2)}) copy-start(bf16[128,1024]{1,0:T(8,128)(2,1)S(1)} %collective-permute-done.4.refs_2_) | copy-start | bytes 786436
  36.4 7.0 %copy-start.5 = (bf16[128,1024]{1,0:T(8,128)(2,1)}, bf16[128,1024]{1,0:T(8,128)(2,1)S(1)}, u32[]{:S(2)}) copy-start(bf16[128,1024]{1,0:T(8,128)(2,1)S(1)} %collective-permute-done.5.refs_3_) | copy-start | bytes 786436
  37.5 8.0 %collective-permute-start.6 = (bf16[512,1024]{1,0:T(8,128)(2,1)S(1)}, bf16[512,1024]{1,0:T(8,128)(2,1)S(1)}, u32[]{:S(2)}, u32[]{:S(2)}) collective-permute-start(bf16[512,1024]{1,0:T(8,128)(2,1)S(1)} %constant_dynamic-update-slice_fusion.x_here), channel_id=1, source_target_pairs={{0,16},{16,0},{32,48},{48,32},{64,80},{80,64},{96,112},{112,96},{1... | collective-permute-start | bytes 3145736 | tf_op jit(solution)/shard_map/ppermute | solution.py:28
  45.5 1.0 copy-start.4
  46.5 0.9 copy-start.6
  51.3 0.9 copy-start.1
  52.2 0.7 copy-start.7
  52.8 0.7 copy-start.9
  53.5 0.7 copy-start.10
  54.2 33.1 %copy-start.2 = (f32[6,64,512]{2,1,0:T(8,128)S(1)}, f32[6,64,512]{2,1,0:T(8,128)}, u32[]{:S(2)}) copy-start(f32[6,64,512]{2,1,0:T(8,128)} %copy-done.1) | copy-start | bytes 2359300
  54.2 12.3 %collective-permute-start.7 = (f32[64,512]{1,0:T(8,128)}, f32[64,512]{1,0:T(8,128)S(1)}, u32[]{:S(2)}, u32[]{:S(2)}) collective-permute-start(f32[64,512]{1,0:T(8,128)} %copy-done.10), channel_id=1, source_target_pairs={{0,1},{1,2},{2,3},{3,4},{4,5},{5,6},{6,7},{7,8},{8,9},{9,10},{10,1... | collective-permute-start | bytes 393224 | tf_op jit(solution)/shard_map/ppermute | solution.py:37
  64.2 7.2 %collective-permute-start.15 = (f32[64,512]{1,0:T(8,128)}, f32[64,512]{1,0:T(8,128)S(1)}, u32[]{:S(2)}, u32[]{:S(2)}) collective-permute-start(f32[64,512]{1,0:T(8,128)} %copy-done.9), channel_id=1, source_target_pairs={{0,15},{1,0},{2,1},{3,2},{4,3},{5,4},{6,5},{7,6},{8,7},{9,8},{10,9... | collective-permute-start | bytes 393224 | tf_op jit(solution)/shard_map/ppermute | solution.py:37
  66.5 7.9 %collective-permute-start.8 = (f32[64,512]{1,0:T(8,128)S(1)}, f32[64,512]{1,0:T(8,128)S(1)}, u32[]{:S(2)}, u32[]{:S(2)}) collective-permute-start(f32[64,512]{1,0:T(8,128)S(1)} %bitcast_add_fusion.12), channel_id=1, source_target_pairs={{0,1},{1,2},{2,3},{3,4},{4,5},{5,6},{6,7},{7,8},{8,9},{9,10},{10,1... | collective-permute-start | bytes 393224 | tf_op jit(solution)/shard_map/ppermute | solution.py:37
  72.3 46.6 %copy-start.8 = (f32[64,512]{1,0:T(8,128)S(1)}, f32[64,512]{1,0:T(8,128)}, u32[]{:S(2)}) copy-start(f32[64,512]{1,0:T(8,128)} %copy-done.7) | copy-start | bytes 393220
  72.3 7.1 %collective-permute-start.16 = (f32[64,512]{1,0:T(8,128)S(1)}, f32[64,512]{1,0:T(8,128)S(1)}, u32[]{:S(2)}, u32[]{:S(2)}) collective-permute-start(f32[64,512]{1,0:T(8,128)S(1)} %bitcast_add_fusion.5), channel_id=1, source_target_pairs={{0,15},{1,0},{2,1},{3,2},{4,3},{5,4},{6,5},{7,6},{8,7},{9,8},{10,9... | collective-permute-start | bytes 393224 | tf_op jit(solution)/shard_map/ppermute | solution.py:37
  74.4 7.8 %collective-permute-start.9 = (f32[64,512]{1,0:T(8,128)S(1)}, f32[64,512]{1,0:T(8,128)S(1)}, u32[]{:S(2)}, u32[]{:S(2)}) collective-permute-start(f32[64,512]{1,0:T(8,128)S(1)} %bitcast_add_fusion.11), channel_id=1, source_target_pairs={{0,1},{1,2},{2,3},{3,4},{4,5},{5,6},{6,7},{7,8},{8,9},{9,10},{10,1... | collective-permute-start | bytes 393224 | tf_op jit(solution)/shard_map/ppermute | solution.py:37
  80.3 6.9 %collective-permute-start.17 = (f32[64,512]{1,0:T(8,128)S(1)}, f32[64,512]{1,0:T(8,128)S(1)}, u32[]{:S(2)}, u32[]{:S(2)}) collective-permute-start(f32[64,512]{1,0:T(8,128)S(1)} %bitcast_add_fusion.4), channel_id=1, source_target_pairs={{0,15},{1,0},{2,1},{3,2},{4,3},{5,4},{6,5},{7,6},{8,7},{9,8},{10,9... | collective-permute-start | bytes 393224 | tf_op jit(solution)/shard_map/ppermute | solution.py:37
  82.3 6.9 %collective-permute-start.10 = (f32[64,512]{1,0:T(8,128)S(1)}, f32[64,512]{1,0:T(8,128)S(1)}, u32[]{:S(2)}, u32[]{:S(2)}) collective-permute-start(f32[64,512]{1,0:T(8,128)S(1)} %bitcast_add_fusion.10), channel_id=1, source_target_pairs={{0,1},{1,2},{2,3},{3,4},{4,5},{5,6},{6,7},{7,8},{8,9},{9,10},{10,1... | collective-permute-start | bytes 393224 | tf_op jit(solution)/shard_map/ppermute | solution.py:37
  87.3 6.9 %collective-permute-start.18 = (f32[64,512]{1,0:T(8,128)S(1)}, f32[64,512]{1,0:T(8,128)S(1)}, u32[]{:S(2)}, u32[]{:S(2)}) collective-permute-start(f32[64,512]{1,0:T(8,128)S(1)} %bitcast_add_fusion.3), channel_id=1, source_target_pairs={{0,15},{1,0},{2,1},{3,2},{4,3},{5,4},{6,5},{7,6},{8,7},{9,8},{10,9... | collective-permute-start | bytes 393224 | tf_op jit(solution)/shard_map/ppermute | solution.py:37
  89.2 7.5 %collective-permute-start.11 = (f32[64,512]{1,0:T(8,128)S(1)}, f32[64,512]{1,0:T(8,128)S(1)}, u32[]{:S(2)}, u32[]{:S(2)}) collective-permute-start(f32[64,512]{1,0:T(8,128)S(1)} %bitcast_add_fusion.9), channel_id=1, source_target_pairs={{0,1},{1,2},{2,3},{3,4},{4,5},{5,6},{6,7},{7,8},{8,9},{9,10},{10,1... | collective-permute-start | bytes 393224 | tf_op jit(solution)/shard_map/ppermute | solution.py:37
  94.2 7.9 %collective-permute-start.19 = (f32[64,512]{1,0:T(8,128)S(1)}, f32[64,512]{1,0:T(8,128)S(1)}, u32[]{:S(2)}, u32[]{:S(2)}) collective-permute-start(f32[64,512]{1,0:T(8,128)S(1)} %bitcast_add_fusion.2), channel_id=1, source_target_pairs={{0,15},{1,0},{2,1},{3,2},{4,3},{5,4},{6,5},{7,6},{8,7},{9,8},{10,9... | collective-permute-start | bytes 393224 | tf_op jit(solution)/shard_map/ppermute | solution.py:37
  96.8 7.5 %collective-permute-start.12 = (f32[64,512]{1,0:T(8,128)S(1)}, f32[64,512]{1,0:T(8,128)S(1)}, u32[]{:S(2)}, u32[]{:S(2)}) collective-permute-start(f32[64,512]{1,0:T(8,128)S(1)} %bitcast_add_fusion.8), channel_id=1, source_target_pairs={{0,1},{1,2},{2,3},{3,4},{4,5},{5,6},{6,7},{7,8},{8,9},{9,10},{10,1... | collective-permute-start | bytes 393224 | tf_op jit(solution)/shard_map/ppermute | solution.py:37
  102.2 7.9 %collective-permute-start.20 = (f32[64,512]{1,0:T(8,128)S(1)}, f32[64,512]{1,0:T(8,128)S(1)}, u32[]{:S(2)}, u32[]{:S(2)}) collective-permute-start(f32[64,512]{1,0:T(8,128)S(1)} %bitcast_add_fusion.1), channel_id=1, source_target_pairs={{0,15},{1,0},{2,1},{3,2},{4,3},{5,4},{6,5},{7,6},{8,7},{9,8},{10,9... | collective-permute-start | bytes 393224 | tf_op jit(solution)/shard_map/ppermute | solution.py:37
  104.4 7.7 %collective-permute-start.13 = (f32[64,512]{1,0:T(8,128)S(1)}, f32[64,512]{1,0:T(8,128)S(1)}, u32[]{:S(2)}, u32[]{:S(2)}) collective-permute-start(f32[64,512]{1,0:T(8,128)S(1)} %bitcast_add_fusion.7), channel_id=1, source_target_pairs={{0,1},{1,2},{2,3},{3,4},{4,5},{5,6},{6,7},{7,8},{8,9},{9,10},{10,1... | collective-permute-start | bytes 393224 | tf_op jit(solution)/shard_map/ppermute | solution.py:37
  110.1 7.3 %collective-permute-start.21 = (f32[64,512]{1,0:T(8,128)S(1)}, f32[64,512]{1,0:T(8,128)S(1)}, u32[]{:S(2)}, u32[]{:S(2)}) collective-permute-start(f32[64,512]{1,0:T(8,128)S(1)} %bitcast_add_fusion), channel_id=1, source_target_pairs={{0,15},{1,0},{2,1},{3,2},{4,3},{5,4},{6,5},{7,6},{8,7},{9,8},{10,9... | collective-permute-start | bytes 393224 | tf_op jit(solution)/shard_map/ppermute | solution.py:37
  112.1 6.9 %collective-permute-start.14 = (f32[64,512]{1,0:T(8,128)S(1)}, f32[64,512]{1,0:T(8,128)S(1)}, u32[]{:S(2)}, u32[]{:S(2)}) collective-permute-start(f32[64,512]{1,0:T(8,128)S(1)} %bitcast_add_fusion.6), channel_id=1, source_target_pairs={{0,1},{1,2},{2,3},{3,4},{4,5},{5,6},{6,7},{7,8},{8,9},{9,10},{10,1... | collective-permute-start | bytes 393224 | tf_op jit(solution)/shard_map/ppermute | solution.py:37
  119.0 7.3 %collective-permute-start.29 = (f32[64,512]{1,0:T(8,128)S(1)}, f32[64,512]{1,0:T(8,128)S(1)}, u32[]{:S(2)}, u32[]{:S(2)}) collective-permute-start(f32[64,512]{1,0:T(8,128)S(1)} %add_add_fusion.refs_0_), channel_id=1, source_target_pairs={{0,1},{1,2},{2,3},{3,4},{4,5},{5,6},{6,7},{7,8},{8,9},{9,10},{10,1... | collective-permute-start | bytes 393224 | tf_op jit(solution)/shard_map/ppermute | solution.py:37
  124.4 6.9 %collective-permute-start.22 = (f32[64,512]{1,0:T(8,128)S(1)}, f32[64,512]{1,0:T(8,128)S(1)}, u32[]{:S(2)}, u32[]{:S(2)}) collective-permute-start(f32[64,512]{1,0:T(8,128)S(1)} %add_add_fusion.refs_0_), channel_id=1, source_target_pairs={{0,15},{1,0},{2,1},{3,2},{4,3},{5,4},{6,5},{7,6},{8,7},{9,8},{10,9... | collective-permute-start | bytes 393224 | tf_op jit(solution)/shard_map/ppermute | solution.py:37
  126.3 6.9 %collective-permute-start.30 = (f32[64,512]{1,0:T(8,128)S(1)}, f32[64,512]{1,0:T(8,128)S(1)}, u32[]{:S(2)}, u32[]{:S(2)}) collective-permute-start(f32[64,512]{1,0:T(8,128)S(1)} %collective-permute-done.29.refs_15_), channel_id=1, source_target_pairs={{0,1},{1,2},{2,3},{3,4},{4,5},{5,6},{6,7},{7,8},{8,9},{9,10},{10,1... | collective-permute-start | bytes 393224 | tf_op jit(solution)/shard_map/ppermute | solution.py:37
  131.3 6.9 %collective-permute-start.23 = (f32[64,512]{1,0:T(8,128)S(1)}, f32[64,512]{1,0:T(8,128)S(1)}, u32[]{:S(2)}, u32[]{:S(2)}) collective-permute-start(f32[64,512]{1,0:T(8,128)S(1)} %collective-permute-done.22.refs_1_), channel_id=1, source_target_pairs={{0,15},{1,0},{2,1},{3,2},{4,3},{5,4},{6,5},{7,6},{8,7},{9,8},{10,9... | collective-permute-start | bytes 393224 | tf_op jit(solution)/shard_map/ppermute | solution.py:37
  133.2 6.9 %collective-permute-start.31 = (f32[64,512]{1,0:T(8,128)S(1)}, f32[64,512]{1,0:T(8,128)S(1)}, u32[]{:S(2)}, u32[]{:S(2)}) collective-permute-start(f32[64,512]{1,0:T(8,128)S(1)} %collective-permute-done.30.refs_14_), channel_id=1, source_target_pairs={{0,1},{1,2},{2,3},{3,4},{4,5},{5,6},{6,7},{7,8},{8,9},{9,10},{10,1... | collective-permute-start | bytes 393224 | tf_op jit(solution)/shard_map/ppermute | solution.py:37
  138.2 6.9 %collective-permute-start.24 = (f32[64,512]{1,0:T(8,128)S(1)}, f32[64,512]{1,0:T(8,128)S(1)}, u32[]{:S(2)}, u32[]{:S(2)}) collective-permute-start(f32[64,512]{1,0:T(8,128)S(1)} %collective-permute-done.23.refs_2_), channel_id=1, source_target_pairs={{0,15},{1,0},{2,1},{3,2},{4,3},{5,4},{6,5},{7,6},{8,7},{9,8},{10,9... | collective-permute-start | bytes 393224 | tf_op jit(solution)/shard_map/ppermute | solution.py:37
  140.2 6.9 %collective-permute-start.32 = (f32[64,512]{1,0:T(8,128)S(1)}, f32[64,512]{1,0:T(8,128)S(1)}, u32[]{:S(2)}, u32[]{:S(2)}) collective-permute-start(f32[64,512]{1,0:T(8,128)S(1)} %collective-permute-done.31.refs_13_), channel_id=1, source_target_pairs={{0,1},{1,2},{2,3},{3,4},{4,5},{5,6},{6,7},{7,8},{8,9},{9,10},{10,1... | collective-permute-start | bytes 393224 | tf_op jit(solution)/shard_map/ppermute | solution.py:37
  145.1 7.2 %collective-permute-start.25 = (f32[64,512]{1,0:T(8,128)S(1)}, f32[64,512]{1,0:T(8,128)S(1)}, u32[]{:S(2)}, u32[]{:S(2)}) collective-permute-start(f32[64,512]{1,0:T(8,128)S(1)} %collective-permute-done.24.refs_3_), channel_id=1, source_target_pairs={{0,15},{1,0},{2,1},{3,2},{4,3},{5,4},{6,5},{7,6},{8,7},{9,8},{10,9... | collective-permute-start | bytes 393224 | tf_op jit(solution)/shard_map/ppermute | solution.py:37
  147.1 7.1 %collective-permute-start.33 = (f32[64,512]{1,0:T(8,128)S(1)}, f32[64,512]{1,0:T(8,128)S(1)}, u32[]{:S(2)}, u32[]{:S(2)}) collective-permute-start(f32[64,512]{1,0:T(8,128)S(1)} %collective-permute-done.32.refs_12_), channel_id=1, source_target_pairs={{0,1},{1,2},{2,3},{3,4},{4,5},{5,6},{6,7},{7,8},{8,9},{9,10},{10,1... | collective-permute-start | bytes 393224 | tf_op jit(solution)/shard_map/ppermute | solution.py:37
  152.3 8.5 %collective-permute-start.26 = (f32[64,512]{1,0:T(8,128)S(1)}, f32[64,512]{1,0:T(8,128)S(1)}, u32[]{:S(2)}, u32[]{:S(2)}) collective-permute-start(f32[64,512]{1,0:T(8,128)S(1)} %collective-permute-done.25.refs_4_), channel_id=1, source_target_pairs={{0,15},{1,0},{2,1},{3,2},{4,3},{5,4},{6,5},{7,6},{8,7},{9,8},{10,9... | collective-permute-start | bytes 393224 | tf_op jit(solution)/shard_map/ppermute | solution.py:37
  154.2 8.5 %collective-permute-start.34 = (f32[64,512]{1,0:T(8,128)S(1)}, f32[64,512]{1,0:T(8,128)S(1)}, u32[]{:S(2)}, u32[]{:S(2)}) collective-permute-start(f32[64,512]{1,0:T(8,128)S(1)} %collective-permute-done.33.refs_11_), channel_id=1, source_target_pairs={{0,1},{1,2},{2,3},{3,4},{4,5},{5,6},{6,7},{7,8},{8,9},{9,10},{10,1... | collective-permute-start | bytes 393224 | tf_op jit(solution)/shard_map/ppermute | solution.py:37
  160.8 7.8 %collective-permute-start.27 = (f32[64,512]{1,0:T(8,128)S(1)}, f32[64,512]{1,0:T(8,128)S(1)}, u32[]{:S(2)}, u32[]{:S(2)}) collective-permute-start(f32[64,512]{1,0:T(8,128)S(1)} %collective-permute-done.26.refs_5_), channel_id=1, source_target_pairs={{0,15},{1,0},{2,1},{3,2},{4,3},{5,4},{6,5},{7,6},{8,7},{9,8},{10,9... | collective-permute-start | bytes 393224 | tf_op jit(solution)/shard_map/ppermute | solution.py:37
  162.8 7.8 %collective-permute-start.35 = (f32[64,512]{1,0:T(8,128)S(1)}, f32[64,512]{1,0:T(8,128)S(1)}, u32[]{:S(2)}, u32[]{:S(2)}) collective-permute-start(f32[64,512]{1,0:T(8,128)S(1)} %collective-permute-done.34.refs_10_), channel_id=1, source_target_pairs={{0,1},{1,2},{2,3},{3,4},{4,5},{5,6},{6,7},{7,8},{8,9},{9,10},{10,1... | collective-permute-start | bytes 393224 | tf_op jit(solution)/shard_map/ppermute | solution.py:37
  168.6 6.9 %collective-permute-start.28 = (f32[64,512]{1,0:T(8,128)S(1)}, f32[64,512]{1,0:T(8,128)S(1)}, u32[]{:S(2)}, u32[]{:S(2)}) collective-permute-start(f32[64,512]{1,0:T(8,128)S(1)} %collective-permute-done.27.refs_6_), channel_id=1, source_target_pairs={{0,15},{1,0},{2,1},{3,2},{4,3},{5,4},{6,5},{7,6},{8,7},{9,8},{10,9... | collective-permute-start | bytes 393224 | tf_op jit(solution)/shard_map/ppermute | solution.py:37
  170.5 6.8 %collective-permute-start.36 = (f32[64,512]{1,0:T(8,128)S(1)}, f32[64,512]{1,0:T(8,128)S(1)}, u32[]{:S(2)}, u32[]{:S(2)}) collective-permute-start(f32[64,512]{1,0:T(8,128)S(1)} %collective-permute-done.35.refs_9_), channel_id=1, source_target_pairs={{0,1},{1,2},{2,3},{3,4},{4,5},{5,6},{6,7},{7,8},{8,9},{9,10},{10,1... | collective-permute-start | bytes 393224 | tf_op jit(solution)/shard_map/ppermute | solution.py:37
Sparse Core Ops, SparseCore 0:
  54.3 69.1 all-gather.1

commit v3 on v2

--- a/solution.py
+++ b/solution.py
@@ -107,7 +107,7 @@
 
 def row_of(parts_ref, log_weight):
     v = log_weight - joined(parts_ref[...])
-    return jnp.concatenate([v[k : k + 1] for k in range(YS)], axis=1)
+    return jnp.concatenate([v[k : k + 1] for k in range(v.shape[0])], axis=1)
 
 
 def copy_out(out_ref):
@@ -116,9 +116,8 @@
         out_ref[k] = whole
 
 
-def row_sums(a_ref, v, out_ref):
-    n = out_ref.shape[2]
-    for k in range(out_ref.shape[1]):
+def row_sums(a_ref, v, out_ref, n):
+    for k in range(a_ref.shape[0] // n):
         value = a_ref[k * n : (k + 1) * n, :]
         if v is not None:
             value = value + v
@@ -129,22 +128,23 @@
     copy_out(out_ref)
 
 
-def first_rows_kernel(place_ref, *refs):
-    chunks, (a_ref, out_ref) = refs[:-2], refs[-2:]
+def first_rows_kernel(a_ref, out_ref):
+    row_sums(a_ref, None, out_ref, out_ref.shape[2])
+
+
+def rows_kernel(log_weight, a_ref, parts_ref, out_ref):
+    row_sums(a_ref, row_of(parts_ref, log_weight), out_ref, out_ref.shape[2])
+
+
+def all_rows_kernel(log_weight, chunks_ref, parts_ref, a_ref, out_ref):
     blocks, n = out_ref.shape[1:]
-    depth = len(chunks)
+    depth = chunks_ref.shape[0]
     high = n // depth
-    z, c = place_ref[0], place_ref[3]
-    for k, chunk in enumerate(chunks):
-        at = jnp.where(c == 0, lax.rem(z + k, depth), lax.rem(z + depth - k, depth)) * high
+    for z in range(depth):
         for block in range(blocks):
-            to = pl.ds(pl.multiple_of(block * n + at, high), high)
-            a_ref[to, :] = chunk[block * high : (block + 1) * high, :]
-    row_sums(a_ref, None, out_ref)
-
-
-def rows_kernel(log_weight, a_ref, parts_ref, out_ref):
-    row_sums(a_ref, row_of(parts_ref, log_weight), out_ref)
+            at = block * n + z * high
+            a_ref[at : at + high, :] = chunks_ref[z, block * high : (block + 1) * high, :]
+    row_sums(a_ref, row_of(parts_ref, log_weight), out_ref, n)
 
 
 def columns_kernel(log_weight, a_ref, parts_ref, u_ref, out_ref, shifted):
@@ -164,9 +164,9 @@
         value = jnp.exp2(shifted[k * n : (k + 1) * n, :] - peak)
         total = total + jnp.sum(value.reshape(n // 8, 8, width), axis=0)
     part = peak + jnp.log(jnp.sum(total, axis=0, keepdims=True)) * LOG2E
-    for k in range(2 * YS):
-        at = k % YS * n
-        out_ref[0, k : k + 1, :] = part[:, at : at + n]
+    lanes = out_ref.shape[2]
+    for k in range(out_ref.shape[1]):
+        out_ref[0, k : k + 1, :] = part[:, k * lanes : (k + 1) * lanes]
     copy_out(out_ref)
 
 
@@ -267,43 +267,58 @@
                 back = back + back_rest[step]
     own = own + ahead + back
 
-    chunks = [own] * depth
-    ahead, back = own, own
-    for step in range(1, middle + 1):
-        ahead = send_z(ahead, 1)
-        chunks[depth - step] = ahead
-        if step < middle:
-            back = send_z(back, -1)
-            chunks[step] = back
-    row_shape = jax.ShapeDtypeStruct((group, group, rows), f32)
-    column_shape = jax.ShapeDtypeStruct((YS, 2 * YS, rows), f32)
-    u_shape = jax.ShapeDtypeStruct((group, rows), f32)
-    a, part = pl.pallas_call(
-        first_rows_kernel,
-        out_shape=[jax.ShapeDtypeStruct((tall, wide), f32), row_shape],
-        in_specs=[SMEM] + [VMEM] * depth,
-        out_specs=[VMEM] * 2,
-        compiler_params=PARAMS,
-    )(place, *chunks)
+    gathered = lax.all_gather(own, "dp")
+    z_groups = [
+        [((y * group) + k) * depth + d for y in range(YS) for d in range(depth)] for k in range(group)
+    ]
+    sharers = YS * depth
+    few = tall // depth
     for step in range(ITERS):
-        if step > 0:
+        last = step == ITERS - 1
+        lines, n = (group, rows) if last else (1, few)
+        row_shape = jax.ShapeDtypeStruct((group, lines, n), f32)
+        if step == 0:
+            part = pl.pallas_call(
+                first_rows_kernel,
+                out_shape=row_shape,
+                in_specs=[VMEM],
+                out_specs=VMEM,
+                compiler_params=PARAMS,
+            )(own)
+        elif not last:
             part = pl.pallas_call(
                 functools.partial(rows_kernel, log_weight),
                 out_shape=row_shape,
                 in_specs=[VMEM] * 2,
                 out_specs=VMEM,
                 compiler_params=PARAMS,
-            )(a, part)
+            )(own, part)
+        else:
+            a, part = pl.pallas_call(
+                functools.partial(all_rows_kernel, log_weight),
+                out_shape=[jax.ShapeDtypeStruct((tall, wide), f32), row_shape],
+                in_specs=[VMEM] * 2,
+                out_specs=[VMEM] * 2,
+                compiler_params=PARAMS,
+            )(gathered, part)
         part = swap(part, x_groups)
         u, part = pl.pallas_call(
             functools.partial(columns_kernel, log_weight),
-            out_shape=[u_shape, column_shape],
+            out_shape=[
+                jax.ShapeDtypeStruct((lines, n), f32),
+                jax.ShapeDtypeStruct((YS if last else sharers, YS, rows), f32),
+            ],
             in_specs=[VMEM] * 2,
             out_specs=[VMEM] * 2,
-            scratch_shapes=[pltpu.VMEM((tall, wide), f32)],
+            scratch_shapes=[pltpu.VMEM((lines * n, wide), f32)],
             compiler_params=PARAMS,
-        )(a, part)
-        part = swap(part, y_groups)
+        )(a if last else own, part)
+        if last:
+            part = swap(part, y_groups)
+        else:
+            part = lax.all_to_all(
+                part, ("noise", "dp"), 0, 0, axis_index_groups=z_groups, tiled=True
+            )
     plan = pl.pallas_call(
         functools.partial(plan_kernel, log_weight),
         out_shape=jax.ShapeDtypeStruct((group, rows + 16, wide), jnp.bfloat16),

time: 298 us -> 292 us (0.980)
  blocking collectives: 99.8 us -> 156 us
  starting transfers between devices: 139 us -> 85.6 us
    all_to_all x0 -> x3, blocking collectives: none -> 69.7 us  [on_device(): lax.all_to_all(part, ('noise', 'dp'), 0, 0, axis_index_groups=z_groups, t...]
    ppermute x30 -> x15, starting transfers between devices: 111 us -> 57.6 us  [send_z(): return lax.ppermute(value, ('noise', 'dp'), pairs)]
    all_to_all x9 -> x6, blocking collectives: 99.8 us -> 86.6 us  [swap(): lax.all_to_all(value, 'noise', 0, 0, axis_index_groups=groups, tiled=True)]
    ppermute x30 -> x15, waiting for transfers between devices: 9.96 us -> 4.14 us  [send_z(): return lax.ppermute(value, ('noise', 'dp'), pairs)]
  transfers between devices with their start and end apart: 38 -> 24, of which waited for: 18 -> 9; matrix products, arithmetic and copies ran while one was open for 1% -> 0% of each run, Pallas kernels for 2% -> 1%
where the time goes in v3:
time: 292 us; the launch traced here: 291 us
  blocking collectives  156 us (53%)
  starting transfers between devices  85.6 us (29%)
  waiting for transfers between devices  16.2 us (6%)
  between operations  14.5 us (5%)
  Pallas kernels  13.9 us (5%)
  local copies, waits for them, and re-layouts  3.53 us (1%)
    all_to_all x6, blocking collectives, swap(): lax.all_to_all(value, 'noise', 0, 0, axis_index_groups=groups, tiled=True)  86.6 us
    all_to_all x3, blocking collectives, on_device(): lax.all_to_all(part, ('noise', 'dp'), 0, 0, axis_index_groups=z_groups, t...  69.7 us
    ppermute x15, starting transfers between devices, send_z(): return lax.ppermute(value, ('noise', 'dp'), pairs)  57.6 us
    ppermute x7, starting transfers between devices, send(): return lax.ppermute(value, 'noise', pairs)  27.9 us
    ppermute x7, waiting for transfers between devices, send(): return lax.ppermute(value, 'noise', pairs)  9.03 us
    pallas_call x1, Pallas kernels, on_device(): pl.pallas_call(functools.partial(target_kernel, epsilon / LOG2E), grid=(Y...  5.89 us
  transfers between devices with their start and end apart: 24, of which 9 were waited for; matrix products, arithmetic and copies ran while one was open for 0% of the time, Pallas kernels for 1%

profile of v3, /device:TPU:1, one launch (start us, length us, event | category | flops | bytes accessed | tf_op | source)
XLA Modules:
  0.0 291.1 jit_solution(2656597570996587759)
XLA Ops:
  7.2 0.0 all-gather.6.cloned.1.call-start
  7.2 4.1 %collective-permute-start = (bf16[128,1024]{1,0:T(8,128)(2,1)}, bf16[128,1024]{1,0:T(8,128)(2,1)S(1)}, u32[]{:S(2)}, u32[]{:S(2)}) collective-permute-start(bf16[128,1024]{1,0:T(8,128)(2,1)} %param.2), channel_id=1, source_target_pairs={{0,32},{16,48},{32,64},{48,80},{64,96},{80,112},{96,0},{112,16},{1... | collective-permute-start | bytes 786440 | tf_op jit(solution)/shard_map/ppermute | solution.py:28
  11.3 4.4 %collective-permute-start.1 = (bf16[128,1024]{1,0:T(8,128)(2,1)}, bf16[128,1024]{1,0:T(8,128)(2,1)S(1)}, u32[]{:S(2)}, u32[]{:S(2)}) collective-permute-start(bf16[128,1024]{1,0:T(8,128)(2,1)} %param.2), channel_id=1, source_target_pairs={{0,64},{16,80},{32,96},{48,112},{64,0},{80,16},{96,32},{112,48},{1... | collective-permute-start | bytes 786440 | tf_op jit(solution)/shard_map/ppermute | solution.py:28
  15.7 3.1 %collective-permute-start.2 = (bf16[128,1024]{1,0:T(8,128)(2,1)}, bf16[128,1024]{1,0:T(8,128)(2,1)S(1)}, u32[]{:S(2)}, u32[]{:S(2)}) collective-permute-start(bf16[128,1024]{1,0:T(8,128)(2,1)} %param.2), channel_id=1, source_target_pairs={{0,96},{16,112},{32,0},{48,16},{64,32},{80,48},{96,64},{112,80},{1... | collective-permute-start | bytes 786440 | tf_op jit(solution)/shard_map/ppermute | solution.py:28
  18.7 3.2 %collective-permute-start.3 = (bf16[128,1024]{1,0:T(8,128)(2,1)}, bf16[128,1024]{1,0:T(8,128)(2,1)S(1)}, u32[]{:S(2)}, u32[]{:S(2)}) collective-permute-start(bf16[128,1024]{1,0:T(8,128)(2,1)} %refs_0_), channel_id=1, source_target_pairs={{0,128},{16,144},{32,160},{48,176},{64,192},{80,208},{96,224},{112... | collective-permute-start | bytes 786440 | tf_op jit(solution)/shard_map/ppermute | solution.py:28
  22.0 4.5 %collective-permute-start.4 = (bf16[128,1024]{1,0:T(8,128)(2,1)}, bf16[128,1024]{1,0:T(8,128)(2,1)S(1)}, u32[]{:S(2)}, u32[]{:S(2)}) collective-permute-start(bf16[128,1024]{1,0:T(8,128)(2,1)} %refs_0_), channel_id=1, source_target_pairs={{0,256},{16,272},{32,288},{48,304},{64,320},{80,336},{96,352},{112... | collective-permute-start | bytes 786440 | tf_op jit(solution)/shard_map/ppermute | solution.py:28
  26.5 0.0 collective-permute-done
  26.5 3.0 %collective-permute-start.5 = (bf16[128,1024]{1,0:T(8,128)(2,1)}, bf16[128,1024]{1,0:T(8,128)(2,1)S(1)}, u32[]{:S(2)}, u32[]{:S(2)}) collective-permute-start(bf16[128,1024]{1,0:T(8,128)(2,1)} %refs_0_), channel_id=1, source_target_pairs={{0,384},{16,400},{32,416},{48,432},{64,448},{80,464},{96,480},{112... | collective-permute-start | bytes 786440 | tf_op jit(solution)/shard_map/ppermute | solution.py:28
  29.5 5.7 %collective-permute-done.4.refs_2_ = bf16[128,1024]{1,0:T(8,128)(2,1)S(1)} collective-permute-done((bf16[128,1024]{1,0:T(8,128)(2,1)}, bf16[128,1024]{1,0:T(8,128)(2,1)S(1)}, u32[]{:S(2)}, u32[]{:S(2)}) %collective-permute-start.4) | collective-permute-done | bytes 262176 | tf_op jit(solution)/shard_map/ppermute | solution.py:28
  35.2 1.1 collective-permute-done.5.refs_3_
  36.4 1.0 constant_dynamic-update-slice_fusion.3
  37.4 5.7 %collective-permute-start.6 = (bf16[512,1024]{1,0:T(8,128)(2,1)S(1)}, bf16[512,1024]{1,0:T(8,128)(2,1)S(1)}, u32[]{:S(2)}, u32[]{:S(2)}) collective-permute-start(bf16[512,1024]{1,0:T(8,128)(2,1)S(1)} %constant_dynamic-update-slice_fusion.x_here), channel_id=1, source_target_pairs={{0,16},{16,0},{32,48},{48,32},{64,80},{80,64},{96,112},{112,96},{1... | collective-permute-start | bytes 3145736 | tf_op jit(solution)/shard_map/ppermute | solution.py:28
  43.2 0.1 pad_add_fusion.place_ref
  43.3 2.1 collective-permute-done.6.x_there
  45.4 3.9 %shard_map.49 = (f32[64,512]{1,0:T(8,128)S(1)}, f32[64,512]{1,0:T(8,128)S(1)}, f32[64,512]{1,0:T(8,128)S(1)}, f32[7,64,512]{2,1,0:T(8,128)S(1)}, f32[6,64,512]{2,1,0:T(8,128)S(1)}) custom-call(s32[4]{0:T(128)S(1)} %pad_add_fusion.place_ref, bf16[512,1024]{1,0:T(8,128)(2,1)S(1)} %constant_dynamic-update-slice_fusion.x_here, ...), custom_call_target="tpu_custom_call" | custom-call | tf_op jit(solution)/shard_map/pallas_call | solution.py:240
  49.3 9.9 %collective-permute-start.7 = (f32[64,512]{1,0:T(8,128)S(1)}, f32[64,512]{1,0:T(8,128)S(1)}, u32[]{:S(2)}, u32[]{:S(2)}) collective-permute-start(f32[64,512]{1,0:T(8,128)S(1)} %get-tuple-element.38), channel_id=1, source_target_pairs={{0,1},{1,2},{2,3},{3,4},{4,5},{5,6},{6,7},{7,8},{8,9},{9,10},{10,1... | collective-permute-start | bytes 393224 | tf_op jit(solution)/shard_map/ppermute | solution.py:37
  59.2 1.9 collective-permute-start.15
  61.2 5.0 %collective-permute-start.8 = (f32[64,512]{1,0:T(8,128)S(1)}, f32[64,512]{1,0:T(8,128)S(1)}, u32[]{:S(2)}, u32[]{:S(2)}) collective-permute-start(f32[64,512]{1,0:T(8,128)S(1)} %bitcast_add_fusion.12), channel_id=1, source_target_pairs={{0,1},{1,2},{2,3},{3,4},{4,5},{5,6},{6,7},{7,8},{8,9},{9,10},{10,1... | collective-permute-start | bytes 393224 | tf_op jit(solution)/shard_map/ppermute | solution.py:37
  66.2 1.9 collective-permute-start.16
  68.2 4.9 %collective-permute-start.9 = (f32[64,512]{1,0:T(8,128)S(1)}, f32[64,512]{1,0:T(8,128)S(1)}, u32[]{:S(2)}, u32[]{:S(2)}) collective-permute-start(f32[64,512]{1,0:T(8,128)S(1)} %bitcast_add_fusion.11), channel_id=1, source_target_pairs={{0,1},{1,2},{2,3},{3,4},{4,5},{5,6},{6,7},{7,8},{8,9},{9,10},{10,1... | collective-permute-start | bytes 393224 | tf_op jit(solution)/shard_map/ppermute | solution.py:37
  73.1 0.0 collective-permute-done.16
  73.2 1.9 collective-permute-start.17
  75.1 4.9 %collective-permute-start.10 = (f32[64,512]{1,0:T(8,128)S(1)}, f32[64,512]{1,0:T(8,128)S(1)}, u32[]{:S(2)}, u32[]{:S(2)}) collective-permute-start(f32[64,512]{1,0:T(8,128)S(1)} %bitcast_add_fusion.10), channel_id=1, source_target_pairs={{0,1},{1,2},{2,3},{3,4},{4,5},{5,6},{6,7},{7,8},{8,9},{9,10},{10,1... | collective-permute-start | bytes 393224 | tf_op jit(solution)/shard_map/ppermute | solution.py:37
  80.1 0.0 collective-permute-done.17
  80.1 1.9 collective-permute-start.18
  82.1 4.9 %collective-permute-start.11 = (f32[64,512]{1,0:T(8,128)S(1)}, f32[64,512]{1,0:T(8,128)S(1)}, u32[]{:S(2)}, u32[]{:S(2)}) collective-permute-start(f32[64,512]{1,0:T(8,128)S(1)} %bitcast_add_fusion.9), channel_id=1, source_target_pairs={{0,1},{1,2},{2,3},{3,4},{4,5},{5,6},{6,7},{7,8},{8,9},{9,10},{10,1... | collective-permute-start | bytes 393224 | tf_op jit(solution)/shard_map/ppermute | solution.py:37
  87.0 0.8 collective-permute-done.18
  87.8 1.9 collective-permute-start.19
  89.8 4.9 %collective-permute-start.12 = (f32[64,512]{1,0:T(8,128)S(1)}, f32[64,512]{1,0:T(8,128)S(1)}, u32[]{:S(2)}, u32[]{:S(2)}) collective-permute-start(f32[64,512]{1,0:T(8,128)S(1)} %bitcast_add_fusion.8), channel_id=1, source_target_pairs={{0,1},{1,2},{2,3},{3,4},{4,5},{5,6},{6,7},{7,8},{8,9},{9,10},{10,1... | collective-permute-start | bytes 393224 | tf_op jit(solution)/shard_map/ppermute | solution.py:37
  94.7 1.2 collective-permute-done.19
  95.9 1.9 collective-permute-start.20
  97.9 4.8 %collective-permute-start.13 = (f32[64,512]{1,0:T(8,128)S(1)}, f32[64,512]{1,0:T(8,128)S(1)}, u32[]{:S(2)}, u32[]{:S(2)}) collective-permute-start(f32[64,512]{1,0:T(8,128)S(1)} %bitcast_add_fusion.7), channel_id=1, source_target_pairs={{0,1},{1,2},{2,3},{3,4},{4,5},{5,6},{6,7},{7,8},{8,9},{9,10},{10,1... | collective-permute-start | bytes 393224 | tf_op jit(solution)/shard_map/ppermute | solution.py:37
  102.7 0.1 collective-permute-done.20
  102.9 1.9 collective-permute-start.21
  104.8 4.8 %collective-permute-start.14 = (f32[64,512]{1,0:T(8,128)S(1)}, f32[64,512]{1,0:T(8,128)S(1)}, u32[]{:S(2)}, u32[]{:S(2)}) collective-permute-start(f32[64,512]{1,0:T(8,128)S(1)} %bitcast_add_fusion.6), channel_id=1, source_target_pairs={{0,1},{1,2},{2,3},{3,4},{4,5},{5,6},{6,7},{7,8},{8,9},{9,10},{10,1... | collective-permute-start | bytes 393224 | tf_op jit(solution)/shard_map/ppermute | solution.py:37
  109.7 0.1 collective-permute-done.21
  109.8 1.8 collective-permute-done.14
  111.6 0.7 add_add_fusion.a_ref
  112.3 0.0 all-gather.6.cloned.1.call-update
  112.3 0.0 all-gather.4.cloned.1.call-start
  112.4 0.7 all-gather.4.cloned.1.call-update
  113.1 0.0 copy-start
  113.1 0.9 copy-done
  114.0 0.2 shard_map.50
  114.2 16.5 %all_to_all.45.parts_ref = f32[8,1,64]{2,1,0:T(1,128)S(1)} all-to-all(f32[8,1,64]{2,1,0:T(1,128)S(1)} %shard_map.50), channel_id=1, replica_groups={{0,16,32,48,64,80,96,112},{128,144,160,176,192,208,224,240},{256,272,28..., dimensions={0} | all-to-all | bytes 4096 | tf_op jit(solution)/shard_map/all_to_all | solution.py:232
  130.6 0.5 shard_map.51
  131.2 28.8 %all_to_all.46.parts_ref = f32[64,4,128]{2,1,0:T(4,128)S(1)} all-to-all(f32[64,4,128]{2,1,0:T(4,128)S(1)} %get-tuple-element.42), channel_id=1, replica_groups={{0,1,2,3,4,5,6,7,8,9,10,11,12,13,14,15,128,129,130,131,132,133,134,135,..., dimensions={0} | all-to-all | bytes 262144 | tf_op jit(solution)/shard_map/all_to_all | solution.py:319
  160.0 0.3 shard_map.52
  160.3 8.8 %all_to_all.47.parts_ref = f32[8,1,64]{2,1,0:T(1,128)S(1)} all-to-all(f32[8,1,64]{2,1,0:T(1,128)S(1)} %shard_map.52), channel_id=1, replica_groups={{0,16,32,48,64,80,96,112},{128,144,160,176,192,208,224,240},{256,272,28..., dimensions={0} | all-to-all | bytes 4096 | tf_op jit(solution)/shard_map/all_to_all | solution.py:232
  169.1 0.5 shard_map.53
  169.7 21.3 %all_to_all.48.parts_ref = f32[64,4,128]{2,1,0:T(4,128)S(1)} all-to-all(f32[64,4,128]{2,1,0:T(4,128)S(1)} %get-tuple-element.43), channel_id=1, replica_groups={{0,1,2,3,4,5,6,7,8,9,10,11,12,13,14,15,128,129,130,131,132,133,134,135,..., dimensions={0} | all-to-all | bytes 262144 | tf_op jit(solution)/shard_map/all_to_all | solution.py:319
  190.9 0.3 shard_map.54
  191.3 9.7 %all_to_all.49.parts_ref = f32[8,1,64]{2,1,0:T(1,128)S(1)} all-to-all(f32[8,1,64]{2,1,0:T(1,128)S(1)} %shard_map.54), channel_id=1, replica_groups={{0,16,32,48,64,80,96,112},{128,144,160,176,192,208,224,240},{256,272,28..., dimensions={0} | all-to-all | bytes 4096 | tf_op jit(solution)/shard_map/all_to_all | solution.py:232
  201.0 0.5 shard_map.55
  201.5 19.6 %all_to_all.50.parts_ref = f32[64,4,128]{2,1,0:T(4,128)S(1)} all-to-all(f32[64,4,128]{2,1,0:T(4,128)S(1)} %get-tuple-element.44), channel_id=1, replica_groups={{0,1,2,3,4,5,6,7,8,9,10,11,12,13,14,15,128,129,130,131,132,133,134,135,..., dimensions={0} | all-to-all | bytes 262144 | tf_op jit(solution)/shard_map/all_to_all | solution.py:319
  221.1 1.6 copy-done.1
  222.7 0.7 shard_map.56
  223.4 10.4 %all_to_all.51.parts_ref = f32[8,8,128]{2,1,0:T(8,128)S(1)} all-to-all(f32[8,8,128]{2,1,0:T(8,128)S(1)} %get-tuple-element.46), channel_id=1, replica_groups={{0,16,32,48,64,80,96,112},{128,144,160,176,192,208,224,240},{256,272,28..., dimensions={0} | all-to-all | bytes 65536 | tf_op jit(solution)/shard_map/all_to_all | solution.py:232
  233.8 0.6 shard_map.57
  234.4 7.5 %all_to_all.52.parts_ref = f32[4,4,128]{2,1,0:T(4,128)S(1)} all-to-all(f32[4,4,128]{2,1,0:T(4,128)S(1)} %get-tuple-element.48), channel_id=1, replica_groups={{0,128,256,384},{16,144,272,400},{32,160,288,416},{48,176,304,432},{64,..., dimensions={0} | all-to-all | bytes 16384 | tf_op jit(solution)/shard_map/all_to_all | solution.py:232
  241.9 0.4 shard_map.58
  242.3 33.7 %all_to_all.53.plan_ref = bf16[8,144,512]{2,1,0:T(8,128)(2,1)S(1)} all-to-all(bf16[8,144,512]{2,1,0:T(8,128)(2,1)S(1)} %shard_map.58), channel_id=1, replica_groups={{0,16,32,48,64,80,96,112},{128,144,160,176,192,208,224,240},{256,272,28..., dimensions={0} | all-to-all | bytes 2359296 | tf_op jit(solution)/shard_map/all_to_all | solution.py:232
  276.0 2.3 all-gather.4.cloned.1.call-done.y_ref
  278.3 5.9 %shard_map.59 = (bf16[128,1024]{1,0:T(8,128)(2,1)}, f32[1,128]{1,0:T(1,128)}, f32[1,256]{1,0:T(1,128)}) custom-call(s32[4]{0:T(128)S(1)} %pad_add_fusion.place_ref, bf16[8,144,512]{2,1,0:T(8,128)(2,1)S(1)} %all_to_all.53.plan_ref, f32[8,128]{1,0:T(8,128)S(1)} %get-tuple-element.47.u_ref, bf16[4096,1024]{1,0:T(8,128)(2,1)} %all-gather.4.cloned.1.call-done.y_ref), custom_call_target="tpu_custom_call" | custom-call | tf_op jit(solution)/shard_map/pallas_call | solution.py:332
  (31 shorter events, 0.4 us)
Async XLA Ops:
  7.2 38.3 %copy-start.2 = (bf16[128,1024]{1,0:T(8,128)(2,1)S(1)}, bf16[128,1024]{1,0:T(8,128)(2,1)}, u32[]{:S(2)}) copy-start(bf16[128,1024]{1,0:T(8,128)(2,1)} %refs_0_) | copy-start | bytes 786436
  7.2 213.9 %all-gather.6.cloned.1.call-start = ((), (), s32[]{:S(2)}) async-start(), calls=%async_computation.10 | async-start | bytes 2228224 | tf_op jit(solution)/shard_map/all_gather | solution.py:270
  7.2 19.3 %collective-permute-start = (bf16[128,1024]{1,0:T(8,128)(2,1)}, bf16[128,1024]{1,0:T(8,128)(2,1)S(1)}, u32[]{:S(2)}, u32[]{:S(2)}) collective-permute-start(bf16[128,1024]{1,0:T(8,128)(2,1)} %param.2), channel_id=1, source_target_pairs={{0,32},{16,48},{32,64},{48,80},{64,96},{80,112},{96,0},{112,16},{1... | collective-permute-start | bytes 786440 | tf_op jit(solution)/shard_map/ppermute | solution.py:28
  11.3 18.2 %collective-permute-start.1 = (bf16[128,1024]{1,0:T(8,128)(2,1)}, bf16[128,1024]{1,0:T(8,128)(2,1)S(1)}, u32[]{:S(2)}, u32[]{:S(2)}) collective-permute-start(bf16[128,1024]{1,0:T(8,128)(2,1)} %param.2), channel_id=1, source_target_pairs={{0,64},{16,80},{32,96},{48,112},{64,0},{80,16},{96,32},{112,48},{1... | collective-permute-start | bytes 786440 | tf_op jit(solution)/shard_map/ppermute | solution.py:28
  15.7 13.8 %collective-permute-start.2 = (bf16[128,1024]{1,0:T(8,128)(2,1)}, bf16[128,1024]{1,0:T(8,128)(2,1)S(1)}, u32[]{:S(2)}, u32[]{:S(2)}) collective-permute-start(bf16[128,1024]{1,0:T(8,128)(2,1)} %param.2), channel_id=1, source_target_pairs={{0,96},{16,112},{32,0},{48,16},{64,32},{80,48},{96,64},{112,80},{1... | collective-permute-start | bytes 786440 | tf_op jit(solution)/shard_map/ppermute | solution.py:28
  18.7 10.8 %collective-permute-start.3 = (bf16[128,1024]{1,0:T(8,128)(2,1)}, bf16[128,1024]{1,0:T(8,128)(2,1)S(1)}, u32[]{:S(2)}, u32[]{:S(2)}) collective-permute-start(bf16[128,1024]{1,0:T(8,128)(2,1)} %refs_0_), channel_id=1, source_target_pairs={{0,128},{16,144},{32,160},{48,176},{64,192},{80,208},{96,224},{112... | collective-permute-start | bytes 786440 | tf_op jit(solution)/shard_map/ppermute | solution.py:28
  22.0 13.3 %collective-permute-start.4 = (bf16[128,1024]{1,0:T(8,128)(2,1)}, bf16[128,1024]{1,0:T(8,128)(2,1)S(1)}, u32[]{:S(2)}, u32[]{:S(2)}) collective-permute-start(bf16[128,1024]{1,0:T(8,128)(2,1)} %refs_0_), channel_id=1, source_target_pairs={{0,256},{16,272},{32,288},{48,304},{64,320},{80,336},{96,352},{112... | collective-permute-start | bytes 786440 | tf_op jit(solution)/shard_map/ppermute | solution.py:28
  26.5 9.9 %collective-permute-start.5 = (bf16[128,1024]{1,0:T(8,128)(2,1)}, bf16[128,1024]{1,0:T(8,128)(2,1)S(1)}, u32[]{:S(2)}, u32[]{:S(2)}) collective-permute-start(bf16[128,1024]{1,0:T(8,128)(2,1)} %refs_0_), channel_id=1, source_target_pairs={{0,384},{16,400},{32,416},{48,432},{64,448},{80,464},{96,480},{112... | collective-permute-start | bytes 786440 | tf_op jit(solution)/shard_map/ppermute | solution.py:28
  37.4 8.0 %collective-permute-start.6 = (bf16[512,1024]{1,0:T(8,128)(2,1)S(1)}, bf16[512,1024]{1,0:T(8,128)(2,1)S(1)}, u32[]{:S(2)}, u32[]{:S(2)}) collective-permute-start(bf16[512,1024]{1,0:T(8,128)(2,1)S(1)} %constant_dynamic-update-slice_fusion.x_here), channel_id=1, source_target_pairs={{0,16},{16,0},{32,48},{48,32},{64,80},{80,64},{96,112},{112,96},{1... | collective-permute-start | bytes 3145736 | tf_op jit(solution)/shard_map/ppermute | solution.py:28
  49.3 11.8 %collective-permute-start.7 = (f32[64,512]{1,0:T(8,128)S(1)}, f32[64,512]{1,0:T(8,128)S(1)}, u32[]{:S(2)}, u32[]{:S(2)}) collective-permute-start(f32[64,512]{1,0:T(8,128)S(1)} %get-tuple-element.38), channel_id=1, source_target_pairs={{0,1},{1,2},{2,3},{3,4},{4,5},{5,6},{6,7},{7,8},{8,9},{9,10},{10,1... | collective-permute-start | bytes 393224 | tf_op jit(solution)/shard_map/ppermute | solution.py:37
  59.2 6.9 %collective-permute-start.15 = (f32[64,512]{1,0:T(8,128)S(1)}, f32[64,512]{1,0:T(8,128)S(1)}, u32[]{:S(2)}, u32[]{:S(2)}) collective-permute-start(f32[64,512]{1,0:T(8,128)S(1)} %get-tuple-element.40), channel_id=1, source_target_pairs={{0,15},{1,0},{2,1},{3,2},{4,3},{5,4},{6,5},{7,6},{8,7},{9,8},{10,9... | collective-permute-start | bytes 393224 | tf_op jit(solution)/shard_map/ppermute | solution.py:37
  61.2 6.9 %collective-permute-start.8 = (f32[64,512]{1,0:T(8,128)S(1)}, f32[64,512]{1,0:T(8,128)S(1)}, u32[]{:S(2)}, u32[]{:S(2)}) collective-permute-start(f32[64,512]{1,0:T(8,128)S(1)} %bitcast_add_fusion.12), channel_id=1, source_target_pairs={{0,1},{1,2},{2,3},{3,4},{4,5},{5,6},{6,7},{7,8},{8,9},{9,10},{10,1... | collective-permute-start | bytes 393224 | tf_op jit(solution)/shard_map/ppermute | solution.py:37
  66.2 6.9 %collective-permute-start.16 = (f32[64,512]{1,0:T(8,128)S(1)}, f32[64,512]{1,0:T(8,128)S(1)}, u32[]{:S(2)}, u32[]{:S(2)}) collective-permute-start(f32[64,512]{1,0:T(8,128)S(1)} %bitcast_add_fusion.5), channel_id=1, source_target_pairs={{0,15},{1,0},{2,1},{3,2},{4,3},{5,4},{6,5},{7,6},{8,7},{9,8},{10,9... | collective-permute-start | bytes 393224 | tf_op jit(solution)/shard_map/ppermute | solution.py:37
  68.2 6.9 %collective-permute-start.9 = (f32[64,512]{1,0:T(8,128)S(1)}, f32[64,512]{1,0:T(8,128)S(1)}, u32[]{:S(2)}, u32[]{:S(2)}) collective-permute-start(f32[64,512]{1,0:T(8,128)S(1)} %bitcast_add_fusion.11), channel_id=1, source_target_pairs={{0,1},{1,2},{2,3},{3,4},{4,5},{5,6},{6,7},{7,8},{8,9},{9,10},{10,1... | collective-permute-start | bytes 393224 | tf_op jit(solution)/shard_map/ppermute | solution.py:37
  73.2 6.9 %collective-permute-start.17 = (f32[64,512]{1,0:T(8,128)S(1)}, f32[64,512]{1,0:T(8,128)S(1)}, u32[]{:S(2)}, u32[]{:S(2)}) collective-permute-start(f32[64,512]{1,0:T(8,128)S(1)} %bitcast_add_fusion.4), channel_id=1, source_target_pairs={{0,15},{1,0},{2,1},{3,2},{4,3},{5,4},{6,5},{7,6},{8,7},{9,8},{10,9... | collective-permute-start | bytes 393224 | tf_op jit(solution)/shard_map/ppermute | solution.py:37
  75.1 6.9 %collective-permute-start.10 = (f32[64,512]{1,0:T(8,128)S(1)}, f32[64,512]{1,0:T(8,128)S(1)}, u32[]{:S(2)}, u32[]{:S(2)}) collective-permute-start(f32[64,512]{1,0:T(8,128)S(1)} %bitcast_add_fusion.10), channel_id=1, source_target_pairs={{0,1},{1,2},{2,3},{3,4},{4,5},{5,6},{6,7},{7,8},{8,9},{9,10},{10,1... | collective-permute-start | bytes 393224 | tf_op jit(solution)/shard_map/ppermute | solution.py:37
  80.1 7.7 %collective-permute-start.18 = (f32[64,512]{1,0:T(8,128)S(1)}, f32[64,512]{1,0:T(8,128)S(1)}, u32[]{:S(2)}, u32[]{:S(2)}) collective-permute-start(f32[64,512]{1,0:T(8,128)S(1)} %bitcast_add_fusion.3), channel_id=1, source_target_pairs={{0,15},{1,0},{2,1},{3,2},{4,3},{5,4},{6,5},{7,6},{8,7},{9,8},{10,9... | collective-permute-start | bytes 393224 | tf_op jit(solution)/shard_map/ppermute | solution.py:37
  82.1 7.7 %collective-permute-start.11 = (f32[64,512]{1,0:T(8,128)S(1)}, f32[64,512]{1,0:T(8,128)S(1)}, u32[]{:S(2)}, u32[]{:S(2)}) collective-permute-start(f32[64,512]{1,0:T(8,128)S(1)} %bitcast_add_fusion.9), channel_id=1, source_target_pairs={{0,1},{1,2},{2,3},{3,4},{4,5},{5,6},{6,7},{7,8},{8,9},{9,10},{10,1... | collective-permute-start | bytes 393224 | tf_op jit(solution)/shard_map/ppermute | solution.py:37
  87.8 8.1 %collective-permute-start.19 = (f32[64,512]{1,0:T(8,128)S(1)}, f32[64,512]{1,0:T(8,128)S(1)}, u32[]{:S(2)}, u32[]{:S(2)}) collective-permute-start(f32[64,512]{1,0:T(8,128)S(1)} %bitcast_add_fusion.2), channel_id=1, source_target_pairs={{0,15},{1,0},{2,1},{3,2},{4,3},{5,4},{6,5},{7,6},{8,7},{9,8},{10,9... | collective-permute-start | bytes 393224 | tf_op jit(solution)/shard_map/ppermute | solution.py:37
  89.8 8.1 %collective-permute-start.12 = (f32[64,512]{1,0:T(8,128)S(1)}, f32[64,512]{1,0:T(8,128)S(1)}, u32[]{:S(2)}, u32[]{:S(2)}) collective-permute-start(f32[64,512]{1,0:T(8,128)S(1)} %bitcast_add_fusion.8), channel_id=1, source_target_pairs={{0,1},{1,2},{2,3},{3,4},{4,5},{5,6},{6,7},{7,8},{8,9},{9,10},{10,1... | collective-permute-start | bytes 393224 | tf_op jit(solution)/shard_map/ppermute | solution.py:37
  95.9 6.9 %collective-permute-start.20 = (f32[64,512]{1,0:T(8,128)S(1)}, f32[64,512]{1,0:T(8,128)S(1)}, u32[]{:S(2)}, u32[]{:S(2)}) collective-permute-start(f32[64,512]{1,0:T(8,128)S(1)} %bitcast_add_fusion.1), channel_id=1, source_target_pairs={{0,15},{1,0},{2,1},{3,2},{4,3},{5,4},{6,5},{7,6},{8,7},{9,8},{10,9... | collective-permute-start | bytes 393224 | tf_op jit(solution)/shard_map/ppermute | solution.py:37
  97.9 6.9 %collective-permute-start.13 = (f32[64,512]{1,0:T(8,128)S(1)}, f32[64,512]{1,0:T(8,128)S(1)}, u32[]{:S(2)}, u32[]{:S(2)}) collective-permute-start(f32[64,512]{1,0:T(8,128)S(1)} %bitcast_add_fusion.7), channel_id=1, source_target_pairs={{0,1},{1,2},{2,3},{3,4},{4,5},{5,6},{6,7},{7,8},{8,9},{9,10},{10,1... | collective-permute-start | bytes 393224 | tf_op jit(solution)/shard_map/ppermute | solution.py:37
  102.9 6.9 %collective-permute-start.21 = (f32[64,512]{1,0:T(8,128)S(1)}, f32[64,512]{1,0:T(8,128)S(1)}, u32[]{:S(2)}, u32[]{:S(2)}) collective-permute-start(f32[64,512]{1,0:T(8,128)S(1)} %bitcast_add_fusion), channel_id=1, source_target_pairs={{0,15},{1,0},{2,1},{3,2},{4,3},{5,4},{6,5},{7,6},{8,7},{9,8},{10,9... | collective-permute-start | bytes 393224 | tf_op jit(solution)/shard_map/ppermute | solution.py:37
  104.8 6.8 %collective-permute-start.14 = (f32[64,512]{1,0:T(8,128)S(1)}, f32[64,512]{1,0:T(8,128)S(1)}, u32[]{:S(2)}, u32[]{:S(2)}) collective-permute-start(f32[64,512]{1,0:T(8,128)S(1)} %bitcast_add_fusion.6), channel_id=1, source_target_pairs={{0,1},{1,2},{2,3},{3,4},{4,5},{5,6},{6,7},{7,8},{8,9},{9,10},{10,1... | collective-permute-start | bytes 393224 | tf_op jit(solution)/shard_map/ppermute | solution.py:37
  112.3 166.0 %all-gather.4.cloned.1.call-start = ((), (), s32[]{:S(2)}) async-start(), calls=%async_computation.9 | async-start | bytes 8650752 | tf_op jit(solution)/shard_map/all_gather | solution.py:331
  113.1 0.9 copy-start
  221.1 1.6 copy-start.1
Sparse Core Ops, SparseCore 0:
  112.4 75.8 all-gather.5
  191.4 86.8 all-gather.3

commit v4 on v3

--- a/solution.py
+++ b/solution.py
@@ -17,30 +17,42 @@
 PARAMS = pltpu.CompilerParams(vmem_limit_bytes=48 * 1024 * 1024)
 
 
-def send(value, dy=0, dx=0, dc=0):
+def noise_pairs(target):
     pairs = []
     for y in range(YS):
         for x in range(XS):
             for c in range(CORES):
-                source = (y * XS + x) * CORES + c
-                target = ((y + dy) % YS * XS + (x + dx) % XS) * CORES + (c + dc) % CORES
-                pairs.append((source, target))
-    return lax.ppermute(value, "noise", pairs)
-
-
-def send_z(value, ahead):
+                to_y, to_x, to_c = target(y, x, c)
+                pairs.append(((y * XS + x) * CORES + c, (to_y * XS + to_x) * CORES + to_c))
+    return pairs
+
+
+def to_other_core(value):
+    return lax.ppermute(value, "noise", noise_pairs(lambda y, x, c: (y, x, 1 - c)))
+
+
+FIRST, SECOND, BOTH = (1, 3), (3, 1), 2
+PLACES = ((0, 0), FIRST, SECOND, (BOTH, BOTH))
+
+
+def swap_x(value, by):
+    return lax.ppermute(value, "noise", noise_pairs(lambda y, x, c: (y, x ^ by[c], c)))
+
+
+def swap_y(value, by):
+    return lax.ppermute(value, "noise", noise_pairs(lambda y, x, c: (y ^ by[c], x, c)))
+
+
+def send_z(value, target):
     size = lax.axis_size("dp")
     pairs = []
     for n in range(YS * XS * CORES):
-        step = ahead if n % CORES == 0 else -ahead
-        pairs += [(n * size + z, n * size + (z + step) % size) for z in range(size)]
+        pairs += [(n * size + z, n * size + target(z, n % CORES) % size) for z in range(size)]
     return lax.ppermute(value, ("noise", "dp"), pairs)
 
 
-def gather4(block, **axis):
-    (name,) = axis
-    before, after = send(block, **{name: 1}), send(block, **{name: -1})
-    return [block, before, send(block, **{name: 2}), after]
+def z_partner(z, c):
+    return z ^ 1 if c == 0 else z + 1 if z % 2 else z - 1
 
 
 def squares_row(block):
@@ -52,23 +64,31 @@
     return jnp.sum(jnp.where(row_at == column_at, column, 0.0), axis=0, keepdims=True)
 
 
-def partial_kernel(scale, place_ref, x_here, x_there, *refs):
-    ys, (own, ahead, back, ahead_rest, back_rest, x_all, y_all, y_squares, chunks) = refs[:YS], refs[YS:]
-    rows = ys[0].shape[0]
+def partial_kernel(scale, place_ref, *refs):
+    here, there, ys = refs[:2], refs[2:4], refs[4:6]
+    keep, give, x_all, y_all, y_squares, chunks = refs[6:]
+    rows = here[0].shape[0] // 2
     depth = chunks.shape[0]
     high = rows // depth
     z, y, x, c = place_ref[0], place_ref[1], place_ref[2], place_ref[3]
-    for k in range(XS):
-        at = lax.rem(x + XS - k, XS) * CORES
-        block = slice(k * rows, (k + 1) * rows)
-        x_all[at + c] = x_here[block, :]
-        x_all[at + 1 - c] = x_there[block, :]
-    for k in range(YS):
-        at = pl.multiple_of(lax.rem(y + YS - k, YS) * rows, rows)
-        y_all[pl.ds(at, rows), :] = ys[k][...]
+    for k, (first, second) in enumerate(PLACES):
+        block = slice(k % 2 * rows, (k % 2 + 1) * rows)
+        mine, other = jnp.where(c == 0, first, second), jnp.where(c == 0, second, first)
+        x_all[lax.bitwise_xor(x, mine) * CORES + c] = here[k // 2][block, :]
+        x_all[lax.bitwise_xor(x, other) * CORES + 1 - c] = there[k // 2][block, :]
+        at = pl.multiple_of(lax.bitwise_xor(y, mine) * rows, rows)
+        y_all[pl.ds(at, rows), :] = ys[k // 2][block, :]
     for k in range(YS):
         block = slice(k * rows, (k + 1) * rows)
         y_squares[:, block] = scale * squares_row(y_all[block, :])
+    up = jnp.where(c == 0, lax.rem(z, 2) == 0, lax.rem(z, 2) == 1)
+    partner = lax.rem(z + jnp.where(up, 1, depth - 1), depth)
+    places = []
+    for t in range(depth):
+        same = lax.rem(z + t, 2) == 0
+        base = jnp.where(same, z, partner)
+        ahead = jnp.where(c == 0, lax.rem(t + depth - base, depth), lax.rem(base + depth - t, depth))
+        places.append(ahead // 2 + jnp.where(same, 0, depth // 2))
     for k in range(XS * CORES):
         value = x_all[k]
         wide = value.astype(jnp.float32)
@@ -78,16 +98,21 @@
         )
         value = (2.0 * scale) * cross - x_squares - y_squares[...]
         for t in range(depth):
-            at = jnp.where(c == 0, lax.rem(t + depth - z, depth), lax.rem(z + depth - t, depth))
-            chunks[at, k * high : (k + 1) * high, :] = value[t * high : (t + 1) * high]
-    middle = depth // 2
-    own[...] = chunks[0]
-    ahead[...] = chunks[middle]
-    back[...] = chunks[middle + 1]
+            chunks[places[t], k * high : (k + 1) * high, :] = value[t * high : (t + 1) * high]
+    for k in range(depth // 2):
+        keep[k] = chunks[k]
+        give[k] = chunks[depth // 2 + k]
+
+
+def pair_kernel(keep, got, own, ahead, back, ahead_rest, back_rest):
+    own[...] = keep[0] + got[0]
+    middle = keep.shape[0] // 2
+    ahead[...] = keep[middle] + got[middle]
+    back[...] = keep[middle + 1] + got[middle + 1]
     for k in range(1, middle):
-        ahead_rest[middle - 1 - k] = chunks[k]
-    for k in range(middle + 2, depth):
-        back_rest[k - middle - 2] = chunks[k]
+        ahead_rest[middle - 1 - k] = keep[k] + got[k]
+    for k in range(middle + 2, keep.shape[0]):
+        back_rest[k - middle - 2] = keep[k] + got[k]
 
 
 def joined(parts):
@@ -170,6 +195,11 @@
     copy_out(out_ref)
 
 
+def join_kernel(parts_ref, out_ref):
+    out_ref[0] = joined(parts_ref[...])
+    copy_out(out_ref)
+
+
 def plan_kernel(log_weight, a_ref, u_ref, parts_ref, out_ref):
     v = row_of(parts_ref, log_weight)
     u = u_ref[...] - log_weight
@@ -231,14 +261,33 @@
     def swap(value, groups):
         return lax.all_to_all(value, "noise", 0, 0, axis_index_groups=groups, tiled=True)
 
-    xs, ys = lax.optimization_barrier((gather4(noise_rows, dx=1), gather4(data_rows, dy=1)))
-    x_here = jnp.concatenate(xs, axis=0)
-    x_there = send(x_here, dc=1)
+    x_near = jnp.concatenate([noise_rows, swap_x(noise_rows, FIRST)], axis=0)
+    y_near = jnp.concatenate([data_rows, swap_y(data_rows, FIRST)], axis=0)
+    x_near, y_near = lax.optimization_barrier((x_near, y_near))
+    x_far, y_far = swap_x(x_near, SECOND), swap_y(y_near, SECOND)
+    x_far, y_far, late_rows = lax.optimization_barrier((x_far, y_far, data_rows))
+    everything = lax.all_gather(late_rows, "noise", axis=0, tiled=True)
     tall, wide = group * rows, YS * rows
-    middle = depth // 2
+    half = depth // 2
+    middle = half // 2
     chunk = (tall // depth, wide)
+    keep, give = pl.pallas_call(
+        functools.partial(partial_kernel, LOG2E / (epsilon * D)),
+        out_shape=[jax.ShapeDtypeStruct((half,) + chunk, f32)] * 2,
+        in_specs=[SMEM] + [VMEM] * 6,
+        out_specs=[VMEM] * 2,
+        scratch_shapes=[
+            pltpu.VMEM((group, rows, features), jnp.bfloat16),
+            pltpu.VMEM((YS * rows, features), jnp.bfloat16),
+            pltpu.VMEM((1, wide), f32),
+            pltpu.VMEM((depth,) + chunk, f32),
+        ],
+        compiler_params=PARAMS,
+    )(place, x_near, x_far, to_other_core(x_near), to_other_core(x_far), y_near, y_far)
+
+    got = send_z(give, z_partner)
     own, ahead, back, ahead_rest, back_rest = pl.pallas_call(
-        functools.partial(partial_kernel, LOG2E / (epsilon * D)),
+        pair_kernel,
         out_shape=[
             jax.ShapeDtypeStruct(chunk, f32),
             jax.ShapeDtypeStruct(chunk, f32),
@@ -246,32 +295,21 @@
             jax.ShapeDtypeStruct((middle - 1,) + chunk, f32),
             jax.ShapeDtypeStruct((middle - 2,) + chunk, f32),
         ],
-        in_specs=[SMEM] + [VMEM] * (2 + YS),
+        in_specs=[VMEM] * 2,
         out_specs=[VMEM] * 5,
-        scratch_shapes=[
-            pltpu.VMEM((group, rows, features), jnp.bfloat16),
-            pltpu.VMEM((YS * rows, features), jnp.bfloat16),
-            pltpu.VMEM((1, wide), f32),
-            pltpu.VMEM((depth,) + chunk, f32),
-        ],
         compiler_params=PARAMS,
-    )(place, x_here, x_there, *ys)
-    late_rows, own = lax.optimization_barrier((data_rows, own))
-
+    )(keep, got)
     for step in range(middle):
-        ahead = send_z(ahead, 1)
+        ahead = send_z(ahead, lambda z, c: z + 2 if c == 0 else z - 2)
         if step < middle - 1:
             ahead = ahead + ahead_rest[step]
-            back = send_z(back, -1)
+            back = send_z(back, lambda z, c: z - 2 if c == 0 else z + 2)
             if step < middle - 2:
                 back = back + back_rest[step]
     own = own + ahead + back
 
+    everything, own = lax.optimization_barrier((everything, own))
     gathered = lax.all_gather(own, "dp")
-    z_groups = [
-        [((y * group) + k) * depth + d for y in range(YS) for d in range(depth)] for k in range(group)
-    ]
-    sharers = YS * depth
     few = tall // depth
     for step in range(ITERS):
         last = step == ITERS - 1
@@ -306,19 +344,22 @@
             functools.partial(columns_kernel, log_weight),
             out_shape=[
                 jax.ShapeDtypeStruct((lines, n), f32),
-                jax.ShapeDtypeStruct((YS if last else sharers, YS, rows), f32),
+                jax.ShapeDtypeStruct((YS if last else depth, YS, rows), f32),
             ],
             in_specs=[VMEM] * 2,
             out_specs=[VMEM] * 2,
             scratch_shapes=[pltpu.VMEM((lines * n, wide), f32)],
             compiler_params=PARAMS,
         )(a if last else own, part)
-        if last:
-            part = swap(part, y_groups)
-        else:
-            part = lax.all_to_all(
-                part, ("noise", "dp"), 0, 0, axis_index_groups=z_groups, tiled=True
-            )
+        if not last:
+            part = pl.pallas_call(
+                join_kernel,
+                out_shape=jax.ShapeDtypeStruct((YS, YS, rows), f32),
+                in_specs=[VMEM],
+                out_specs=VMEM,
+                compiler_params=PARAMS,
+            )(lax.all_to_all(part, "dp", 0, 0, tiled=True))
+        part = swap(part, y_groups)
     plan = pl.pallas_call(
         functools.partial(plan_kernel, log_weight),
         out_shape=jax.ShapeDtypeStruct((group, rows + 16, wide), jnp.bfloat16),
@@ -328,7 +369,6 @@
     )(a, u, part)
     plan = swap(plan, x_groups)
 
-    everything = lax.all_gather(late_rows, "noise", axis=0, tiled=True)
     targets, noise_potential, data_potential = pl.pallas_call(
         functools.partial(target_kernel, epsilon / LOG2E),
         grid=(YS,),

time: 292 us -> 270 us (0.925)
  starting transfers between devices: 85.6 us -> 53.7 us
  waiting for transfers between devices: 16.2 us -> 40.6 us
  blocking collectives: 156 us -> 139 us
    ppermute x15 -> x8, starting transfers between devices: 57.6 us -> 30.3 us  [send_z(): return lax.ppermute(value, ('noise', 'dp'), pairs)]
    ppermute x15 -> x8, waiting for transfers between devices: 4.14 us -> 26.8 us  [send_z(): return lax.ppermute(value, ('noise', 'dp'), pairs)]
    all_to_all x3, blocking collectives: 69.7 us -> 52 us  [on_device(): lax.all_to_all(part, 'dp', 0, 0, tiled=True)]
    ppermute x7 -> x6, starting transfers between devices: 27.9 us -> 23.3 us  [the longest x2 9.35 us: to_other_core(): lax.ppermute(value, 'noise', noise_pairs(lambda y, x, c: (y, x, 1 - c)))]
    ppermute x7 -> x6, waiting for transfers between devices: 9.03 us -> 12.7 us  [the longest x2 6.07 us: swap_x(): lax.ppermute(value, 'noise', noise_pairs(lambda y, x, c: (y, x ^ by[c], c)))]
    all_to_all x6 -> x9, blocking collectives: 86.6 us -> 87.4 us  [swap(): lax.all_to_all(value, 'noise', 0, 0, axis_index_groups=groups, tiled=True)]
  transfers between devices with their start and end apart: 24 -> 16, of which waited for: 9 -> 13; matrix products, arithmetic and copies ran while one was open for 0% -> 1% of each run, Pallas kernels for 1% -> 2%
where the time goes in v4:
time: 270 us; the launch traced here: 269 us
  blocking collectives  139 us (51%)
  starting transfers between devices  53.7 us (20%)
  waiting for transfers between devices  40.6 us (15%)
  between operations  14.3 us (5%)
  Pallas kernels  13.8 us (5%)
  local copies, waits for them, and re-layouts  4.3 us (2%)
  other arithmetic  2.82 us (1%)
    all_to_all x9, blocking collectives, swap(): lax.all_to_all(value, 'noise', 0, 0, axis_index_groups=groups, tiled=True)  87.4 us
    all_to_all x3, blocking collectives, on_device(): lax.all_to_all(part, 'dp', 0, 0, tiled=True)  52 us
    ppermute x8, starting transfers between devices, send_z(): return lax.ppermute(value, ('noise', 'dp'), pairs)  30.3 us
    ppermute x8, waiting for transfers between devices, send_z(): return lax.ppermute(value, ('noise', 'dp'), pairs)  26.8 us
    ppermute x2, starting transfers between devices, to_other_core(): lax.ppermute(value, 'noise', noise_pairs(lambda y, x, c: (y, x, 1 - c)))  9.35 us
    ppermute x2, starting transfers between devices, swap_x(): lax.ppermute(value, 'noise', noise_pairs(lambda y, x, c: (y, x ^ by[c], c)))  7.14 us
    ppermute x2, starting transfers between devices, swap_y(): lax.ppermute(value, 'noise', noise_pairs(lambda y, x, c: (y ^ by[c], x, c)))  6.86 us
    ppermute x2, waiting for transfers between devices, swap_x(): lax.ppermute(value, 'noise', noise_pairs(lambda y, x, c: (y, x ^ by[c], c)))  6.07 us
  transfers between devices with their start and end apart: 16, of which 13 were waited for; matrix products, arithmetic and copies ran while one was open for 1% of the time, Pallas kernels for 2%

profile of v4, /device:TPU:1, one launch (start us, length us, event | category | flops | bytes accessed | tf_op | source)
XLA Modules:
  0.0 268.9 jit_solution(8568303567402477743)
XLA Ops:
  7.2 0.0 all-gather.4.cloned.1.call-start
  7.2 5.2 %collective-permute-start = (bf16[128,1024]{1,0:T(8,128)(2,1)}, bf16[128,1024]{1,0:T(8,128)(2,1)S(1)}, u32[]{:S(2)}, u32[]{:S(2)}) collective-permute-start(bf16[128,1024]{1,0:T(8,128)(2,1)} %param.2), channel_id=1, source_target_pairs={{0,32},{16,112},{32,0},{48,80},{64,96},{80,48},{96,64},{112,16},{1... | collective-permute-start | bytes 786440 | tf_op jit(solution)/shard_map/ppermute | solution.py:39
  12.4 4.6 %collective-permute-start.1 = (bf16[128,1024]{1,0:T(8,128)(2,1)}, bf16[128,1024]{1,0:T(8,128)(2,1)S(1)}, u32[]{:S(2)}, u32[]{:S(2)}) collective-permute-start(bf16[128,1024]{1,0:T(8,128)(2,1)} %param.3), channel_id=1, source_target_pairs={{0,128},{16,400},{32,160},{48,432},{64,192},{80,464},{96,224},{112... | collective-permute-start | bytes 786440 | tf_op jit(solution)/shard_map/ppermute | solution.py:43
  17.1 1.0 pad_maximum_fusion.refs_0_
  18.1 3.0 %collective-permute-done.1 = bf16[128,1024]{1,0:T(8,128)(2,1)S(1)} collective-permute-done((bf16[128,1024]{1,0:T(8,128)(2,1)}, bf16[128,1024]{1,0:T(8,128)(2,1)S(1)}, u32[]{:S(2)}, u32[]{:S(2)}) %collective-permute-start.1) | collective-permute-done | bytes 262176 | tf_op jit(solution)/shard_map/ppermute | solution.py:43
  21.0 1.0 pad_maximum_fusion.1.refs_4_
  22.0 1.9 collective-permute-start.2
  24.0 2.2 collective-permute-start.3
  26.2 6.1 %collective-permute-done.2.refs_1_ = bf16[256,1024]{1,0:T(8,128)(2,1)S(1)} collective-permute-done((bf16[256,1024]{1,0:T(8,128)(2,1)S(1)}, bf16[256,1024]{1,0:T(8,128)(2,1)S(1)}, u32[]{:S(2)}, u32[]{:S(2)}) %collective-permute-start.2) | collective-permute-done | bytes 524320 | tf_op jit(solution)/shard_map/ppermute | solution.py:39
  32.2 1.9 collective-permute-done.3.refs_5_
  34.2 0.0 all-gather.4.cloned.1.call-update
  34.2 0.0 all-gather.6.cloned.1.call-start
  34.3 7.4 %collective-permute-start.4 = (bf16[256,1024]{1,0:T(8,128)(2,1)S(1)}, bf16[256,1024]{1,0:T(8,128)(2,1)S(1)}, u32[]{:S(2)}, u32[]{:S(2)}) collective-permute-start(bf16[256,1024]{1,0:T(8,128)(2,1)S(1)} %pad_maximum_fusion.refs_0_), channel_id=1, source_target_pairs={{0,16},{16,0},{32,48},{48,32},{64,80},{80,64},{96,112},{112,96},{1... | collective-permute-start | bytes 1572872 | tf_op jit(solution)/shard_map/ppermute | solution.py:31
  41.7 1.9 collective-permute-start.5
  43.7 0.1 pad_add_fusion.place_ref
  43.7 1.8 collective-permute-done.5.refs_3_
  45.5 3.8 %shard_map.49 = (f32[8,64,512]{2,1,0:T(8,128)S(1)}, f32[8,64,512]{2,1,0:T(8,128)S(1)}) custom-call(s32[4]{0:T(128)S(1)} %pad_add_fusion.place_ref, bf16[256,1024]{1,0:T(8,128)(2,1)S(1)} %pad_maximum_fusion.refs_0_, bf16[256,1024]{1,0:T(8,128)(2,1)S(1)} %collective-permute-done.2.refs_1_, bf16[256,1024]{1,0:T(8,128)(2,1)S(1)} %collective-permute-done.4.refs_2_, ...), custom_call_target="tpu_custom_call" | custom-call | tf_op jit(solution)/shard_map/pallas_call | solution.py:274
  49.3 9.3 %collective-permute-start.6 = (f32[8,64,512]{2,1,0:T(8,128)S(1)}, f32[8,64,512]{2,1,0:T(8,128)S(1)}, u32[]{:S(2)}, u32[]{:S(2)}) collective-permute-start(f32[8,64,512]{2,1,0:T(8,128)S(1)} %get-tuple-element.33), channel_id=1, source_target_pairs={{0,1},{1,0},{2,3},{3,2},{4,5},{5,4},{6,7},{7,6},{8,9},{9,8},{10,11... | collective-permute-start | bytes 3145736 | tf_op jit(solution)/shard_map/ppermute | solution.py:51
  58.6 12.5 %collective-permute-done.6.got = f32[8,64,512]{2,1,0:T(8,128)S(1)} collective-permute-done((f32[8,64,512]{2,1,0:T(8,128)S(1)}, f32[8,64,512]{2,1,0:T(8,128)S(1)}, u32[]{:S(2)}, u32[]{:S(2)}) %collective-permute-start.6) | collective-permute-done | bytes 1048608 | tf_op jit(solution)/shard_map/ppermute | solution.py:51
  71.1 0.1 shard_map.50
  71.2 3.9 %collective-permute-start.7 = (f32[64,512]{1,0:T(8,128)S(1)}, f32[64,512]{1,0:T(8,128)S(1)}, u32[]{:S(2)}, u32[]{:S(2)}) collective-permute-start(f32[64,512]{1,0:T(8,128)S(1)} %get-tuple-element.35), channel_id=1, source_target_pairs={{0,2},{1,3},{2,4},{3,5},{4,6},{5,7},{6,8},{7,9},{8,10},{9,11},{10,... | collective-permute-start | bytes 393224 | tf_op jit(solution)/shard_map/ppermute | solution.py:51
  75.1 2.3 collective-permute-start.11
  77.4 3.2 %collective-permute-done.7 = f32[64,512]{1,0:T(8,128)S(1)} collective-permute-done((f32[64,512]{1,0:T(8,128)S(1)}, f32[64,512]{1,0:T(8,128)S(1)}, u32[]{:S(2)}, u32[]{:S(2)}) %collective-permute-start.7) | collective-permute-done | bytes 131104 | tf_op jit(solution)/shard_map/ppermute | solution.py:51
  80.6 2.3 collective-permute-start.8
  82.9 1.3 collective-permute-done.11
  84.3 2.5 collective-permute-start.12
  86.8 0.7 collective-permute-done.8
  87.5 4.2 %collective-permute-start.9 = (f32[64,512]{1,0:T(8,128)S(1)}, f32[64,512]{1,0:T(8,128)S(1)}, u32[]{:S(2)}, u32[]{:S(2)}) collective-permute-start(f32[64,512]{1,0:T(8,128)S(1)} %bitcast_add_fusion.3), channel_id=1, source_target_pairs={{0,2},{1,3},{2,4},{3,5},{4,6},{5,7},{6,8},{7,9},{8,10},{9,11},{10,... | collective-permute-start | bytes 393224 | tf_op jit(solution)/shard_map/ppermute | solution.py:51
  91.7 0.5 collective-permute-done.12
  92.3 2.6 collective-permute-start.13
  94.9 1.7 collective-permute-done.9
  96.5 3.2 %collective-permute-start.10 = (f32[64,512]{1,0:T(8,128)S(1)}, f32[64,512]{1,0:T(8,128)S(1)}, u32[]{:S(2)}, u32[]{:S(2)}) collective-permute-start(f32[64,512]{1,0:T(8,128)S(1)} %bitcast_add_fusion.2), channel_id=1, source_target_pairs={{0,2},{1,3},{2,4},{3,5},{4,6},{5,7},{6,8},{7,9},{8,10},{9,11},{10,... | collective-permute-start | bytes 393224 | tf_op jit(solution)/shard_map/ppermute | solution.py:51
  99.7 1.0 collective-permute-done.13
  100.7 5.9 %collective-permute-done.10 = f32[64,512]{1,0:T(8,128)S(1)} collective-permute-done((f32[64,512]{1,0:T(8,128)S(1)}, f32[64,512]{1,0:T(8,128)S(1)}, u32[]{:S(2)}, u32[]{:S(2)}) %collective-permute-start.10) | collective-permute-done | bytes 131104 | tf_op jit(solution)/shard_map/ppermute | solution.py:51
  106.7 0.7 add_add_fusion.a_ref
  107.4 1.1 all-gather.4.cloned.1.call-done.y_ref
  108.4 0.0 all-gather.6.cloned.1.call-update
  108.5 0.0 copy-start
  108.5 0.9 copy-done
  109.4 0.2 shard_map.51
  109.6 8.9 %all_to_all.60.parts_ref = f32[8,1,64]{2,1,0:T(1,128)S(1)} all-to-all(f32[8,1,64]{2,1,0:T(1,128)S(1)} %shard_map.51), channel_id=1, replica_groups={{0,16,32,48,64,80,96,112},{128,144,160,176,192,208,224,240},{256,272,28..., dimensions={0} | all-to-all | bytes 4096 | tf_op jit(solution)/shard_map/all_to_all | solution.py:262
  118.4 0.5 shard_map.52
  119.0 24.0 %all_to_all.61.parts_ref = f32[16,4,128]{2,1,0:T(4,128)S(1)} all-to-all(f32[16,4,128]{2,1,0:T(4,128)S(1)} %get-tuple-element.40), channel_id=1, replica_groups=mesh['noise'=32,'dp'=16] {'dp'}, dimensions={0} | all-to-all | bytes 65536 | tf_op jit(solution)/shard_map/all_to_all | solution.py:361
  143.0 7.9 %all_to_all.62.parts_ref = f32[4,4,128]{2,1,0:T(4,128)S(1)} all-to-all(f32[4,4,128]{2,1,0:T(4,128)S(1)} %shard_map.53), channel_id=1, replica_groups={{0,128,256,384},{16,144,272,400},{32,160,288,416},{48,176,304,432},{64,..., dimensions={0} | all-to-all | bytes 16384 | tf_op jit(solution)/shard_map/all_to_all | solution.py:262
  150.9 0.9 copy-done.1
  151.8 0.2 shard_map.54
  152.1 10.3 %all_to_all.63.parts_ref = f32[8,1,64]{2,1,0:T(1,128)S(1)} all-to-all(f32[8,1,64]{2,1,0:T(1,128)S(1)} %shard_map.54), channel_id=1, replica_groups={{0,16,32,48,64,80,96,112},{128,144,160,176,192,208,224,240},{256,272,28..., dimensions={0} | all-to-all | bytes 4096 | tf_op jit(solution)/shard_map/all_to_all | solution.py:262
  162.4 0.5 shard_map.55
  162.9 14.0 %all_to_all.64.parts_ref = f32[16,4,128]{2,1,0:T(4,128)S(1)} all-to-all(f32[16,4,128]{2,1,0:T(4,128)S(1)} %get-tuple-element.41), channel_id=1, replica_groups=mesh['noise'=32,'dp'=16] {'dp'}, dimensions={0} | all-to-all | bytes 65536 | tf_op jit(solution)/shard_map/all_to_all | solution.py:361
  176.9 6.5 %all_to_all.65.parts_ref = f32[4,4,128]{2,1,0:T(4,128)S(1)} all-to-all(f32[4,4,128]{2,1,0:T(4,128)S(1)} %shard_map.56), channel_id=1, replica_groups={{0,128,256,384},{16,144,272,400},{32,160,288,416},{48,176,304,432},{64,..., dimensions={0} | all-to-all | bytes 16384 | tf_op jit(solution)/shard_map/all_to_all | solution.py:262
  183.5 0.9 copy-done.2
  184.4 0.2 shard_map.57
  184.6 9.8 %all_to_all.66.parts_ref = f32[8,1,64]{2,1,0:T(1,128)S(1)} all-to-all(f32[8,1,64]{2,1,0:T(1,128)S(1)} %shard_map.57), channel_id=1, replica_groups={{0,16,32,48,64,80,96,112},{128,144,160,176,192,208,224,240},{256,272,28..., dimensions={0} | all-to-all | bytes 4096 | tf_op jit(solution)/shard_map/all_to_all | solution.py:262
  194.4 0.5 shard_map.58
  195.0 14.0 %all_to_all.67.parts_ref = f32[16,4,128]{2,1,0:T(4,128)S(1)} all-to-all(f32[16,4,128]{2,1,0:T(4,128)S(1)} %get-tuple-element.42), channel_id=1, replica_groups=mesh['noise'=32,'dp'=16] {'dp'}, dimensions={0} | all-to-all | bytes 65536 | tf_op jit(solution)/shard_map/all_to_all | solution.py:361
  209.0 6.5 %all_to_all.68.parts_ref = f32[4,4,128]{2,1,0:T(4,128)S(1)} all-to-all(f32[4,4,128]{2,1,0:T(4,128)S(1)} %shard_map.59), channel_id=1, replica_groups={{0,128,256,384},{16,144,272,400},{32,160,288,416},{48,176,304,432},{64,..., dimensions={0} | all-to-all | bytes 16384 | tf_op jit(solution)/shard_map/all_to_all | solution.py:262
  215.5 1.6 copy-done.3
  217.1 0.7 shard_map.60
  217.8 10.0 %all_to_all.69.parts_ref = f32[8,8,128]{2,1,0:T(8,128)S(1)} all-to-all(f32[8,8,128]{2,1,0:T(8,128)S(1)} %get-tuple-element.44), channel_id=1, replica_groups={{0,16,32,48,64,80,96,112},{128,144,160,176,192,208,224,240},{256,272,28..., dimensions={0} | all-to-all | bytes 65536 | tf_op jit(solution)/shard_map/all_to_all | solution.py:262
  227.8 0.6 shard_map.61
  228.4 6.5 %all_to_all.70.parts_ref = f32[4,4,128]{2,1,0:T(4,128)S(1)} all-to-all(f32[4,4,128]{2,1,0:T(4,128)S(1)} %get-tuple-element.46), channel_id=1, replica_groups={{0,128,256,384},{16,144,272,400},{32,160,288,416},{48,176,304,432},{64,..., dimensions={0} | all-to-all | bytes 16384 | tf_op jit(solution)/shard_map/all_to_all | solution.py:262
  234.9 0.4 shard_map.62
  235.3 20.9 %all_to_all.71.plan_ref = bf16[8,144,512]{2,1,0:T(8,128)(2,1)S(1)} all-to-all(bf16[8,144,512]{2,1,0:T(8,128)(2,1)S(1)} %shard_map.62), channel_id=1, replica_groups={{0,16,32,48,64,80,96,112},{128,144,160,176,192,208,224,240},{256,272,28..., dimensions={0} | all-to-all | bytes 2359296 | tf_op jit(solution)/shard_map/all_to_all | solution.py:262
  256.2 5.9 %shard_map.63 = (bf16[128,1024]{1,0:T(8,128)(2,1)}, f32[1,128]{1,0:T(1,128)}, f32[1,256]{1,0:T(1,128)}) custom-call(s32[4]{0:T(128)S(1)} %pad_add_fusion.place_ref, bf16[8,144,512]{2,1,0:T(8,128)(2,1)S(1)} %all_to_all.71.plan_ref, f32[8,128]{1,0:T(8,128)S(1)} %get-tuple-element.45.u_ref, bf16[4096,1024]{1,0:T(8,128)(2,1)} %all-gather.4.cloned.1.call-done.y_ref), custom_call_target="tpu_custom_call" | custom-call | tf_op jit(solution)/shard_map/pallas_call | solution.py:372
  (14 shorter events, 0.2 us)
Async XLA Ops:
  7.2 101.3 %all-gather.4.cloned.1.call-start = ((), (), s32[]{:S(2)}) async-start(), calls=%async_computation.12 | async-start | bytes 8650752 | tf_op jit(solution)/shard_map/all_gather | solution.py:269
  7.2 9.9 %collective-permute-start = (bf16[128,1024]{1,0:T(8,128)(2,1)}, bf16[128,1024]{1,0:T(8,128)(2,1)S(1)}, u32[]{:S(2)}, u32[]{:S(2)}) collective-permute-start(bf16[128,1024]{1,0:T(8,128)(2,1)} %param.2), channel_id=1, source_target_pairs={{0,32},{16,112},{32,0},{48,80},{64,96},{80,48},{96,64},{112,16},{1... | collective-permute-start | bytes 786440 | tf_op jit(solution)/shard_map/ppermute | solution.py:39
  12.4 8.6 %collective-permute-start.1 = (bf16[128,1024]{1,0:T(8,128)(2,1)}, bf16[128,1024]{1,0:T(8,128)(2,1)S(1)}, u32[]{:S(2)}, u32[]{:S(2)}) collective-permute-start(bf16[128,1024]{1,0:T(8,128)(2,1)} %param.3), channel_id=1, source_target_pairs={{0,128},{16,400},{32,160},{48,432},{64,192},{80,464},{96,224},{112... | collective-permute-start | bytes 786440 | tf_op jit(solution)/shard_map/ppermute | solution.py:43
  22.0 10.2 %collective-permute-start.2 = (bf16[256,1024]{1,0:T(8,128)(2,1)S(1)}, bf16[256,1024]{1,0:T(8,128)(2,1)S(1)}, u32[]{:S(2)}, u32[]{:S(2)}) collective-permute-start(bf16[256,1024]{1,0:T(8,128)(2,1)S(1)} %pad_maximum_fusion.refs_0_), channel_id=1, source_target_pairs={{0,96},{16,48},{32,64},{48,16},{64,32},{80,112},{96,0},{112,80},{1... | collective-permute-start | bytes 1572872 | tf_op jit(solution)/shard_map/ppermute | solution.py:39
  24.0 10.2 %collective-permute-start.3 = (bf16[256,1024]{1,0:T(8,128)(2,1)S(1)}, bf16[256,1024]{1,0:T(8,128)(2,1)S(1)}, u32[]{:S(2)}, u32[]{:S(2)}) collective-permute-start(bf16[256,1024]{1,0:T(8,128)(2,1)S(1)} %pad_maximum_fusion.1.refs_4_), channel_id=1, source_target_pairs={{0,384},{16,144},{32,416},{48,176},{64,448},{80,208},{96,480},{112... | collective-permute-start | bytes 1572872 | tf_op jit(solution)/shard_map/ppermute | solution.py:43
  34.2 181.3 %all-gather.6.cloned.1.call-start = ((), (), s32[]{:S(2)}) async-start(), calls=%async_computation.13 | async-start | bytes 2228224 | tf_op jit(solution)/shard_map/all_gather | solution.py:312
  34.3 9.5 %collective-permute-start.4 = (bf16[256,1024]{1,0:T(8,128)(2,1)S(1)}, bf16[256,1024]{1,0:T(8,128)(2,1)S(1)}, u32[]{:S(2)}, u32[]{:S(2)}) collective-permute-start(bf16[256,1024]{1,0:T(8,128)(2,1)S(1)} %pad_maximum_fusion.refs_0_), channel_id=1, source_target_pairs={{0,16},{16,0},{32,48},{48,32},{64,80},{80,64},{96,112},{112,96},{1... | collective-permute-start | bytes 1572872 | tf_op jit(solution)/shard_map/ppermute | solution.py:31
  41.7 3.8 %collective-permute-start.5 = (bf16[256,1024]{1,0:T(8,128)(2,1)S(1)}, bf16[256,1024]{1,0:T(8,128)(2,1)S(1)}, u32[]{:S(2)}, u32[]{:S(2)}) collective-permute-start(bf16[256,1024]{1,0:T(8,128)(2,1)S(1)} %collective-permute-done.2.refs_1_), channel_id=1, source_target_pairs={{0,16},{16,0},{32,48},{48,32},{64,80},{80,64},{96,112},{112,96},{1... | collective-permute-start | bytes 1572872 | tf_op jit(solution)/shard_map/ppermute | solution.py:31
  49.3 21.8 %collective-permute-start.6 = (f32[8,64,512]{2,1,0:T(8,128)S(1)}, f32[8,64,512]{2,1,0:T(8,128)S(1)}, u32[]{:S(2)}, u32[]{:S(2)}) collective-permute-start(f32[8,64,512]{2,1,0:T(8,128)S(1)} %get-tuple-element.33), channel_id=1, source_target_pairs={{0,1},{1,0},{2,3},{3,2},{4,5},{5,4},{6,7},{7,6},{8,9},{9,8},{10,11... | collective-permute-start | bytes 3145736 | tf_op jit(solution)/shard_map/ppermute | solution.py:51
  71.2 9.4 %collective-permute-start.7 = (f32[64,512]{1,0:T(8,128)S(1)}, f32[64,512]{1,0:T(8,128)S(1)}, u32[]{:S(2)}, u32[]{:S(2)}) collective-permute-start(f32[64,512]{1,0:T(8,128)S(1)} %get-tuple-element.35), channel_id=1, source_target_pairs={{0,2},{1,3},{2,4},{3,5},{4,6},{5,7},{6,8},{7,9},{8,10},{9,11},{10,... | collective-permute-start | bytes 393224 | tf_op jit(solution)/shard_map/ppermute | solution.py:51
  75.1 9.2 %collective-permute-start.11 = (f32[64,512]{1,0:T(8,128)S(1)}, f32[64,512]{1,0:T(8,128)S(1)}, u32[]{:S(2)}, u32[]{:S(2)}) collective-permute-start(f32[64,512]{1,0:T(8,128)S(1)} %get-tuple-element.37), channel_id=1, source_target_pairs={{0,14},{1,15},{2,0},{3,1},{4,2},{5,3},{6,4},{7,5},{8,6},{9,7},{10,... | collective-permute-start | bytes 393224 | tf_op jit(solution)/shard_map/ppermute | solution.py:51
  80.6 6.9 %collective-permute-start.8 = (f32[64,512]{1,0:T(8,128)S(1)}, f32[64,512]{1,0:T(8,128)S(1)}, u32[]{:S(2)}, u32[]{:S(2)}) collective-permute-start(f32[64,512]{1,0:T(8,128)S(1)} %bitcast_add_fusion.4), channel_id=1, source_target_pairs={{0,2},{1,3},{2,4},{3,5},{4,6},{5,7},{6,8},{7,9},{8,10},{9,11},{10,... | collective-permute-start | bytes 393224 | tf_op jit(solution)/shard_map/ppermute | solution.py:51
  84.3 8.0 %collective-permute-start.12 = (f32[64,512]{1,0:T(8,128)S(1)}, f32[64,512]{1,0:T(8,128)S(1)}, u32[]{:S(2)}, u32[]{:S(2)}) collective-permute-start(f32[64,512]{1,0:T(8,128)S(1)} %bitcast_add_fusion.1), channel_id=1, source_target_pairs={{0,14},{1,15},{2,0},{3,1},{4,2},{5,3},{6,4},{7,5},{8,6},{9,7},{10,... | collective-permute-start | bytes 393224 | tf_op jit(solution)/shard_map/ppermute | solution.py:51
  87.5 9.0 %collective-permute-start.9 = (f32[64,512]{1,0:T(8,128)S(1)}, f32[64,512]{1,0:T(8,128)S(1)}, u32[]{:S(2)}, u32[]{:S(2)}) collective-permute-start(f32[64,512]{1,0:T(8,128)S(1)} %bitcast_add_fusion.3), channel_id=1, source_target_pairs={{0,2},{1,3},{2,4},{3,5},{4,6},{5,7},{6,8},{7,9},{8,10},{9,11},{10,... | collective-permute-start | bytes 393224 | tf_op jit(solution)/shard_map/ppermute | solution.py:51
  92.3 8.5 %collective-permute-start.13 = (f32[64,512]{1,0:T(8,128)S(1)}, f32[64,512]{1,0:T(8,128)S(1)}, u32[]{:S(2)}, u32[]{:S(2)}) collective-permute-start(f32[64,512]{1,0:T(8,128)S(1)} %bitcast_add_fusion), channel_id=1, source_target_pairs={{0,14},{1,15},{2,0},{3,1},{4,2},{5,3},{6,4},{7,5},{8,6},{9,7},{10,... | collective-permute-start | bytes 393224 | tf_op jit(solution)/shard_map/ppermute | solution.py:51
  96.5 10.1 %collective-permute-start.10 = (f32[64,512]{1,0:T(8,128)S(1)}, f32[64,512]{1,0:T(8,128)S(1)}, u32[]{:S(2)}, u32[]{:S(2)}) collective-permute-start(f32[64,512]{1,0:T(8,128)S(1)} %bitcast_add_fusion.2), channel_id=1, source_target_pairs={{0,2},{1,3},{2,4},{3,5},{4,6},{5,7},{6,8},{7,9},{8,10},{9,11},{10,... | collective-permute-start | bytes 393224 | tf_op jit(solution)/shard_map/ppermute | solution.py:51
  108.5 0.9 copy-start
  150.9 0.9 copy-start.1
  183.4 0.9 copy-start.2
  215.5 1.6 copy-start.3
Sparse Core Ops, SparseCore 0:
  34.3 74.0 all-gather.3
  111.1 64.5 all-gather.5

commit v5 on v4

--- a/solution.py
+++ b/solution.py
@@ -81,8 +81,7 @@
     for k in range(YS):
         block = slice(k * rows, (k + 1) * rows)
         y_squares[:, block] = scale * squares_row(y_all[block, :])
-    up = jnp.where(c == 0, lax.rem(z, 2) == 0, lax.rem(z, 2) == 1)
-    partner = lax.rem(z + jnp.where(up, 1, depth - 1), depth)
+    partner = lax.rem(z + jnp.where(lax.rem(z + c, 2) == 0, 1, depth - 1), depth)
     places = []
     for t in range(depth):
         same = lax.rem(z + t, 2) == 0
@@ -161,14 +160,19 @@
     row_sums(a_ref, row_of(parts_ref, log_weight), out_ref, out_ref.shape[2])
 
 
-def all_rows_kernel(log_weight, chunks_ref, parts_ref, a_ref, out_ref):
+def all_rows_kernel(log_weight, place_ref, pairs_ref, parts_ref, a_ref, out_ref):
     blocks, n = out_ref.shape[1:]
-    depth = chunks_ref.shape[0]
+    depth = 2 * pairs_ref.shape[0]
     high = n // depth
-    for z in range(depth):
-        for block in range(blocks):
-            at = block * n + z * high
-            a_ref[at : at + high, :] = chunks_ref[z, block * high : (block + 1) * high, :]
+    z = place_ref[0]
+    for k in range(depth // 2):
+        source = 2 * k + lax.rem(z, 2)
+        partner = lax.bitwise_xor(source, 1)
+        for half, t in enumerate((source, partner)):
+            for block in range(blocks):
+                at = pl.multiple_of(block * n + t * high, high)
+                rows = pairs_ref[k, half * blocks * high + block * high : half * blocks * high + (block + 1) * high, :]
+                a_ref[pl.ds(at, high), :] = rows
     row_sums(a_ref, row_of(parts_ref, log_weight), out_ref, n)
 
 
@@ -195,11 +199,6 @@
     copy_out(out_ref)
 
 
-def join_kernel(parts_ref, out_ref):
-    out_ref[0] = joined(parts_ref[...])
-    copy_out(out_ref)
-
-
 def plan_kernel(log_weight, a_ref, u_ref, parts_ref, out_ref):
     v = row_of(parts_ref, log_weight)
     u = u_ref[...] - log_weight
@@ -265,7 +264,9 @@
     y_near = jnp.concatenate([data_rows, swap_y(data_rows, FIRST)], axis=0)
     x_near, y_near = lax.optimization_barrier((x_near, y_near))
     x_far, y_far = swap_x(x_near, SECOND), swap_y(y_near, SECOND)
-    x_far, y_far, late_rows = lax.optimization_barrier((x_far, y_far, data_rows))
+    x_far, y_far, x_there, late_rows = lax.optimization_barrier(
+        (x_far, y_far, to_other_core(x_near), data_rows)
+    )
     everything = lax.all_gather(late_rows, "noise", axis=0, tiled=True)
     tall, wide = group * rows, YS * rows
     half = depth // 2
@@ -283,7 +284,7 @@
             pltpu.VMEM((depth,) + chunk, f32),
         ],
         compiler_params=PARAMS,
-    )(place, x_near, x_far, to_other_core(x_near), to_other_core(x_far), y_near, y_far)
+    )(place, x_near, x_far, x_there, to_other_core(x_far), y_near, y_far)
 
     got = send_z(give, z_partner)
     own, ahead, back, ahead_rest, back_rest = pl.pallas_call(
@@ -308,58 +309,63 @@
                 back = back + back_rest[step]
     own = own + ahead + back
 
-    everything, own = lax.optimization_barrier((everything, own))
-    gathered = lax.all_gather(own, "dp")
-    few = tall // depth
+    pair = jnp.concatenate([own, send_z(own, lambda z, c: z ^ 1)], axis=0)
+    everything, sent_pair = lax.optimization_barrier((everything, pair))
+    gathered = lax.all_gather(
+        sent_pair, "dp", axis_index_groups=[list(range(k, depth, 2)) for k in range(2)]
+    )
+    z_groups = [
+        [((y * group) + k) * depth + d for y in range(YS) for d in range(parity, depth, 2)]
+        for k in range(group)
+        for parity in range(2)
+    ]
+    few = 2 * tall // depth
+    row_shape = jax.ShapeDtypeStruct((group, 1, few), f32)
+    part = pl.pallas_call(
+        first_rows_kernel,
+        out_shape=row_shape,
+        in_specs=[VMEM],
+        out_specs=VMEM,
+        compiler_params=PARAMS,
+    )(pair)
     for step in range(ITERS):
-        last = step == ITERS - 1
-        lines, n = (group, rows) if last else (1, few)
+        first = step == 0
+        lines, n = (1, few) if first else (group, rows)
         row_shape = jax.ShapeDtypeStruct((group, lines, n), f32)
-        if step == 0:
-            part = pl.pallas_call(
-                first_rows_kernel,
-                out_shape=row_shape,
-                in_specs=[VMEM],
-                out_specs=VMEM,
+        if step == 1:
+            a, part = pl.pallas_call(
+                functools.partial(all_rows_kernel, log_weight),
+                out_shape=[jax.ShapeDtypeStruct((tall, wide), f32), row_shape],
+                in_specs=[SMEM] + [VMEM] * 2,
+                out_specs=[VMEM] * 2,
                 compiler_params=PARAMS,
-            )(own)
-        elif not last:
+            )(place, gathered, part)
+        elif step > 1:
             part = pl.pallas_call(
                 functools.partial(rows_kernel, log_weight),
                 out_shape=row_shape,
                 in_specs=[VMEM] * 2,
                 out_specs=VMEM,
                 compiler_params=PARAMS,
-            )(own, part)
-        else:
-            a, part = pl.pallas_call(
-                functools.partial(all_rows_kernel, log_weight),
-                out_shape=[jax.ShapeDtypeStruct((tall, wide), f32), row_shape],
-                in_specs=[VMEM] * 2,
-                out_specs=[VMEM] * 2,
-                compiler_params=PARAMS,
-            )(gathered, part)
+            )(a, part)
         part = swap(part, x_groups)
         u, part = pl.pallas_call(
             functools.partial(columns_kernel, log_weight),
             out_shape=[
                 jax.ShapeDtypeStruct((lines, n), f32),
-                jax.ShapeDtypeStruct((YS if last else depth, YS, rows), f32),
+                jax.ShapeDtypeStruct((YS * half if first else YS, YS, rows), f32),
             ],
             in_specs=[VMEM] * 2,
             out_specs=[VMEM] * 2,
             scratch_shapes=[pltpu.VMEM((lines * n, wide), f32)],
             compiler_params=PARAMS,
-        )(a if last else own, part)
-        if not last:
-            part = pl.pallas_call(
-                join_kernel,
-                out_shape=jax.ShapeDtypeStruct((YS, YS, rows), f32),
-                in_specs=[VMEM],
-                out_specs=VMEM,
-                compiler_params=PARAMS,
-            )(lax.all_to_all(part, "dp", 0, 0, tiled=True))
-        part = swap(part, y_groups)
+        )(pair if first else a, part)
+        if first:
+            part = lax.all_to_all(
+                part, ("noise", "dp"), 0, 0, axis_index_groups=z_groups, tiled=True
+            )
+        else:
+            part = swap(part, y_groups)
     plan = pl.pallas_call(
         functools.partial(plan_kernel, log_weight),
         out_shape=jax.ShapeDtypeStruct((group, rows + 16, wide), jnp.bfloat16),

time: 270 us -> 274 us (1.015)
  blocking collectives: 139 us -> 113 us
  waiting for transfers between devices: 40.6 us -> 63.3 us
  starting transfers between devices: 53.7 us -> 61.2 us
    all_gather x1, waiting for transfers between devices: 0.01 us -> 26.3 us  [on_device(): lax.all_gather(sent_pair, 'dp', axis_index_groups=[list(range(k, depth, 2...]
    all_to_all x3 -> x1, blocking collectives: 52 us -> 30.9 us  [on_device(): lax.all_to_all(part, ('noise', 'dp'), 0, 0, axis_index_groups=z_groups, t...]
    ppermute x8 -> x9, starting transfers between devices: 30.3 us -> 38.1 us  [send_z(): return lax.ppermute(value, ('noise', 'dp'), pairs)]
    all_to_all x9 -> x8, blocking collectives: 87.4 us -> 81.7 us  [swap(): lax.all_to_all(value, 'noise', 0, 0, axis_index_groups=groups, tiled=True)]
    ppermute x2, waiting for transfers between devices: 4.89 us -> 10.3 us  [swap_y(): lax.ppermute(value, 'noise', noise_pairs(lambda y, x, c: (y ^ by[c], x, c)))]
    ppermute x2, waiting for transfers between devices: 6.07 us -> 1 us  [swap_x(): lax.ppermute(value, 'noise', noise_pairs(lambda y, x, c: (y, x ^ by[c], c)))]
    ppermute x8 -> x9, waiting for transfers between devices: 26.8 us -> 24.4 us  [send_z(): return lax.ppermute(value, ('noise', 'dp'), pairs)]
  transfers between devices with their start and end apart: 16 -> 17, of which waited for: 13 -> 12; matrix products, arithmetic and copies ran while one was open for 1% -> 1% of each run, Pallas kernels for 2% -> 2%
where the time goes in v5:
time: 274 us; the launch traced here: 273 us
  blocking collectives  113 us (41%)
  waiting for transfers between devices  63.3 us (23%)
  starting transfers between devices  61.2 us (22%)
  Pallas kernels  15.8 us (6%)
  between operations  14.3 us (5%)
  other arithmetic  2.89 us (1%)
    all_to_all x8, blocking collectives, swap(): lax.all_to_all(value, 'noise', 0, 0, axis_index_groups=groups, tiled=True)  81.7 us
    ppermute x9, starting transfers between devices, send_z(): return lax.ppermute(value, ('noise', 'dp'), pairs)  38.1 us
    all_to_all x1, blocking collectives, on_device(): lax.all_to_all(part, ('noise', 'dp'), 0, 0, axis_index_groups=z_groups, t...  30.9 us
    all_gather x1, waiting for transfers between devices, on_device(): lax.all_gather(sent_pair, 'dp', axis_index_groups=[list(range(k, depth, 2...  26.3 us
    ppermute x9, waiting for transfers between devices, send_z(): return lax.ppermute(value, ('noise', 'dp'), pairs)  24.4 us
    ppermute x2, waiting for transfers between devices, swap_y(): lax.ppermute(value, 'noise', noise_pairs(lambda y, x, c: (y ^ by[c], x, c)))  10.3 us
    ppermute x2, starting transfers between devices, to_other_core(): lax.ppermute(value, 'noise', noise_pairs(lambda y, x, c: (y, x, 1 - c)))  9.35 us
    ppermute x2, starting transfers between devices, swap_x(): lax.ppermute(value, 'noise', noise_pairs(lambda y, x, c: (y, x ^ by[c], c)))  7.14 us
  transfers between devices with their start and end apart: 17, of which 12 were waited for; matrix products, arithmetic and copies ran while one was open for 1% of the time, Pallas kernels for 2%

profile of v5, /device:TPU:1, one launch (start us, length us, event | category | flops | bytes accessed | tf_op | source)
XLA Modules:
  0.0 272.7 jit_solution(483222372029848198)
XLA Ops:
  7.2 0.0 all-gather.4.cloned.1.call-start
  7.2 5.2 %collective-permute-start = (bf16[128,1024]{1,0:T(8,128)(2,1)}, bf16[128,1024]{1,0:T(8,128)(2,1)S(1)}, u32[]{:S(2)}, u32[]{:S(2)}) collective-permute-start(bf16[128,1024]{1,0:T(8,128)(2,1)} %param.2), channel_id=1, source_target_pairs={{0,32},{16,112},{32,0},{48,80},{64,96},{80,48},{96,64},{112,16},{1... | collective-permute-start | bytes 786440 | tf_op jit(solution)/shard_map/ppermute | solution.py:39
  12.4 4.6 %collective-permute-start.1 = (bf16[128,1024]{1,0:T(8,128)(2,1)}, bf16[128,1024]{1,0:T(8,128)(2,1)S(1)}, u32[]{:S(2)}, u32[]{:S(2)}) collective-permute-start(bf16[128,1024]{1,0:T(8,128)(2,1)} %param.3), channel_id=1, source_target_pairs={{0,128},{16,400},{32,160},{48,432},{64,192},{80,464},{96,224},{112... | collective-permute-start | bytes 786440 | tf_op jit(solution)/shard_map/ppermute | solution.py:43
  17.1 0.0 collective-permute-done
  17.1 1.0 pad_maximum_fusion.refs_0_
  18.1 3.0 %collective-permute-done.1 = bf16[128,1024]{1,0:T(8,128)(2,1)S(1)} collective-permute-done((bf16[128,1024]{1,0:T(8,128)(2,1)}, bf16[128,1024]{1,0:T(8,128)(2,1)S(1)}, u32[]{:S(2)}, u32[]{:S(2)}) %collective-permute-start.1) | collective-permute-done | bytes 262176 | tf_op jit(solution)/shard_map/ppermute | solution.py:43
  21.0 1.0 pad_maximum_fusion.1.refs_4_
  22.0 1.9 collective-permute-start.2
  24.0 5.4 %collective-permute-start.4 = (bf16[256,1024]{1,0:T(8,128)(2,1)S(1)}, bf16[256,1024]{1,0:T(8,128)(2,1)S(1)}, u32[]{:S(2)}, u32[]{:S(2)}) collective-permute-start(bf16[256,1024]{1,0:T(8,128)(2,1)S(1)} %pad_maximum_fusion.refs_0_), channel_id=1, source_target_pairs={{0,16},{16,0},{32,48},{48,32},{64,80},{80,64},{96,112},{112,96},{1... | collective-permute-start | bytes 1572872 | tf_op jit(solution)/shard_map/ppermute | solution.py:31
  29.3 1.9 collective-permute-start.3
  31.3 1.0 collective-permute-done.2.refs_1_
  32.2 0.0 collective-permute-done.4.refs_2_
  32.3 7.3 %collective-permute-done.3.refs_5_ = bf16[256,1024]{1,0:T(8,128)(2,1)S(1)} collective-permute-done((bf16[256,1024]{1,0:T(8,128)(2,1)S(1)}, bf16[256,1024]{1,0:T(8,128)(2,1)S(1)}, u32[]{:S(2)}, u32[]{:S(2)}) %collective-permute-start.3) | collective-permute-done | bytes 524320 | tf_op jit(solution)/shard_map/ppermute | solution.py:43
  39.5 0.0 all-gather.4.cloned.1.call-update
  39.6 0.0 all-gather.6.cloned.1.call-start
  39.6 4.0 %collective-permute-start.5 = (bf16[256,1024]{1,0:T(8,128)(2,1)S(1)}, bf16[256,1024]{1,0:T(8,128)(2,1)S(1)}, u32[]{:S(2)}, u32[]{:S(2)}) collective-permute-start(bf16[256,1024]{1,0:T(8,128)(2,1)S(1)} %collective-permute-done.2.refs_1_), channel_id=1, source_target_pairs={{0,16},{16,0},{32,48},{48,32},{64,80},{80,64},{96,112},{112,96},{1... | collective-permute-start | bytes 1572872 | tf_op jit(solution)/shard_map/ppermute | solution.py:31
  43.7 0.1 pad_add_fusion.place_ref
  43.7 1.4 collective-permute-done.5.refs_3_
  45.1 3.8 %shard_map.49 = (f32[8,64,512]{2,1,0:T(8,128)S(1)}, f32[8,64,512]{2,1,0:T(8,128)S(1)}) custom-call(s32[4]{0:T(128)S(1)} %pad_add_fusion.place_ref, bf16[256,1024]{1,0:T(8,128)(2,1)S(1)} %pad_maximum_fusion.refs_0_, bf16[256,1024]{1,0:T(8,128)(2,1)S(1)} %collective-permute-done.2.refs_1_, bf16[256,1024]{1,0:T(8,128)(2,1)S(1)} %collective-permute-done.4.refs_2_, ...), custom_call_target="tpu_custom_call" | custom-call | tf_op jit(solution)/shard_map/pallas_call | solution.py:275
  48.9 9.3 %collective-permute-start.6 = (f32[8,64,512]{2,1,0:T(8,128)S(1)}, f32[8,64,512]{2,1,0:T(8,128)S(1)}, u32[]{:S(2)}, u32[]{:S(2)}) collective-permute-start(f32[8,64,512]{2,1,0:T(8,128)S(1)} %get-tuple-element.35), channel_id=1, source_target_pairs={{0,1},{1,0},{2,3},{3,2},{4,5},{5,4},{6,7},{7,6},{8,9},{9,8},{10,11... | collective-permute-start | bytes 3145736 | tf_op jit(solution)/shard_map/ppermute | solution.py:51
  58.2 12.2 %collective-permute-done.6.got = f32[8,64,512]{2,1,0:T(8,128)S(1)} collective-permute-done((f32[8,64,512]{2,1,0:T(8,128)S(1)}, f32[8,64,512]{2,1,0:T(8,128)S(1)}, u32[]{:S(2)}, u32[]{:S(2)}) %collective-permute-start.6) | collective-permute-done | bytes 1048608 | tf_op jit(solution)/shard_map/ppermute | solution.py:51
  70.4 0.1 shard_map.50
  70.5 4.1 %collective-permute-start.7 = (f32[64,512]{1,0:T(8,128)S(1)}, f32[64,512]{1,0:T(8,128)S(1)}, u32[]{:S(2)}, u32[]{:S(2)}) collective-permute-start(f32[64,512]{1,0:T(8,128)S(1)} %get-tuple-element.37), channel_id=1, source_target_pairs={{0,2},{1,3},{2,4},{3,5},{4,6},{5,7},{6,8},{7,9},{8,10},{9,11},{10,... | collective-permute-start | bytes 393224 | tf_op jit(solution)/shard_map/ppermute | solution.py:51
  74.6 2.1 collective-permute-start.11
  76.7 1.1 collective-permute-done.7
  77.9 4.6 %collective-permute-start.8 = (f32[64,512]{1,0:T(8,128)S(1)}, f32[64,512]{1,0:T(8,128)S(1)}, u32[]{:S(2)}, u32[]{:S(2)}) collective-permute-start(f32[64,512]{1,0:T(8,128)S(1)} %bitcast_add_fusion.4), channel_id=1, source_target_pairs={{0,2},{1,3},{2,4},{3,5},{4,6},{5,7},{6,8},{7,9},{8,10},{9,11},{10,... | collective-permute-start | bytes 393224 | tf_op jit(solution)/shard_map/ppermute | solution.py:51
  82.5 1.4 collective-permute-done.11
  83.9 1.9 collective-permute-start.12
  85.9 0.0 collective-permute-done.8
  85.9 5.5 %collective-permute-start.9 = (f32[64,512]{1,0:T(8,128)S(1)}, f32[64,512]{1,0:T(8,128)S(1)}, u32[]{:S(2)}, u32[]{:S(2)}) collective-permute-start(f32[64,512]{1,0:T(8,128)S(1)} %bitcast_add_fusion.3), channel_id=1, source_target_pairs={{0,2},{1,3},{2,4},{3,5},{4,6},{5,7},{6,8},{7,9},{8,10},{9,11},{10,... | collective-permute-start | bytes 393224 | tf_op jit(solution)/shard_map/ppermute | solution.py:51
  91.4 0.9 collective-permute-done.12
  92.3 1.9 collective-permute-start.13
  94.2 0.0 collective-permute-done.9
  94.2 6.8 %collective-permute-start.10 = (f32[64,512]{1,0:T(8,128)S(1)}, f32[64,512]{1,0:T(8,128)S(1)}, u32[]{:S(2)}, u32[]{:S(2)}) collective-permute-start(f32[64,512]{1,0:T(8,128)S(1)} %bitcast_add_fusion.2), channel_id=1, source_target_pairs={{0,2},{1,3},{2,4},{3,5},{4,6},{5,7},{6,8},{7,9},{8,10},{9,11},{10,... | collective-permute-start | bytes 393224 | tf_op jit(solution)/shard_map/ppermute | solution.py:51
  101.0 0.6 collective-permute-done.13
  101.6 4.4 %collective-permute-done.10 = f32[64,512]{1,0:T(8,128)S(1)} collective-permute-done((f32[64,512]{1,0:T(8,128)S(1)}, f32[64,512]{1,0:T(8,128)S(1)}, u32[]{:S(2)}, u32[]{:S(2)}) %collective-permute-start.10) | collective-permute-done | bytes 131104 | tf_op jit(solution)/shard_map/ppermute | solution.py:51
  106.0 1.9 collective-permute-start.14
  107.9 3.8 %collective-permute-done.14 = f32[64,512]{1,0:T(8,128)S(1)} collective-permute-done((f32[64,512]{1,0:T(8,128)S(1)}, f32[64,512]{1,0:T(8,128)S(1)}, u32[]{:S(2)}, u32[]{:S(2)}) %collective-permute-start.14) | collective-permute-done | bytes 131104 | tf_op jit(solution)/shard_map/ppermute | solution.py:51
  111.7 0.7 pad_maximum_fusion.2.a_ref
  112.4 0.0 all-gather.6.cloned.1.call-update
  112.5 0.0 copy-start
  112.5 0.9 copy-done
  113.4 0.2 shard_map.51
  113.6 11.0 %all_to_all.45.parts_ref = f32[8,1,128]{2,1,0:T(1,128)S(1)} all-to-all(f32[8,1,128]{2,1,0:T(1,128)S(1)} %shard_map.51), channel_id=1, replica_groups={{0,16,32,48,64,80,96,112},{128,144,160,176,192,208,224,240},{256,272,28..., dimensions={0} | all-to-all | bytes 8192 | tf_op jit(solution)/shard_map/all_to_all | solution.py:261
  124.7 0.6 shard_map.52
  125.3 30.9 %all_to_all.46.parts_ref = f32[32,4,128]{2,1,0:T(4,128)S(1)} all-to-all(f32[32,4,128]{2,1,0:T(4,128)S(1)} %get-tuple-element.42), channel_id=1, replica_groups={{0,2,4,6,8,10,12,14,128,130,132,134,136,138,140,142,256,258,260,262,264..., dimensions={0} | all-to-all | bytes 131072 | tf_op jit(solution)/shard_map/all_to_all | solution.py:364
  156.2 26.3 %all-gather.6.cloned.1.call-done = f32[1024,512]{1,0:T(8,128)} async-done(((f32[128,512]{1,0:T(8,128)}), f32[1024,512]{1,0:T(8,128)}) %all-gather.6.cloned.1.call-update) | async-done | bytes 2097168 | tf_op jit(solution)/shard_map/all_gather | solution.py:314
  182.5 0.0 copy-start.1
  182.5 1.6 copy-done.1
  184.1 1.3 shard_map.53
  185.4 10.9 %all_to_all.47.parts_ref = f32[8,8,128]{2,1,0:T(8,128)S(1)} all-to-all(f32[8,8,128]{2,1,0:T(8,128)S(1)} %get-tuple-element.44), channel_id=1, replica_groups={{0,16,32,48,64,80,96,112},{128,144,160,176,192,208,224,240},{256,272,28..., dimensions={0} | all-to-all | bytes 65536 | tf_op jit(solution)/shard_map/all_to_all | solution.py:261
  196.2 0.9 shard_map.54
  197.1 7.6 %all_to_all.48.parts_ref = f32[4,4,128]{2,1,0:T(4,128)S(1)} all-to-all(f32[4,4,128]{2,1,0:T(4,128)S(1)} %get-tuple-element.45), channel_id=1, replica_groups={{0,128,256,384},{16,144,272,400},{32,160,288,416},{48,176,304,432},{64,..., dimensions={0} | all-to-all | bytes 16384 | tf_op jit(solution)/shard_map/all_to_all | solution.py:261
  204.7 0.6 shard_map.55
  205.4 9.2 %all_to_all.49.parts_ref = f32[8,8,128]{2,1,0:T(8,128)S(1)} all-to-all(f32[8,8,128]{2,1,0:T(8,128)S(1)} %shard_map.55), channel_id=1, replica_groups={{0,16,32,48,64,80,96,112},{128,144,160,176,192,208,224,240},{256,272,28..., dimensions={0} | all-to-all | bytes 65536 | tf_op jit(solution)/shard_map/all_to_all | solution.py:261
  214.6 0.9 shard_map.56
  215.5 6.5 %all_to_all.50.parts_ref = f32[4,4,128]{2,1,0:T(4,128)S(1)} all-to-all(f32[4,4,128]{2,1,0:T(4,128)S(1)} %get-tuple-element.46), channel_id=1, replica_groups={{0,128,256,384},{16,144,272,400},{32,160,288,416},{48,176,304,432},{64,..., dimensions={0} | all-to-all | bytes 16384 | tf_op jit(solution)/shard_map/all_to_all | solution.py:261
  222.0 0.6 shard_map.57
  222.6 9.0 %all_to_all.51.parts_ref = f32[8,8,128]{2,1,0:T(8,128)S(1)} all-to-all(f32[8,8,128]{2,1,0:T(8,128)S(1)} %shard_map.57), channel_id=1, replica_groups={{0,16,32,48,64,80,96,112},{128,144,160,176,192,208,224,240},{256,272,28..., dimensions={0} | all-to-all | bytes 65536 | tf_op jit(solution)/shard_map/all_to_all | solution.py:261
  231.6 0.6 shard_map.58
  232.1 6.5 %all_to_all.52.parts_ref = f32[4,4,128]{2,1,0:T(4,128)S(1)} all-to-all(f32[4,4,128]{2,1,0:T(4,128)S(1)} %get-tuple-element.48), channel_id=1, replica_groups={{0,128,256,384},{16,144,272,400},{32,160,288,416},{48,176,304,432},{64,..., dimensions={0} | all-to-all | bytes 16384 | tf_op jit(solution)/shard_map/all_to_all | solution.py:261
  238.6 0.4 shard_map.59
  239.0 20.9 %all_to_all.53.plan_ref = bf16[8,144,512]{2,1,0:T(8,128)(2,1)S(1)} all-to-all(bf16[8,144,512]{2,1,0:T(8,128)(2,1)S(1)} %shard_map.59), channel_id=1, replica_groups={{0,16,32,48,64,80,96,112},{128,144,160,176,192,208,224,240},{256,272,28..., dimensions={0} | all-to-all | bytes 2359296 | tf_op jit(solution)/shard_map/all_to_all | solution.py:261
  259.9 5.9 %shard_map.60 = (bf16[128,1024]{1,0:T(8,128)(2,1)}, f32[1,128]{1,0:T(1,128)}, f32[1,256]{1,0:T(1,128)}) custom-call(s32[4]{0:T(128)S(1)} %pad_add_fusion.place_ref, bf16[8,144,512]{2,1,0:T(8,128)(2,1)S(1)} %all_to_all.53.plan_ref, f32[8,128]{1,0:T(8,128)S(1)} %get-tuple-element.47.u_ref, bf16[4096,1024]{1,0:T(8,128)(2,1)} %all-gather.4.cloned.1.call-done.y_ref), custom_call_target="tpu_custom_call" | custom-call | tf_op jit(solution)/shard_map/pallas_call | solution.py:378
  (7 shorter events, 0.1 us)
Async XLA Ops:
  7.2 105.3 %all-gather.4.cloned.1.call-start = ((), (), s32[]{:S(2)}) async-start(), calls=%async_computation.9 | async-start | bytes 8650752 | tf_op jit(solution)/shard_map/all_gather | solution.py:270
  7.2 9.9 %collective-permute-start = (bf16[128,1024]{1,0:T(8,128)(2,1)}, bf16[128,1024]{1,0:T(8,128)(2,1)S(1)}, u32[]{:S(2)}, u32[]{:S(2)}) collective-permute-start(bf16[128,1024]{1,0:T(8,128)(2,1)} %param.2), channel_id=1, source_target_pairs={{0,32},{16,112},{32,0},{48,80},{64,96},{80,48},{96,64},{112,16},{1... | collective-permute-start | bytes 786440 | tf_op jit(solution)/shard_map/ppermute | solution.py:39
  12.4 8.6 %collective-permute-start.1 = (bf16[128,1024]{1,0:T(8,128)(2,1)}, bf16[128,1024]{1,0:T(8,128)(2,1)S(1)}, u32[]{:S(2)}, u32[]{:S(2)}) collective-permute-start(bf16[128,1024]{1,0:T(8,128)(2,1)} %param.3), channel_id=1, source_target_pairs={{0,128},{16,400},{32,160},{48,432},{64,192},{80,464},{96,224},{112... | collective-permute-start | bytes 786440 | tf_op jit(solution)/shard_map/ppermute | solution.py:43
  22.0 10.2 %collective-permute-start.2 = (bf16[256,1024]{1,0:T(8,128)(2,1)S(1)}, bf16[256,1024]{1,0:T(8,128)(2,1)S(1)}, u32[]{:S(2)}, u32[]{:S(2)}) collective-permute-start(bf16[256,1024]{1,0:T(8,128)(2,1)S(1)} %pad_maximum_fusion.refs_0_), channel_id=1, source_target_pairs={{0,96},{16,48},{32,64},{48,16},{64,32},{80,112},{96,0},{112,80},{1... | collective-permute-start | bytes 1572872 | tf_op jit(solution)/shard_map/ppermute | solution.py:39
  24.0 8.3 %collective-permute-start.4 = (bf16[256,1024]{1,0:T(8,128)(2,1)S(1)}, bf16[256,1024]{1,0:T(8,128)(2,1)S(1)}, u32[]{:S(2)}, u32[]{:S(2)}) collective-permute-start(bf16[256,1024]{1,0:T(8,128)(2,1)S(1)} %pad_maximum_fusion.refs_0_), channel_id=1, source_target_pairs={{0,16},{16,0},{32,48},{48,32},{64,80},{80,64},{96,112},{112,96},{1... | collective-permute-start | bytes 1572872 | tf_op jit(solution)/shard_map/ppermute | solution.py:31
  29.3 10.2 %collective-permute-start.3 = (bf16[256,1024]{1,0:T(8,128)(2,1)S(1)}, bf16[256,1024]{1,0:T(8,128)(2,1)S(1)}, u32[]{:S(2)}, u32[]{:S(2)}) collective-permute-start(bf16[256,1024]{1,0:T(8,128)(2,1)S(1)} %pad_maximum_fusion.1.refs_4_), channel_id=1, source_target_pairs={{0,384},{16,144},{32,416},{48,176},{64,448},{80,208},{96,480},{112... | collective-permute-start | bytes 1572872 | tf_op jit(solution)/shard_map/ppermute | solution.py:43
  39.6 142.9 %all-gather.6.cloned.1.call-start = ((), (), s32[]{:S(2)}) async-start(), calls=%async_computation.10 | async-start | bytes 2359296 | tf_op jit(solution)/shard_map/all_gather | solution.py:314
  39.6 5.5 %collective-permute-start.5 = (bf16[256,1024]{1,0:T(8,128)(2,1)S(1)}, bf16[256,1024]{1,0:T(8,128)(2,1)S(1)}, u32[]{:S(2)}, u32[]{:S(2)}) collective-permute-start(bf16[256,1024]{1,0:T(8,128)(2,1)S(1)} %collective-permute-done.2.refs_1_), channel_id=1, source_target_pairs={{0,16},{16,0},{32,48},{48,32},{64,80},{80,64},{96,112},{112,96},{1... | collective-permute-start | bytes 1572872 | tf_op jit(solution)/shard_map/ppermute | solution.py:31
  48.9 21.5 %collective-permute-start.6 = (f32[8,64,512]{2,1,0:T(8,128)S(1)}, f32[8,64,512]{2,1,0:T(8,128)S(1)}, u32[]{:S(2)}, u32[]{:S(2)}) collective-permute-start(f32[8,64,512]{2,1,0:T(8,128)S(1)} %get-tuple-element.35), channel_id=1, source_target_pairs={{0,1},{1,0},{2,3},{3,2},{4,5},{5,4},{6,7},{7,6},{8,9},{9,8},{10,11... | collective-permute-start | bytes 3145736 | tf_op jit(solution)/shard_map/ppermute | solution.py:51
  70.5 7.3 %collective-permute-start.7 = (f32[64,512]{1,0:T(8,128)S(1)}, f32[64,512]{1,0:T(8,128)S(1)}, u32[]{:S(2)}, u32[]{:S(2)}) collective-permute-start(f32[64,512]{1,0:T(8,128)S(1)} %get-tuple-element.37), channel_id=1, source_target_pairs={{0,2},{1,3},{2,4},{3,5},{4,6},{5,7},{6,8},{7,9},{8,10},{9,11},{10,... | collective-permute-start | bytes 393224 | tf_op jit(solution)/shard_map/ppermute | solution.py:51
  74.6 9.3 %collective-permute-start.11 = (f32[64,512]{1,0:T(8,128)S(1)}, f32[64,512]{1,0:T(8,128)S(1)}, u32[]{:S(2)}, u32[]{:S(2)}) collective-permute-start(f32[64,512]{1,0:T(8,128)S(1)} %get-tuple-element.39), channel_id=1, source_target_pairs={{0,14},{1,15},{2,0},{3,1},{4,2},{5,3},{6,4},{7,5},{8,6},{9,7},{10,... | collective-permute-start | bytes 393224 | tf_op jit(solution)/shard_map/ppermute | solution.py:51
  77.9 8.0 %collective-permute-start.8 = (f32[64,512]{1,0:T(8,128)S(1)}, f32[64,512]{1,0:T(8,128)S(1)}, u32[]{:S(2)}, u32[]{:S(2)}) collective-permute-start(f32[64,512]{1,0:T(8,128)S(1)} %bitcast_add_fusion.4), channel_id=1, source_target_pairs={{0,2},{1,3},{2,4},{3,5},{4,6},{5,7},{6,8},{7,9},{8,10},{9,11},{10,... | collective-permute-start | bytes 393224 | tf_op jit(solution)/shard_map/ppermute | solution.py:51
  83.9 8.3 %collective-permute-start.12 = (f32[64,512]{1,0:T(8,128)S(1)}, f32[64,512]{1,0:T(8,128)S(1)}, u32[]{:S(2)}, u32[]{:S(2)}) collective-permute-start(f32[64,512]{1,0:T(8,128)S(1)} %bitcast_add_fusion.1), channel_id=1, source_target_pairs={{0,14},{1,15},{2,0},{3,1},{4,2},{5,3},{6,4},{7,5},{8,6},{9,7},{10,... | collective-permute-start | bytes 393224 | tf_op jit(solution)/shard_map/ppermute | solution.py:51
  85.9 8.3 %collective-permute-start.9 = (f32[64,512]{1,0:T(8,128)S(1)}, f32[64,512]{1,0:T(8,128)S(1)}, u32[]{:S(2)}, u32[]{:S(2)}) collective-permute-start(f32[64,512]{1,0:T(8,128)S(1)} %bitcast_add_fusion.3), channel_id=1, source_target_pairs={{0,2},{1,3},{2,4},{3,5},{4,6},{5,7},{6,8},{7,9},{8,10},{9,11},{10,... | collective-permute-start | bytes 393224 | tf_op jit(solution)/shard_map/ppermute | solution.py:51
  92.3 9.3 %collective-permute-start.13 = (f32[64,512]{1,0:T(8,128)S(1)}, f32[64,512]{1,0:T(8,128)S(1)}, u32[]{:S(2)}, u32[]{:S(2)}) collective-permute-start(f32[64,512]{1,0:T(8,128)S(1)} %bitcast_add_fusion), channel_id=1, source_target_pairs={{0,14},{1,15},{2,0},{3,1},{4,2},{5,3},{6,4},{7,5},{8,6},{9,7},{10,... | collective-permute-start | bytes 393224 | tf_op jit(solution)/shard_map/ppermute | solution.py:51
  94.2 11.7 %collective-permute-start.10 = (f32[64,512]{1,0:T(8,128)S(1)}, f32[64,512]{1,0:T(8,128)S(1)}, u32[]{:S(2)}, u32[]{:S(2)}) collective-permute-start(f32[64,512]{1,0:T(8,128)S(1)} %bitcast_add_fusion.2), channel_id=1, source_target_pairs={{0,2},{1,3},{2,4},{3,5},{4,6},{5,7},{6,8},{7,9},{8,10},{9,11},{10,... | collective-permute-start | bytes 393224 | tf_op jit(solution)/shard_map/ppermute | solution.py:51
  106.0 5.7 %collective-permute-start.14 = (f32[64,512]{1,0:T(8,128)S(1)}, f32[64,512]{1,0:T(8,128)S(1)}, u32[]{:S(2)}, u32[]{:S(2)}) collective-permute-start(f32[64,512]{1,0:T(8,128)S(1)} %add_add_fusion), channel_id=1, source_target_pairs={{0,1},{1,0},{2,3},{3,2},{4,5},{5,4},{6,7},{7,6},{8,9},{9,8},{10,11... | collective-permute-start | bytes 393224 | tf_op jit(solution)/shard_map/ppermute | solution.py:51
  112.5 1.0 copy-start
  182.5 1.6 copy-start.1
Sparse Core Ops, SparseCore 0:
  39.7 70.6 all-gather.3
  113.0 69.4 all-gather.5

commit v6 on v4

--- a/solution.py
+++ b/solution.py
@@ -10,6 +10,7 @@
 
 D = 16384
 ITERS = 4
+EARLY = 2
 YS, XS, CORES = 4, 4, 2
 LOG2E = math.log2(math.e)
 VMEM = pl.BlockSpec(memory_space=pltpu.VMEM)
@@ -195,11 +196,6 @@
     copy_out(out_ref)
 
 
-def join_kernel(parts_ref, out_ref):
-    out_ref[0] = joined(parts_ref[...])
-    copy_out(out_ref)
-
-
 def plan_kernel(log_weight, a_ref, u_ref, parts_ref, out_ref):
     v = row_of(parts_ref, log_weight)
     u = u_ref[...] - log_weight
@@ -265,7 +261,9 @@
     y_near = jnp.concatenate([data_rows, swap_y(data_rows, FIRST)], axis=0)
     x_near, y_near = lax.optimization_barrier((x_near, y_near))
     x_far, y_far = swap_x(x_near, SECOND), swap_y(y_near, SECOND)
-    x_far, y_far, late_rows = lax.optimization_barrier((x_far, y_far, data_rows))
+    x_far, y_far, x_there, late_rows = lax.optimization_barrier(
+        (x_far, y_far, to_other_core(x_near), data_rows)
+    )
     everything = lax.all_gather(late_rows, "noise", axis=0, tiled=True)
     tall, wide = group * rows, YS * rows
     half = depth // 2
@@ -283,7 +281,7 @@
             pltpu.VMEM((depth,) + chunk, f32),
         ],
         compiler_params=PARAMS,
-    )(place, x_near, x_far, to_other_core(x_near), to_other_core(x_far), y_near, y_far)
+    )(place, x_near, x_far, x_there, to_other_core(x_far), y_near, y_far)
 
     got = send_z(give, z_partner)
     own, ahead, back, ahead_rest, back_rest = pl.pallas_call(
@@ -310,10 +308,13 @@
 
     everything, own = lax.optimization_barrier((everything, own))
     gathered = lax.all_gather(own, "dp")
+    z_groups = [
+        [((y * group) + k) * depth + d for y in range(YS) for d in range(depth)] for k in range(group)
+    ]
     few = tall // depth
     for step in range(ITERS):
-        last = step == ITERS - 1
-        lines, n = (group, rows) if last else (1, few)
+        early = step < EARLY
+        lines, n = (1, few) if early else (group, rows)
         row_shape = jax.ShapeDtypeStruct((group, lines, n), f32)
         if step == 0:
             part = pl.pallas_call(
@@ -323,15 +324,7 @@
                 out_specs=VMEM,
                 compiler_params=PARAMS,
             )(own)
-        elif not last:
-            part = pl.pallas_call(
-                functools.partial(rows_kernel, log_weight),
-                out_shape=row_shape,
-                in_specs=[VMEM] * 2,
-                out_specs=VMEM,
-                compiler_params=PARAMS,
-            )(own, part)
-        else:
+        elif step == EARLY:
             a, part = pl.pallas_call(
                 functools.partial(all_rows_kernel, log_weight),
                 out_shape=[jax.ShapeDtypeStruct((tall, wide), f32), row_shape],
@@ -339,27 +332,32 @@
                 out_specs=[VMEM] * 2,
                 compiler_params=PARAMS,
             )(gathered, part)
+        else:
+            part = pl.pallas_call(
+                functools.partial(rows_kernel, log_weight),
+                out_shape=row_shape,
+                in_specs=[VMEM] * 2,
+                out_specs=VMEM,
+                compiler_params=PARAMS,
+            )(own if early else a, part)
         part = swap(part, x_groups)
         u, part = pl.pallas_call(
             functools.partial(columns_kernel, log_weight),
             out_shape=[
                 jax.ShapeDtypeStruct((lines, n), f32),
-                jax.ShapeDtypeStruct((YS if last else depth, YS, rows), f32),
+                jax.ShapeDtypeStruct((YS * depth if early else YS, YS, rows), f32),
             ],
             in_specs=[VMEM] * 2,
             out_specs=[VMEM] * 2,
             scratch_shapes=[pltpu.VMEM((lines * n, wide), f32)],
             compiler_params=PARAMS,
-        )(a if last else own, part)
-        if not last:
-            part = pl.pallas_call(
-                join_kernel,
-                out_shape=jax.ShapeDtypeStruct((YS, YS, rows), f32),
-                in_specs=[VMEM],
-                out_specs=VMEM,
-                compiler_params=PARAMS,
-            )(lax.all_to_all(part, "dp", 0, 0, tiled=True))
-        part = swap(part, y_groups)
+        )(own if early else a, part)
+        if early:
+            part = lax.all_to_all(
+                part, ("noise", "dp"), 0, 0, axis_index_groups=z_groups, tiled=True
+            )
+        else:
+            part = swap(part, y_groups)
     plan = pl.pallas_call(
         functools.partial(plan_kernel, log_weight),
         out_shape=jax.ShapeDtypeStruct((group, rows + 16, wide), jnp.bfloat16),

time: 270 us -> 265 us (0.981)
  blocking collectives: 139 us -> 133 us
  starting transfers between devices: 53.7 us -> 58.5 us
    all_to_all x9 -> x7, blocking collectives: 87.4 us -> 80.9 us  [swap(): lax.all_to_all(value, 'noise', 0, 0, axis_index_groups=groups, tiled=True)]
    ppermute x8, waiting for transfers between devices: 26.8 us -> 21.5 us  [send_z(): return lax.ppermute(value, ('noise', 'dp'), pairs)]
    ppermute x2, waiting for transfers between devices: 4.89 us -> 10.3 us  [swap_y(): lax.ppermute(value, 'noise', noise_pairs(lambda y, x, c: (y ^ by[c], x, c)))]
    ppermute x8, starting transfers between devices: 30.3 us -> 35.4 us  [send_z(): return lax.ppermute(value, ('noise', 'dp'), pairs)]
    ppermute x2, waiting for transfers between devices: 6.07 us -> 1 us  [swap_x(): lax.ppermute(value, 'noise', noise_pairs(lambda y, x, c: (y, x ^ by[c], c)))]
    all_to_all x3 -> x2, blocking collectives: 52 us -> 52.2 us  [on_device(): lax.all_to_all(part, ('noise', 'dp'), 0, 0, axis_index_groups=z_groups, t...]
where the time goes in v6:
time: 265 us; the launch traced here: 264 us
  blocking collectives  133 us (50%)
  starting transfers between devices  58.5 us (22%)
  waiting for transfers between devices  38.5 us (15%)
  Pallas kernels  14.5 us (5%)
  between operations  14.3 us (5%)
  other arithmetic  2.83 us (1%)
    all_to_all x7, blocking collectives, swap(): lax.all_to_all(value, 'noise', 0, 0, axis_index_groups=groups, tiled=True)  80.9 us
    all_to_all x2, blocking collectives, on_device(): lax.all_to_all(part, ('noise', 'dp'), 0, 0, axis_index_groups=z_groups, t...  52.2 us
    ppermute x8, starting transfers between devices, send_z(): return lax.ppermute(value, ('noise', 'dp'), pairs)  35.4 us
    ppermute x8, waiting for transfers between devices, send_z(): return lax.ppermute(value, ('noise', 'dp'), pairs)  21.5 us
    ppermute x2, waiting for transfers between devices, swap_y(): lax.ppermute(value, 'noise', noise_pairs(lambda y, x, c: (y ^ by[c], x, c)))  10.3 us
    ppermute x2, starting transfers between devices, to_other_core(): lax.ppermute(value, 'noise', noise_pairs(lambda y, x, c: (y, x, 1 - c)))  9.35 us
    ppermute x2, starting transfers between devices, swap_x(): lax.ppermute(value, 'noise', noise_pairs(lambda y, x, c: (y, x ^ by[c], c)))  7.14 us
    ppermute x2, starting transfers between devices, swap_y(): lax.ppermute(value, 'noise', noise_pairs(lambda y, x, c: (y ^ by[c], x, c)))  6.57 us
  transfers between devices with their start and end apart: 16, of which 13 were waited for; matrix products, arithmetic and copies ran while one was open for 1% of the time, Pallas kernels for 2%

profile of v6, /device:TPU:1, one launch (start us, length us, event | category | flops | bytes accessed | tf_op | source)
XLA Modules:
  0.0 264.2 jit_solution(17994624090698209040)
XLA Ops:
  7.2 0.0 all-gather.4.cloned.1.call-start
  7.2 5.2 %collective-permute-start = (bf16[128,1024]{1,0:T(8,128)(2,1)}, bf16[128,1024]{1,0:T(8,128)(2,1)S(1)}, u32[]{:S(2)}, u32[]{:S(2)}) collective-permute-start(bf16[128,1024]{1,0:T(8,128)(2,1)} %param.2), channel_id=1, source_target_pairs={{0,32},{16,112},{32,0},{48,80},{64,96},{80,48},{96,64},{112,16},{1... | collective-permute-start | bytes 786440 | tf_op jit(solution)/shard_map/ppermute | solution.py:40
  12.4 4.6 %collective-permute-start.1 = (bf16[128,1024]{1,0:T(8,128)(2,1)}, bf16[128,1024]{1,0:T(8,128)(2,1)S(1)}, u32[]{:S(2)}, u32[]{:S(2)}) collective-permute-start(bf16[128,1024]{1,0:T(8,128)(2,1)} %param.3), channel_id=1, source_target_pairs={{0,128},{16,400},{32,160},{48,432},{64,192},{80,464},{96,224},{112... | collective-permute-start | bytes 786440 | tf_op jit(solution)/shard_map/ppermute | solution.py:44
  17.1 0.0 collective-permute-done
  17.1 1.0 pad_maximum_fusion.refs_0_
  18.1 3.0 %collective-permute-done.1 = bf16[128,1024]{1,0:T(8,128)(2,1)S(1)} collective-permute-done((bf16[128,1024]{1,0:T(8,128)(2,1)}, bf16[128,1024]{1,0:T(8,128)(2,1)S(1)}, u32[]{:S(2)}, u32[]{:S(2)}) %collective-permute-start.1) | collective-permute-done | bytes 262176 | tf_op jit(solution)/shard_map/ppermute | solution.py:44
  21.0 1.0 pad_maximum_fusion.1.refs_4_
  22.0 1.9 collective-permute-start.2
  24.0 5.4 %collective-permute-start.4 = (bf16[256,1024]{1,0:T(8,128)(2,1)S(1)}, bf16[256,1024]{1,0:T(8,128)(2,1)S(1)}, u32[]{:S(2)}, u32[]{:S(2)}) collective-permute-start(bf16[256,1024]{1,0:T(8,128)(2,1)S(1)} %pad_maximum_fusion.refs_0_), channel_id=1, source_target_pairs={{0,16},{16,0},{32,48},{48,32},{64,80},{80,64},{96,112},{112,96},{1... | collective-permute-start | bytes 1572872 | tf_op jit(solution)/shard_map/ppermute | solution.py:32
  29.3 1.9 collective-permute-start.3
  31.3 1.0 collective-permute-done.2.refs_1_
  32.2 0.0 collective-permute-done.4.refs_2_
  32.3 7.3 %collective-permute-done.3.refs_5_ = bf16[256,1024]{1,0:T(8,128)(2,1)S(1)} collective-permute-done((bf16[256,1024]{1,0:T(8,128)(2,1)S(1)}, bf16[256,1024]{1,0:T(8,128)(2,1)S(1)}, u32[]{:S(2)}, u32[]{:S(2)}) %collective-permute-start.3) | collective-permute-done | bytes 524320 | tf_op jit(solution)/shard_map/ppermute | solution.py:44
  39.5 0.0 all-gather.4.cloned.1.call-update
  39.6 0.0 all-gather.6.cloned.1.call-start
  39.6 4.0 %collective-permute-start.5 = (bf16[256,1024]{1,0:T(8,128)(2,1)S(1)}, bf16[256,1024]{1,0:T(8,128)(2,1)S(1)}, u32[]{:S(2)}, u32[]{:S(2)}) collective-permute-start(bf16[256,1024]{1,0:T(8,128)(2,1)S(1)} %collective-permute-done.2.refs_1_), channel_id=1, source_target_pairs={{0,16},{16,0},{32,48},{48,32},{64,80},{80,64},{96,112},{112,96},{1... | collective-permute-start | bytes 1572872 | tf_op jit(solution)/shard_map/ppermute | solution.py:32
  43.7 0.1 pad_add_fusion.place_ref
  43.7 1.4 collective-permute-done.5.refs_3_
  45.1 3.8 %shard_map.49 = (f32[8,64,512]{2,1,0:T(8,128)S(1)}, f32[8,64,512]{2,1,0:T(8,128)S(1)}) custom-call(s32[4]{0:T(128)S(1)} %pad_add_fusion.place_ref, bf16[256,1024]{1,0:T(8,128)(2,1)S(1)} %pad_maximum_fusion.refs_0_, bf16[256,1024]{1,0:T(8,128)(2,1)S(1)} %collective-permute-done.2.refs_1_, bf16[256,1024]{1,0:T(8,128)(2,1)S(1)} %collective-permute-done.4.refs_2_, ...), custom_call_target="tpu_custom_call" | custom-call | tf_op jit(solution)/shard_map/pallas_call | solution.py:272
  48.9 9.3 %collective-permute-start.6 = (f32[8,64,512]{2,1,0:T(8,128)S(1)}, f32[8,64,512]{2,1,0:T(8,128)S(1)}, u32[]{:S(2)}, u32[]{:S(2)}) collective-permute-start(f32[8,64,512]{2,1,0:T(8,128)S(1)} %get-tuple-element.35), channel_id=1, source_target_pairs={{0,1},{1,0},{2,3},{3,2},{4,5},{5,4},{6,7},{7,6},{8,9},{9,8},{10,11... | collective-permute-start | bytes 3145736 | tf_op jit(solution)/shard_map/ppermute | solution.py:52
  58.2 12.2 %collective-permute-done.6.got = f32[8,64,512]{2,1,0:T(8,128)S(1)} collective-permute-done((f32[8,64,512]{2,1,0:T(8,128)S(1)}, f32[8,64,512]{2,1,0:T(8,128)S(1)}, u32[]{:S(2)}, u32[]{:S(2)}) %collective-permute-start.6) | collective-permute-done | bytes 1048608 | tf_op jit(solution)/shard_map/ppermute | solution.py:52
  70.4 0.1 shard_map.50
  70.5 4.1 %collective-permute-start.7 = (f32[64,512]{1,0:T(8,128)S(1)}, f32[64,512]{1,0:T(8,128)S(1)}, u32[]{:S(2)}, u32[]{:S(2)}) collective-permute-start(f32[64,512]{1,0:T(8,128)S(1)} %get-tuple-element.37), channel_id=1, source_target_pairs={{0,2},{1,3},{2,4},{3,5},{4,6},{5,7},{6,8},{7,9},{8,10},{9,11},{10,... | collective-permute-start | bytes 393224 | tf_op jit(solution)/shard_map/ppermute | solution.py:52
  74.6 2.1 collective-permute-start.11
  76.7 1.1 collective-permute-done.7
  77.9 4.6 %collective-permute-start.8 = (f32[64,512]{1,0:T(8,128)S(1)}, f32[64,512]{1,0:T(8,128)S(1)}, u32[]{:S(2)}, u32[]{:S(2)}) collective-permute-start(f32[64,512]{1,0:T(8,128)S(1)} %bitcast_add_fusion.4), channel_id=1, source_target_pairs={{0,2},{1,3},{2,4},{3,5},{4,6},{5,7},{6,8},{7,9},{8,10},{9,11},{10,... | collective-permute-start | bytes 393224 | tf_op jit(solution)/shard_map/ppermute | solution.py:52
  82.5 1.4 collective-permute-done.11
  83.9 1.9 collective-permute-start.12
  85.9 0.0 collective-permute-done.8
  85.9 5.5 %collective-permute-start.9 = (f32[64,512]{1,0:T(8,128)S(1)}, f32[64,512]{1,0:T(8,128)S(1)}, u32[]{:S(2)}, u32[]{:S(2)}) collective-permute-start(f32[64,512]{1,0:T(8,128)S(1)} %bitcast_add_fusion.3), channel_id=1, source_target_pairs={{0,2},{1,3},{2,4},{3,5},{4,6},{5,7},{6,8},{7,9},{8,10},{9,11},{10,... | collective-permute-start | bytes 393224 | tf_op jit(solution)/shard_map/ppermute | solution.py:52
  91.4 0.9 collective-permute-done.12
  92.3 1.9 collective-permute-start.13
  94.2 0.8 collective-permute-done.9
  95.0 6.0 %collective-permute-start.10 = (f32[64,512]{1,0:T(8,128)S(1)}, f32[64,512]{1,0:T(8,128)S(1)}, u32[]{:S(2)}, u32[]{:S(2)}) collective-permute-start(f32[64,512]{1,0:T(8,128)S(1)} %bitcast_add_fusion.2), channel_id=1, source_target_pairs={{0,2},{1,3},{2,4},{3,5},{4,6},{5,7},{6,8},{7,9},{8,10},{9,11},{10,... | collective-permute-start | bytes 393224 | tf_op jit(solution)/shard_map/ppermute | solution.py:52
  101.0 0.6 collective-permute-done.13
  101.6 4.4 %collective-permute-done.10 = f32[64,512]{1,0:T(8,128)S(1)} collective-permute-done((f32[64,512]{1,0:T(8,128)S(1)}, f32[64,512]{1,0:T(8,128)S(1)}, u32[]{:S(2)}, u32[]{:S(2)}) %collective-permute-start.10) | collective-permute-done | bytes 131104 | tf_op jit(solution)/shard_map/ppermute | solution.py:52
  106.1 0.7 add_add_fusion.a_ref
  106.7 3.6 %all-gather.4.cloned.1.call-done.y_ref = bf16[4096,1024]{1,0:T(8,128)(2,1)} async-done(((bf16[128,1024]{1,0:T(8,128)(2,1)}), bf16[4096,1024]{1,0:T(8,128)(2,1)}) %all-gather.4.cloned.1.call-update) | async-done | bytes 8388624 | tf_op jit(solution)/shard_map/all_gather | solution.py:267
  110.4 0.0 all-gather.6.cloned.1.call-update
  110.4 0.0 copy-start
  110.4 0.9 copy-done
  111.3 0.2 shard_map.51
  111.5 8.9 %all_to_all.45.parts_ref = f32[8,1,64]{2,1,0:T(1,128)S(1)} all-to-all(f32[8,1,64]{2,1,0:T(1,128)S(1)} %shard_map.51), channel_id=1, replica_groups={{0,16,32,48,64,80,96,112},{128,144,160,176,192,208,224,240},{256,272,28..., dimensions={0} | all-to-all | bytes 4096 | tf_op jit(solution)/shard_map/all_to_all | solution.py:258
  120.4 0.5 shard_map.52
  120.9 30.2 %all_to_all.46.parts_ref = f32[64,4,128]{2,1,0:T(4,128)S(1)} all-to-all(f32[64,4,128]{2,1,0:T(4,128)S(1)} %get-tuple-element.42), channel_id=1, replica_groups={{0,1,2,3,4,5,6,7,8,9,10,11,12,13,14,15,128,129,130,131,132,133,134,135,..., dimensions={0} | all-to-all | bytes 262144 | tf_op jit(solution)/shard_map/all_to_all | solution.py:356
  151.1 0.3 shard_map.53
  151.4 9.4 %all_to_all.47.parts_ref = f32[8,1,64]{2,1,0:T(1,128)S(1)} all-to-all(f32[8,1,64]{2,1,0:T(1,128)S(1)} %shard_map.53), channel_id=1, replica_groups={{0,16,32,48,64,80,96,112},{128,144,160,176,192,208,224,240},{256,272,28..., dimensions={0} | all-to-all | bytes 4096 | tf_op jit(solution)/shard_map/all_to_all | solution.py:258
  160.8 0.5 shard_map.54
  161.3 22.0 %all_to_all.48.parts_ref = f32[64,4,128]{2,1,0:T(4,128)S(1)} all-to-all(f32[64,4,128]{2,1,0:T(4,128)S(1)} %get-tuple-element.43), channel_id=1, replica_groups={{0,1,2,3,4,5,6,7,8,9,10,11,12,13,14,15,128,129,130,131,132,133,134,135,..., dimensions={0} | all-to-all | bytes 262144 | tf_op jit(solution)/shard_map/all_to_all | solution.py:356
  183.4 0.7 all-gather.6.cloned.1.call-done
  184.0 0.0 copy-start.1
  184.1 1.6 copy-done.1
  185.6 0.7 shard_map.55
  186.3 17.7 %all_to_all.49.parts_ref = f32[8,8,128]{2,1,0:T(8,128)S(1)} all-to-all(f32[8,8,128]{2,1,0:T(8,128)S(1)} %get-tuple-element.45), channel_id=1, replica_groups={{0,16,32,48,64,80,96,112},{128,144,160,176,192,208,224,240},{256,272,28..., dimensions={0} | all-to-all | bytes 65536 | tf_op jit(solution)/shard_map/all_to_all | solution.py:258
  204.1 0.9 shard_map.56
  204.9 8.3 %all_to_all.50.parts_ref = f32[4,4,128]{2,1,0:T(4,128)S(1)} all-to-all(f32[4,4,128]{2,1,0:T(4,128)S(1)} %get-tuple-element.46), channel_id=1, replica_groups={{0,128,256,384},{16,144,272,400},{32,160,288,416},{48,176,304,432},{64,..., dimensions={0} | all-to-all | bytes 16384 | tf_op jit(solution)/shard_map/all_to_all | solution.py:258
  213.2 0.6 shard_map.57
  213.8 9.2 %all_to_all.51.parts_ref = f32[8,8,128]{2,1,0:T(8,128)S(1)} all-to-all(f32[8,8,128]{2,1,0:T(8,128)S(1)} %shard_map.57), channel_id=1, replica_groups={{0,16,32,48,64,80,96,112},{128,144,160,176,192,208,224,240},{256,272,28..., dimensions={0} | all-to-all | bytes 65536 | tf_op jit(solution)/shard_map/all_to_all | solution.py:258
  223.0 0.6 shard_map.58
  223.6 6.5 %all_to_all.52.parts_ref = f32[4,4,128]{2,1,0:T(4,128)S(1)} all-to-all(f32[4,4,128]{2,1,0:T(4,128)S(1)} %get-tuple-element.48), channel_id=1, replica_groups={{0,128,256,384},{16,144,272,400},{32,160,288,416},{48,176,304,432},{64,..., dimensions={0} | all-to-all | bytes 16384 | tf_op jit(solution)/shard_map/all_to_all | solution.py:258
  230.1 0.4 shard_map.59
  230.5 20.9 %all_to_all.53.plan_ref = bf16[8,144,512]{2,1,0:T(8,128)(2,1)S(1)} all-to-all(bf16[8,144,512]{2,1,0:T(8,128)(2,1)S(1)} %shard_map.59), channel_id=1, replica_groups={{0,16,32,48,64,80,96,112},{128,144,160,176,192,208,224,240},{256,272,28..., dimensions={0} | all-to-all | bytes 2359296 | tf_op jit(solution)/shard_map/all_to_all | solution.py:258
  251.4 5.9 %shard_map.60 = (bf16[128,1024]{1,0:T(8,128)(2,1)}, f32[1,128]{1,0:T(1,128)}, f32[1,256]{1,0:T(1,128)}) custom-call(s32[4]{0:T(128)S(1)} %pad_add_fusion.place_ref, bf16[8,144,512]{2,1,0:T(8,128)(2,1)S(1)} %all_to_all.53.plan_ref, f32[8,128]{1,0:T(8,128)S(1)} %get-tuple-element.47.u_ref, bf16[4096,1024]{1,0:T(8,128)(2,1)} %all-gather.4.cloned.1.call-done.y_ref), custom_call_target="tpu_custom_call" | custom-call | tf_op jit(solution)/shard_map/pallas_call | solution.py:370
  (5 shorter events, 0.1 us)
Async XLA Ops:
  7.2 103.2 %all-gather.4.cloned.1.call-start = ((), (), s32[]{:S(2)}) async-start(), calls=%async_computation.9 | async-start | bytes 8650752 | tf_op jit(solution)/shard_map/all_gather | solution.py:267
  7.2 9.9 %collective-permute-start = (bf16[128,1024]{1,0:T(8,128)(2,1)}, bf16[128,1024]{1,0:T(8,128)(2,1)S(1)}, u32[]{:S(2)}, u32[]{:S(2)}) collective-permute-start(bf16[128,1024]{1,0:T(8,128)(2,1)} %param.2), channel_id=1, source_target_pairs={{0,32},{16,112},{32,0},{48,80},{64,96},{80,48},{96,64},{112,16},{1... | collective-permute-start | bytes 786440 | tf_op jit(solution)/shard_map/ppermute | solution.py:40
  12.4 8.6 %collective-permute-start.1 = (bf16[128,1024]{1,0:T(8,128)(2,1)}, bf16[128,1024]{1,0:T(8,128)(2,1)S(1)}, u32[]{:S(2)}, u32[]{:S(2)}) collective-permute-start(bf16[128,1024]{1,0:T(8,128)(2,1)} %param.3), channel_id=1, source_target_pairs={{0,128},{16,400},{32,160},{48,432},{64,192},{80,464},{96,224},{112... | collective-permute-start | bytes 786440 | tf_op jit(solution)/shard_map/ppermute | solution.py:44
  22.0 10.2 %collective-permute-start.2 = (bf16[256,1024]{1,0:T(8,128)(2,1)S(1)}, bf16[256,1024]{1,0:T(8,128)(2,1)S(1)}, u32[]{:S(2)}, u32[]{:S(2)}) collective-permute-start(bf16[256,1024]{1,0:T(8,128)(2,1)S(1)} %pad_maximum_fusion.refs_0_), channel_id=1, source_target_pairs={{0,96},{16,48},{32,64},{48,16},{64,32},{80,112},{96,0},{112,80},{1... | collective-permute-start | bytes 1572872 | tf_op jit(solution)/shard_map/ppermute | solution.py:40
  24.0 8.3 %collective-permute-start.4 = (bf16[256,1024]{1,0:T(8,128)(2,1)S(1)}, bf16[256,1024]{1,0:T(8,128)(2,1)S(1)}, u32[]{:S(2)}, u32[]{:S(2)}) collective-permute-start(bf16[256,1024]{1,0:T(8,128)(2,1)S(1)} %pad_maximum_fusion.refs_0_), channel_id=1, source_target_pairs={{0,16},{16,0},{32,48},{48,32},{64,80},{80,64},{96,112},{112,96},{1... | collective-permute-start | bytes 1572872 | tf_op jit(solution)/shard_map/ppermute | solution.py:32
  29.3 10.2 %collective-permute-start.3 = (bf16[256,1024]{1,0:T(8,128)(2,1)S(1)}, bf16[256,1024]{1,0:T(8,128)(2,1)S(1)}, u32[]{:S(2)}, u32[]{:S(2)}) collective-permute-start(bf16[256,1024]{1,0:T(8,128)(2,1)S(1)} %pad_maximum_fusion.1.refs_4_), channel_id=1, source_target_pairs={{0,384},{16,144},{32,416},{48,176},{64,448},{80,208},{96,480},{112... | collective-permute-start | bytes 1572872 | tf_op jit(solution)/shard_map/ppermute | solution.py:44
  39.6 144.5 %all-gather.6.cloned.1.call-start = ((), (), s32[]{:S(2)}) async-start(), calls=%async_computation.10 | async-start | bytes 2228224 | tf_op jit(solution)/shard_map/all_gather | solution.py:310
  39.6 5.5 %collective-permute-start.5 = (bf16[256,1024]{1,0:T(8,128)(2,1)S(1)}, bf16[256,1024]{1,0:T(8,128)(2,1)S(1)}, u32[]{:S(2)}, u32[]{:S(2)}) collective-permute-start(bf16[256,1024]{1,0:T(8,128)(2,1)S(1)} %collective-permute-done.2.refs_1_), channel_id=1, source_target_pairs={{0,16},{16,0},{32,48},{48,32},{64,80},{80,64},{96,112},{112,96},{1... | collective-permute-start | bytes 1572872 | tf_op jit(solution)/shard_map/ppermute | solution.py:32
  48.9 21.5 %collective-permute-start.6 = (f32[8,64,512]{2,1,0:T(8,128)S(1)}, f32[8,64,512]{2,1,0:T(8,128)S(1)}, u32[]{:S(2)}, u32[]{:S(2)}) collective-permute-start(f32[8,64,512]{2,1,0:T(8,128)S(1)} %get-tuple-element.35), channel_id=1, source_target_pairs={{0,1},{1,0},{2,3},{3,2},{4,5},{5,4},{6,7},{7,6},{8,9},{9,8},{10,11... | collective-permute-start | bytes 3145736 | tf_op jit(solution)/shard_map/ppermute | solution.py:52
  70.5 7.3 %collective-permute-start.7 = (f32[64,512]{1,0:T(8,128)S(1)}, f32[64,512]{1,0:T(8,128)S(1)}, u32[]{:S(2)}, u32[]{:S(2)}) collective-permute-start(f32[64,512]{1,0:T(8,128)S(1)} %get-tuple-element.37), channel_id=1, source_target_pairs={{0,2},{1,3},{2,4},{3,5},{4,6},{5,7},{6,8},{7,9},{8,10},{9,11},{10,... | collective-permute-start | bytes 393224 | tf_op jit(solution)/shard_map/ppermute | solution.py:52
  74.6 9.3 %collective-permute-start.11 = (f32[64,512]{1,0:T(8,128)S(1)}, f32[64,512]{1,0:T(8,128)S(1)}, u32[]{:S(2)}, u32[]{:S(2)}) collective-permute-start(f32[64,512]{1,0:T(8,128)S(1)} %get-tuple-element.39), channel_id=1, source_target_pairs={{0,14},{1,15},{2,0},{3,1},{4,2},{5,3},{6,4},{7,5},{8,6},{9,7},{10,... | collective-permute-start | bytes 393224 | tf_op jit(solution)/shard_map/ppermute | solution.py:52
  77.9 8.0 %collective-permute-start.8 = (f32[64,512]{1,0:T(8,128)S(1)}, f32[64,512]{1,0:T(8,128)S(1)}, u32[]{:S(2)}, u32[]{:S(2)}) collective-permute-start(f32[64,512]{1,0:T(8,128)S(1)} %bitcast_add_fusion.4), channel_id=1, source_target_pairs={{0,2},{1,3},{2,4},{3,5},{4,6},{5,7},{6,8},{7,9},{8,10},{9,11},{10,... | collective-permute-start | bytes 393224 | tf_op jit(solution)/shard_map/ppermute | solution.py:52
  83.9 8.3 %collective-permute-start.12 = (f32[64,512]{1,0:T(8,128)S(1)}, f32[64,512]{1,0:T(8,128)S(1)}, u32[]{:S(2)}, u32[]{:S(2)}) collective-permute-start(f32[64,512]{1,0:T(8,128)S(1)} %bitcast_add_fusion.1), channel_id=1, source_target_pairs={{0,14},{1,15},{2,0},{3,1},{4,2},{5,3},{6,4},{7,5},{8,6},{9,7},{10,... | collective-permute-start | bytes 393224 | tf_op jit(solution)/shard_map/ppermute | solution.py:52
  85.9 9.1 %collective-permute-start.9 = (f32[64,512]{1,0:T(8,128)S(1)}, f32[64,512]{1,0:T(8,128)S(1)}, u32[]{:S(2)}, u32[]{:S(2)}) collective-permute-start(f32[64,512]{1,0:T(8,128)S(1)} %bitcast_add_fusion.3), channel_id=1, source_target_pairs={{0,2},{1,3},{2,4},{3,5},{4,6},{5,7},{6,8},{7,9},{8,10},{9,11},{10,... | collective-permute-start | bytes 393224 | tf_op jit(solution)/shard_map/ppermute | solution.py:52
  92.3 9.4 %collective-permute-start.13 = (f32[64,512]{1,0:T(8,128)S(1)}, f32[64,512]{1,0:T(8,128)S(1)}, u32[]{:S(2)}, u32[]{:S(2)}) collective-permute-start(f32[64,512]{1,0:T(8,128)S(1)} %bitcast_add_fusion), channel_id=1, source_target_pairs={{0,14},{1,15},{2,0},{3,1},{4,2},{5,3},{6,4},{7,5},{8,6},{9,7},{10,... | collective-permute-start | bytes 393224 | tf_op jit(solution)/shard_map/ppermute | solution.py:52
  95.0 11.0 %collective-permute-start.10 = (f32[64,512]{1,0:T(8,128)S(1)}, f32[64,512]{1,0:T(8,128)S(1)}, u32[]{:S(2)}, u32[]{:S(2)}) collective-permute-start(f32[64,512]{1,0:T(8,128)S(1)} %bitcast_add_fusion.2), channel_id=1, source_target_pairs={{0,2},{1,3},{2,4},{3,5},{4,6},{5,7},{6,8},{7,9},{8,10},{9,11},{10,... | collective-permute-start | bytes 393224 | tf_op jit(solution)/shard_map/ppermute | solution.py:52
  110.4 0.9 copy-start
  184.0 1.6 copy-start.1
Sparse Core Ops, SparseCore 0:
  39.7 70.6 all-gather.3
  113.0 70.9 all-gather.5

commit v7 on v6

--- a/solution.py
+++ b/solution.py
@@ -75,8 +75,10 @@
     for k, (first, second) in enumerate(PLACES):
         block = slice(k % 2 * rows, (k % 2 + 1) * rows)
         mine, other = jnp.where(c == 0, first, second), jnp.where(c == 0, second, first)
-        x_all[lax.bitwise_xor(x, mine) * CORES + c] = here[k // 2][block, :]
-        x_all[lax.bitwise_xor(x, other) * CORES + 1 - c] = there[k // 2][block, :]
+        at = pl.multiple_of((lax.bitwise_xor(x, mine) * CORES + c) * rows, rows)
+        x_all[pl.ds(at, rows), :] = here[k // 2][block, :]
+        at = pl.multiple_of((lax.bitwise_xor(x, other) * CORES + 1 - c) * rows, rows)
+        x_all[pl.ds(at, rows), :] = there[k // 2][block, :]
         at = pl.multiple_of(lax.bitwise_xor(y, mine) * rows, rows)
         y_all[pl.ds(at, rows), :] = ys[k // 2][block, :]
     for k in range(YS):
@@ -90,16 +92,18 @@
         base = jnp.where(same, z, partner)
         ahead = jnp.where(c == 0, lax.rem(t + depth - base, depth), lax.rem(base + depth - t, depth))
         places.append(ahead // 2 + jnp.where(same, 0, depth // 2))
-    for k in range(XS * CORES):
-        value = x_all[k]
+    tall = 4 * rows
+    for k in range(XS * CORES // 4):
+        value = x_all[k * tall : (k + 1) * tall, :]
         wide = value.astype(jnp.float32)
         x_squares = scale * jnp.sum(wide * wide, axis=1, keepdims=True)
         cross = lax.dot_general(
             value, y_all[...], (((1,), (1,)), ((), ())), preferred_element_type=jnp.float32
         )
         value = (2.0 * scale) * cross - x_squares - y_squares[...]
-        for t in range(depth):
-            chunks[places[t], k * high : (k + 1) * high, :] = value[t * high : (t + 1) * high]
+        for i in range(4 * depth):
+            block = k * 4 + i // depth
+            chunks[places[i % depth], block * high : (block + 1) * high, :] = value[i * high : (i + 1) * high]
     for k in range(depth // 2):
         keep[k] = chunks[k]
         give[k] = chunks[depth // 2 + k]
@@ -162,20 +166,8 @@
     row_sums(a_ref, row_of(parts_ref, log_weight), out_ref, out_ref.shape[2])
 
 
-def all_rows_kernel(log_weight, chunks_ref, parts_ref, a_ref, out_ref):
-    blocks, n = out_ref.shape[1:]
-    depth = chunks_ref.shape[0]
-    high = n // depth
-    for z in range(depth):
-        for block in range(blocks):
-            at = block * n + z * high
-            a_ref[at : at + high, :] = chunks_ref[z, block * high : (block + 1) * high, :]
-    row_sums(a_ref, row_of(parts_ref, log_weight), out_ref, n)
-
-
-def columns_kernel(log_weight, a_ref, parts_ref, u_ref, out_ref, shifted):
+def columns_kernel(log_weight, a_ref, parts_ref, out_ref, shifted):
     u = log_weight - joined(parts_ref[...])
-    u_ref[...] = u
     blocks, n = u.shape
     width = a_ref.shape[1]
     peak = None
@@ -196,48 +188,79 @@
     copy_out(out_ref)
 
 
-def plan_kernel(log_weight, a_ref, u_ref, parts_ref, out_ref):
-    v = row_of(parts_ref, log_weight)
-    u = u_ref[...] - log_weight
-    blocks, n = u.shape
-    top = v.astype(jnp.bfloat16).astype(jnp.float32)
-    rest = v - top
-    middle = rest.astype(jnp.bfloat16).astype(jnp.float32)
-    extra = out_ref.shape[1] - n
-    row = lax.broadcasted_iota(jnp.int32, (extra, v.shape[1]), 0)
-    under = jnp.where(row == 0, top, jnp.where(row == 1, middle, jnp.where(row == 2, rest - middle, 0.0)))
-    under = under.astype(jnp.bfloat16)
-    for k in range(blocks):
-        value = a_ref[k * n : (k + 1) * n, :] + (column_of(u, k) + v)
-        out_ref[k, :n, :] = jnp.exp2(value).astype(jnp.bfloat16)
-        out_ref[k, n:, :] = under
-
-
-def target_kernel(unit, place_ref, plan_ref, u_ref, y_ref, out_ref, f_ref, g_ref, total, mass):
+def join_kernel(parts_ref, out_ref):
+    out_ref[0] = joined(parts_ref[...])
+    copy_out(out_ref)
+
+
+def half_steps(log_weight, a_ref, v, u_ref, l_ref):
+    rows, columns = a_ref.shape
+    lanes = u_ref.shape[1]
+    copies, high, width = l_ref.shape
+
+    @pl.loop(0, rows // 8, step=2)
+    def _(base):
+        for i in range(2):
+            at = pl.ds(pl.multiple_of((base + i) * 8, 8), 8)
+            value = a_ref[at, :] + v
+            peak = jnp.max(value, axis=1, keepdims=True)
+            total = jnp.sum(jnp.exp2(value - peak), axis=1, keepdims=True)
+            u = log_weight - (peak + jnp.log(total) * LOG2E)
+            u_ref[at, :] = jnp.broadcast_to(u, (8, lanes))
+
+    for k in range(high):
+        for i in range(width // lanes):
+            at = pl.ds(k * width + i * lanes, lanes)
+            value = a_ref[:, at] + u_ref[...]
+            peak = jnp.max(value, axis=0, keepdims=True)
+            total = jnp.sum(jnp.exp2(value - peak), axis=0, keepdims=True)
+            l_ref[0, k : k + 1, i * lanes : (i + 1) * lanes] = peak + jnp.log(total) * LOG2E
+    whole = l_ref[0]
+    for k in range(1, copies):
+        l_ref[k] = whole
+
+
+def whole_rows_kernel(log_weight, pieces_ref, parts_ref, a_ref, u_ref, l_ref):
+    depth, blocks, high, width = pieces_ref.shape
+    n = width // YS
+    v = log_weight - parts_ref[...]
+    for z in range(depth):
+        for y in range(YS):
+            for k in range(blocks):
+                at = (y * blocks + k) * n
+                a_ref[z * high : (z + 1) * high, at : at + n] = pieces_ref[z, k, :, y * n : (y + 1) * n]
+    v = jnp.concatenate([v[k, y : y + 1] for y in range(YS) for k in range(blocks)], axis=1)
+    half_steps(log_weight, a_ref, v, u_ref, l_ref)
+
+
+def next_kernel(log_weight, a_ref, parts_ref, u_ref, l_ref):
+    v = log_weight - joined(parts_ref[...])
+    v = jnp.concatenate([v[k : k + 1] for k in range(v.shape[0])], axis=1)
+    half_steps(log_weight, a_ref, v, u_ref, l_ref)
+
+
+def target_kernel(log_weight, unit, steps, a_ref, u_ref, parts_ref, y_ref, out_ref, f_ref, g_ref, total, mass):
     step = pl.program_id(0)
-    z, x, c = place_ref[0], place_ref[2], place_ref[3]
-    blocks = plan_ref.shape[0]
-    n = out_ref.shape[0]
+    lines = g_ref.shape[0] // steps
 
     @pl.when(step == 0)
     def _():
         total[...] = jnp.zeros_like(total)
         mass[...] = jnp.zeros_like(mass)
-        f_ref[...] = unit * u_ref[pl.ds(x * CORES + c, 1), :]
-
-    plan = jnp.concatenate([plan_ref[k, :n, :] for k in range(blocks)], axis=1)
+        u = u_ref[...]
+        f_ref[...] = unit * jnp.sum(jnp.where(on_diagonal(u.shape[0]), u, 0.0), axis=0, keepdims=True)
+        g_ref[...] = log_weight - joined(parts_ref[...])
+
+    v = jnp.concatenate([g_ref[pl.ds(step * lines + k, 1), :] for k in range(lines)], axis=1)
+    u = u_ref[:, :1]
+    plan = jnp.exp2((u - log_weight + v) + a_ref[...]).astype(jnp.bfloat16)
     mass[...] += jnp.sum(plan.astype(jnp.float32), axis=1, keepdims=True)
     total[...] += jnp.dot(plan, y_ref[...], preferred_element_type=jnp.float32)
 
-    @pl.when(step == z // XS)
-    def _():
-        for k in range(CORES):
-            v = plan_ref[lax.rem(z, XS) * CORES + k, n:, :].astype(jnp.float32)
-            g_ref[:, k * n : (k + 1) * n] = unit * (v[0:1] + v[1:2] + v[2:3])
-
-    @pl.when(step == YS - 1)
+    @pl.when(step == steps - 1)
     def _():
         out_ref[...] = (total[...] / mass[...]).astype(out_ref.dtype)
+        g_ref[...] = unit * g_ref[...]
 
 
 def on_device(noise_rows, data_rows):
@@ -275,7 +298,7 @@
         in_specs=[SMEM] + [VMEM] * 6,
         out_specs=[VMEM] * 2,
         scratch_shapes=[
-            pltpu.VMEM((group, rows, features), jnp.bfloat16),
+            pltpu.VMEM((group * rows, features), jnp.bfloat16),
             pltpu.VMEM((YS * rows, features), jnp.bfloat16),
             pltpu.VMEM((1, wide), f32),
             pltpu.VMEM((depth,) + chunk, f32),
@@ -306,16 +329,15 @@
                 back = back + back_rest[step]
     own = own + ahead + back
 
-    everything, own = lax.optimization_barrier((everything, own))
-    gathered = lax.all_gather(own, "dp")
+    pieces = swap(own.reshape(group, rows // depth, wide), x_groups)
+    everything, pieces = lax.optimization_barrier((everything, pieces))
+    gathered = lax.all_gather(pieces, "dp")
     z_groups = [
         [((y * group) + k) * depth + d for y in range(YS) for d in range(depth)] for k in range(group)
     ]
     few = tall // depth
-    for step in range(ITERS):
-        early = step < EARLY
-        lines, n = (1, few) if early else (group, rows)
-        row_shape = jax.ShapeDtypeStruct((group, lines, n), f32)
+    row_shape = jax.ShapeDtypeStruct((group, 1, few), f32)
+    for step in range(EARLY):
         if step == 0:
             part = pl.pallas_call(
                 first_rows_kernel,
@@ -324,14 +346,6 @@
                 out_specs=VMEM,
                 compiler_params=PARAMS,
             )(own)
-        elif step == EARLY:
-            a, part = pl.pallas_call(
-                functools.partial(all_rows_kernel, log_weight),
-                out_shape=[jax.ShapeDtypeStruct((tall, wide), f32), row_shape],
-                in_specs=[VMEM] * 2,
-                out_specs=[VMEM] * 2,
-                compiler_params=PARAMS,
-            )(gathered, part)
         else:
             part = pl.pallas_call(
                 functools.partial(rows_kernel, log_weight),
@@ -339,60 +353,83 @@
                 in_specs=[VMEM] * 2,
                 out_specs=VMEM,
                 compiler_params=PARAMS,
-            )(own if early else a, part)
+            )(own, part)
         part = swap(part, x_groups)
-        u, part = pl.pallas_call(
+        part = pl.pallas_call(
             functools.partial(columns_kernel, log_weight),
-            out_shape=[
-                jax.ShapeDtypeStruct((lines, n), f32),
-                jax.ShapeDtypeStruct((YS * depth if early else YS, YS, rows), f32),
-            ],
+            out_shape=jax.ShapeDtypeStruct((YS * depth, YS, rows), f32),
             in_specs=[VMEM] * 2,
-            out_specs=[VMEM] * 2,
-            scratch_shapes=[pltpu.VMEM((lines * n, wide), f32)],
+            out_specs=VMEM,
+            scratch_shapes=[pltpu.VMEM((few, wide), f32)],
             compiler_params=PARAMS,
-        )(own if early else a, part)
-        if early:
-            part = lax.all_to_all(
-                part, ("noise", "dp"), 0, 0, axis_index_groups=z_groups, tiled=True
-            )
-        else:
-            part = swap(part, y_groups)
-    plan = pl.pallas_call(
-        functools.partial(plan_kernel, log_weight),
-        out_shape=jax.ShapeDtypeStruct((group, rows + 16, wide), jnp.bfloat16),
-        in_specs=[VMEM] * 3,
+        )(own, part)
+        part = lax.all_to_all(
+            part, ("noise", "dp"), 0, 0, axis_index_groups=z_groups, tiled=True
+        )
+    part = pl.pallas_call(
+        join_kernel,
+        out_shape=jax.ShapeDtypeStruct((group, YS, rows), f32),
+        in_specs=[VMEM],
         out_specs=VMEM,
         compiler_params=PARAMS,
-    )(a, u, part)
-    plan = swap(plan, x_groups)
-
+    )(part)
+    part = swap(part, x_groups)
+
+    copies = lax.axis_size("noise")
+    high = 8
+    block = tokens // high
+    u_shape = jax.ShapeDtypeStruct((rows, rows), f32)
+    l_shape = jax.ShapeDtypeStruct((copies, high, block), f32)
+    for step in range(EARLY, ITERS):
+        if step == EARLY:
+            a, u, part = pl.pallas_call(
+                functools.partial(whole_rows_kernel, log_weight),
+                out_shape=[jax.ShapeDtypeStruct((rows, tokens), f32), u_shape, l_shape],
+                in_specs=[VMEM] * 2,
+                out_specs=[VMEM] * 3,
+                compiler_params=PARAMS,
+            )(gathered, part)
+        else:
+            u, part = pl.pallas_call(
+                functools.partial(next_kernel, log_weight),
+                out_shape=[u_shape, l_shape],
+                in_specs=[VMEM] * 2,
+                out_specs=[VMEM] * 2,
+                compiler_params=PARAMS,
+            )(a, part)
+        part = lax.all_to_all(part, "noise", 0, 0, tiled=True)
+
+    steps = 4
     targets, noise_potential, data_potential = pl.pallas_call(
-        functools.partial(target_kernel, epsilon / LOG2E),
-        grid=(YS,),
+        functools.partial(target_kernel, log_weight, epsilon / LOG2E, steps),
+        grid=(steps,),
         out_shape=[
             jax.ShapeDtypeStruct((rows, features), jnp.bfloat16),
             jax.ShapeDtypeStruct((1, rows), f32),
-            jax.ShapeDtypeStruct((1, CORES * rows), f32),
+            jax.ShapeDtypeStruct((high, block), f32),
         ],
         in_specs=[
-            SMEM,
-            pl.BlockSpec((group, rows + 16, rows), lambda k: (0, 0, k)),
-            pl.BlockSpec((group, rows), lambda k: (0, 0)),
-            pl.BlockSpec((group * rows, features), lambda k: (k, 0)),
+            pl.BlockSpec((rows, tokens // steps), lambda k: (0, k)),
+            pl.BlockSpec((rows, rows), lambda k: (0, 0)),
+            pl.BlockSpec((copies, high, block), lambda k: (0, 0, 0)),
+            pl.BlockSpec((tokens // steps, features), lambda k: (k, 0)),
         ],
         out_specs=[
             pl.BlockSpec((rows, features), lambda k: (0, 0)),
             pl.BlockSpec((1, rows), lambda k: (0, 0)),
-            pl.BlockSpec((1, CORES * rows), lambda k: (0, 0)),
+            pl.BlockSpec((high, block), lambda k: (0, 0)),
         ],
         scratch_shapes=[
             pltpu.VMEM((rows, features), f32),
             pltpu.VMEM((rows, 1), f32),
         ],
         compiler_params=PARAMS,
-    )(place, plan, u, everything)
-    return targets, noise_potential.reshape(rows), data_potential.reshape(CORES * rows)
+    )(a, u, part, everything)
+    share = tokens // depth
+    data_potential = lax.dynamic_slice(
+        data_potential, (z * share // block, z * share % block), (1, share)
+    )
+    return targets, noise_potential.reshape(rows), data_potential.reshape(share)
 
 
 def solution(mesh):

time: 265 us -> 254 us (0.958)
  blocking collectives: 133 us -> 110 us
  waiting for transfers between devices: 38.5 us -> 52 us
    all_to_all x7 -> x4, blocking collectives: 80.9 us -> 36.9 us  [swap(): lax.all_to_all(value, 'noise', 0, 0, axis_index_groups=groups, tiled=True)]
    all_to_all x0 -> x1, blocking collectives: none -> 19.1 us  [on_device(): part = lax.all_to_all(part, 'noise', 0, 0, tiled=True)]
    all_to_all x0 -> x1, waiting for transfers between devices: none -> 11.6 us  [on_device(): part = lax.all_to_all(part, 'noise', 0, 0, tiled=True)]
    ppermute x8, waiting for transfers between devices: 21.5 us -> 27.7 us  [send_z(): return lax.ppermute(value, ('noise', 'dp'), pairs)]
    ppermute x8, starting transfers between devices: 35.4 us -> 29.7 us  [send_z(): return lax.ppermute(value, ('noise', 'dp'), pairs)]
    all_to_all x0 -> x1, starting transfers between devices: none -> 3.99 us  [on_device(): part = lax.all_to_all(part, 'noise', 0, 0, tiled=True)]
    all_gather x1, waiting for transfers between devices: 3.62 us -> 0.01 us  [on_device(): everything = lax.all_gather(late_rows, 'noise', axis=0, tiled=True)]
    pallas_call x7 -> x6, Pallas kernels: 9.46 us -> 12.6 us  [the longest x1 6.13 us: on_device(): pl.pallas_call(functools.partial(target_kernel, log_weight, epsilon / LOG...]
  transfers between devices with their start and end apart: 16 -> 17, of which waited for: 13 -> 13; matrix products, arithmetic and copies ran while one was open for 1% -> 0% of each run, Pallas kernels for 2% -> 1%
where the time goes in v7:
time: 254 us; the launch traced here: 253 us
  blocking collectives  110 us (43%)
  starting transfers between devices  56.8 us (22%)
  waiting for transfers between devices  52 us (20%)
  Pallas kernels  15.6 us (6%)
  between operations  14.3 us (6%)
    all_to_all x2, blocking collectives, on_device(): lax.all_to_all(part, ('noise', 'dp'), 0, 0, axis_index_groups=z_groups, t...  54.1 us
    all_to_all x4, blocking collectives, swap(): lax.all_to_all(value, 'noise', 0, 0, axis_index_groups=groups, tiled=True)  36.9 us
    ppermute x8, starting transfers between devices, send_z(): return lax.ppermute(value, ('noise', 'dp'), pairs)  29.7 us
    ppermute x8, waiting for transfers between devices, send_z(): return lax.ppermute(value, ('noise', 'dp'), pairs)  27.7 us
    all_to_all x1, blocking collectives, on_device(): part = lax.all_to_all(part, 'noise', 0, 0, tiled=True)  19.1 us
    all_to_all x1, waiting for transfers between devices, on_device(): part = lax.all_to_all(part, 'noise', 0, 0, tiled=True)  11.6 us
    ppermute x2, waiting for transfers between devices, swap_y(): lax.ppermute(value, 'noise', noise_pairs(lambda y, x, c: (y ^ by[c], x, c)))  10.3 us
    ppermute x2, starting transfers between devices, to_other_core(): lax.ppermute(value, 'noise', noise_pairs(lambda y, x, c: (y, x, 1 - c)))  9.35 us
  transfers between devices with their start and end apart: 17, of which 13 were waited for; matrix products, arithmetic and copies ran while one was open for 0% of the time, Pallas kernels for 1%

profile of v7, /device:TPU:1, one launch (start us, length us, event | category | flops | bytes accessed | tf_op | source)
XLA Modules:
  0.0 253.3 jit_solution(17562999445941092131)
XLA Ops:
  7.2 0.0 all-gather.4.cloned.1.call-start
  7.2 5.2 %collective-permute-start = (bf16[128,1024]{1,0:T(8,128)(2,1)}, bf16[128,1024]{1,0:T(8,128)(2,1)S(1)}, u32[]{:S(2)}, u32[]{:S(2)}) collective-permute-start(bf16[128,1024]{1,0:T(8,128)(2,1)} %param.2), channel_id=1, source_target_pairs={{0,32},{16,112},{32,0},{48,80},{64,96},{80,48},{96,64},{112,16},{1... | collective-permute-start | bytes 786440 | tf_op jit(solution)/shard_map/ppermute | solution.py:40
  12.4 4.6 %collective-permute-start.1 = (bf16[128,1024]{1,0:T(8,128)(2,1)}, bf16[128,1024]{1,0:T(8,128)(2,1)S(1)}, u32[]{:S(2)}, u32[]{:S(2)}) collective-permute-start(bf16[128,1024]{1,0:T(8,128)(2,1)} %param.3), channel_id=1, source_target_pairs={{0,128},{16,400},{32,160},{48,432},{64,192},{80,464},{96,224},{112... | collective-permute-start | bytes 786440 | tf_op jit(solution)/shard_map/ppermute | solution.py:44
  17.1 0.0 collective-permute-done
  17.1 1.0 pad_maximum_fusion.refs_0_
  18.1 3.0 %collective-permute-done.1 = bf16[128,1024]{1,0:T(8,128)(2,1)S(1)} collective-permute-done((bf16[128,1024]{1,0:T(8,128)(2,1)}, bf16[128,1024]{1,0:T(8,128)(2,1)S(1)}, u32[]{:S(2)}, u32[]{:S(2)}) %collective-permute-start.1) | collective-permute-done | bytes 262176 | tf_op jit(solution)/shard_map/ppermute | solution.py:44
  21.0 1.0 pad_maximum_fusion.1.refs_4_
  22.0 1.9 collective-permute-start.2
  24.0 5.4 %collective-permute-start.4 = (bf16[256,1024]{1,0:T(8,128)(2,1)S(1)}, bf16[256,1024]{1,0:T(8,128)(2,1)S(1)}, u32[]{:S(2)}, u32[]{:S(2)}) collective-permute-start(bf16[256,1024]{1,0:T(8,128)(2,1)S(1)} %pad_maximum_fusion.refs_0_), channel_id=1, source_target_pairs={{0,16},{16,0},{32,48},{48,32},{64,80},{80,64},{96,112},{112,96},{1... | collective-permute-start | bytes 1572872 | tf_op jit(solution)/shard_map/ppermute | solution.py:32
  29.3 1.9 collective-permute-start.3
  31.3 1.0 collective-permute-done.2.refs_1_
  32.2 0.0 collective-permute-done.4.refs_2_
  32.3 7.3 %collective-permute-done.3.refs_5_ = bf16[256,1024]{1,0:T(8,128)(2,1)S(1)} collective-permute-done((bf16[256,1024]{1,0:T(8,128)(2,1)S(1)}, bf16[256,1024]{1,0:T(8,128)(2,1)S(1)}, u32[]{:S(2)}, u32[]{:S(2)}) %collective-permute-start.3) | collective-permute-done | bytes 524320 | tf_op jit(solution)/shard_map/ppermute | solution.py:44
  39.5 0.0 all-gather.4.cloned.1.call-update
  39.6 0.0 all-gather.6.cloned.1.call-start
  39.6 4.0 %collective-permute-start.5 = (bf16[256,1024]{1,0:T(8,128)(2,1)S(1)}, bf16[256,1024]{1,0:T(8,128)(2,1)S(1)}, u32[]{:S(2)}, u32[]{:S(2)}) collective-permute-start(bf16[256,1024]{1,0:T(8,128)(2,1)S(1)} %collective-permute-done.2.refs_1_), channel_id=1, source_target_pairs={{0,16},{16,0},{32,48},{48,32},{64,80},{80,64},{96,112},{112,96},{1... | collective-permute-start | bytes 1572872 | tf_op jit(solution)/shard_map/ppermute | solution.py:32
  43.7 0.1 pad_add_fusion.place_ref
  43.7 1.4 collective-permute-done.5.refs_3_
  45.1 2.3 shard_map.49
  47.5 9.3 %collective-permute-start.6 = (f32[8,64,512]{2,1,0:T(8,128)S(1)}, f32[8,64,512]{2,1,0:T(8,128)S(1)}, u32[]{:S(2)}, u32[]{:S(2)}) collective-permute-start(f32[8,64,512]{2,1,0:T(8,128)S(1)} %get-tuple-element.32), channel_id=1, source_target_pairs={{0,1},{1,0},{2,3},{3,2},{4,5},{5,4},{6,7},{7,6},{8,9},{9,8},{10,11... | collective-permute-start | bytes 3145736 | tf_op jit(solution)/shard_map/ppermute | solution.py:52
  56.8 12.6 %collective-permute-done.6.got = f32[8,64,512]{2,1,0:T(8,128)S(1)} collective-permute-done((f32[8,64,512]{2,1,0:T(8,128)S(1)}, f32[8,64,512]{2,1,0:T(8,128)S(1)}, u32[]{:S(2)}, u32[]{:S(2)}) %collective-permute-start.6) | collective-permute-done | bytes 1048608 | tf_op jit(solution)/shard_map/ppermute | solution.py:52
  69.4 0.1 shard_map.50
  69.5 3.8 %collective-permute-start.7 = (f32[64,512]{1,0:T(8,128)S(1)}, f32[64,512]{1,0:T(8,128)S(1)}, u32[]{:S(2)}, u32[]{:S(2)}) collective-permute-start(f32[64,512]{1,0:T(8,128)S(1)} %get-tuple-element.34), channel_id=1, source_target_pairs={{0,2},{1,3},{2,4},{3,5},{4,6},{5,7},{6,8},{7,9},{8,10},{9,11},{10,... | collective-permute-start | bytes 393224 | tf_op jit(solution)/shard_map/ppermute | solution.py:52
  73.3 2.4 collective-permute-start.11
  75.7 3.0 %collective-permute-done.7 = f32[64,512]{1,0:T(8,128)S(1)} collective-permute-done((f32[64,512]{1,0:T(8,128)S(1)}, f32[64,512]{1,0:T(8,128)S(1)}, u32[]{:S(2)}, u32[]{:S(2)}) %collective-permute-start.7) | collective-permute-done | bytes 131104 | tf_op jit(solution)/shard_map/ppermute | solution.py:52
  78.7 2.5 collective-permute-start.8
  81.2 1.6 collective-permute-done.11
  82.8 2.1 collective-permute-start.12
  84.9 1.2 collective-permute-done.8
  86.1 4.1 %collective-permute-start.9 = (f32[64,512]{1,0:T(8,128)S(1)}, f32[64,512]{1,0:T(8,128)S(1)}, u32[]{:S(2)}, u32[]{:S(2)}) collective-permute-start(f32[64,512]{1,0:T(8,128)S(1)} %bitcast_add_fusion.3), channel_id=1, source_target_pairs={{0,2},{1,3},{2,4},{3,5},{4,6},{5,7},{6,8},{7,9},{8,10},{9,11},{10,... | collective-permute-start | bytes 393224 | tf_op jit(solution)/shard_map/ppermute | solution.py:52
  90.3 0.6 collective-permute-done.12
  90.9 2.3 collective-permute-start.13
  93.2 1.9 collective-permute-done.9
  95.1 3.2 %collective-permute-start.10 = (f32[64,512]{1,0:T(8,128)S(1)}, f32[64,512]{1,0:T(8,128)S(1)}, u32[]{:S(2)}, u32[]{:S(2)}) collective-permute-start(f32[64,512]{1,0:T(8,128)S(1)} %bitcast_add_fusion.2), channel_id=1, source_target_pairs={{0,2},{1,3},{2,4},{3,5},{4,6},{5,7},{6,8},{7,9},{8,10},{9,11},{10,... | collective-permute-start | bytes 393224 | tf_op jit(solution)/shard_map/ppermute | solution.py:52
  98.3 2.4 collective-permute-done.13
  100.7 4.5 %collective-permute-done.10 = f32[64,512]{1,0:T(8,128)S(1)} collective-permute-done((f32[64,512]{1,0:T(8,128)S(1)}, f32[64,512]{1,0:T(8,128)S(1)}, u32[]{:S(2)}, u32[]{:S(2)}) %collective-permute-start.10) | collective-permute-done | bytes 131104 | tf_op jit(solution)/shard_map/ppermute | solution.py:52
  105.2 11.3 %all_to_all.40 = f32[8,8,512]{2,1,0:T(8,128)} all-to-all(f32[8,8,512]{2,1,0:T(8,128)S(1)} %bitcast.18), channel_id=1, replica_groups={{0,16,32,48,64,80,96,112},{128,144,160,176,192,208,224,240},{256,272,28..., dimensions={0} | all-to-all | bytes 262144 | tf_op jit(solution)/shard_map/all_to_all | solution.py:281
  116.6 0.0 all-gather.4.cloned.1.call-done.y_ref
  116.6 0.0 all-gather.6.cloned.1.call-update
  116.6 0.2 shard_map.51
  116.8 7.8 %all_to_all.41.parts_ref = f32[8,1,64]{2,1,0:T(1,128)S(1)} all-to-all(f32[8,1,64]{2,1,0:T(1,128)S(1)} %shard_map.51), channel_id=1, replica_groups={{0,16,32,48,64,80,96,112},{128,144,160,176,192,208,224,240},{256,272,28..., dimensions={0} | all-to-all | bytes 4096 | tf_op jit(solution)/shard_map/all_to_all | solution.py:281
  124.6 0.2 shard_map.52
  124.8 31.6 %all_to_all.42.parts_ref = f32[64,4,128]{2,1,0:T(4,128)S(1)} all-to-all(f32[64,4,128]{2,1,0:T(4,128)S(1)} %shard_map.52), channel_id=1, replica_groups={{0,1,2,3,4,5,6,7,8,9,10,11,12,13,14,15,128,129,130,131,132,133,134,135,..., dimensions={0} | all-to-all | bytes 262144 | tf_op jit(solution)/shard_map/all_to_all | solution.py:366
  156.4 0.3 shard_map.53
  156.7 9.2 %all_to_all.43.parts_ref = f32[8,1,64]{2,1,0:T(1,128)S(1)} all-to-all(f32[8,1,64]{2,1,0:T(1,128)S(1)} %shard_map.53), channel_id=1, replica_groups={{0,16,32,48,64,80,96,112},{128,144,160,176,192,208,224,240},{256,272,28..., dimensions={0} | all-to-all | bytes 4096 | tf_op jit(solution)/shard_map/all_to_all | solution.py:281
  165.9 0.2 shard_map.54
  166.1 22.5 %all_to_all.44.parts_ref = f32[64,4,128]{2,1,0:T(4,128)S(1)} all-to-all(f32[64,4,128]{2,1,0:T(4,128)S(1)} %shard_map.54), channel_id=1, replica_groups={{0,1,2,3,4,5,6,7,8,9,10,11,12,13,14,15,128,129,130,131,132,133,134,135,..., dimensions={0} | all-to-all | bytes 262144 | tf_op jit(solution)/shard_map/all_to_all | solution.py:366
  188.5 0.1 shard_map.55
  188.7 8.6 %all_to_all.45.parts_ref = f32[8,4,128]{2,1,0:T(4,128)S(1)} all-to-all(f32[8,4,128]{2,1,0:T(4,128)S(1)} %shard_map.55), channel_id=1, replica_groups={{0,16,32,48,64,80,96,112},{128,144,160,176,192,208,224,240},{256,272,28..., dimensions={0} | all-to-all | bytes 32768 | tf_op jit(solution)/shard_map/all_to_all | solution.py:281
  197.3 0.0 all-gather.6.cloned.1.call-done
  197.3 0.0 copy-start
  197.3 1.6 copy-done
  198.9 2.6 %shard_map.56 = (f32[128,4096]{1,0:T(8,128)S(1)}, f32[128,128]{1,0:T(8,128)}, f32[32,8,512]{2,1,0:T(8,128)S(1)}) custom-call(f32[16,8,8,512]{3,2,1,0:T(8,128)S(1)} %bitcast.19, f32[8,4,128]{2,1,0:T(4,128)S(1)} %all_to_all.45.parts_ref), custom_call_target="tpu_custom_call" | custom-call | tf_op jit(solution)/shard_map/pallas_call | solution.py:385
  201.5 19.1 %all_to_all.46.parts_ref = f32[32,8,512]{2,1,0:T(8,128)S(1)} all-to-all(f32[32,8,512]{2,1,0:T(8,128)S(1)} %get-tuple-element.40), channel_id=1, replica_groups=mesh['noise'=32,'dp'=16] {'noise'}, dimensions={0} | all-to-all | bytes 1048576 | tf_op jit(solution)/shard_map/all_to_all | solution.py:400
  220.7 3.4 %shard_map.57 = (f32[128,128]{1,0:T(8,128)S(1)}, f32[32,8,512]{2,1,0:T(8,128)}) custom-call(f32[128,4096]{1,0:T(8,128)S(1)} %get-tuple-element.39.a_ref, f32[32,8,512]{2,1,0:T(8,128)S(1)} %all_to_all.46.parts_ref), custom_call_target="tpu_custom_call" | custom-call | tf_op jit(solution)/shard_map/pallas_call | solution.py:393
  224.0 4.0 %all-to-all-start.7 = ((f32[32,8,512]{2,1,0:T(8,128)}), f32[32,8,512]{2,1,0:T(8,128)S(1)}, u32[]{:S(2)}, u32[]{:S(2)}) async-start(f32[32,8,512]{2,1,0:T(8,128)} %get-tuple-element.42), calls=%async_computation.7 | async-start | bytes 1048576 | tf_op jit(solution)/shard_map/all_to_all | solution.py:400
  228.0 11.6 %all-to-all-done.7.parts_ref = f32[32,8,512]{2,1,0:T(8,128)S(1)} async-done(((f32[32,8,512]{2,1,0:T(8,128)}), f32[32,8,512]{2,1,0:T(8,128)S(1)}, u32[]{:S(2)}, u32[]{:S(2)}) %all-to-all-start.7) | async-done | bytes 524320 | tf_op jit(solution)/shard_map/all_to_all | solution.py:400
  239.7 6.1 %shard_map.58 = (bf16[128,1024]{1,0:T(8,128)(2,1)}, f32[1,128]{1,0:T(1,128)}, f32[8,512]{1,0:T(8,128)S(1)}) custom-call(f32[128,4096]{1,0:T(8,128)S(1)} %get-tuple-element.39.a_ref, f32[128,128]{1,0:T(8,128)S(1)} %get-tuple-element.41.u_ref, f32[32,8,512]{2,1,0:T(8,128)S(1)} %all-to-all-done.7.parts_ref, bf16[4096,1024]{1,0:T(8,128)(2,1)} %all-gather.4.cloned.1.call-done.y_ref), custom_call_target="tpu_custom_call" | custom-call | tf_op jit(solution)/shard_map/pallas_call | solution.py:403
  245.8 0.6 dynamic_slice.3
  (6 shorter events, 0.1 us)
Async XLA Ops:
  7.2 109.4 %all-gather.4.cloned.1.call-start = ((), (), s32[]{:S(2)}) async-start(), calls=%async_computation.8 | async-start | bytes 8650752 | tf_op jit(solution)/shard_map/all_gather | solution.py:290
  7.2 9.9 %collective-permute-start = (bf16[128,1024]{1,0:T(8,128)(2,1)}, bf16[128,1024]{1,0:T(8,128)(2,1)S(1)}, u32[]{:S(2)}, u32[]{:S(2)}) collective-permute-start(bf16[128,1024]{1,0:T(8,128)(2,1)} %param.2), channel_id=1, source_target_pairs={{0,32},{16,112},{32,0},{48,80},{64,96},{80,48},{96,64},{112,16},{1... | collective-permute-start | bytes 786440 | tf_op jit(solution)/shard_map/ppermute | solution.py:40
  12.4 8.6 %collective-permute-start.1 = (bf16[128,1024]{1,0:T(8,128)(2,1)}, bf16[128,1024]{1,0:T(8,128)(2,1)S(1)}, u32[]{:S(2)}, u32[]{:S(2)}) collective-permute-start(bf16[128,1024]{1,0:T(8,128)(2,1)} %param.3), channel_id=1, source_target_pairs={{0,128},{16,400},{32,160},{48,432},{64,192},{80,464},{96,224},{112... | collective-permute-start | bytes 786440 | tf_op jit(solution)/shard_map/ppermute | solution.py:44
  22.0 10.2 %collective-permute-start.2 = (bf16[256,1024]{1,0:T(8,128)(2,1)S(1)}, bf16[256,1024]{1,0:T(8,128)(2,1)S(1)}, u32[]{:S(2)}, u32[]{:S(2)}) collective-permute-start(bf16[256,1024]{1,0:T(8,128)(2,1)S(1)} %pad_maximum_fusion.refs_0_), channel_id=1, source_target_pairs={{0,96},{16,48},{32,64},{48,16},{64,32},{80,112},{96,0},{112,80},{1... | collective-permute-start | bytes 1572872 | tf_op jit(solution)/shard_map/ppermute | solution.py:40
  24.0 8.3 %collective-permute-start.4 = (bf16[256,1024]{1,0:T(8,128)(2,1)S(1)}, bf16[256,1024]{1,0:T(8,128)(2,1)S(1)}, u32[]{:S(2)}, u32[]{:S(2)}) collective-permute-start(bf16[256,1024]{1,0:T(8,128)(2,1)S(1)} %pad_maximum_fusion.refs_0_), channel_id=1, source_target_pairs={{0,16},{16,0},{32,48},{48,32},{64,80},{80,64},{96,112},{112,96},{1... | collective-permute-start | bytes 1572872 | tf_op jit(solution)/shard_map/ppermute | solution.py:32
  29.3 10.2 %collective-permute-start.3 = (bf16[256,1024]{1,0:T(8,128)(2,1)S(1)}, bf16[256,1024]{1,0:T(8,128)(2,1)S(1)}, u32[]{:S(2)}, u32[]{:S(2)}) collective-permute-start(bf16[256,1024]{1,0:T(8,128)(2,1)S(1)} %pad_maximum_fusion.1.refs_4_), channel_id=1, source_target_pairs={{0,384},{16,144},{32,416},{48,176},{64,448},{80,208},{96,480},{112... | collective-permute-start | bytes 1572872 | tf_op jit(solution)/shard_map/ppermute | solution.py:44
  39.6 157.7 %all-gather.6.cloned.1.call-start = ((), (), s32[]{:S(2)}) async-start(), calls=%async_computation.9 | async-start | bytes 2228224 | tf_op jit(solution)/shard_map/all_gather | solution.py:334
  39.6 5.5 %collective-permute-start.5 = (bf16[256,1024]{1,0:T(8,128)(2,1)S(1)}, bf16[256,1024]{1,0:T(8,128)(2,1)S(1)}, u32[]{:S(2)}, u32[]{:S(2)}) collective-permute-start(bf16[256,1024]{1,0:T(8,128)(2,1)S(1)} %collective-permute-done.2.refs_1_), channel_id=1, source_target_pairs={{0,16},{16,0},{32,48},{48,32},{64,80},{80,64},{96,112},{112,96},{1... | collective-permute-start | bytes 1572872 | tf_op jit(solution)/shard_map/ppermute | solution.py:32
  47.5 21.9 %collective-permute-start.6 = (f32[8,64,512]{2,1,0:T(8,128)S(1)}, f32[8,64,512]{2,1,0:T(8,128)S(1)}, u32[]{:S(2)}, u32[]{:S(2)}) collective-permute-start(f32[8,64,512]{2,1,0:T(8,128)S(1)} %get-tuple-element.32), channel_id=1, source_target_pairs={{0,1},{1,0},{2,3},{3,2},{4,5},{5,4},{6,7},{7,6},{8,9},{9,8},{10,11... | collective-permute-start | bytes 3145736 | tf_op jit(solution)/shard_map/ppermute | solution.py:52
  69.5 9.2 %collective-permute-start.7 = (f32[64,512]{1,0:T(8,128)S(1)}, f32[64,512]{1,0:T(8,128)S(1)}, u32[]{:S(2)}, u32[]{:S(2)}) collective-permute-start(f32[64,512]{1,0:T(8,128)S(1)} %get-tuple-element.34), channel_id=1, source_target_pairs={{0,2},{1,3},{2,4},{3,5},{4,6},{5,7},{6,8},{7,9},{8,10},{9,11},{10,... | collective-permute-start | bytes 393224 | tf_op jit(solution)/shard_map/ppermute | solution.py:52
  73.3 9.5 %collective-permute-start.11 = (f32[64,512]{1,0:T(8,128)S(1)}, f32[64,512]{1,0:T(8,128)S(1)}, u32[]{:S(2)}, u32[]{:S(2)}) collective-permute-start(f32[64,512]{1,0:T(8,128)S(1)} %get-tuple-element.36), channel_id=1, source_target_pairs={{0,14},{1,15},{2,0},{3,1},{4,2},{5,3},{6,4},{7,5},{8,6},{9,7},{10,... | collective-permute-start | bytes 393224 | tf_op jit(solution)/shard_map/ppermute | solution.py:52
  78.7 7.4 %collective-permute-start.8 = (f32[64,512]{1,0:T(8,128)S(1)}, f32[64,512]{1,0:T(8,128)S(1)}, u32[]{:S(2)}, u32[]{:S(2)}) collective-permute-start(f32[64,512]{1,0:T(8,128)S(1)} %bitcast_add_fusion.4), channel_id=1, source_target_pairs={{0,2},{1,3},{2,4},{3,5},{4,6},{5,7},{6,8},{7,9},{8,10},{9,11},{10,... | collective-permute-start | bytes 393224 | tf_op jit(solution)/shard_map/ppermute | solution.py:52
  82.8 8.0 %collective-permute-start.12 = (f32[64,512]{1,0:T(8,128)S(1)}, f32[64,512]{1,0:T(8,128)S(1)}, u32[]{:S(2)}, u32[]{:S(2)}) collective-permute-start(f32[64,512]{1,0:T(8,128)S(1)} %bitcast_add_fusion.1), channel_id=1, source_target_pairs={{0,14},{1,15},{2,0},{3,1},{4,2},{5,3},{6,4},{7,5},{8,6},{9,7},{10,... | collective-permute-start | bytes 393224 | tf_op jit(solution)/shard_map/ppermute | solution.py:52
  86.1 8.9 %collective-permute-start.9 = (f32[64,512]{1,0:T(8,128)S(1)}, f32[64,512]{1,0:T(8,128)S(1)}, u32[]{:S(2)}, u32[]{:S(2)}) collective-permute-start(f32[64,512]{1,0:T(8,128)S(1)} %bitcast_add_fusion.3), channel_id=1, source_target_pairs={{0,2},{1,3},{2,4},{3,5},{4,6},{5,7},{6,8},{7,9},{8,10},{9,11},{10,... | collective-permute-start | bytes 393224 | tf_op jit(solution)/shard_map/ppermute | solution.py:52
  90.9 9.9 %collective-permute-start.13 = (f32[64,512]{1,0:T(8,128)S(1)}, f32[64,512]{1,0:T(8,128)S(1)}, u32[]{:S(2)}, u32[]{:S(2)}) collective-permute-start(f32[64,512]{1,0:T(8,128)S(1)} %bitcast_add_fusion), channel_id=1, source_target_pairs={{0,14},{1,15},{2,0},{3,1},{4,2},{5,3},{6,4},{7,5},{8,6},{9,7},{10,... | collective-permute-start | bytes 393224 | tf_op jit(solution)/shard_map/ppermute | solution.py:52
  95.1 10.1 %collective-permute-start.10 = (f32[64,512]{1,0:T(8,128)S(1)}, f32[64,512]{1,0:T(8,128)S(1)}, u32[]{:S(2)}, u32[]{:S(2)}) collective-permute-start(f32[64,512]{1,0:T(8,128)S(1)} %bitcast_add_fusion.2), channel_id=1, source_target_pairs={{0,2},{1,3},{2,4},{3,5},{4,6},{5,7},{6,8},{7,9},{8,10},{9,11},{10,... | collective-permute-start | bytes 393224 | tf_op jit(solution)/shard_map/ppermute | solution.py:52
  197.3 1.6 copy-start
  224.0 15.7 %all-to-all-start.7 = ((f32[32,8,512]{2,1,0:T(8,128)}), f32[32,8,512]{2,1,0:T(8,128)S(1)}, u32[]{:S(2)}, u32[]{:S(2)}) async-start(f32[32,8,512]{2,1,0:T(8,128)} %get-tuple-element.42), calls=%async_computation.7 | async-start | bytes 1048576 | tf_op jit(solution)/shard_map/all_to_all | solution.py:400
Sparse Core Ops, SparseCore 0:
  39.7 70.6 all-gather.3
  116.7 71.3 all-gather.5

commit v8 on v7

--- a/solution.py
+++ b/solution.py
@@ -67,7 +67,7 @@
 
 def partial_kernel(scale, place_ref, *refs):
     here, there, ys = refs[:2], refs[2:4], refs[4:6]
-    keep, give, x_all, y_all, y_squares, chunks = refs[6:]
+    keep, give, y_all, x_all, y_squares, chunks = refs[6:]
     rows = here[0].shape[0] // 2
     depth = chunks.shape[0]
     high = rows // depth
@@ -109,15 +109,9 @@
         give[k] = chunks[depth // 2 + k]
 
 
-def pair_kernel(keep, got, own, ahead, back, ahead_rest, back_rest):
-    own[...] = keep[0] + got[0]
-    middle = keep.shape[0] // 2
-    ahead[...] = keep[middle] + got[middle]
-    back[...] = keep[middle + 1] + got[middle + 1]
-    for k in range(1, middle):
-        ahead_rest[middle - 1 - k] = keep[k] + got[k]
-    for k in range(middle + 2, keep.shape[0]):
-        back_rest[k - middle - 2] = keep[k] + got[k]
+def pair_kernel(keep, got, *outs):
+    for k, out in enumerate(outs):
+        out[...] = keep[k] + got[k]
 
 
 def joined(parts):
@@ -239,9 +233,11 @@
     half_steps(log_weight, a_ref, v, u_ref, l_ref)
 
 
-def target_kernel(log_weight, unit, steps, a_ref, u_ref, parts_ref, y_ref, out_ref, f_ref, g_ref, total, mass):
+def target_kernel(
+    log_weight, unit, steps, place_ref, a_ref, u_ref, parts_ref, y_ref, out_ref, f_ref, g_ref, total, mass, v_ref
+):
     step = pl.program_id(0)
-    lines = g_ref.shape[0] // steps
+    lines = v_ref.shape[0] // steps
 
     @pl.when(step == 0)
     def _():
@@ -249,18 +245,22 @@
         mass[...] = jnp.zeros_like(mass)
         u = u_ref[...]
         f_ref[...] = unit * jnp.sum(jnp.where(on_diagonal(u.shape[0]), u, 0.0), axis=0, keepdims=True)
-        g_ref[...] = log_weight - joined(parts_ref[...])
-
-    v = jnp.concatenate([g_ref[pl.ds(step * lines + k, 1), :] for k in range(lines)], axis=1)
+        v_ref[...] = log_weight - joined(parts_ref[...])
+        share = g_ref.shape[1]
+        z = place_ref[0]
+        line = v_ref[pl.ds(z // 2, 1), :]
+        g_ref[...] = unit * jnp.where(lax.rem(z, 2) == 0, line[:, :share], line[:, share:])
+
+    v = jnp.concatenate([v_ref[pl.ds(step * lines + k, 1), :] for k in range(lines)], axis=1)
     u = u_ref[:, :1]
     plan = jnp.exp2((u - log_weight + v) + a_ref[...]).astype(jnp.bfloat16)
     mass[...] += jnp.sum(plan.astype(jnp.float32), axis=1, keepdims=True)
-    total[...] += jnp.dot(plan, y_ref[...], preferred_element_type=jnp.float32)
+    y = y_ref[...].reshape(plan.shape[1], y_ref.shape[2])
+    total[...] += jnp.dot(plan, y, preferred_element_type=jnp.float32)
 
     @pl.when(step == steps - 1)
     def _():
         out_ref[...] = (total[...] / mass[...]).astype(out_ref.dtype)
-        g_ref[...] = unit * g_ref[...]
 
 
 def on_device(noise_rows, data_rows):
@@ -284,50 +284,43 @@
     y_near = jnp.concatenate([data_rows, swap_y(data_rows, FIRST)], axis=0)
     x_near, y_near = lax.optimization_barrier((x_near, y_near))
     x_far, y_far = swap_x(x_near, SECOND), swap_y(y_near, SECOND)
-    x_far, y_far, x_there, late_rows = lax.optimization_barrier(
-        (x_far, y_far, to_other_core(x_near), data_rows)
-    )
-    everything = lax.all_gather(late_rows, "noise", axis=0, tiled=True)
+    x_far, y_far, x_there = lax.optimization_barrier((x_far, y_far, to_other_core(x_near)))
     tall, wide = group * rows, YS * rows
     half = depth // 2
-    middle = half // 2
     chunk = (tall // depth, wide)
-    keep, give = pl.pallas_call(
+    keep, give, y_all = pl.pallas_call(
         functools.partial(partial_kernel, LOG2E / (epsilon * D)),
-        out_shape=[jax.ShapeDtypeStruct((half,) + chunk, f32)] * 2,
+        out_shape=[jax.ShapeDtypeStruct((half,) + chunk, f32)] * 2
+        + [jax.ShapeDtypeStruct((wide, features), jnp.bfloat16)],
         in_specs=[SMEM] + [VMEM] * 6,
-        out_specs=[VMEM] * 2,
+        out_specs=[VMEM] * 3,
         scratch_shapes=[
             pltpu.VMEM((group * rows, features), jnp.bfloat16),
-            pltpu.VMEM((YS * rows, features), jnp.bfloat16),
             pltpu.VMEM((1, wide), f32),
             pltpu.VMEM((depth,) + chunk, f32),
         ],
         compiler_params=PARAMS,
     )(place, x_near, x_far, x_there, to_other_core(x_far), y_near, y_far)
 
+    everything = lax.all_gather(y_all, "noise", axis_index_groups=x_groups)
+    everything = everything.reshape(group, YS, rows, features)
+
     got = send_z(give, z_partner)
-    own, ahead, back, ahead_rest, back_rest = pl.pallas_call(
+    sums = pl.pallas_call(
         pair_kernel,
-        out_shape=[
-            jax.ShapeDtypeStruct(chunk, f32),
-            jax.ShapeDtypeStruct(chunk, f32),
-            jax.ShapeDtypeStruct(chunk, f32),
-            jax.ShapeDtypeStruct((middle - 1,) + chunk, f32),
-            jax.ShapeDtypeStruct((middle - 2,) + chunk, f32),
-        ],
+        out_shape=[jax.ShapeDtypeStruct(chunk, f32)] * half,
         in_specs=[VMEM] * 2,
-        out_specs=[VMEM] * 5,
+        out_specs=[VMEM] * half,
         compiler_params=PARAMS,
     )(keep, got)
-    for step in range(middle):
-        ahead = send_z(ahead, lambda z, c: z + 2 if c == 0 else z - 2)
-        if step < middle - 1:
-            ahead = ahead + ahead_rest[step]
-            back = send_z(back, lambda z, c: z - 2 if c == 0 else z + 2)
-            if step < middle - 2:
-                back = back + back_rest[step]
-    own = own + ahead + back
+
+    def ahead(value, k):
+        return send_z(value, lambda z, c: z + 2 * k if c == 0 else z - 2 * k)
+
+    back = sums[6] + ahead(sums[4], -2) + ahead(sums[5], -1)
+    fore = sums[2] + ahead(sums[3], 1)
+    near = sums[0] + ahead(sums[7], -1) + ahead(sums[1], 1)
+    own = near + ahead(back, -2) + ahead(fore, 2)
 
     pieces = swap(own.reshape(group, rows // depth, wide), x_groups)
     everything, pieces = lax.optimization_barrier((everything, pieces))
@@ -399,37 +392,35 @@
             )(a, part)
         part = lax.all_to_all(part, "noise", 0, 0, tiled=True)
 
-    steps = 4
+    steps = YS
     targets, noise_potential, data_potential = pl.pallas_call(
         functools.partial(target_kernel, log_weight, epsilon / LOG2E, steps),
         grid=(steps,),
         out_shape=[
             jax.ShapeDtypeStruct((rows, features), jnp.bfloat16),
             jax.ShapeDtypeStruct((1, rows), f32),
-            jax.ShapeDtypeStruct((high, block), f32),
+            jax.ShapeDtypeStruct((1, block // 2), f32),
         ],
         in_specs=[
+            SMEM,
             pl.BlockSpec((rows, tokens // steps), lambda k: (0, k)),
             pl.BlockSpec((rows, rows), lambda k: (0, 0)),
             pl.BlockSpec((copies, high, block), lambda k: (0, 0, 0)),
-            pl.BlockSpec((tokens // steps, features), lambda k: (k, 0)),
+            pl.BlockSpec((group, None, rows, features), lambda k: (0, k, 0, 0)),
         ],
         out_specs=[
             pl.BlockSpec((rows, features), lambda k: (0, 0)),
             pl.BlockSpec((1, rows), lambda k: (0, 0)),
-            pl.BlockSpec((high, block), lambda k: (0, 0)),
+            pl.BlockSpec((1, block // 2), lambda k: (0, 0)),
         ],
         scratch_shapes=[
             pltpu.VMEM((rows, features), f32),
             pltpu.VMEM((rows, 1), f32),
+            pltpu.VMEM((high, block), f32),
         ],
         compiler_params=PARAMS,
-    )(a, u, part, everything)
-    share = tokens // depth
-    data_potential = lax.dynamic_slice(
-        data_potential, (z * share // block, z * share % block), (1, share)
-    )
-    return targets, noise_potential.reshape(rows), data_potential.reshape(share)
+    )(place, a, u, part, everything)
+    return targets, noise_potential.reshape(rows), data_potential.reshape(block // 2)
 
 
 def solution(mesh):

time: 254 us -> 255 us (level)
  waiting for transfers between devices: 52 us -> 31.7 us
  blocking collectives: 110 us -> 119 us
  starting transfers between devices: 56.8 us -> 64.8 us
  local copies, waits for them, and re-layouts: 2.23 us -> 6.29 us
    all_to_all x1 -> x2, blocking collectives: 19.1 us -> 34.4 us  [on_device(): part = lax.all_to_all(part, 'noise', 0, 0, tiled=True)]
    all_to_all x1 -> x0, waiting for transfers between devices: 11.6 us -> none  [on_device(): part = lax.all_to_all(part, 'noise', 0, 0, tiled=True)]
    ppermute x8, starting transfers between devices: 29.7 us -> 40.3 us  [send_z(): return lax.ppermute(value, ('noise', 'dp'), pairs)]
    all_to_all x2, blocking collectives: 54.1 us -> 46 us  [on_device(): lax.all_to_all(part, ('noise', 'dp'), 0, 0, axis_index_groups=z_groups, t...]
    ppermute x2, waiting for transfers between devices: 10.3 us -> 2.96 us  [swap_y(): lax.ppermute(value, 'noise', noise_pairs(lambda y, x, c: (y ^ by[c], x, c)))]
    ppermute x8, waiting for transfers between devices: 27.7 us -> 21.2 us  [send_z(): return lax.ppermute(value, ('noise', 'dp'), pairs)]
    ppermute x2, waiting for transfers between devices: 1 us -> 6.83 us  [swap_x(): lax.ppermute(value, 'noise', noise_pairs(lambda y, x, c: (y, x ^ by[c], c)))]
    unnamed x2 -> x12, local copies, waits for them, and re-layouts: 1.59 us -> 6.29 us
  transfers between devices with their start and end apart: 17 -> 16, of which waited for: 13 -> 7; matrix products, arithmetic and copies ran while one was open for 0% -> 0% of each run, Pallas kernels for 1% -> 0%
where the time goes in v8:
time: 255 us; the launch traced here: 254 us
  blocking collectives  119 us (47%)
  starting transfers between devices  64.8 us (25%)
  waiting for transfers between devices  31.7 us (12%)
  Pallas kernels  15.6 us (6%)
  between operations  14.3 us (6%)
  local copies, waits for them, and re-layouts  6.29 us (2%)
    all_to_all x2, blocking collectives, on_device(): lax.all_to_all(part, ('noise', 'dp'), 0, 0, axis_index_groups=z_groups, t...  46 us
    ppermute x8, starting transfers between devices, send_z(): return lax.ppermute(value, ('noise', 'dp'), pairs)  40.3 us
    all_to_all x4, blocking collectives, swap(): lax.all_to_all(value, 'noise', 0, 0, axis_index_groups=groups, tiled=True)  38.7 us
    all_to_all x2, blocking collectives, on_device(): part = lax.all_to_all(part, 'noise', 0, 0, tiled=True)  34.4 us
    ppermute x8, waiting for transfers between devices, send_z(): return lax.ppermute(value, ('noise', 'dp'), pairs)  21.2 us
    ppermute x2, starting transfers between devices, swap_x(): lax.ppermute(value, 'noise', noise_pairs(lambda y, x, c: (y, x ^ by[c], c)))  8.86 us
    ppermute x2, starting transfers between devices, to_other_core(): lax.ppermute(value, 'noise', noise_pairs(lambda y, x, c: (y, x, 1 - c)))  8.76 us
    ppermute x2, starting transfers between devices, swap_y(): lax.ppermute(value, 'noise', noise_pairs(lambda y, x, c: (y ^ by[c], x, c)))  6.86 us
  transfers between devices with their start and end apart: 16, of which 7 were waited for; matrix products, arithmetic and copies ran while one was open for 0% of the time, Pallas kernels for 0%

profile of v8, /device:TPU:1, one launch (start us, length us, event | category | flops | bytes accessed | tf_op | source)
XLA Modules:
  0.0 253.9 jit_solution(17137093443801182259)
XLA Ops:
  7.2 0.0 all-gather.5.cloned.1.call-start
  7.2 5.2 %collective-permute-start = (bf16[128,1024]{1,0:T(8,128)(2,1)}, bf16[128,1024]{1,0:T(8,128)(2,1)S(1)}, u32[]{:S(2)}, u32[]{:S(2)}) collective-permute-start(bf16[128,1024]{1,0:T(8,128)(2,1)} %param.2), channel_id=1, source_target_pairs={{0,32},{16,112},{32,0},{48,80},{64,96},{80,48},{96,64},{112,16},{1... | collective-permute-start | bytes 786440 | tf_op jit(solution)/shard_map/ppermute | solution.py:40
  12.4 4.6 %collective-permute-start.1 = (bf16[128,1024]{1,0:T(8,128)(2,1)}, bf16[128,1024]{1,0:T(8,128)(2,1)S(1)}, u32[]{:S(2)}, u32[]{:S(2)}) collective-permute-start(bf16[128,1024]{1,0:T(8,128)(2,1)} %param.3), channel_id=1, source_target_pairs={{0,128},{16,400},{32,160},{48,432},{64,192},{80,464},{96,224},{112... | collective-permute-start | bytes 786440 | tf_op jit(solution)/shard_map/ppermute | solution.py:44
  17.1 0.0 collective-permute-done
  17.1 1.0 pad_maximum_fusion.refs_0_
  18.1 3.0 %collective-permute-done.1 = bf16[128,1024]{1,0:T(8,128)(2,1)S(1)} collective-permute-done((bf16[128,1024]{1,0:T(8,128)(2,1)}, bf16[128,1024]{1,0:T(8,128)(2,1)S(1)}, u32[]{:S(2)}, u32[]{:S(2)}) %collective-permute-start.1) | collective-permute-done | bytes 262176 | tf_op jit(solution)/shard_map/ppermute | solution.py:44
  21.0 1.0 pad_maximum_fusion.1.refs_4_
  22.0 2.2 collective-permute-start.3
  24.3 5.1 %collective-permute-start.4 = (bf16[256,1024]{1,0:T(8,128)(2,1)S(1)}, bf16[256,1024]{1,0:T(8,128)(2,1)S(1)}, u32[]{:S(2)}, u32[]{:S(2)}) collective-permute-start(bf16[256,1024]{1,0:T(8,128)(2,1)S(1)} %pad_maximum_fusion.refs_0_), channel_id=1, source_target_pairs={{0,16},{16,0},{32,48},{48,32},{64,80},{80,64},{96,112},{112,96},{1... | collective-permute-start | bytes 1572872 | tf_op jit(solution)/shard_map/ppermute | solution.py:32
  29.3 3.6 %collective-permute-start.2 = (bf16[256,1024]{1,0:T(8,128)(2,1)S(1)}, bf16[256,1024]{1,0:T(8,128)(2,1)S(1)}, u32[]{:S(2)}, u32[]{:S(2)}) collective-permute-start(bf16[256,1024]{1,0:T(8,128)(2,1)S(1)} %pad_maximum_fusion.refs_0_), channel_id=1, source_target_pairs={{0,96},{16,48},{32,64},{48,16},{64,32},{80,112},{96,0},{112,80},{1... | collective-permute-start | bytes 1572872 | tf_op jit(solution)/shard_map/ppermute | solution.py:40
  33.0 0.0 collective-permute-done.3.refs_5_
  33.0 0.0 collective-permute-done.4.refs_2_
  33.0 6.8 %collective-permute-done.2.refs_1_ = bf16[256,1024]{1,0:T(8,128)(2,1)S(1)} collective-permute-done((bf16[256,1024]{1,0:T(8,128)(2,1)S(1)}, bf16[256,1024]{1,0:T(8,128)(2,1)S(1)}, u32[]{:S(2)}, u32[]{:S(2)}) %collective-permute-start.2) | collective-permute-done | bytes 524320 | tf_op jit(solution)/shard_map/ppermute | solution.py:40
  39.8 3.7 %collective-permute-start.5 = (bf16[256,1024]{1,0:T(8,128)(2,1)S(1)}, bf16[256,1024]{1,0:T(8,128)(2,1)S(1)}, u32[]{:S(2)}, u32[]{:S(2)}) collective-permute-start(bf16[256,1024]{1,0:T(8,128)(2,1)S(1)} %collective-permute-done.2.refs_1_), channel_id=1, source_target_pairs={{0,16},{16,0},{32,48},{48,32},{64,80},{80,64},{96,112},{112,96},{1... | collective-permute-start | bytes 1572872 | tf_op jit(solution)/shard_map/ppermute | solution.py:32
  43.5 0.0 copy-start.1
  43.5 0.8 copy-done.1
  44.4 0.1 pad_add_fusion.place_ref
  44.4 0.6 collective-permute-done.5.refs_3_
  45.0 0.0 copy-start.3
  45.0 0.8 copy-done.3
  45.8 0.0 copy-start.2
  45.9 1.0 copy-done.2
  46.9 0.0 copy-start.4
  46.9 1.0 copy-done.4
  47.9 3.2 %shard_map.49 = (f32[8,64,512]{2,1,0:T(8,128)S(1)}, f32[8,64,512]{2,1,0:T(8,128)S(1)}, bf16[512,1024]{1,0:T(8,128)(2,1)}) custom-call(s32[4]{0:T(128)S(1)} %pad_add_fusion.place_ref, bf16[256,1024]{1,0:T(8,128)(2,1)S(1)} %pad_maximum_fusion.refs_0_, bf16[256,1024]{1,0:T(8,128)(2,1)S(1)} %copy-done.2, bf16[256,1024]{1,0:T(8,128)(2,1)S(1)} %collective-permute-done.4.refs_2_, ...), custom_call_target="tpu_custom_call" | custom-call | tf_op jit(solution)/shard_map/pallas_call | solution.py:291
  51.2 0.0 copy-start.5
  51.2 1.0 copy-done.5
  52.2 0.0 all-gather.5.cloned.1.call-update
  52.2 0.0 all-gather.7.cloned.1.call-start
  52.2 10.2 %collective-permute-start.6 = (f32[8,64,512]{2,1,0:T(8,128)}, f32[8,64,512]{2,1,0:T(8,128)S(1)}, u32[]{:S(2)}, u32[]{:S(2)}) collective-permute-start(f32[8,64,512]{2,1,0:T(8,128)} %copy-done.5), channel_id=1, source_target_pairs={{0,1},{1,0},{2,3},{3,2},{4,5},{5,4},{6,7},{7,6},{8,9},{9,8},{10,11... | collective-permute-start | bytes 3145736 | tf_op jit(solution)/shard_map/ppermute | solution.py:52
  62.5 12.8 %collective-permute-done.6.got = f32[8,64,512]{2,1,0:T(8,128)S(1)} collective-permute-done((f32[8,64,512]{2,1,0:T(8,128)}, f32[8,64,512]{2,1,0:T(8,128)S(1)}, u32[]{:S(2)}, u32[]{:S(2)}) %collective-permute-start.6) | collective-permute-done | bytes 1048608 | tf_op jit(solution)/shard_map/ppermute | solution.py:52
  75.3 0.1 shard_map.50
  75.4 1.9 collective-permute-start.9
  77.3 3.9 %collective-permute-start.10 = (f32[64,512]{1,0:T(8,128)S(1)}, f32[64,512]{1,0:T(8,128)S(1)}, u32[]{:S(2)}, u32[]{:S(2)}) collective-permute-start(f32[64,512]{1,0:T(8,128)S(1)} %get-tuple-element.41), channel_id=1, source_target_pairs={{0,14},{1,15},{2,0},{3,1},{4,2},{5,3},{6,4},{7,5},{8,6},{9,7},{10,... | collective-permute-start | bytes 393224 | tf_op jit(solution)/shard_map/ppermute | solution.py:52
  81.2 7.0 %collective-permute-start.7 = (f32[64,512]{1,0:T(8,128)S(1)}, f32[64,512]{1,0:T(8,128)S(1)}, u32[]{:S(2)}, u32[]{:S(2)}) collective-permute-start(f32[64,512]{1,0:T(8,128)S(1)} %get-tuple-element.37), channel_id=1, source_target_pairs={{0,14},{1,15},{2,0},{3,1},{4,2},{5,3},{6,4},{7,5},{8,6},{9,7},{10,... | collective-permute-start | bytes 393224 | tf_op jit(solution)/shard_map/ppermute | solution.py:52
  88.3 1.9 collective-permute-start.8
  90.2 1.9 collective-permute-start.12
  92.1 0.0 collective-permute-done.9
  92.1 0.0 collective-permute-done.10
  92.2 7.5 %collective-permute-start.11 = (f32[64,512]{1,0:T(8,128)S(1)}, f32[64,512]{1,0:T(8,128)S(1)}, u32[]{:S(2)}, u32[]{:S(2)}) collective-permute-start(f32[64,512]{1,0:T(8,128)S(1)} %add_add_fusion.1), channel_id=1, source_target_pairs={{0,12},{1,13},{2,14},{3,15},{4,0},{5,1},{6,2},{7,3},{8,4},{9,5},{1... | collective-permute-start | bytes 393224 | tf_op jit(solution)/shard_map/ppermute | solution.py:52
  99.7 0.8 collective-permute-done.12
  100.6 5.8 %collective-permute-start.13 = (f32[64,512]{1,0:T(8,128)S(1)}, f32[64,512]{1,0:T(8,128)S(1)}, u32[]{:S(2)}, u32[]{:S(2)}) collective-permute-start(f32[64,512]{1,0:T(8,128)S(1)} %add.37), channel_id=1, source_target_pairs={{0,4},{1,5},{2,6},{3,7},{4,8},{5,9},{6,10},{7,11},{8,12},{9,13},{1... | collective-permute-start | bytes 393224 | tf_op jit(solution)/shard_map/ppermute | solution.py:52
  106.4 0.0 collective-permute-done.7
  106.4 0.0 collective-permute-done.8
  106.4 2.5 collective-permute-done.11
  108.9 5.1 %collective-permute-done.13 = f32[64,512]{1,0:T(8,128)S(1)} collective-permute-done((f32[64,512]{1,0:T(8,128)S(1)}, f32[64,512]{1,0:T(8,128)S(1)}, u32[]{:S(2)}, u32[]{:S(2)}) %collective-permute-start.13) | collective-permute-done | bytes 131104 | tf_op jit(solution)/shard_map/ppermute | solution.py:52
  114.1 13.0 %all_to_all.40 = f32[8,8,512]{2,1,0:T(8,128)} all-to-all(f32[8,8,512]{2,1,0:T(8,128)S(1)} %bitcast.9), channel_id=1, replica_groups={{0,16,32,48,64,80,96,112},{128,144,160,176,192,208,224,240},{256,272,28..., dimensions={0} | all-to-all | bytes 262144 | tf_op jit(solution)/shard_map/all_to_all | solution.py:281
  127.1 0.0 all-gather.7.cloned.1.call-update
  127.1 0.2 shard_map.51
  127.3 7.8 %all_to_all.41.parts_ref = f32[8,1,64]{2,1,0:T(1,128)S(1)} all-to-all(f32[8,1,64]{2,1,0:T(1,128)S(1)} %shard_map.51), channel_id=1, replica_groups={{0,16,32,48,64,80,96,112},{128,144,160,176,192,208,224,240},{256,272,28..., dimensions={0} | all-to-all | bytes 4096 | tf_op jit(solution)/shard_map/all_to_all | solution.py:281
  135.1 0.2 shard_map.52
  135.3 23.7 %all_to_all.42.parts_ref = f32[64,4,128]{2,1,0:T(4,128)S(1)} all-to-all(f32[64,4,128]{2,1,0:T(4,128)S(1)} %shard_map.52), channel_id=1, replica_groups={{0,1,2,3,4,5,6,7,8,9,10,11,12,13,14,15,128,129,130,131,132,133,134,135,..., dimensions={0} | all-to-all | bytes 262144 | tf_op jit(solution)/shard_map/all_to_all | solution.py:359
  159.0 0.3 shard_map.53
  159.3 9.2 %all_to_all.43.parts_ref = f32[8,1,64]{2,1,0:T(1,128)S(1)} all-to-all(f32[8,1,64]{2,1,0:T(1,128)S(1)} %shard_map.53), channel_id=1, replica_groups={{0,16,32,48,64,80,96,112},{128,144,160,176,192,208,224,240},{256,272,28..., dimensions={0} | all-to-all | bytes 4096 | tf_op jit(solution)/shard_map/all_to_all | solution.py:281
  168.5 0.2 shard_map.54
  168.7 22.3 %all_to_all.44.parts_ref = f32[64,4,128]{2,1,0:T(4,128)S(1)} all-to-all(f32[64,4,128]{2,1,0:T(4,128)S(1)} %shard_map.54), channel_id=1, replica_groups={{0,1,2,3,4,5,6,7,8,9,10,11,12,13,14,15,128,129,130,131,132,133,134,135,..., dimensions={0} | all-to-all | bytes 262144 | tf_op jit(solution)/shard_map/all_to_all | solution.py:359
  190.9 0.1 shard_map.55
  191.0 8.7 %all_to_all.45.parts_ref = f32[8,4,128]{2,1,0:T(4,128)S(1)} all-to-all(f32[8,4,128]{2,1,0:T(4,128)S(1)} %shard_map.55), channel_id=1, replica_groups={{0,16,32,48,64,80,96,112},{128,144,160,176,192,208,224,240},{256,272,28..., dimensions={0} | all-to-all | bytes 32768 | tf_op jit(solution)/shard_map/all_to_all | solution.py:281
  199.8 1.6 copy-done
  201.3 2.6 %shard_map.56 = (f32[128,4096]{1,0:T(8,128)S(1)}, f32[128,128]{1,0:T(8,128)}, f32[32,8,512]{2,1,0:T(8,128)S(1)}) custom-call(f32[16,8,8,512]{3,2,1,0:T(8,128)S(1)} %bitcast.10, f32[8,4,128]{2,1,0:T(4,128)S(1)} %all_to_all.45.parts_ref), custom_call_target="tpu_custom_call" | custom-call | tf_op jit(solution)/shard_map/pallas_call | solution.py:378
  204.0 19.2 %all_to_all.46.parts_ref = f32[32,8,512]{2,1,0:T(8,128)S(1)} all-to-all(f32[32,8,512]{2,1,0:T(8,128)S(1)} %get-tuple-element.46), channel_id=1, replica_groups=mesh['noise'=32,'dp'=16] {'noise'}, dimensions={0} | all-to-all | bytes 1048576 | tf_op jit(solution)/shard_map/all_to_all | solution.py:393
  223.2 2.5 shard_map.57
  225.6 15.2 %all_to_all.47.parts_ref = f32[32,8,512]{2,1,0:T(8,128)S(1)} all-to-all(f32[32,8,512]{2,1,0:T(8,128)S(1)} %get-tuple-element.48), channel_id=1, replica_groups=mesh['noise'=32,'dp'=16] {'noise'}, dimensions={0} | all-to-all | bytes 1048576 | tf_op jit(solution)/shard_map/all_to_all | solution.py:393
  240.9 6.2 %shard_map.58 = (bf16[128,1024]{1,0:T(8,128)(2,1)}, f32[1,128]{1,0:T(1,128)}, f32[1,256]{1,0:T(1,128)}) custom-call(s32[4]{0:T(128)S(1)} %pad_add_fusion.place_ref, f32[128,4096]{1,0:T(8,128)S(1)} %get-tuple-element.45.a_ref, f32[128,128]{1,0:T(8,128)S(1)} %get-tuple-element.47.u_ref, f32[32,8,512]{2,1,0:T(8,128)S(1)} %all_to_all.47.parts_ref, ...), custom_call_target="tpu_custom_call" | custom-call | tf_op jit(solution)/shard_map/pallas_call | solution.py:396
  (6 shorter events, 0.1 us)
Async XLA Ops:
  7.2 119.9 %all-gather.5.cloned.1.call-start = ((), (), s32[]{:S(2)}) async-start(), calls=%async_computation.8 | async-start | bytes 9437184 | tf_op jit(solution)/shard_map/all_gather | solution.py:305
  7.2 9.9 %collective-permute-start = (bf16[128,1024]{1,0:T(8,128)(2,1)}, bf16[128,1024]{1,0:T(8,128)(2,1)S(1)}, u32[]{:S(2)}, u32[]{:S(2)}) collective-permute-start(bf16[128,1024]{1,0:T(8,128)(2,1)} %param.2), channel_id=1, source_target_pairs={{0,32},{16,112},{32,0},{48,80},{64,96},{80,48},{96,64},{112,16},{1... | collective-permute-start | bytes 786440 | tf_op jit(solution)/shard_map/ppermute | solution.py:40
  12.4 8.6 %collective-permute-start.1 = (bf16[128,1024]{1,0:T(8,128)(2,1)}, bf16[128,1024]{1,0:T(8,128)(2,1)S(1)}, u32[]{:S(2)}, u32[]{:S(2)}) collective-permute-start(bf16[128,1024]{1,0:T(8,128)(2,1)} %param.3), channel_id=1, source_target_pairs={{0,128},{16,400},{32,160},{48,432},{64,192},{80,464},{96,224},{112... | collective-permute-start | bytes 786440 | tf_op jit(solution)/shard_map/ppermute | solution.py:44
  22.0 10.9 %collective-permute-start.3 = (bf16[256,1024]{1,0:T(8,128)(2,1)S(1)}, bf16[256,1024]{1,0:T(8,128)(2,1)S(1)}, u32[]{:S(2)}, u32[]{:S(2)}) collective-permute-start(bf16[256,1024]{1,0:T(8,128)(2,1)S(1)} %pad_maximum_fusion.1.refs_4_), channel_id=1, source_target_pairs={{0,384},{16,144},{32,416},{48,176},{64,448},{80,208},{96,480},{112... | collective-permute-start | bytes 1572872 | tf_op jit(solution)/shard_map/ppermute | solution.py:44
  24.3 8.7 %collective-permute-start.4 = (bf16[256,1024]{1,0:T(8,128)(2,1)S(1)}, bf16[256,1024]{1,0:T(8,128)(2,1)S(1)}, u32[]{:S(2)}, u32[]{:S(2)}) collective-permute-start(bf16[256,1024]{1,0:T(8,128)(2,1)S(1)} %pad_maximum_fusion.refs_0_), channel_id=1, source_target_pairs={{0,16},{16,0},{32,48},{48,32},{64,80},{80,64},{96,112},{112,96},{1... | collective-permute-start | bytes 1572872 | tf_op jit(solution)/shard_map/ppermute | solution.py:32
  29.3 10.5 %collective-permute-start.2 = (bf16[256,1024]{1,0:T(8,128)(2,1)S(1)}, bf16[256,1024]{1,0:T(8,128)(2,1)S(1)}, u32[]{:S(2)}, u32[]{:S(2)}) collective-permute-start(bf16[256,1024]{1,0:T(8,128)(2,1)S(1)} %pad_maximum_fusion.refs_0_), channel_id=1, source_target_pairs={{0,96},{16,48},{32,64},{48,16},{64,32},{80,112},{96,0},{112,80},{1... | collective-permute-start | bytes 1572872 | tf_op jit(solution)/shard_map/ppermute | solution.py:40
  39.8 5.2 %collective-permute-start.5 = (bf16[256,1024]{1,0:T(8,128)(2,1)S(1)}, bf16[256,1024]{1,0:T(8,128)(2,1)S(1)}, u32[]{:S(2)}, u32[]{:S(2)}) collective-permute-start(bf16[256,1024]{1,0:T(8,128)(2,1)S(1)} %collective-permute-done.2.refs_1_), channel_id=1, source_target_pairs={{0,16},{16,0},{32,48},{48,32},{64,80},{80,64},{96,112},{112,96},{1... | collective-permute-start | bytes 1572872 | tf_op jit(solution)/shard_map/ppermute | solution.py:32
  43.5 0.8 copy-start.1
  45.0 0.8 copy-start.3
  45.8 1.0 copy-start.2
  46.9 1.0 copy-start.4
  51.2 1.0 copy-start.5
  52.2 147.6 %all-gather.7.cloned.1.call-start = ((), (), s32[]{:S(2)}) async-start(), calls=%async_computation.9 | async-start | bytes 2228224 | tf_op jit(solution)/shard_map/all_gather | solution.py:327
  52.2 23.0 %collective-permute-start.6 = (f32[8,64,512]{2,1,0:T(8,128)}, f32[8,64,512]{2,1,0:T(8,128)S(1)}, u32[]{:S(2)}, u32[]{:S(2)}) collective-permute-start(f32[8,64,512]{2,1,0:T(8,128)} %copy-done.5), channel_id=1, source_target_pairs={{0,1},{1,0},{2,3},{3,2},{4,5},{5,4},{6,7},{7,6},{8,9},{9,8},{10,11... | collective-permute-start | bytes 3145736 | tf_op jit(solution)/shard_map/ppermute | solution.py:52
  75.4 16.8 %collective-permute-start.9 = (f32[64,512]{1,0:T(8,128)S(1)}, f32[64,512]{1,0:T(8,128)S(1)}, u32[]{:S(2)}, u32[]{:S(2)}) collective-permute-start(f32[64,512]{1,0:T(8,128)S(1)} %get-tuple-element.40), channel_id=1, source_target_pairs={{0,12},{1,13},{2,14},{3,15},{4,0},{5,1},{6,2},{7,3},{8,4},{9,5},{1... | collective-permute-start | bytes 393224 | tf_op jit(solution)/shard_map/ppermute | solution.py:52
  77.3 14.8 %collective-permute-start.10 = (f32[64,512]{1,0:T(8,128)S(1)}, f32[64,512]{1,0:T(8,128)S(1)}, u32[]{:S(2)}, u32[]{:S(2)}) collective-permute-start(f32[64,512]{1,0:T(8,128)S(1)} %get-tuple-element.41), channel_id=1, source_target_pairs={{0,14},{1,15},{2,0},{3,1},{4,2},{5,3},{6,4},{7,5},{8,6},{9,7},{10,... | collective-permute-start | bytes 393224 | tf_op jit(solution)/shard_map/ppermute | solution.py:52
  81.2 25.1 %collective-permute-start.7 = (f32[64,512]{1,0:T(8,128)S(1)}, f32[64,512]{1,0:T(8,128)S(1)}, u32[]{:S(2)}, u32[]{:S(2)}) collective-permute-start(f32[64,512]{1,0:T(8,128)S(1)} %get-tuple-element.37), channel_id=1, source_target_pairs={{0,14},{1,15},{2,0},{3,1},{4,2},{5,3},{6,4},{7,5},{8,6},{9,7},{10,... | collective-permute-start | bytes 393224 | tf_op jit(solution)/shard_map/ppermute | solution.py:52
  88.3 18.1 %collective-permute-start.8 = (f32[64,512]{1,0:T(8,128)S(1)}, f32[64,512]{1,0:T(8,128)S(1)}, u32[]{:S(2)}, u32[]{:S(2)}) collective-permute-start(f32[64,512]{1,0:T(8,128)S(1)} %get-tuple-element.38), channel_id=1, source_target_pairs={{0,2},{1,3},{2,4},{3,5},{4,6},{5,7},{6,8},{7,9},{8,10},{9,11},{10,... | collective-permute-start | bytes 393224 | tf_op jit(solution)/shard_map/ppermute | solution.py:52
  90.2 10.4 %collective-permute-start.12 = (f32[64,512]{1,0:T(8,128)S(1)}, f32[64,512]{1,0:T(8,128)S(1)}, u32[]{:S(2)}, u32[]{:S(2)}) collective-permute-start(f32[64,512]{1,0:T(8,128)S(1)} %get-tuple-element.43), channel_id=1, source_target_pairs={{0,2},{1,3},{2,4},{3,5},{4,6},{5,7},{6,8},{7,9},{8,10},{9,11},{10,... | collective-permute-start | bytes 393224 | tf_op jit(solution)/shard_map/ppermute | solution.py:52
  92.2 16.7 %collective-permute-start.11 = (f32[64,512]{1,0:T(8,128)S(1)}, f32[64,512]{1,0:T(8,128)S(1)}, u32[]{:S(2)}, u32[]{:S(2)}) collective-permute-start(f32[64,512]{1,0:T(8,128)S(1)} %add_add_fusion.1), channel_id=1, source_target_pairs={{0,12},{1,13},{2,14},{3,15},{4,0},{5,1},{6,2},{7,3},{8,4},{9,5},{1... | collective-permute-start | bytes 393224 | tf_op jit(solution)/shard_map/ppermute | solution.py:52
  100.6 13.4 %collective-permute-start.13 = (f32[64,512]{1,0:T(8,128)S(1)}, f32[64,512]{1,0:T(8,128)S(1)}, u32[]{:S(2)}, u32[]{:S(2)}) collective-permute-start(f32[64,512]{1,0:T(8,128)S(1)} %add.37), channel_id=1, source_target_pairs={{0,4},{1,5},{2,6},{3,7},{4,8},{5,9},{6,10},{7,11},{8,12},{9,13},{1... | collective-permute-start | bytes 393224 | tf_op jit(solution)/shard_map/ppermute | solution.py:52
  199.8 1.6 copy-start
Sparse Core Ops, SparseCore 0:
  52.3 57.5 all-gather.4
  127.2 63.6 all-gather.6

commit v9 on v7

--- a/solution.py
+++ b/solution.py
@@ -208,13 +208,15 @@
             u = log_weight - (peak + jnp.log(total) * LOG2E)
             u_ref[at, :] = jnp.broadcast_to(u, (8, lanes))
 
+    u = jnp.concatenate([u_ref[...]] * 2, axis=1)
+    step = 2 * lanes
     for k in range(high):
-        for i in range(width // lanes):
-            at = pl.ds(k * width + i * lanes, lanes)
-            value = a_ref[:, at] + u_ref[...]
-            peak = jnp.max(value, axis=0, keepdims=True)
-            total = jnp.sum(jnp.exp2(value - peak), axis=0, keepdims=True)
-            l_ref[0, k : k + 1, i * lanes : (i + 1) * lanes] = peak + jnp.log(total) * LOG2E
+        for i in range(width // step):
+            at = k * width + i * step
+            value = (a_ref[:, at : at + step] + u).reshape(rows // 8, 8, step)
+            peak = jnp.max(jnp.max(value, axis=0), axis=0, keepdims=True)
+            total = jnp.sum(jnp.sum(jnp.exp2(value - peak), axis=0), axis=0, keepdims=True)
+            l_ref[0, k : k + 1, i * step : (i + 1) * step] = peak + jnp.log(total) * LOG2E
     whole = l_ref[0]
     for k in range(1, copies):
         l_ref[k] = whole
@@ -239,9 +241,11 @@
     half_steps(log_weight, a_ref, v, u_ref, l_ref)
 
 
-def target_kernel(log_weight, unit, steps, a_ref, u_ref, parts_ref, y_ref, out_ref, f_ref, g_ref, total, mass):
+def target_kernel(
+    log_weight, unit, steps, place_ref, a_ref, u_ref, parts_ref, y_ref, out_ref, f_ref, g_ref, total, mass, v_ref
+):
     step = pl.program_id(0)
-    lines = g_ref.shape[0] // steps
+    lines = v_ref.shape[0] // steps
 
     @pl.when(step == 0)
     def _():
@@ -249,9 +253,13 @@
         mass[...] = jnp.zeros_like(mass)
         u = u_ref[...]
         f_ref[...] = unit * jnp.sum(jnp.where(on_diagonal(u.shape[0]), u, 0.0), axis=0, keepdims=True)
-        g_ref[...] = log_weight - joined(parts_ref[...])
-
-    v = jnp.concatenate([g_ref[pl.ds(step * lines + k, 1), :] for k in range(lines)], axis=1)
+        v_ref[...] = log_weight - joined(parts_ref[...])
+        share = g_ref.shape[1]
+        z = place_ref[0]
+        line = v_ref[pl.ds(z // 2, 1), :]
+        g_ref[...] = unit * jnp.where(lax.rem(z, 2) == 0, line[:, :share], line[:, share:])
+
+    v = jnp.concatenate([v_ref[pl.ds(step * lines + k, 1), :] for k in range(lines)], axis=1)
     u = u_ref[:, :1]
     plan = jnp.exp2((u - log_weight + v) + a_ref[...]).astype(jnp.bfloat16)
     mass[...] += jnp.sum(plan.astype(jnp.float32), axis=1, keepdims=True)
@@ -260,7 +268,6 @@
     @pl.when(step == steps - 1)
     def _():
         out_ref[...] = (total[...] / mass[...]).astype(out_ref.dtype)
-        g_ref[...] = unit * g_ref[...]
 
 
 def on_device(noise_rows, data_rows):
@@ -284,8 +291,8 @@
     y_near = jnp.concatenate([data_rows, swap_y(data_rows, FIRST)], axis=0)
     x_near, y_near = lax.optimization_barrier((x_near, y_near))
     x_far, y_far = swap_x(x_near, SECOND), swap_y(y_near, SECOND)
-    x_far, y_far, x_there, late_rows = lax.optimization_barrier(
-        (x_far, y_far, to_other_core(x_near), data_rows)
+    x_there, x_far_there, y_far, late_rows = lax.optimization_barrier(
+        (to_other_core(x_near), to_other_core(x_far), y_far, data_rows)
     )
     everything = lax.all_gather(late_rows, "noise", axis=0, tiled=True)
     tall, wide = group * rows, YS * rows
@@ -304,7 +311,7 @@
             pltpu.VMEM((depth,) + chunk, f32),
         ],
         compiler_params=PARAMS,
-    )(place, x_near, x_far, x_there, to_other_core(x_far), y_near, y_far)
+    )(place, x_near, x_far, x_there, x_far_there, y_near, y_far)
 
     got = send_z(give, z_partner)
     own, ahead, back, ahead_rest, back_rest = pl.pallas_call(
@@ -406,9 +413,10 @@
         out_shape=[
             jax.ShapeDtypeStruct((rows, features), jnp.bfloat16),
             jax.ShapeDtypeStruct((1, rows), f32),
-            jax.ShapeDtypeStruct((high, block), f32),
+            jax.ShapeDtypeStruct((1, block // 2), f32),
         ],
         in_specs=[
+            SMEM,
             pl.BlockSpec((rows, tokens // steps), lambda k: (0, k)),
             pl.BlockSpec((rows, rows), lambda k: (0, 0)),
             pl.BlockSpec((copies, high, block), lambda k: (0, 0, 0)),
@@ -417,19 +425,16 @@
         out_specs=[
             pl.BlockSpec((rows, features), lambda k: (0, 0)),
             pl.BlockSpec((1, rows), lambda k: (0, 0)),
-            pl.BlockSpec((high, block), lambda k: (0, 0)),
+            pl.BlockSpec((1, block // 2), lambda k: (0, 0)),
         ],
         scratch_shapes=[
             pltpu.VMEM((rows, features), f32),
             pltpu.VMEM((rows, 1), f32),
+            pltpu.VMEM((high, block), f32),
         ],
         compiler_params=PARAMS,
-    )(a, u, part, everything)
-    share = tokens // depth
-    data_potential = lax.dynamic_slice(
-        data_potential, (z * share // block, z * share % block), (1, share)
-    )
-    return targets, noise_potential.reshape(rows), data_potential.reshape(share)
+    )(place, a, u, part, everything)
+    return targets, noise_potential.reshape(rows), data_potential.reshape(block // 2)
 
 
 def solution(mesh):

time: 254 us -> 251 us (0.988)
  waiting for transfers between devices: 52 us -> 28.6 us
  blocking collectives: 110 us -> 127 us
  starting transfers between devices: 56.8 us -> 61.1 us
    all_to_all x1 -> x2, blocking collectives: 19.1 us -> 34.6 us  [on_device(): part = lax.all_to_all(part, 'noise', 0, 0, tiled=True)]
    all_to_all x1 -> x0, waiting for transfers between devices: 11.6 us -> none  [on_device(): part = lax.all_to_all(part, 'noise', 0, 0, tiled=True)]
    ppermute x2, waiting for transfers between devices: 10.3 us -> 2.96 us  [swap_y(): lax.ppermute(value, 'noise', noise_pairs(lambda y, x, c: (y ^ by[c], x, c)))]
    ppermute x8, starting transfers between devices: 29.7 us -> 34.5 us  [send_z(): return lax.ppermute(value, ('noise', 'dp'), pairs)]
    ppermute x8, waiting for transfers between devices: 27.7 us -> 23.1 us  [send_z(): return lax.ppermute(value, ('noise', 'dp'), pairs)]
    all_to_all x1 -> x0, starting transfers between devices: 3.99 us -> none  [on_device(): part = lax.all_to_all(part, 'noise', 0, 0, tiled=True)]
    ppermute x2, starting transfers between devices: 9.35 us -> 12.8 us  [to_other_core(): lax.ppermute(value, 'noise', noise_pairs(lambda y, x, c: (y, x, 1 - c)))]
    all_to_all x2, blocking collectives: 54.1 us -> 56.7 us  [on_device(): lax.all_to_all(part, ('noise', 'dp'), 0, 0, axis_index_groups=z_groups, t...]
  transfers between devices with their start and end apart: 17 -> 16, of which waited for: 13 -> 9; matrix products, arithmetic and copies ran while one was open for 0% -> 0% of each run, Pallas kernels for 1% -> 1%
where the time goes in v9:
time: 251 us; the launch traced here: 250 us
  blocking collectives  127 us (51%)
  starting transfers between devices  61.1 us (24%)
  waiting for transfers between devices  28.6 us (11%)
  Pallas kernels  15.2 us (6%)
  between operations  14.3 us (6%)
    all_to_all x2, blocking collectives, on_device(): lax.all_to_all(part, ('noise', 'dp'), 0, 0, axis_index_groups=z_groups, t...  56.7 us
    all_to_all x4, blocking collectives, swap(): lax.all_to_all(value, 'noise', 0, 0, axis_index_groups=groups, tiled=True)  36.2 us
    all_to_all x2, blocking collectives, on_device(): part = lax.all_to_all(part, 'noise', 0, 0, tiled=True)  34.6 us
    ppermute x8, starting transfers between devices, send_z(): return lax.ppermute(value, ('noise', 'dp'), pairs)  34.5 us
    ppermute x8, waiting for transfers between devices, send_z(): return lax.ppermute(value, ('noise', 'dp'), pairs)  23.1 us
    ppermute x2, starting transfers between devices, to_other_core(): lax.ppermute(value, 'noise', noise_pairs(lambda y, x, c: (y, x, 1 - c)))  12.8 us
    ppermute x2, starting transfers between devices, swap_x(): lax.ppermute(value, 'noise', noise_pairs(lambda y, x, c: (y, x ^ by[c], c)))  7.14 us
    ppermute x2, starting transfers between devices, swap_y(): lax.ppermute(value, 'noise', noise_pairs(lambda y, x, c: (y ^ by[c], x, c)))  6.57 us
  transfers between devices with their start and end apart: 16, of which 9 were waited for; matrix products, arithmetic and copies ran while one was open for 0% of the time, Pallas kernels for 1%

profile of v9, /device:TPU:1, one launch (start us, length us, event | category | flops | bytes accessed | tf_op | source)
XLA Modules:
  0.0 250.3 jit_solution(16625306379823474250)
XLA Ops:
  7.2 0.0 all-gather.4.cloned.1.call-start
  7.2 5.2 %collective-permute-start = (bf16[128,1024]{1,0:T(8,128)(2,1)}, bf16[128,1024]{1,0:T(8,128)(2,1)S(1)}, u32[]{:S(2)}, u32[]{:S(2)}) collective-permute-start(bf16[128,1024]{1,0:T(8,128)(2,1)} %param.2), channel_id=1, source_target_pairs={{0,32},{16,112},{32,0},{48,80},{64,96},{80,48},{96,64},{112,16},{1... | collective-permute-start | bytes 786440 | tf_op jit(solution)/shard_map/ppermute | solution.py:40
  12.4 4.6 %collective-permute-start.1 = (bf16[128,1024]{1,0:T(8,128)(2,1)}, bf16[128,1024]{1,0:T(8,128)(2,1)S(1)}, u32[]{:S(2)}, u32[]{:S(2)}) collective-permute-start(bf16[128,1024]{1,0:T(8,128)(2,1)} %param.3), channel_id=1, source_target_pairs={{0,128},{16,400},{32,160},{48,432},{64,192},{80,464},{96,224},{112... | collective-permute-start | bytes 786440 | tf_op jit(solution)/shard_map/ppermute | solution.py:44
  17.1 0.0 collective-permute-done
  17.1 1.0 pad_maximum_fusion.refs_0_
  18.1 3.0 %collective-permute-done.1 = bf16[128,1024]{1,0:T(8,128)(2,1)S(1)} collective-permute-done((bf16[128,1024]{1,0:T(8,128)(2,1)}, bf16[128,1024]{1,0:T(8,128)(2,1)S(1)}, u32[]{:S(2)}, u32[]{:S(2)}) %collective-permute-start.1) | collective-permute-done | bytes 262176 | tf_op jit(solution)/shard_map/ppermute | solution.py:44
  21.0 1.0 pad_maximum_fusion.1.refs_4_
  22.0 1.9 collective-permute-start.3
  24.0 5.4 %collective-permute-start.2 = (bf16[256,1024]{1,0:T(8,128)(2,1)S(1)}, bf16[256,1024]{1,0:T(8,128)(2,1)S(1)}, u32[]{:S(2)}, u32[]{:S(2)}) collective-permute-start(bf16[256,1024]{1,0:T(8,128)(2,1)S(1)} %pad_maximum_fusion.refs_0_), channel_id=1, source_target_pairs={{0,16},{16,0},{32,48},{48,32},{64,80},{80,64},{96,112},{112,96},{1... | collective-permute-start | bytes 1572872 | tf_op jit(solution)/shard_map/ppermute | solution.py:32
  29.3 1.9 collective-permute-start.5
  31.3 1.0 collective-permute-done.3.refs_1_
  32.2 7.4 %collective-permute-start.4 = (bf16[256,1024]{1,0:T(8,128)(2,1)S(1)}, bf16[256,1024]{1,0:T(8,128)(2,1)S(1)}, u32[]{:S(2)}, u32[]{:S(2)}) collective-permute-start(bf16[256,1024]{1,0:T(8,128)(2,1)S(1)} %collective-permute-done.3.refs_1_), channel_id=1, source_target_pairs={{0,16},{16,0},{32,48},{48,32},{64,80},{80,64},{96,112},{112,96},{1... | collective-permute-start | bytes 1572872 | tf_op jit(solution)/shard_map/ppermute | solution.py:32
  39.7 0.0 collective-permute-done.2.refs_2_
  39.7 0.0 collective-permute-done.5.refs_5_
  39.7 1.5 collective-permute-done.4.refs_3_
  41.2 0.0 all-gather.4.cloned.1.call-update
  41.2 0.0 all-gather.6.cloned.1.call-start
  41.3 0.1 pad_add_fusion.place_ref
  41.4 2.3 shard_map.49
  43.7 7.7 %collective-permute-start.6 = (f32[8,64,512]{2,1,0:T(8,128)S(1)}, f32[8,64,512]{2,1,0:T(8,128)S(1)}, u32[]{:S(2)}, u32[]{:S(2)}) collective-permute-start(f32[8,64,512]{2,1,0:T(8,128)S(1)} %get-tuple-element.32), channel_id=1, source_target_pairs={{0,1},{1,0},{2,3},{3,2},{4,5},{5,4},{6,7},{7,6},{8,9},{9,8},{10,11... | collective-permute-start | bytes 3145736 | tf_op jit(solution)/shard_map/ppermute | solution.py:52
  51.4 12.2 %collective-permute-done.6.got = f32[8,64,512]{2,1,0:T(8,128)S(1)} collective-permute-done((f32[8,64,512]{2,1,0:T(8,128)S(1)}, f32[8,64,512]{2,1,0:T(8,128)S(1)}, u32[]{:S(2)}, u32[]{:S(2)}) %collective-permute-start.6) | collective-permute-done | bytes 1048608 | tf_op jit(solution)/shard_map/ppermute | solution.py:52
  63.6 0.1 shard_map.50
  63.7 4.1 %collective-permute-start.7 = (f32[64,512]{1,0:T(8,128)S(1)}, f32[64,512]{1,0:T(8,128)S(1)}, u32[]{:S(2)}, u32[]{:S(2)}) collective-permute-start(f32[64,512]{1,0:T(8,128)S(1)} %get-tuple-element.34), channel_id=1, source_target_pairs={{0,2},{1,3},{2,4},{3,5},{4,6},{5,7},{6,8},{7,9},{8,10},{9,11},{10,... | collective-permute-start | bytes 393224 | tf_op jit(solution)/shard_map/ppermute | solution.py:52
  67.8 2.1 collective-permute-start.11
  69.9 0.5 collective-permute-done.7
  70.4 5.3 %collective-permute-start.8 = (f32[64,512]{1,0:T(8,128)S(1)}, f32[64,512]{1,0:T(8,128)S(1)}, u32[]{:S(2)}, u32[]{:S(2)}) collective-permute-start(f32[64,512]{1,0:T(8,128)S(1)} %bitcast_add_fusion.4), channel_id=1, source_target_pairs={{0,2},{1,3},{2,4},{3,5},{4,6},{5,7},{6,8},{7,9},{8,10},{9,11},{10,... | collective-permute-start | bytes 393224 | tf_op jit(solution)/shard_map/ppermute | solution.py:52
  75.7 0.0 collective-permute-done.11
  75.8 1.9 collective-permute-start.12
  77.7 0.7 collective-permute-done.8
  78.4 5.6 %collective-permute-start.9 = (f32[64,512]{1,0:T(8,128)S(1)}, f32[64,512]{1,0:T(8,128)S(1)}, u32[]{:S(2)}, u32[]{:S(2)}) collective-permute-start(f32[64,512]{1,0:T(8,128)S(1)} %bitcast_add_fusion.3), channel_id=1, source_target_pairs={{0,2},{1,3},{2,4},{3,5},{4,6},{5,7},{6,8},{7,9},{8,10},{9,11},{10,... | collective-permute-start | bytes 393224 | tf_op jit(solution)/shard_map/ppermute | solution.py:52
  84.0 0.8 collective-permute-done.12
  84.9 1.9 collective-permute-start.13
  86.8 2.6 %collective-permute-done.9 = f32[64,512]{1,0:T(8,128)S(1)} collective-permute-done((f32[64,512]{1,0:T(8,128)S(1)}, f32[64,512]{1,0:T(8,128)S(1)}, u32[]{:S(2)}, u32[]{:S(2)}) %collective-permute-start.9) | collective-permute-done | bytes 131104 | tf_op jit(solution)/shard_map/ppermute | solution.py:52
  89.4 5.9 %collective-permute-start.10 = (f32[64,512]{1,0:T(8,128)S(1)}, f32[64,512]{1,0:T(8,128)S(1)}, u32[]{:S(2)}, u32[]{:S(2)}) collective-permute-start(f32[64,512]{1,0:T(8,128)S(1)} %bitcast_add_fusion.2), channel_id=1, source_target_pairs={{0,2},{1,3},{2,4},{3,5},{4,6},{5,7},{6,8},{7,9},{8,10},{9,11},{10,... | collective-permute-start | bytes 393224 | tf_op jit(solution)/shard_map/ppermute | solution.py:52
  95.3 0.0 collective-permute-done.13
  95.3 6.3 %collective-permute-done.10 = f32[64,512]{1,0:T(8,128)S(1)} collective-permute-done((f32[64,512]{1,0:T(8,128)S(1)}, f32[64,512]{1,0:T(8,128)S(1)}, u32[]{:S(2)}, u32[]{:S(2)}) %collective-permute-start.10) | collective-permute-done | bytes 131104 | tf_op jit(solution)/shard_map/ppermute | solution.py:52
  101.7 11.0 %all_to_all.40 = f32[8,8,512]{2,1,0:T(8,128)} all-to-all(f32[8,8,512]{2,1,0:T(8,128)S(1)} %bitcast.18), channel_id=1, replica_groups={{0,16,32,48,64,80,96,112},{128,144,160,176,192,208,224,240},{256,272,28..., dimensions={0} | all-to-all | bytes 262144 | tf_op jit(solution)/shard_map/all_to_all | solution.py:288
  112.7 0.0 all-gather.4.cloned.1.call-done.y_ref
  112.7 0.0 all-gather.6.cloned.1.call-update
  112.7 0.2 shard_map.51
  112.9 7.8 %all_to_all.41.parts_ref = f32[8,1,64]{2,1,0:T(1,128)S(1)} all-to-all(f32[8,1,64]{2,1,0:T(1,128)S(1)} %shard_map.51), channel_id=1, replica_groups={{0,16,32,48,64,80,96,112},{128,144,160,176,192,208,224,240},{256,272,28..., dimensions={0} | all-to-all | bytes 4096 | tf_op jit(solution)/shard_map/all_to_all | solution.py:288
  120.7 0.2 shard_map.52
  120.9 33.9 %all_to_all.42.parts_ref = f32[64,4,128]{2,1,0:T(4,128)S(1)} all-to-all(f32[64,4,128]{2,1,0:T(4,128)S(1)} %shard_map.52), channel_id=1, replica_groups={{0,1,2,3,4,5,6,7,8,9,10,11,12,13,14,15,128,129,130,131,132,133,134,135,..., dimensions={0} | all-to-all | bytes 262144 | tf_op jit(solution)/shard_map/all_to_all | solution.py:373
  154.8 0.3 shard_map.53
  155.1 9.2 %all_to_all.43.parts_ref = f32[8,1,64]{2,1,0:T(1,128)S(1)} all-to-all(f32[8,1,64]{2,1,0:T(1,128)S(1)} %shard_map.53), channel_id=1, replica_groups={{0,16,32,48,64,80,96,112},{128,144,160,176,192,208,224,240},{256,272,28..., dimensions={0} | all-to-all | bytes 4096 | tf_op jit(solution)/shard_map/all_to_all | solution.py:288
  164.3 0.2 shard_map.54
  164.5 22.8 %all_to_all.44.parts_ref = f32[64,4,128]{2,1,0:T(4,128)S(1)} all-to-all(f32[64,4,128]{2,1,0:T(4,128)S(1)} %shard_map.54), channel_id=1, replica_groups={{0,1,2,3,4,5,6,7,8,9,10,11,12,13,14,15,128,129,130,131,132,133,134,135,..., dimensions={0} | all-to-all | bytes 262144 | tf_op jit(solution)/shard_map/all_to_all | solution.py:373
  187.3 0.1 shard_map.55
  187.4 8.2 %all_to_all.45.parts_ref = f32[8,4,128]{2,1,0:T(4,128)S(1)} all-to-all(f32[8,4,128]{2,1,0:T(4,128)S(1)} %shard_map.55), channel_id=1, replica_groups={{0,16,32,48,64,80,96,112},{128,144,160,176,192,208,224,240},{256,272,28..., dimensions={0} | all-to-all | bytes 32768 | tf_op jit(solution)/shard_map/all_to_all | solution.py:288
  195.6 0.0 all-gather.6.cloned.1.call-done
  195.6 0.0 copy-start
  195.6 1.6 copy-done
  197.2 3.1 %shard_map.56 = (f32[128,4096]{1,0:T(8,128)S(1)}, f32[128,128]{1,0:T(8,128)}, f32[32,8,512]{2,1,0:T(8,128)S(1)}) custom-call(f32[16,8,8,512]{3,2,1,0:T(8,128)S(1)} %bitcast.19, f32[8,4,128]{2,1,0:T(4,128)S(1)} %all_to_all.45.parts_ref), custom_call_target="tpu_custom_call" | custom-call | tf_op jit(solution)/shard_map/pallas_call | solution.py:392
  200.2 19.4 %all_to_all.46.parts_ref = f32[32,8,512]{2,1,0:T(8,128)S(1)} all-to-all(f32[32,8,512]{2,1,0:T(8,128)S(1)} %get-tuple-element.40), channel_id=1, replica_groups=mesh['noise'=32,'dp'=16] {'noise'}, dimensions={0} | all-to-all | bytes 1048576 | tf_op jit(solution)/shard_map/all_to_all | solution.py:407
  219.6 2.5 shard_map.57
  222.1 15.2 %all_to_all.47.parts_ref = f32[32,8,512]{2,1,0:T(8,128)S(1)} all-to-all(f32[32,8,512]{2,1,0:T(8,128)S(1)} %get-tuple-element.42), channel_id=1, replica_groups=mesh['noise'=32,'dp'=16] {'noise'}, dimensions={0} | all-to-all | bytes 1048576 | tf_op jit(solution)/shard_map/all_to_all | solution.py:407
  237.3 6.2 %shard_map.58 = (bf16[128,1024]{1,0:T(8,128)(2,1)}, f32[1,128]{1,0:T(1,128)}, f32[1,256]{1,0:T(1,128)}) custom-call(s32[4]{0:T(128)S(1)} %pad_add_fusion.place_ref, f32[128,4096]{1,0:T(8,128)S(1)} %get-tuple-element.39.a_ref, f32[128,128]{1,0:T(8,128)S(1)} %get-tuple-element.41.u_ref, f32[32,8,512]{2,1,0:T(8,128)S(1)} %all_to_all.47.parts_ref, ...), custom_call_target="tpu_custom_call" | custom-call | tf_op jit(solution)/shard_map/pallas_call | solution.py:410
  (6 shorter events, 0.1 us)
Async XLA Ops:
  7.2 105.5 %all-gather.4.cloned.1.call-start = ((), (), s32[]{:S(2)}) async-start(), calls=%async_computation.8 | async-start | bytes 8650752 | tf_op jit(solution)/shard_map/all_gather | solution.py:297
  7.2 9.9 %collective-permute-start = (bf16[128,1024]{1,0:T(8,128)(2,1)}, bf16[128,1024]{1,0:T(8,128)(2,1)S(1)}, u32[]{:S(2)}, u32[]{:S(2)}) collective-permute-start(bf16[128,1024]{1,0:T(8,128)(2,1)} %param.2), channel_id=1, source_target_pairs={{0,32},{16,112},{32,0},{48,80},{64,96},{80,48},{96,64},{112,16},{1... | collective-permute-start | bytes 786440 | tf_op jit(solution)/shard_map/ppermute | solution.py:40
  12.4 8.6 %collective-permute-start.1 = (bf16[128,1024]{1,0:T(8,128)(2,1)}, bf16[128,1024]{1,0:T(8,128)(2,1)S(1)}, u32[]{:S(2)}, u32[]{:S(2)}) collective-permute-start(bf16[128,1024]{1,0:T(8,128)(2,1)} %param.3), channel_id=1, source_target_pairs={{0,128},{16,400},{32,160},{48,432},{64,192},{80,464},{96,224},{112... | collective-permute-start | bytes 786440 | tf_op jit(solution)/shard_map/ppermute | solution.py:44
  22.0 10.2 %collective-permute-start.3 = (bf16[256,1024]{1,0:T(8,128)(2,1)S(1)}, bf16[256,1024]{1,0:T(8,128)(2,1)S(1)}, u32[]{:S(2)}, u32[]{:S(2)}) collective-permute-start(bf16[256,1024]{1,0:T(8,128)(2,1)S(1)} %pad_maximum_fusion.refs_0_), channel_id=1, source_target_pairs={{0,96},{16,48},{32,64},{48,16},{64,32},{80,112},{96,0},{112,80},{1... | collective-permute-start | bytes 1572872 | tf_op jit(solution)/shard_map/ppermute | solution.py:40
  24.0 15.7 %collective-permute-start.2 = (bf16[256,1024]{1,0:T(8,128)(2,1)S(1)}, bf16[256,1024]{1,0:T(8,128)(2,1)S(1)}, u32[]{:S(2)}, u32[]{:S(2)}) collective-permute-start(bf16[256,1024]{1,0:T(8,128)(2,1)S(1)} %pad_maximum_fusion.refs_0_), channel_id=1, source_target_pairs={{0,16},{16,0},{32,48},{48,32},{64,80},{80,64},{96,112},{112,96},{1... | collective-permute-start | bytes 1572872 | tf_op jit(solution)/shard_map/ppermute | solution.py:32
  29.3 10.4 %collective-permute-start.5 = (bf16[256,1024]{1,0:T(8,128)(2,1)S(1)}, bf16[256,1024]{1,0:T(8,128)(2,1)S(1)}, u32[]{:S(2)}, u32[]{:S(2)}) collective-permute-start(bf16[256,1024]{1,0:T(8,128)(2,1)S(1)} %pad_maximum_fusion.1.refs_4_), channel_id=1, source_target_pairs={{0,384},{16,144},{32,416},{48,176},{64,448},{80,208},{96,480},{112... | collective-permute-start | bytes 1572872 | tf_op jit(solution)/shard_map/ppermute | solution.py:44
  32.2 8.9 %collective-permute-start.4 = (bf16[256,1024]{1,0:T(8,128)(2,1)S(1)}, bf16[256,1024]{1,0:T(8,128)(2,1)S(1)}, u32[]{:S(2)}, u32[]{:S(2)}) collective-permute-start(bf16[256,1024]{1,0:T(8,128)(2,1)S(1)} %collective-permute-done.3.refs_1_), channel_id=1, source_target_pairs={{0,16},{16,0},{32,48},{48,32},{64,80},{80,64},{96,112},{112,96},{1... | collective-permute-start | bytes 1572872 | tf_op jit(solution)/shard_map/ppermute | solution.py:32
  41.2 154.4 %all-gather.6.cloned.1.call-start = ((), (), s32[]{:S(2)}) async-start(), calls=%async_computation.9 | async-start | bytes 2228224 | tf_op jit(solution)/shard_map/all_gather | solution.py:341
  43.7 19.9 %collective-permute-start.6 = (f32[8,64,512]{2,1,0:T(8,128)S(1)}, f32[8,64,512]{2,1,0:T(8,128)S(1)}, u32[]{:S(2)}, u32[]{:S(2)}) collective-permute-start(f32[8,64,512]{2,1,0:T(8,128)S(1)} %get-tuple-element.32), channel_id=1, source_target_pairs={{0,1},{1,0},{2,3},{3,2},{4,5},{5,4},{6,7},{7,6},{8,9},{9,8},{10,11... | collective-permute-start | bytes 3145736 | tf_op jit(solution)/shard_map/ppermute | solution.py:52
  63.7 6.7 %collective-permute-start.7 = (f32[64,512]{1,0:T(8,128)S(1)}, f32[64,512]{1,0:T(8,128)S(1)}, u32[]{:S(2)}, u32[]{:S(2)}) collective-permute-start(f32[64,512]{1,0:T(8,128)S(1)} %get-tuple-element.34), channel_id=1, source_target_pairs={{0,2},{1,3},{2,4},{3,5},{4,6},{5,7},{6,8},{7,9},{8,10},{9,11},{10,... | collective-permute-start | bytes 393224 | tf_op jit(solution)/shard_map/ppermute | solution.py:52
  67.8 7.9 %collective-permute-start.11 = (f32[64,512]{1,0:T(8,128)S(1)}, f32[64,512]{1,0:T(8,128)S(1)}, u32[]{:S(2)}, u32[]{:S(2)}) collective-permute-start(f32[64,512]{1,0:T(8,128)S(1)} %get-tuple-element.36), channel_id=1, source_target_pairs={{0,14},{1,15},{2,0},{3,1},{4,2},{5,3},{6,4},{7,5},{8,6},{9,7},{10,... | collective-permute-start | bytes 393224 | tf_op jit(solution)/shard_map/ppermute | solution.py:52
  70.4 8.0 %collective-permute-start.8 = (f32[64,512]{1,0:T(8,128)S(1)}, f32[64,512]{1,0:T(8,128)S(1)}, u32[]{:S(2)}, u32[]{:S(2)}) collective-permute-start(f32[64,512]{1,0:T(8,128)S(1)} %bitcast_add_fusion.4), channel_id=1, source_target_pairs={{0,2},{1,3},{2,4},{3,5},{4,6},{5,7},{6,8},{7,9},{8,10},{9,11},{10,... | collective-permute-start | bytes 393224 | tf_op jit(solution)/shard_map/ppermute | solution.py:52
  75.8 9.1 %collective-permute-start.12 = (f32[64,512]{1,0:T(8,128)S(1)}, f32[64,512]{1,0:T(8,128)S(1)}, u32[]{:S(2)}, u32[]{:S(2)}) collective-permute-start(f32[64,512]{1,0:T(8,128)S(1)} %bitcast_add_fusion.1), channel_id=1, source_target_pairs={{0,14},{1,15},{2,0},{3,1},{4,2},{5,3},{6,4},{7,5},{8,6},{9,7},{10,... | collective-permute-start | bytes 393224 | tf_op jit(solution)/shard_map/ppermute | solution.py:52
  78.4 10.9 %collective-permute-start.9 = (f32[64,512]{1,0:T(8,128)S(1)}, f32[64,512]{1,0:T(8,128)S(1)}, u32[]{:S(2)}, u32[]{:S(2)}) collective-permute-start(f32[64,512]{1,0:T(8,128)S(1)} %bitcast_add_fusion.3), channel_id=1, source_target_pairs={{0,2},{1,3},{2,4},{3,5},{4,6},{5,7},{6,8},{7,9},{8,10},{9,11},{10,... | collective-permute-start | bytes 393224 | tf_op jit(solution)/shard_map/ppermute | solution.py:52
  84.9 10.4 %collective-permute-start.13 = (f32[64,512]{1,0:T(8,128)S(1)}, f32[64,512]{1,0:T(8,128)S(1)}, u32[]{:S(2)}, u32[]{:S(2)}) collective-permute-start(f32[64,512]{1,0:T(8,128)S(1)} %bitcast_add_fusion), channel_id=1, source_target_pairs={{0,14},{1,15},{2,0},{3,1},{4,2},{5,3},{6,4},{7,5},{8,6},{9,7},{10,... | collective-permute-start | bytes 393224 | tf_op jit(solution)/shard_map/ppermute | solution.py:52
  89.4 12.3 %collective-permute-start.10 = (f32[64,512]{1,0:T(8,128)S(1)}, f32[64,512]{1,0:T(8,128)S(1)}, u32[]{:S(2)}, u32[]{:S(2)}) collective-permute-start(f32[64,512]{1,0:T(8,128)S(1)} %bitcast_add_fusion.2), channel_id=1, source_target_pairs={{0,2},{1,3},{2,4},{3,5},{4,6},{5,7},{6,8},{7,9},{8,10},{9,11},{10,... | collective-permute-start | bytes 393224 | tf_op jit(solution)/shard_map/ppermute | solution.py:52
  195.6 1.6 copy-start
Sparse Core Ops, SparseCore 0:
  41.3 68.9 all-gather.3
  112.8 73.5 all-gather.5

commit v10 on v9

--- a/solution.py
+++ b/solution.py
@@ -42,6 +42,13 @@
 
 def swap_y(value, by):
     return lax.ppermute(value, "noise", noise_pairs(lambda y, x, c: (y ^ by[c], x, c)))
+
+
+def stacked(block, received):
+    rows, features = block.shape
+    both = lax.dynamic_update_slice(jnp.zeros((2 * rows, features), block.dtype), block, (0, 0))
+    both = lax.optimization_barrier(both)
+    return lax.dynamic_update_slice(both, received, (rows, 0))
 
 
 def send_z(value, target):
@@ -158,16 +165,23 @@
     copy_out(out_ref)
 
 
-def first_rows_kernel(a_ref, out_ref):
-    row_sums(a_ref, None, out_ref, out_ref.shape[2])
+def first_rows_kernel(a_ref, out_ref, sums):
+    copies, both, width = out_ref.shape
+    high, n = both // 2, a_ref.shape[0]
+    row_sums(a_ref, None, sums, n)
+    for k in range(copies):
+        out_ref[k, :high, :] = a_ref[k * high : (k + 1) * high, :]
+        out_ref[k, high:, :] = jnp.zeros((high, width), jnp.float32)
+        out_ref[k, high : high + 1, :n] = sums[0]
 
 
 def rows_kernel(log_weight, a_ref, parts_ref, out_ref):
     row_sums(a_ref, row_of(parts_ref, log_weight), out_ref, out_ref.shape[2])
 
 
-def columns_kernel(log_weight, a_ref, parts_ref, out_ref, shifted):
-    u = log_weight - joined(parts_ref[...])
+def columns_kernel(log_weight, under, a_ref, parts_ref, out_ref, shifted):
+    parts = parts_ref[:, under : under + 1, : a_ref.shape[0]]
+    u = log_weight - joined(parts)
     blocks, n = u.shape
     width = a_ref.shape[1]
     peak = None
@@ -222,15 +236,17 @@
         l_ref[k] = whole
 
 
-def whole_rows_kernel(log_weight, pieces_ref, parts_ref, a_ref, u_ref, l_ref):
+def whole_rows_kernel(log_weight, place_ref, pieces_ref, parts_ref, a_ref, u_ref, l_ref):
     depth, blocks, high, width = pieces_ref.shape
     n = width // YS
     v = log_weight - parts_ref[...]
+    c = place_ref[3]
     for z in range(depth):
+        to = pl.ds(pl.multiple_of(jnp.where(c == 0, z, depth - 1 - z) * high, high), high)
         for y in range(YS):
             for k in range(blocks):
                 at = (y * blocks + k) * n
-                a_ref[z * high : (z + 1) * high, at : at + n] = pieces_ref[z, k, :, y * n : (y + 1) * n]
+                a_ref[to, at : at + n] = pieces_ref[z, k, :, y * n : (y + 1) * n]
     v = jnp.concatenate([v[k, y : y + 1] for y in range(YS) for k in range(blocks)], axis=1)
     half_steps(log_weight, a_ref, v, u_ref, l_ref)
 
@@ -287,8 +303,8 @@
     def swap(value, groups):
         return lax.all_to_all(value, "noise", 0, 0, axis_index_groups=groups, tiled=True)
 
-    x_near = jnp.concatenate([noise_rows, swap_x(noise_rows, FIRST)], axis=0)
-    y_near = jnp.concatenate([data_rows, swap_y(data_rows, FIRST)], axis=0)
+    x_near = stacked(noise_rows, swap_x(noise_rows, FIRST))
+    y_near = stacked(data_rows, swap_y(data_rows, FIRST))
     x_near, y_near = lax.optimization_barrier((x_near, y_near))
     x_far, y_far = swap_x(x_near, SECOND), swap_y(y_near, SECOND)
     x_there, x_far_there, y_far, late_rows = lax.optimization_barrier(
@@ -336,24 +352,28 @@
                 back = back + back_rest[step]
     own = own + ahead + back
 
-    pieces = swap(own.reshape(group, rows // depth, wide), x_groups)
-    everything, pieces = lax.optimization_barrier((everything, pieces))
-    gathered = lax.all_gather(pieces, "dp")
+    few = tall // depth
+    high = rows // depth
+    part = pl.pallas_call(
+        first_rows_kernel,
+        out_shape=jax.ShapeDtypeStruct((group, 2 * high, wide), f32),
+        in_specs=[VMEM],
+        out_specs=VMEM,
+        scratch_shapes=[pltpu.VMEM((1, 1, few), f32)],
+        compiler_params=PARAMS,
+    )(own)
+    part = swap(part, x_groups)
+    everything, pieces = lax.optimization_barrier((everything, part[:, :high]))
+    ring_groups = [
+        [n * depth + (depth - 1 - d if n % CORES else d) for d in range(depth)] for n in range(YS * group)
+    ]
+    gathered = lax.all_gather(pieces, ("noise", "dp"), axis_index_groups=ring_groups)
     z_groups = [
         [((y * group) + k) * depth + d for y in range(YS) for d in range(depth)] for k in range(group)
     ]
-    few = tall // depth
     row_shape = jax.ShapeDtypeStruct((group, 1, few), f32)
     for step in range(EARLY):
-        if step == 0:
-            part = pl.pallas_call(
-                first_rows_kernel,
-                out_shape=row_shape,
-                in_specs=[VMEM],
-                out_specs=VMEM,
-                compiler_params=PARAMS,
-            )(own)
-        else:
+        if step > 0:
             part = pl.pallas_call(
                 functools.partial(rows_kernel, log_weight),
                 out_shape=row_shape,
@@ -361,9 +381,9 @@
                 out_specs=VMEM,
                 compiler_params=PARAMS,
             )(own, part)
-        part = swap(part, x_groups)
+            part = swap(part, x_groups)
         part = pl.pallas_call(
-            functools.partial(columns_kernel, log_weight),
+            functools.partial(columns_kernel, log_weight, 0 if step > 0 else high),
             out_shape=jax.ShapeDtypeStruct((YS * depth, YS, rows), f32),
             in_specs=[VMEM] * 2,
             out_specs=VMEM,
@@ -383,19 +403,19 @@
     part = swap(part, x_groups)
 
     copies = lax.axis_size("noise")
-    high = 8
-    block = tokens // high
+    lines = 8
+    block = tokens // lines
     u_shape = jax.ShapeDtypeStruct((rows, rows), f32)
-    l_shape = jax.ShapeDtypeStruct((copies, high, block), f32)
+    l_shape = jax.ShapeDtypeStruct((copies, lines, block), f32)
     for step in range(EARLY, ITERS):
         if step == EARLY:
             a, u, part = pl.pallas_call(
                 functools.partial(whole_rows_kernel, log_weight),
                 out_shape=[jax.ShapeDtypeStruct((rows, tokens), f32), u_shape, l_shape],
-                in_specs=[VMEM] * 2,
+                in_specs=[SMEM] + [VMEM] * 2,
                 out_specs=[VMEM] * 3,
                 compiler_params=PARAMS,
-            )(gathered, part)
+            )(place, gathered, part)
         else:
             u, part = pl.pallas_call(
                 functools.partial(next_kernel, log_weight),
@@ -419,7 +439,7 @@
             SMEM,
             pl.BlockSpec((rows, tokens // steps), lambda k: (0, k)),
             pl.BlockSpec((rows, rows), lambda k: (0, 0)),
-            pl.BlockSpec((copies, high, block), lambda k: (0, 0, 0)),
+            pl.BlockSpec((copies, lines, block), lambda k: (0, 0, 0)),
             pl.BlockSpec((tokens // steps, features), lambda k: (k, 0)),
         ],
         out_specs=[
@@ -430,7 +450,7 @@
         scratch_shapes=[
             pltpu.VMEM((rows, features), f32),
             pltpu.VMEM((rows, 1), f32),
-            pltpu.VMEM((high, block), f32),
+            pltpu.VMEM((lines, block), f32),
         ],
         compiler_params=PARAMS,
     )(place, a, u, part, everything)

time: 251 us -> 249 us (level)
  blocking collectives: 127 us -> 124 us
  local copies, waits for them, and re-layouts: 1.59 us -> 4.28 us
    all_to_all x2, blocking collectives: 56.7 us -> 47.8 us  [on_device(): lax.all_to_all(part, ('noise', 'dp'), 0, 0, axis_index_groups=z_groups, t...]
    all_to_all x2, blocking collectives: 34.6 us -> 39.8 us  [on_device(): part = lax.all_to_all(part, 'noise', 0, 0, tiled=True)]
    ppermute x2, waiting for transfers between devices: 2.96 us -> 0.2 us  [swap_y(): lax.ppermute(value, 'noise', noise_pairs(lambda y, x, c: (y ^ by[c], x, c)))]
    ppermute x2, starting transfers between devices: 6.57 us -> 9.17 us  [swap_y(): lax.ppermute(value, 'noise', noise_pairs(lambda y, x, c: (y ^ by[c], x, c)))]
    all_to_all x4 -> x3, blocking collectives: 36.2 us -> 36.7 us  [swap(): lax.all_to_all(value, 'noise', 0, 0, axis_index_groups=groups, tiled=True)]
  transfers between devices with their start and end apart: 16 -> 16, of which waited for: 9 -> 11; matrix products, arithmetic and copies ran while one was open for 0% -> 1% of each run, Pallas kernels for 1% -> 1%
where the time goes in v10:
time: 249 us
  blocking collectives  124 us (50%)
  starting transfers between devices  62.5 us (25%)
  waiting for transfers between devices  27.1 us (11%)
  Pallas kernels  15.8 us (6%)
  between operations  14.3 us (6%)
  local copies, waits for them, and re-layouts  4.28 us (2%)
    all_to_all x2, blocking collectives, on_device(): lax.all_to_all(part, ('noise', 'dp'), 0, 0, axis_index_groups=z_groups, t...  47.8 us
    all_to_all x2, blocking collectives, on_device(): part = lax.all_to_all(part, 'noise', 0, 0, tiled=True)  39.8 us
    all_to_all x3, blocking collectives, swap(): lax.all_to_all(value, 'noise', 0, 0, axis_index_groups=groups, tiled=True)  36.7 us
    ppermute x8, starting transfers between devices, send_z(): return lax.ppermute(value, ('noise', 'dp'), pairs)  35.1 us
    ppermute x8, waiting for transfers between devices, send_z(): return lax.ppermute(value, ('noise', 'dp'), pairs)  23.3 us
    ppermute x2, starting transfers between devices, to_other_core(): lax.ppermute(value, 'noise', noise_pairs(lambda y, x, c: (y, x, 1 - c)))  11.5 us
    ppermute x2, starting transfers between devices, swap_y(): lax.ppermute(value, 'noise', noise_pairs(lambda y, x, c: (y ^ by[c], x, c)))  9.17 us
    ppermute x2, starting transfers between devices, swap_x(): lax.ppermute(value, 'noise', noise_pairs(lambda y, x, c: (y, x ^ by[c], c)))  6.59 us
  transfers between devices with their start and end apart: 16, of which 11 were waited for; matrix products, arithmetic and copies ran while one was open for 1% of the time, Pallas kernels for 1%

profile of v10, /device:TPU:1, one launch (start us, length us, event | category | flops | bytes accessed | tf_op | source)
XLA Modules:
  0.0 248.5 jit_solution(13160799930353739072)
XLA Ops:
  7.2 0.0 all-gather.4.cloned.1.call-start
  7.2 5.5 %collective-permute-start.1 = (bf16[128,1024]{1,0:T(8,128)(2,1)}, bf16[128,1024]{1,0:T(8,128)(2,1)S(1)}, u32[]{:S(2)}, u32[]{:S(2)}) collective-permute-start(bf16[128,1024]{1,0:T(8,128)(2,1)} %param.3), channel_id=1, source_target_pairs={{0,128},{16,400},{32,160},{48,432},{64,192},{80,464},{96,224},{112... | collective-permute-start | bytes 786440 | tf_op jit(solution)/shard_map/ppermute | solution.py:44
  12.7 4.4 %collective-permute-start = (bf16[128,1024]{1,0:T(8,128)(2,1)}, bf16[128,1024]{1,0:T(8,128)(2,1)S(1)}, u32[]{:S(2)}, u32[]{:S(2)}) collective-permute-start(bf16[128,1024]{1,0:T(8,128)(2,1)} %param.2), channel_id=1, source_target_pairs={{0,32},{16,112},{32,0},{48,80},{64,96},{80,48},{96,64},{112,16},{1... | collective-permute-start | bytes 786440 | tf_op jit(solution)/shard_map/ppermute | solution.py:40
  17.1 1.0 dynamic_update_slice.14
  18.1 1.0 dynamic_update_slice.12
  19.1 0.0 collective-permute-done.1
  19.1 2.1 collective-permute-done
  21.2 2.2 collective-permute-start.3
  23.5 4.9 %collective-permute-start.2 = (bf16[256,1024]{1,0:T(8,128)(2,1)S(1)}, bf16[256,1024]{1,0:T(8,128)(2,1)S(1)}, u32[]{:S(2)}, u32[]{:S(2)}) collective-permute-start(bf16[256,1024]{1,0:T(8,128)(2,1)S(1)} %constant_dynamic-update-slice_fusion.1.refs_0_), channel_id=1, source_target_pairs={{0,16},{16,0},{32,48},{48,32},{64,80},{80,64},{96,112},{112,96},{1... | collective-permute-start | bytes 1572872 | tf_op jit(solution)/shard_map/ppermute | solution.py:32
  28.4 3.7 %collective-permute-start.5 = (bf16[256,1024]{1,0:T(8,128)(2,1)S(1)}, bf16[256,1024]{1,0:T(8,128)(2,1)S(1)}, u32[]{:S(2)}, u32[]{:S(2)}) collective-permute-start(bf16[256,1024]{1,0:T(8,128)(2,1)S(1)} %constant_dynamic-update-slice_fusion.refs_4_), channel_id=1, source_target_pairs={{0,384},{16,144},{32,416},{48,176},{64,448},{80,208},{96,480},{112... | collective-permute-start | bytes 1572872 | tf_op jit(solution)/shard_map/ppermute | solution.py:44
  32.1 0.0 collective-permute-done.3.refs_1_
  32.1 6.6 %collective-permute-start.4 = (bf16[256,1024]{1,0:T(8,128)(2,1)S(1)}, bf16[256,1024]{1,0:T(8,128)(2,1)S(1)}, u32[]{:S(2)}, u32[]{:S(2)}) collective-permute-start(bf16[256,1024]{1,0:T(8,128)(2,1)S(1)} %collective-permute-done.3.refs_1_), channel_id=1, source_target_pairs={{0,16},{16,0},{32,48},{48,32},{64,80},{80,64},{96,112},{112,96},{1... | collective-permute-start | bytes 1572872 | tf_op jit(solution)/shard_map/ppermute | solution.py:32
  38.7 0.0 collective-permute-done.2.refs_2_
  38.7 0.2 collective-permute-done.5.refs_5_
  38.9 1.3 collective-permute-done.4.refs_3_
  40.2 0.0 all-gather.4.cloned.1.call-update
  40.2 0.0 all-gather.6.cloned.1.call-start
  40.3 0.1 pad_add_fusion.place_ref
  40.4 2.4 shard_map.49
  42.8 8.4 %collective-permute-start.6 = (f32[8,64,512]{2,1,0:T(8,128)S(1)}, f32[8,64,512]{2,1,0:T(8,128)S(1)}, u32[]{:S(2)}, u32[]{:S(2)}) collective-permute-start(f32[8,64,512]{2,1,0:T(8,128)S(1)} %get-tuple-element.32), channel_id=1, source_target_pairs={{0,1},{1,0},{2,3},{3,2},{4,5},{5,4},{6,7},{7,6},{8,9},{9,8},{10,11... | collective-permute-start | bytes 3145736 | tf_op jit(solution)/shard_map/ppermute | solution.py:59
  51.2 12.6 %collective-permute-done.6.got = f32[8,64,512]{2,1,0:T(8,128)S(1)} collective-permute-done((f32[8,64,512]{2,1,0:T(8,128)S(1)}, f32[8,64,512]{2,1,0:T(8,128)S(1)}, u32[]{:S(2)}, u32[]{:S(2)}) %collective-permute-start.6) | collective-permute-done | bytes 1048608 | tf_op jit(solution)/shard_map/ppermute | solution.py:59
  63.8 0.1 shard_map.50
  63.9 3.7 %collective-permute-start.7 = (f32[64,512]{1,0:T(8,128)S(1)}, f32[64,512]{1,0:T(8,128)S(1)}, u32[]{:S(2)}, u32[]{:S(2)}) collective-permute-start(f32[64,512]{1,0:T(8,128)S(1)} %get-tuple-element.34), channel_id=1, source_target_pairs={{0,2},{1,3},{2,4},{3,5},{4,6},{5,7},{6,8},{7,9},{8,10},{9,11},{10,... | collective-permute-start | bytes 393224 | tf_op jit(solution)/shard_map/ppermute | solution.py:59
  67.6 2.5 collective-permute-start.11
  70.1 0.8 collective-permute-done.7
  70.9 4.5 %collective-permute-start.8 = (f32[64,512]{1,0:T(8,128)S(1)}, f32[64,512]{1,0:T(8,128)S(1)}, u32[]{:S(2)}, u32[]{:S(2)}) collective-permute-start(f32[64,512]{1,0:T(8,128)S(1)} %bitcast_add_fusion.4), channel_id=1, source_target_pairs={{0,2},{1,3},{2,4},{3,5},{4,6},{5,7},{6,8},{7,9},{8,10},{9,11},{10,... | collective-permute-start | bytes 393224 | tf_op jit(solution)/shard_map/ppermute | solution.py:59
  75.4 0.1 collective-permute-done.11
  75.5 2.0 collective-permute-start.12
  77.5 0.1 collective-permute-done.8
  77.6 6.0 %collective-permute-start.9 = (f32[64,512]{1,0:T(8,128)S(1)}, f32[64,512]{1,0:T(8,128)S(1)}, u32[]{:S(2)}, u32[]{:S(2)}) collective-permute-start(f32[64,512]{1,0:T(8,128)S(1)} %bitcast_add_fusion.3), channel_id=1, source_target_pairs={{0,2},{1,3},{2,4},{3,5},{4,6},{5,7},{6,8},{7,9},{8,10},{9,11},{10,... | collective-permute-start | bytes 393224 | tf_op jit(solution)/shard_map/ppermute | solution.py:59
  83.7 1.0 collective-permute-done.12
  84.6 1.9 collective-permute-start.13
  86.6 3.2 %collective-permute-done.9 = f32[64,512]{1,0:T(8,128)S(1)} collective-permute-done((f32[64,512]{1,0:T(8,128)S(1)}, f32[64,512]{1,0:T(8,128)S(1)}, u32[]{:S(2)}, u32[]{:S(2)}) %collective-permute-start.9) | collective-permute-done | bytes 131104 | tf_op jit(solution)/shard_map/ppermute | solution.py:59
  89.8 6.1 %collective-permute-start.10 = (f32[64,512]{1,0:T(8,128)S(1)}, f32[64,512]{1,0:T(8,128)S(1)}, u32[]{:S(2)}, u32[]{:S(2)}) collective-permute-start(f32[64,512]{1,0:T(8,128)S(1)} %bitcast_add_fusion.2), channel_id=1, source_target_pairs={{0,2},{1,3},{2,4},{3,5},{4,6},{5,7},{6,8},{7,9},{8,10},{9,11},{10,... | collective-permute-start | bytes 393224 | tf_op jit(solution)/shard_map/ppermute | solution.py:59
  95.9 0.0 collective-permute-done.13
  95.9 5.6 %collective-permute-done.10 = f32[64,512]{1,0:T(8,128)S(1)} collective-permute-done((f32[64,512]{1,0:T(8,128)S(1)}, f32[64,512]{1,0:T(8,128)S(1)}, u32[]{:S(2)}, u32[]{:S(2)}) %collective-permute-start.10) | collective-permute-done | bytes 131104 | tf_op jit(solution)/shard_map/ppermute | solution.py:59
  101.5 0.2 shard_map.51
  101.7 15.3 %all_to_all.35.parts_ref = f32[8,16,512]{2,1,0:T(8,128)S(1)} all-to-all(f32[8,16,512]{2,1,0:T(8,128)S(1)} %shard_map.51), channel_id=1, replica_groups={{0,16,32,48,64,80,96,112},{128,144,160,176,192,208,224,240},{256,272,28..., dimensions={0} | all-to-all | bytes 524288 | tf_op jit(solution)/shard_map/all_to_all | solution.py:304
  117.0 0.7 slice.24
  117.7 0.0 all-gather.4.cloned.1.call-done.y_ref
  117.7 0.0 all-gather.6.cloned.1.call-update
  117.7 0.2 shard_map.52
  117.9 27.1 %all_to_all.36.parts_ref = f32[64,4,128]{2,1,0:T(4,128)S(1)} all-to-all(f32[64,4,128]{2,1,0:T(4,128)S(1)} %shard_map.52), channel_id=1, replica_groups={{0,1,2,3,4,5,6,7,8,9,10,11,12,13,14,15,128,129,130,131,132,133,134,135,..., dimensions={0} | all-to-all | bytes 262144 | tf_op jit(solution)/shard_map/all_to_all | solution.py:393
  145.0 0.3 shard_map.53
  145.3 11.1 %all_to_all.37.parts_ref = f32[8,1,64]{2,1,0:T(1,128)S(1)} all-to-all(f32[8,1,64]{2,1,0:T(1,128)S(1)} %shard_map.53), channel_id=1, replica_groups={{0,16,32,48,64,80,96,112},{128,144,160,176,192,208,224,240},{256,272,28..., dimensions={0} | all-to-all | bytes 4096 | tf_op jit(solution)/shard_map/all_to_all | solution.py:304
  156.4 0.2 shard_map.54
  156.6 20.7 %all_to_all.38.parts_ref = f32[64,4,128]{2,1,0:T(4,128)S(1)} all-to-all(f32[64,4,128]{2,1,0:T(4,128)S(1)} %shard_map.54), channel_id=1, replica_groups={{0,1,2,3,4,5,6,7,8,9,10,11,12,13,14,15,128,129,130,131,132,133,134,135,..., dimensions={0} | all-to-all | bytes 262144 | tf_op jit(solution)/shard_map/all_to_all | solution.py:393
  177.3 0.1 shard_map.55
  177.4 10.2 %all_to_all.39.parts_ref = f32[8,4,128]{2,1,0:T(4,128)S(1)} all-to-all(f32[8,4,128]{2,1,0:T(4,128)S(1)} %shard_map.55), channel_id=1, replica_groups={{0,16,32,48,64,80,96,112},{128,144,160,176,192,208,224,240},{256,272,28..., dimensions={0} | all-to-all | bytes 32768 | tf_op jit(solution)/shard_map/all_to_all | solution.py:304
  187.7 0.2 all-gather.6.cloned.1.call-done
  187.9 0.0 copy-start
  187.9 1.6 copy-done
  189.5 3.6 %shard_map.56 = (f32[128,4096]{1,0:T(8,128)S(1)}, f32[128,128]{1,0:T(8,128)}, f32[32,8,512]{2,1,0:T(8,128)S(1)}) custom-call(s32[4]{0:T(128)S(1)} %pad_add_fusion.place_ref, f32[16,8,8,512]{3,2,1,0:T(8,128)S(1)} %bitcast.17, f32[8,4,128]{2,1,0:T(4,128)S(1)} %all_to_all.39.parts_ref), custom_call_target="tpu_custom_call" | custom-call | tf_op jit(solution)/shard_map/pallas_call | solution.py:412
  193.1 24.6 %all_to_all.40.parts_ref = f32[32,8,512]{2,1,0:T(8,128)S(1)} all-to-all(f32[32,8,512]{2,1,0:T(8,128)S(1)} %get-tuple-element.40), channel_id=1, replica_groups=mesh['noise'=32,'dp'=16] {'noise'}, dimensions={0} | all-to-all | bytes 1048576 | tf_op jit(solution)/shard_map/all_to_all | solution.py:427
  217.7 2.5 %shard_map.57 = (f32[128,128]{1,0:T(8,128)S(1)}, f32[32,8,512]{2,1,0:T(8,128)S(1)}) custom-call(f32[128,4096]{1,0:T(8,128)S(1)} %get-tuple-element.39.a_ref, f32[32,8,512]{2,1,0:T(8,128)S(1)} %all_to_all.40.parts_ref), custom_call_target="tpu_custom_call" | custom-call | tf_op jit(solution)/shard_map/pallas_call | solution.py:420
  220.3 15.2 %all_to_all.41.parts_ref = f32[32,8,512]{2,1,0:T(8,128)S(1)} all-to-all(f32[32,8,512]{2,1,0:T(8,128)S(1)} %get-tuple-element.42), channel_id=1, replica_groups=mesh['noise'=32,'dp'=16] {'noise'}, dimensions={0} | all-to-all | bytes 1048576 | tf_op jit(solution)/shard_map/all_to_all | solution.py:427
  235.5 6.2 %shard_map.58 = (bf16[128,1024]{1,0:T(8,128)(2,1)}, f32[1,128]{1,0:T(1,128)}, f32[1,256]{1,0:T(1,128)}) custom-call(s32[4]{0:T(128)S(1)} %pad_add_fusion.place_ref, f32[128,4096]{1,0:T(8,128)S(1)} %get-tuple-element.39.a_ref, f32[128,128]{1,0:T(8,128)S(1)} %get-tuple-element.41.u_ref, f32[32,8,512]{2,1,0:T(8,128)S(1)} %all_to_all.41.parts_ref, ...), custom_call_target="tpu_custom_call" | custom-call | tf_op jit(solution)/shard_map/pallas_call | solution.py:430
  (8 shorter events, 0.2 us)
Async XLA Ops:
  7.2 110.5 %all-gather.4.cloned.1.call-start = ((), (), s32[]{:S(2)}) async-start(), calls=%async_computation.7 | async-start | bytes 8650752 | tf_op jit(solution)/shard_map/all_gather | solution.py:313
  7.2 11.9 %collective-permute-start.1 = (bf16[128,1024]{1,0:T(8,128)(2,1)}, bf16[128,1024]{1,0:T(8,128)(2,1)S(1)}, u32[]{:S(2)}, u32[]{:S(2)}) collective-permute-start(bf16[128,1024]{1,0:T(8,128)(2,1)} %param.3), channel_id=1, source_target_pairs={{0,128},{16,400},{32,160},{48,432},{64,192},{80,464},{96,224},{112... | collective-permute-start | bytes 786440 | tf_op jit(solution)/shard_map/ppermute | solution.py:44
  12.7 8.5 %collective-permute-start = (bf16[128,1024]{1,0:T(8,128)(2,1)}, bf16[128,1024]{1,0:T(8,128)(2,1)S(1)}, u32[]{:S(2)}, u32[]{:S(2)}) collective-permute-start(bf16[128,1024]{1,0:T(8,128)(2,1)} %param.2), channel_id=1, source_target_pairs={{0,32},{16,112},{32,0},{48,80},{64,96},{80,48},{96,64},{112,16},{1... | collective-permute-start | bytes 786440 | tf_op jit(solution)/shard_map/ppermute | solution.py:40
  21.2 10.8 %collective-permute-start.3 = (bf16[256,1024]{1,0:T(8,128)(2,1)S(1)}, bf16[256,1024]{1,0:T(8,128)(2,1)S(1)}, u32[]{:S(2)}, u32[]{:S(2)}) collective-permute-start(bf16[256,1024]{1,0:T(8,128)(2,1)S(1)} %constant_dynamic-update-slice_fusion.1.refs_0_), channel_id=1, source_target_pairs={{0,96},{16,48},{32,64},{48,16},{64,32},{80,112},{96,0},{112,80},{1... | collective-permute-start | bytes 1572872 | tf_op jit(solution)/shard_map/ppermute | solution.py:40
  23.5 15.2 %collective-permute-start.2 = (bf16[256,1024]{1,0:T(8,128)(2,1)S(1)}, bf16[256,1024]{1,0:T(8,128)(2,1)S(1)}, u32[]{:S(2)}, u32[]{:S(2)}) collective-permute-start(bf16[256,1024]{1,0:T(8,128)(2,1)S(1)} %constant_dynamic-update-slice_fusion.1.refs_0_), channel_id=1, source_target_pairs={{0,16},{16,0},{32,48},{48,32},{64,80},{80,64},{96,112},{112,96},{1... | collective-permute-start | bytes 1572872 | tf_op jit(solution)/shard_map/ppermute | solution.py:32
  28.4 10.6 %collective-permute-start.5 = (bf16[256,1024]{1,0:T(8,128)(2,1)S(1)}, bf16[256,1024]{1,0:T(8,128)(2,1)S(1)}, u32[]{:S(2)}, u32[]{:S(2)}) collective-permute-start(bf16[256,1024]{1,0:T(8,128)(2,1)S(1)} %constant_dynamic-update-slice_fusion.refs_4_), channel_id=1, source_target_pairs={{0,384},{16,144},{32,416},{48,176},{64,448},{80,208},{96,480},{112... | collective-permute-start | bytes 1572872 | tf_op jit(solution)/shard_map/ppermute | solution.py:44
  32.1 8.1 %collective-permute-start.4 = (bf16[256,1024]{1,0:T(8,128)(2,1)S(1)}, bf16[256,1024]{1,0:T(8,128)(2,1)S(1)}, u32[]{:S(2)}, u32[]{:S(2)}) collective-permute-start(bf16[256,1024]{1,0:T(8,128)(2,1)S(1)} %collective-permute-done.3.refs_1_), channel_id=1, source_target_pairs={{0,16},{16,0},{32,48},{48,32},{64,80},{80,64},{96,112},{112,96},{1... | collective-permute-start | bytes 1572872 | tf_op jit(solution)/shard_map/ppermute | solution.py:32
  40.2 147.7 %all-gather.6.cloned.1.call-start = ((), (), s32[]{:S(2)}) async-start(), calls=%async_computation.8 | async-start | bytes 2228224 | tf_op jit(solution)/shard_map/all_gather | solution.py:370
  42.8 21.0 %collective-permute-start.6 = (f32[8,64,512]{2,1,0:T(8,128)S(1)}, f32[8,64,512]{2,1,0:T(8,128)S(1)}, u32[]{:S(2)}, u32[]{:S(2)}) collective-permute-start(f32[8,64,512]{2,1,0:T(8,128)S(1)} %get-tuple-element.32), channel_id=1, source_target_pairs={{0,1},{1,0},{2,3},{3,2},{4,5},{5,4},{6,7},{7,6},{8,9},{9,8},{10,11... | collective-permute-start | bytes 3145736 | tf_op jit(solution)/shard_map/ppermute | solution.py:59
  63.9 7.0 %collective-permute-start.7 = (f32[64,512]{1,0:T(8,128)S(1)}, f32[64,512]{1,0:T(8,128)S(1)}, u32[]{:S(2)}, u32[]{:S(2)}) collective-permute-start(f32[64,512]{1,0:T(8,128)S(1)} %get-tuple-element.34), channel_id=1, source_target_pairs={{0,2},{1,3},{2,4},{3,5},{4,6},{5,7},{6,8},{7,9},{8,10},{9,11},{10,... | collective-permute-start | bytes 393224 | tf_op jit(solution)/shard_map/ppermute | solution.py:59
  67.6 7.9 %collective-permute-start.11 = (f32[64,512]{1,0:T(8,128)S(1)}, f32[64,512]{1,0:T(8,128)S(1)}, u32[]{:S(2)}, u32[]{:S(2)}) collective-permute-start(f32[64,512]{1,0:T(8,128)S(1)} %get-tuple-element.36), channel_id=1, source_target_pairs={{0,14},{1,15},{2,0},{3,1},{4,2},{5,3},{6,4},{7,5},{8,6},{9,7},{10,... | collective-permute-start | bytes 393224 | tf_op jit(solution)/shard_map/ppermute | solution.py:59
  70.9 6.7 %collective-permute-start.8 = (f32[64,512]{1,0:T(8,128)S(1)}, f32[64,512]{1,0:T(8,128)S(1)}, u32[]{:S(2)}, u32[]{:S(2)}) collective-permute-start(f32[64,512]{1,0:T(8,128)S(1)} %bitcast_add_fusion.4), channel_id=1, source_target_pairs={{0,2},{1,3},{2,4},{3,5},{4,6},{5,7},{6,8},{7,9},{8,10},{9,11},{10,... | collective-permute-start | bytes 393224 | tf_op jit(solution)/shard_map/ppermute | solution.py:59
  75.5 9.1 %collective-permute-start.12 = (f32[64,512]{1,0:T(8,128)S(1)}, f32[64,512]{1,0:T(8,128)S(1)}, u32[]{:S(2)}, u32[]{:S(2)}) collective-permute-start(f32[64,512]{1,0:T(8,128)S(1)} %bitcast_add_fusion.1), channel_id=1, source_target_pairs={{0,14},{1,15},{2,0},{3,1},{4,2},{5,3},{6,4},{7,5},{8,6},{9,7},{10,... | collective-permute-start | bytes 393224 | tf_op jit(solution)/shard_map/ppermute | solution.py:59
  77.6 12.1 %collective-permute-start.9 = (f32[64,512]{1,0:T(8,128)S(1)}, f32[64,512]{1,0:T(8,128)S(1)}, u32[]{:S(2)}, u32[]{:S(2)}) collective-permute-start(f32[64,512]{1,0:T(8,128)S(1)} %bitcast_add_fusion.3), channel_id=1, source_target_pairs={{0,2},{1,3},{2,4},{3,5},{4,6},{5,7},{6,8},{7,9},{8,10},{9,11},{10,... | collective-permute-start | bytes 393224 | tf_op jit(solution)/shard_map/ppermute | solution.py:59
  84.6 11.2 %collective-permute-start.13 = (f32[64,512]{1,0:T(8,128)S(1)}, f32[64,512]{1,0:T(8,128)S(1)}, u32[]{:S(2)}, u32[]{:S(2)}) collective-permute-start(f32[64,512]{1,0:T(8,128)S(1)} %bitcast_add_fusion), channel_id=1, source_target_pairs={{0,14},{1,15},{2,0},{3,1},{4,2},{5,3},{6,4},{7,5},{8,6},{9,7},{10,... | collective-permute-start | bytes 393224 | tf_op jit(solution)/shard_map/ppermute | solution.py:59
  89.8 11.7 %collective-permute-start.10 = (f32[64,512]{1,0:T(8,128)S(1)}, f32[64,512]{1,0:T(8,128)S(1)}, u32[]{:S(2)}, u32[]{:S(2)}) collective-permute-start(f32[64,512]{1,0:T(8,128)S(1)} %bitcast_add_fusion.2), channel_id=1, source_target_pairs={{0,2},{1,3},{2,4},{3,5},{4,6},{5,7},{6,8},{7,9},{8,10},{9,11},{10,... | collective-permute-start | bytes 393224 | tf_op jit(solution)/shard_map/ppermute | solution.py:59
  187.9 1.6 copy-start
Sparse Core Ops, SparseCore 0:
  40.4 68.5 all-gather.3
  117.8 70.0 all-gather.5

commit v11 on v10

--- a/solution.py
+++ b/solution.py
@@ -166,21 +166,21 @@
 
 
 def first_rows_kernel(a_ref, out_ref, sums):
-    copies, both, width = out_ref.shape
-    high, n = both // 2, a_ref.shape[0]
+    copies, high, width = out_ref.shape
+    n, columns = a_ref.shape
     row_sums(a_ref, None, sums, n)
     for k in range(copies):
-        out_ref[k, :high, :] = a_ref[k * high : (k + 1) * high, :]
-        out_ref[k, high:, :] = jnp.zeros((high, width), jnp.float32)
-        out_ref[k, high : high + 1, :n] = sums[0]
+        out_ref[k, :, :columns] = a_ref[k * high : (k + 1) * high, :]
+        out_ref[k, :, columns:] = jnp.zeros((high, width - columns), jnp.float32)
+        out_ref[k, :1, columns : columns + n] = sums[0]
 
 
 def rows_kernel(log_weight, a_ref, parts_ref, out_ref):
     row_sums(a_ref, row_of(parts_ref, log_weight), out_ref, out_ref.shape[2])
 
 
-def columns_kernel(log_weight, under, a_ref, parts_ref, out_ref, shifted):
-    parts = parts_ref[:, under : under + 1, : a_ref.shape[0]]
+def columns_kernel(log_weight, beside, a_ref, parts_ref, out_ref, shifted):
+    parts = parts_ref[:, :1, beside : beside + a_ref.shape[0]]
     u = log_weight - joined(parts)
     blocks, n = u.shape
     width = a_ref.shape[1]
@@ -207,21 +207,16 @@
     copy_out(out_ref)
 
 
-def half_steps(log_weight, a_ref, v, u_ref, l_ref):
-    rows, columns = a_ref.shape
-    lanes = u_ref.shape[1]
+def row_step(log_weight, value, u_ref, at):
+    peak = jnp.max(value, axis=1, keepdims=True)
+    total = jnp.sum(jnp.exp2(value - peak), axis=1, keepdims=True)
+    u = log_weight - (peak + jnp.log(total) * LOG2E)
+    u_ref[at, :] = jnp.broadcast_to(u, (value.shape[0], u_ref.shape[1]))
+
+
+def column_step(a_ref, u_ref, l_ref):
+    rows, lanes = u_ref.shape
     copies, high, width = l_ref.shape
-
-    @pl.loop(0, rows // 8, step=2)
-    def _(base):
-        for i in range(2):
-            at = pl.ds(pl.multiple_of((base + i) * 8, 8), 8)
-            value = a_ref[at, :] + v
-            peak = jnp.max(value, axis=1, keepdims=True)
-            total = jnp.sum(jnp.exp2(value - peak), axis=1, keepdims=True)
-            u = log_weight - (peak + jnp.log(total) * LOG2E)
-            u_ref[at, :] = jnp.broadcast_to(u, (8, lanes))
-
     u = jnp.concatenate([u_ref[...]] * 2, axis=1)
     step = 2 * lanes
     for k in range(high):
@@ -231,30 +226,37 @@
             peak = jnp.max(jnp.max(value, axis=0), axis=0, keepdims=True)
             total = jnp.sum(jnp.sum(jnp.exp2(value - peak), axis=0), axis=0, keepdims=True)
             l_ref[0, k : k + 1, i * step : (i + 1) * step] = peak + jnp.log(total) * LOG2E
-    whole = l_ref[0]
-    for k in range(1, copies):
-        l_ref[k] = whole
-
-
-def whole_rows_kernel(log_weight, place_ref, pieces_ref, parts_ref, a_ref, u_ref, l_ref):
-    depth, blocks, high, width = pieces_ref.shape
+    copy_out(l_ref)
+
+
+def whole_rows_kernel(log_weight, pieces_ref, parts_ref, a_ref, u_ref, l_ref, pieces, arrived):
+    depth, blocks, high, width = pieces.shape
     n = width // YS
+    copies = [pltpu.make_async_copy(pieces_ref.at[z], pieces.at[z], arrived.at[z]) for z in range(depth)]
+    for copy in copies:
+        copy.start()
     v = log_weight - parts_ref[...]
-    c = place_ref[3]
+    v = jnp.concatenate([v[k, y : y + 1] for y in range(YS) for k in range(blocks)], axis=1)
     for z in range(depth):
-        to = pl.ds(pl.multiple_of(jnp.where(c == 0, z, depth - 1 - z) * high, high), high)
-        for y in range(YS):
-            for k in range(blocks):
-                at = (y * blocks + k) * n
-                a_ref[to, at : at + n] = pieces_ref[z, k, :, y * n : (y + 1) * n]
-    v = jnp.concatenate([v[k, y : y + 1] for y in range(YS) for k in range(blocks)], axis=1)
-    half_steps(log_weight, a_ref, v, u_ref, l_ref)
+        copies[z].wait()
+        value = [pieces[z, k, :, y * n : (y + 1) * n] for y in range(YS) for k in range(blocks)]
+        value = jnp.concatenate(value, axis=1)
+        at = pl.ds(z * high, high)
+        a_ref[at, :] = value
+        row_step(log_weight, value + v, u_ref, at)
+    column_step(a_ref, u_ref, l_ref)
 
 
 def next_kernel(log_weight, a_ref, parts_ref, u_ref, l_ref):
-    v = log_weight - joined(parts_ref[...])
-    v = jnp.concatenate([v[k : k + 1] for k in range(v.shape[0])], axis=1)
-    half_steps(log_weight, a_ref, v, u_ref, l_ref)
+    v = row_of(parts_ref, log_weight)
+
+    @pl.loop(0, a_ref.shape[0] // 8, step=2)
+    def _(base):
+        for i in range(2):
+            at = pl.ds(pl.multiple_of((base + i) * 8, 8), 8)
+            row_step(log_weight, a_ref[at, :] + v, u_ref, at)
+
+    column_step(a_ref, u_ref, l_ref)
 
 
 def target_kernel(
@@ -356,18 +358,15 @@
     high = rows // depth
     part = pl.pallas_call(
         first_rows_kernel,
-        out_shape=jax.ShapeDtypeStruct((group, 2 * high, wide), f32),
+        out_shape=jax.ShapeDtypeStruct((group, high, wide + rows), f32),
         in_specs=[VMEM],
         out_specs=VMEM,
         scratch_shapes=[pltpu.VMEM((1, 1, few), f32)],
         compiler_params=PARAMS,
     )(own)
     part = swap(part, x_groups)
-    everything, pieces = lax.optimization_barrier((everything, part[:, :high]))
-    ring_groups = [
-        [n * depth + (depth - 1 - d if n % CORES else d) for d in range(depth)] for n in range(YS * group)
-    ]
-    gathered = lax.all_gather(pieces, ("noise", "dp"), axis_index_groups=ring_groups)
+    everything, pieces = lax.optimization_barrier((everything, part[:, :, :wide]))
+    gathered = lax.all_gather(pieces, "dp")
     z_groups = [
         [((y * group) + k) * depth + d for y in range(YS) for d in range(depth)] for k in range(group)
     ]
@@ -383,7 +382,7 @@
             )(own, part)
             part = swap(part, x_groups)
         part = pl.pallas_call(
-            functools.partial(columns_kernel, log_weight, 0 if step > 0 else high),
+            functools.partial(columns_kernel, log_weight, 0 if step > 0 else wide),
             out_shape=jax.ShapeDtypeStruct((YS * depth, YS, rows), f32),
             in_specs=[VMEM] * 2,
             out_specs=VMEM,
@@ -412,10 +411,14 @@
             a, u, part = pl.pallas_call(
                 functools.partial(whole_rows_kernel, log_weight),
                 out_shape=[jax.ShapeDtypeStruct((rows, tokens), f32), u_shape, l_shape],
-                in_specs=[SMEM] + [VMEM] * 2,
+                in_specs=[pl.BlockSpec(memory_space=pl.ANY), VMEM],
                 out_specs=[VMEM] * 3,
+                scratch_shapes=[
+                    pltpu.VMEM((depth, group, high, wide), f32),
+                    pltpu.SemaphoreType.DMA((depth,)),
+                ],
                 compiler_params=PARAMS,
-            )(place, gathered, part)
+            )(gathered, part)
         else:
             u, part = pl.pallas_call(
                 functools.partial(next_kernel, log_weight),

time: 249 us -> 252 us (1.012)
  Pallas kernels: 15.8 us -> 19.5 us
    pallas_call x1, Pallas kernels: 3.64 us -> 7.34 us  [on_device(): pl.pallas_call(functools.partial(whole_rows_kernel, log_weight), out_shap...]
  transfers between devices with their start and end apart: 16 -> 16, of which waited for: 11 -> 10; matrix products, arithmetic and copies ran while one was open for 1% -> 1% of each run, Pallas kernels for 1% -> 1%
where the time goes in v11:
time: 252 us; the launch traced here: 251 us
  blocking collectives  124 us (49%)
  starting transfers between devices  62.5 us (25%)
  waiting for transfers between devices  26.9 us (11%)
  Pallas kernels  19.5 us (8%)
  between operations  14.3 us (6%)
  local copies, waits for them, and re-layouts  4.29 us (2%)
    all_to_all x2, blocking collectives, on_device(): lax.all_to_all(part, ('noise', 'dp'), 0, 0, axis_index_groups=z_groups, t...  48.7 us
    all_to_all x2, blocking collectives, on_device(): part = lax.all_to_all(part, 'noise', 0, 0, tiled=True)  40.1 us
    ppermute x8, starting transfers between devices, send_z(): return lax.ppermute(value, ('noise', 'dp'), pairs)  35.1 us
    all_to_all x3, blocking collectives, swap(): lax.all_to_all(value, 'noise', 0, 0, axis_index_groups=groups, tiled=True)  34.9 us
    ppermute x8, waiting for transfers between devices, send_z(): return lax.ppermute(value, ('noise', 'dp'), pairs)  23.3 us
    ppermute x2, starting transfers between devices, to_other_core(): lax.ppermute(value, 'noise', noise_pairs(lambda y, x, c: (y, x, 1 - c)))  11.5 us
    ppermute x2, starting transfers between devices, swap_y(): lax.ppermute(value, 'noise', noise_pairs(lambda y, x, c: (y ^ by[c], x, c)))  9.17 us
    pallas_call x1, Pallas kernels, on_device(): pl.pallas_call(functools.partial(whole_rows_kernel, log_weight), out_shap...  7.34 us
  transfers between devices with their start and end apart: 16, of which 10 were waited for; matrix products, arithmetic and copies ran while one was open for 1% of the time, Pallas kernels for 1%

profile of v11, /device:TPU:1, one launch (start us, length us, event | category | flops | bytes accessed | tf_op | source)
XLA Modules:
  0.0 251.3 jit_solution(15950267554505721926)
XLA Ops:
  7.2 0.0 all-gather.4.cloned.1.call-start
  7.2 5.5 %collective-permute-start.1 = (bf16[128,1024]{1,0:T(8,128)(2,1)}, bf16[128,1024]{1,0:T(8,128)(2,1)S(1)}, u32[]{:S(2)}, u32[]{:S(2)}) collective-permute-start(bf16[128,1024]{1,0:T(8,128)(2,1)} %param.3), channel_id=1, source_target_pairs={{0,128},{16,400},{32,160},{48,432},{64,192},{80,464},{96,224},{112... | collective-permute-start | bytes 786440 | tf_op jit(solution)/shard_map/ppermute | solution.py:44
  12.7 4.4 %collective-permute-start = (bf16[128,1024]{1,0:T(8,128)(2,1)}, bf16[128,1024]{1,0:T(8,128)(2,1)S(1)}, u32[]{:S(2)}, u32[]{:S(2)}) collective-permute-start(bf16[128,1024]{1,0:T(8,128)(2,1)} %param.2), channel_id=1, source_target_pairs={{0,32},{16,112},{32,0},{48,80},{64,96},{80,48},{96,64},{112,16},{1... | collective-permute-start | bytes 786440 | tf_op jit(solution)/shard_map/ppermute | solution.py:40
  17.1 1.0 dynamic_update_slice.14
  18.1 1.0 dynamic_update_slice.12
  19.1 0.0 collective-permute-done.1
  19.1 2.1 collective-permute-done
  21.2 2.2 collective-permute-start.3
  23.5 4.9 %collective-permute-start.2 = (bf16[256,1024]{1,0:T(8,128)(2,1)S(1)}, bf16[256,1024]{1,0:T(8,128)(2,1)S(1)}, u32[]{:S(2)}, u32[]{:S(2)}) collective-permute-start(bf16[256,1024]{1,0:T(8,128)(2,1)S(1)} %constant_dynamic-update-slice_fusion.1.refs_0_), channel_id=1, source_target_pairs={{0,16},{16,0},{32,48},{48,32},{64,80},{80,64},{96,112},{112,96},{1... | collective-permute-start | bytes 1572872 | tf_op jit(solution)/shard_map/ppermute | solution.py:32
  28.4 3.7 %collective-permute-start.5 = (bf16[256,1024]{1,0:T(8,128)(2,1)S(1)}, bf16[256,1024]{1,0:T(8,128)(2,1)S(1)}, u32[]{:S(2)}, u32[]{:S(2)}) collective-permute-start(bf16[256,1024]{1,0:T(8,128)(2,1)S(1)} %constant_dynamic-update-slice_fusion.refs_4_), channel_id=1, source_target_pairs={{0,384},{16,144},{32,416},{48,176},{64,448},{80,208},{96,480},{112... | collective-permute-start | bytes 1572872 | tf_op jit(solution)/shard_map/ppermute | solution.py:44
  32.1 0.0 collective-permute-done.3.refs_1_
  32.1 6.6 %collective-permute-start.4 = (bf16[256,1024]{1,0:T(8,128)(2,1)S(1)}, bf16[256,1024]{1,0:T(8,128)(2,1)S(1)}, u32[]{:S(2)}, u32[]{:S(2)}) collective-permute-start(bf16[256,1024]{1,0:T(8,128)(2,1)S(1)} %collective-permute-done.3.refs_1_), channel_id=1, source_target_pairs={{0,16},{16,0},{32,48},{48,32},{64,80},{80,64},{96,112},{112,96},{1... | collective-permute-start | bytes 1572872 | tf_op jit(solution)/shard_map/ppermute | solution.py:32
  38.7 0.0 collective-permute-done.2.refs_2_
  38.7 0.2 collective-permute-done.5.refs_5_
  38.9 1.3 collective-permute-done.4.refs_3_
  40.2 0.0 all-gather.4.cloned.1.call-update
  40.2 0.0 all-gather.6.cloned.1.call-start
  40.3 0.1 pad_add_fusion.place_ref
  40.4 2.4 shard_map.49
  42.8 8.4 %collective-permute-start.6 = (f32[8,64,512]{2,1,0:T(8,128)S(1)}, f32[8,64,512]{2,1,0:T(8,128)S(1)}, u32[]{:S(2)}, u32[]{:S(2)}) collective-permute-start(f32[8,64,512]{2,1,0:T(8,128)S(1)} %get-tuple-element.32), channel_id=1, source_target_pairs={{0,1},{1,0},{2,3},{3,2},{4,5},{5,4},{6,7},{7,6},{8,9},{9,8},{10,11... | collective-permute-start | bytes 3145736 | tf_op jit(solution)/shard_map/ppermute | solution.py:59
  51.2 12.6 %collective-permute-done.6.got = f32[8,64,512]{2,1,0:T(8,128)S(1)} collective-permute-done((f32[8,64,512]{2,1,0:T(8,128)S(1)}, f32[8,64,512]{2,1,0:T(8,128)S(1)}, u32[]{:S(2)}, u32[]{:S(2)}) %collective-permute-start.6) | collective-permute-done | bytes 1048608 | tf_op jit(solution)/shard_map/ppermute | solution.py:59
  63.8 0.1 shard_map.50
  63.9 3.7 %collective-permute-start.7 = (f32[64,512]{1,0:T(8,128)S(1)}, f32[64,512]{1,0:T(8,128)S(1)}, u32[]{:S(2)}, u32[]{:S(2)}) collective-permute-start(f32[64,512]{1,0:T(8,128)S(1)} %get-tuple-element.34), channel_id=1, source_target_pairs={{0,2},{1,3},{2,4},{3,5},{4,6},{5,7},{6,8},{7,9},{8,10},{9,11},{10,... | collective-permute-start | bytes 393224 | tf_op jit(solution)/shard_map/ppermute | solution.py:59
  67.6 2.5 collective-permute-start.11
  70.1 0.8 collective-permute-done.7
  70.9 4.5 %collective-permute-start.8 = (f32[64,512]{1,0:T(8,128)S(1)}, f32[64,512]{1,0:T(8,128)S(1)}, u32[]{:S(2)}, u32[]{:S(2)}) collective-permute-start(f32[64,512]{1,0:T(8,128)S(1)} %bitcast_add_fusion.4), channel_id=1, source_target_pairs={{0,2},{1,3},{2,4},{3,5},{4,6},{5,7},{6,8},{7,9},{8,10},{9,11},{10,... | collective-permute-start | bytes 393224 | tf_op jit(solution)/shard_map/ppermute | solution.py:59
  75.4 0.1 collective-permute-done.11
  75.5 2.0 collective-permute-start.12
  77.5 0.1 collective-permute-done.8
  77.6 6.0 %collective-permute-start.9 = (f32[64,512]{1,0:T(8,128)S(1)}, f32[64,512]{1,0:T(8,128)S(1)}, u32[]{:S(2)}, u32[]{:S(2)}) collective-permute-start(f32[64,512]{1,0:T(8,128)S(1)} %bitcast_add_fusion.3), channel_id=1, source_target_pairs={{0,2},{1,3},{2,4},{3,5},{4,6},{5,7},{6,8},{7,9},{8,10},{9,11},{10,... | collective-permute-start | bytes 393224 | tf_op jit(solution)/shard_map/ppermute | solution.py:59
  83.7 1.0 collective-permute-done.12
  84.6 1.9 collective-permute-start.13
  86.6 3.2 %collective-permute-done.9 = f32[64,512]{1,0:T(8,128)S(1)} collective-permute-done((f32[64,512]{1,0:T(8,128)S(1)}, f32[64,512]{1,0:T(8,128)S(1)}, u32[]{:S(2)}, u32[]{:S(2)}) %collective-permute-start.9) | collective-permute-done | bytes 131104 | tf_op jit(solution)/shard_map/ppermute | solution.py:59
  89.8 6.1 %collective-permute-start.10 = (f32[64,512]{1,0:T(8,128)S(1)}, f32[64,512]{1,0:T(8,128)S(1)}, u32[]{:S(2)}, u32[]{:S(2)}) collective-permute-start(f32[64,512]{1,0:T(8,128)S(1)} %bitcast_add_fusion.2), channel_id=1, source_target_pairs={{0,2},{1,3},{2,4},{3,5},{4,6},{5,7},{6,8},{7,9},{8,10},{9,11},{10,... | collective-permute-start | bytes 393224 | tf_op jit(solution)/shard_map/ppermute | solution.py:59
  95.9 0.0 collective-permute-done.13
  95.9 5.6 %collective-permute-done.10 = f32[64,512]{1,0:T(8,128)S(1)} collective-permute-done((f32[64,512]{1,0:T(8,128)S(1)}, f32[64,512]{1,0:T(8,128)S(1)}, u32[]{:S(2)}, u32[]{:S(2)}) %collective-permute-start.10) | collective-permute-done | bytes 131104 | tf_op jit(solution)/shard_map/ppermute | solution.py:59
  101.5 0.2 shard_map.51
  101.7 14.4 %all_to_all.35.parts_ref = f32[8,8,640]{2,1,0:T(8,128)S(1)} all-to-all(f32[8,8,640]{2,1,0:T(8,128)S(1)} %shard_map.51), channel_id=1, replica_groups={{0,16,32,48,64,80,96,112},{128,144,160,176,192,208,224,240},{256,272,28..., dimensions={0} | all-to-all | bytes 327680 | tf_op jit(solution)/shard_map/all_to_all | solution.py:306
  116.1 0.7 slice.24
  116.7 0.0 all-gather.4.cloned.1.call-done.y_ref
  116.7 0.0 all-gather.6.cloned.1.call-update
  116.8 0.2 shard_map.52
  116.9 27.2 %all_to_all.36.parts_ref = f32[64,4,128]{2,1,0:T(4,128)S(1)} all-to-all(f32[64,4,128]{2,1,0:T(4,128)S(1)} %shard_map.52), channel_id=1, replica_groups={{0,1,2,3,4,5,6,7,8,9,10,11,12,13,14,15,128,129,130,131,132,133,134,135,..., dimensions={0} | all-to-all | bytes 262144 | tf_op jit(solution)/shard_map/all_to_all | solution.py:392
  144.1 0.3 shard_map.53
  144.4 10.9 %all_to_all.37.parts_ref = f32[8,1,64]{2,1,0:T(1,128)S(1)} all-to-all(f32[8,1,64]{2,1,0:T(1,128)S(1)} %shard_map.53), channel_id=1, replica_groups={{0,16,32,48,64,80,96,112},{128,144,160,176,192,208,224,240},{256,272,28..., dimensions={0} | all-to-all | bytes 4096 | tf_op jit(solution)/shard_map/all_to_all | solution.py:306
  155.3 0.2 shard_map.54
  155.5 21.6 %all_to_all.38.parts_ref = f32[64,4,128]{2,1,0:T(4,128)S(1)} all-to-all(f32[64,4,128]{2,1,0:T(4,128)S(1)} %shard_map.54), channel_id=1, replica_groups={{0,1,2,3,4,5,6,7,8,9,10,11,12,13,14,15,128,129,130,131,132,133,134,135,..., dimensions={0} | all-to-all | bytes 262144 | tf_op jit(solution)/shard_map/all_to_all | solution.py:392
  177.1 0.1 shard_map.55
  177.2 9.6 %all_to_all.39.parts_ref = f32[8,4,128]{2,1,0:T(4,128)S(1)} all-to-all(f32[8,4,128]{2,1,0:T(4,128)S(1)} %shard_map.55), channel_id=1, replica_groups={{0,16,32,48,64,80,96,112},{128,144,160,176,192,208,224,240},{256,272,28..., dimensions={0} | all-to-all | bytes 32768 | tf_op jit(solution)/shard_map/all_to_all | solution.py:306
  186.8 0.0 all-gather.6.cloned.1.call-done
  186.8 0.0 copy-start
  186.8 1.6 copy-done
  188.4 7.3 %shard_map.56 = (f32[128,4096]{1,0:T(8,128)S(1)}, f32[128,128]{1,0:T(8,128)}, f32[32,8,512]{2,1,0:T(8,128)S(1)}) custom-call(f32[16,8,8,512]{3,2,1,0:T(8,128)S(1)} %bitcast.17, f32[8,4,128]{2,1,0:T(4,128)S(1)} %all_to_all.39.parts_ref), custom_call_target="tpu_custom_call" | custom-call | tf_op jit(solution)/shard_map/pallas_call | solution.py:411
  195.7 24.8 %all_to_all.40.parts_ref = f32[32,8,512]{2,1,0:T(8,128)S(1)} all-to-all(f32[32,8,512]{2,1,0:T(8,128)S(1)} %get-tuple-element.40), channel_id=1, replica_groups=mesh['noise'=32,'dp'=16] {'noise'}, dimensions={0} | all-to-all | bytes 1048576 | tf_op jit(solution)/shard_map/all_to_all | solution.py:430
  220.6 2.5 shard_map.57
  223.1 15.2 %all_to_all.41.parts_ref = f32[32,8,512]{2,1,0:T(8,128)S(1)} all-to-all(f32[32,8,512]{2,1,0:T(8,128)S(1)} %get-tuple-element.42), channel_id=1, replica_groups=mesh['noise'=32,'dp'=16] {'noise'}, dimensions={0} | all-to-all | bytes 1048576 | tf_op jit(solution)/shard_map/all_to_all | solution.py:430
  238.3 6.2 %shard_map.58 = (bf16[128,1024]{1,0:T(8,128)(2,1)}, f32[1,128]{1,0:T(1,128)}, f32[1,256]{1,0:T(1,128)}) custom-call(s32[4]{0:T(128)S(1)} %pad_add_fusion.place_ref, f32[128,4096]{1,0:T(8,128)S(1)} %get-tuple-element.39.a_ref, f32[128,128]{1,0:T(8,128)S(1)} %get-tuple-element.41.u_ref, f32[32,8,512]{2,1,0:T(8,128)S(1)} %all_to_all.41.parts_ref, ...), custom_call_target="tpu_custom_call" | custom-call | tf_op jit(solution)/shard_map/pallas_call | solution.py:433
  (8 shorter events, 0.2 us)
Async XLA Ops:
  7.2 109.6 %all-gather.4.cloned.1.call-start = ((), (), s32[]{:S(2)}) async-start(), calls=%async_computation.7 | async-start | bytes 8650752 | tf_op jit(solution)/shard_map/all_gather | solution.py:315
  7.2 11.9 %collective-permute-start.1 = (bf16[128,1024]{1,0:T(8,128)(2,1)}, bf16[128,1024]{1,0:T(8,128)(2,1)S(1)}, u32[]{:S(2)}, u32[]{:S(2)}) collective-permute-start(bf16[128,1024]{1,0:T(8,128)(2,1)} %param.3), channel_id=1, source_target_pairs={{0,128},{16,400},{32,160},{48,432},{64,192},{80,464},{96,224},{112... | collective-permute-start | bytes 786440 | tf_op jit(solution)/shard_map/ppermute | solution.py:44
  12.7 8.5 %collective-permute-start = (bf16[128,1024]{1,0:T(8,128)(2,1)}, bf16[128,1024]{1,0:T(8,128)(2,1)S(1)}, u32[]{:S(2)}, u32[]{:S(2)}) collective-permute-start(bf16[128,1024]{1,0:T(8,128)(2,1)} %param.2), channel_id=1, source_target_pairs={{0,32},{16,112},{32,0},{48,80},{64,96},{80,48},{96,64},{112,16},{1... | collective-permute-start | bytes 786440 | tf_op jit(solution)/shard_map/ppermute | solution.py:40
  21.2 10.8 %collective-permute-start.3 = (bf16[256,1024]{1,0:T(8,128)(2,1)S(1)}, bf16[256,1024]{1,0:T(8,128)(2,1)S(1)}, u32[]{:S(2)}, u32[]{:S(2)}) collective-permute-start(bf16[256,1024]{1,0:T(8,128)(2,1)S(1)} %constant_dynamic-update-slice_fusion.1.refs_0_), channel_id=1, source_target_pairs={{0,96},{16,48},{32,64},{48,16},{64,32},{80,112},{96,0},{112,80},{1... | collective-permute-start | bytes 1572872 | tf_op jit(solution)/shard_map/ppermute | solution.py:40
  23.5 15.2 %collective-permute-start.2 = (bf16[256,1024]{1,0:T(8,128)(2,1)S(1)}, bf16[256,1024]{1,0:T(8,128)(2,1)S(1)}, u32[]{:S(2)}, u32[]{:S(2)}) collective-permute-start(bf16[256,1024]{1,0:T(8,128)(2,1)S(1)} %constant_dynamic-update-slice_fusion.1.refs_0_), channel_id=1, source_target_pairs={{0,16},{16,0},{32,48},{48,32},{64,80},{80,64},{96,112},{112,96},{1... | collective-permute-start | bytes 1572872 | tf_op jit(solution)/shard_map/ppermute | solution.py:32
  28.4 10.6 %collective-permute-start.5 = (bf16[256,1024]{1,0:T(8,128)(2,1)S(1)}, bf16[256,1024]{1,0:T(8,128)(2,1)S(1)}, u32[]{:S(2)}, u32[]{:S(2)}) collective-permute-start(bf16[256,1024]{1,0:T(8,128)(2,1)S(1)} %constant_dynamic-update-slice_fusion.refs_4_), channel_id=1, source_target_pairs={{0,384},{16,144},{32,416},{48,176},{64,448},{80,208},{96,480},{112... | collective-permute-start | bytes 1572872 | tf_op jit(solution)/shard_map/ppermute | solution.py:44
  32.1 8.1 %collective-permute-start.4 = (bf16[256,1024]{1,0:T(8,128)(2,1)S(1)}, bf16[256,1024]{1,0:T(8,128)(2,1)S(1)}, u32[]{:S(2)}, u32[]{:S(2)}) collective-permute-start(bf16[256,1024]{1,0:T(8,128)(2,1)S(1)} %collective-permute-done.3.refs_1_), channel_id=1, source_target_pairs={{0,16},{16,0},{32,48},{48,32},{64,80},{80,64},{96,112},{112,96},{1... | collective-permute-start | bytes 1572872 | tf_op jit(solution)/shard_map/ppermute | solution.py:32
  40.2 146.6 %all-gather.6.cloned.1.call-start = ((), (), s32[]{:S(2)}) async-start(), calls=%async_computation.8 | async-start | bytes 2228224 | tf_op jit(solution)/shard_map/all_gather | solution.py:369
  42.8 21.0 %collective-permute-start.6 = (f32[8,64,512]{2,1,0:T(8,128)S(1)}, f32[8,64,512]{2,1,0:T(8,128)S(1)}, u32[]{:S(2)}, u32[]{:S(2)}) collective-permute-start(f32[8,64,512]{2,1,0:T(8,128)S(1)} %get-tuple-element.32), channel_id=1, source_target_pairs={{0,1},{1,0},{2,3},{3,2},{4,5},{5,4},{6,7},{7,6},{8,9},{9,8},{10,11... | collective-permute-start | bytes 3145736 | tf_op jit(solution)/shard_map/ppermute | solution.py:59
  63.9 7.0 %collective-permute-start.7 = (f32[64,512]{1,0:T(8,128)S(1)}, f32[64,512]{1,0:T(8,128)S(1)}, u32[]{:S(2)}, u32[]{:S(2)}) collective-permute-start(f32[64,512]{1,0:T(8,128)S(1)} %get-tuple-element.34), channel_id=1, source_target_pairs={{0,2},{1,3},{2,4},{3,5},{4,6},{5,7},{6,8},{7,9},{8,10},{9,11},{10,... | collective-permute-start | bytes 393224 | tf_op jit(solution)/shard_map/ppermute | solution.py:59
  67.6 7.9 %collective-permute-start.11 = (f32[64,512]{1,0:T(8,128)S(1)}, f32[64,512]{1,0:T(8,128)S(1)}, u32[]{:S(2)}, u32[]{:S(2)}) collective-permute-start(f32[64,512]{1,0:T(8,128)S(1)} %get-tuple-element.36), channel_id=1, source_target_pairs={{0,14},{1,15},{2,0},{3,1},{4,2},{5,3},{6,4},{7,5},{8,6},{9,7},{10,... | collective-permute-start | bytes 393224 | tf_op jit(solution)/shard_map/ppermute | solution.py:59
  70.9 6.7 %collective-permute-start.8 = (f32[64,512]{1,0:T(8,128)S(1)}, f32[64,512]{1,0:T(8,128)S(1)}, u32[]{:S(2)}, u32[]{:S(2)}) collective-permute-start(f32[64,512]{1,0:T(8,128)S(1)} %bitcast_add_fusion.4), channel_id=1, source_target_pairs={{0,2},{1,3},{2,4},{3,5},{4,6},{5,7},{6,8},{7,9},{8,10},{9,11},{10,... | collective-permute-start | bytes 393224 | tf_op jit(solution)/shard_map/ppermute | solution.py:59
  75.5 9.1 %collective-permute-start.12 = (f32[64,512]{1,0:T(8,128)S(1)}, f32[64,512]{1,0:T(8,128)S(1)}, u32[]{:S(2)}, u32[]{:S(2)}) collective-permute-start(f32[64,512]{1,0:T(8,128)S(1)} %bitcast_add_fusion.1), channel_id=1, source_target_pairs={{0,14},{1,15},{2,0},{3,1},{4,2},{5,3},{6,4},{7,5},{8,6},{9,7},{10,... | collective-permute-start | bytes 393224 | tf_op jit(solution)/shard_map/ppermute | solution.py:59
  77.6 12.1 %collective-permute-start.9 = (f32[64,512]{1,0:T(8,128)S(1)}, f32[64,512]{1,0:T(8,128)S(1)}, u32[]{:S(2)}, u32[]{:S(2)}) collective-permute-start(f32[64,512]{1,0:T(8,128)S(1)} %bitcast_add_fusion.3), channel_id=1, source_target_pairs={{0,2},{1,3},{2,4},{3,5},{4,6},{5,7},{6,8},{7,9},{8,10},{9,11},{10,... | collective-permute-start | bytes 393224 | tf_op jit(solution)/shard_map/ppermute | solution.py:59
  84.6 11.2 %collective-permute-start.13 = (f32[64,512]{1,0:T(8,128)S(1)}, f32[64,512]{1,0:T(8,128)S(1)}, u32[]{:S(2)}, u32[]{:S(2)}) collective-permute-start(f32[64,512]{1,0:T(8,128)S(1)} %bitcast_add_fusion), channel_id=1, source_target_pairs={{0,14},{1,15},{2,0},{3,1},{4,2},{5,3},{6,4},{7,5},{8,6},{9,7},{10,... | collective-permute-start | bytes 393224 | tf_op jit(solution)/shard_map/ppermute | solution.py:59
  89.8 11.7 %collective-permute-start.10 = (f32[64,512]{1,0:T(8,128)S(1)}, f32[64,512]{1,0:T(8,128)S(1)}, u32[]{:S(2)}, u32[]{:S(2)}) collective-permute-start(f32[64,512]{1,0:T(8,128)S(1)} %bitcast_add_fusion.2), channel_id=1, source_target_pairs={{0,2},{1,3},{2,4},{3,5},{4,6},{5,7},{6,8},{7,9},{8,10},{9,11},{10,... | collective-permute-start | bytes 393224 | tf_op jit(solution)/shard_map/ppermute | solution.py:59
  186.8 1.6 copy-start
Sparse Core Ops, SparseCore 0:
  40.4 68.5 all-gather.3
  116.9 69.3 all-gather.5

commit v12 on v10

--- a/solution.py
+++ b/solution.py
@@ -166,21 +166,21 @@
 
 
 def first_rows_kernel(a_ref, out_ref, sums):
-    copies, both, width = out_ref.shape
-    high, n = both // 2, a_ref.shape[0]
+    copies, high, width = out_ref.shape
+    n, columns = a_ref.shape
     row_sums(a_ref, None, sums, n)
     for k in range(copies):
-        out_ref[k, :high, :] = a_ref[k * high : (k + 1) * high, :]
-        out_ref[k, high:, :] = jnp.zeros((high, width), jnp.float32)
-        out_ref[k, high : high + 1, :n] = sums[0]
+        out_ref[k, :, :columns] = a_ref[k * high : (k + 1) * high, :]
+        out_ref[k, :, columns:] = jnp.zeros((high, width - columns), jnp.float32)
+        out_ref[k, :1, columns : columns + n] = sums[0]
 
 
 def rows_kernel(log_weight, a_ref, parts_ref, out_ref):
     row_sums(a_ref, row_of(parts_ref, log_weight), out_ref, out_ref.shape[2])
 
 
-def columns_kernel(log_weight, under, a_ref, parts_ref, out_ref, shifted):
-    parts = parts_ref[:, under : under + 1, : a_ref.shape[0]]
+def columns_kernel(log_weight, beside, a_ref, parts_ref, out_ref, shifted):
+    parts = parts_ref[:, :1, beside : beside + a_ref.shape[0]]
     u = log_weight - joined(parts)
     blocks, n = u.shape
     width = a_ref.shape[1]
@@ -222,31 +222,27 @@
             u = log_weight - (peak + jnp.log(total) * LOG2E)
             u_ref[at, :] = jnp.broadcast_to(u, (8, lanes))
 
-    u = jnp.concatenate([u_ref[...]] * 2, axis=1)
-    step = 2 * lanes
     for k in range(high):
-        for i in range(width // step):
-            at = k * width + i * step
-            value = (a_ref[:, at : at + step] + u).reshape(rows // 8, 8, step)
-            peak = jnp.max(jnp.max(value, axis=0), axis=0, keepdims=True)
-            total = jnp.sum(jnp.sum(jnp.exp2(value - peak), axis=0), axis=0, keepdims=True)
-            l_ref[0, k : k + 1, i * step : (i + 1) * step] = peak + jnp.log(total) * LOG2E
+        for i in range(width // lanes):
+            at = pl.ds(k * width + i * lanes, lanes)
+            value = a_ref[:, at] + u_ref[...]
+            peak = jnp.max(value, axis=0, keepdims=True)
+            total = jnp.sum(jnp.exp2(value - peak), axis=0, keepdims=True)
+            l_ref[0, k : k + 1, i * lanes : (i + 1) * lanes] = peak + jnp.log(total) * LOG2E
     whole = l_ref[0]
     for k in range(1, copies):
         l_ref[k] = whole
 
 
-def whole_rows_kernel(log_weight, place_ref, pieces_ref, parts_ref, a_ref, u_ref, l_ref):
+def whole_rows_kernel(log_weight, pieces_ref, parts_ref, a_ref, u_ref, l_ref):
     depth, blocks, high, width = pieces_ref.shape
     n = width // YS
     v = log_weight - parts_ref[...]
-    c = place_ref[3]
     for z in range(depth):
-        to = pl.ds(pl.multiple_of(jnp.where(c == 0, z, depth - 1 - z) * high, high), high)
         for y in range(YS):
             for k in range(blocks):
                 at = (y * blocks + k) * n
-                a_ref[to, at : at + n] = pieces_ref[z, k, :, y * n : (y + 1) * n]
+                a_ref[z * high : (z + 1) * high, at : at + n] = pieces_ref[z, k, :, y * n : (y + 1) * n]
     v = jnp.concatenate([v[k, y : y + 1] for y in range(YS) for k in range(blocks)], axis=1)
     half_steps(log_weight, a_ref, v, u_ref, l_ref)
 
@@ -356,18 +352,15 @@
     high = rows // depth
     part = pl.pallas_call(
         first_rows_kernel,
-        out_shape=jax.ShapeDtypeStruct((group, 2 * high, wide), f32),
+        out_shape=jax.ShapeDtypeStruct((group, high, wide + rows), f32),
         in_specs=[VMEM],
         out_specs=VMEM,
         scratch_shapes=[pltpu.VMEM((1, 1, few), f32)],
         compiler_params=PARAMS,
     )(own)
     part = swap(part, x_groups)
-    everything, pieces = lax.optimization_barrier((everything, part[:, :high]))
-    ring_groups = [
-        [n * depth + (depth - 1 - d if n % CORES else d) for d in range(depth)] for n in range(YS * group)
-    ]
-    gathered = lax.all_gather(pieces, ("noise", "dp"), axis_index_groups=ring_groups)
+    everything, pieces = lax.optimization_barrier((everything, part[:, :, :wide]))
+    gathered = lax.all_gather(pieces, "dp")
     z_groups = [
         [((y * group) + k) * depth + d for y in range(YS) for d in range(depth)] for k in range(group)
     ]
@@ -383,7 +376,7 @@
             )(own, part)
             part = swap(part, x_groups)
         part = pl.pallas_call(
-            functools.partial(columns_kernel, log_weight, 0 if step > 0 else high),
+            functools.partial(columns_kernel, log_weight, 0 if step > 0 else wide),
             out_shape=jax.ShapeDtypeStruct((YS * depth, YS, rows), f32),
             in_specs=[VMEM] * 2,
             out_specs=VMEM,
@@ -412,10 +405,10 @@
             a, u, part = pl.pallas_call(
                 functools.partial(whole_rows_kernel, log_weight),
                 out_shape=[jax.ShapeDtypeStruct((rows, tokens), f32), u_shape, l_shape],
-                in_specs=[SMEM] + [VMEM] * 2,
+                in_specs=[VMEM] * 2,
                 out_specs=[VMEM] * 3,
                 compiler_params=PARAMS,
-            )(place, gathered, part)
+            )(gathered, part)
         else:
             u, part = pl.pallas_call(
                 functools.partial(next_kernel, log_weight),

time: 249 us -> 247 us (level)
  transfers between devices with their start and end apart: 16 -> 16, of which waited for: 11 -> 10; matrix products, arithmetic and copies ran while one was open for 1% -> 1% of each run, Pallas kernels for 1% -> 1%
where the time goes in v12:
time: 247 us
  blocking collectives  124 us (50%)
  starting transfers between devices  62.5 us (25%)
  waiting for transfers between devices  26.9 us (11%)
  Pallas kernels  14.7 us (6%)
  between operations  14.3 us (6%)
  local copies, waits for them, and re-layouts  4.29 us (2%)
    all_to_all x2, blocking collectives, on_device(): lax.all_to_all(part, ('noise', 'dp'), 0, 0, axis_index_groups=z_groups, t...  48.7 us
    all_to_all x2, blocking collectives, on_device(): part = lax.all_to_all(part, 'noise', 0, 0, tiled=True)  40 us
    ppermute x8, starting transfers between devices, send_z(): return lax.ppermute(value, ('noise', 'dp'), pairs)  35.1 us
    all_to_all x3, blocking collectives, swap(): lax.all_to_all(value, 'noise', 0, 0, axis_index_groups=groups, tiled=True)  34.9 us
    ppermute x8, waiting for transfers between devices, send_z(): return lax.ppermute(value, ('noise', 'dp'), pairs)  23.3 us
    ppermute x2, starting transfers between devices, to_other_core(): lax.ppermute(value, 'noise', noise_pairs(lambda y, x, c: (y, x, 1 - c)))  11.5 us
    ppermute x2, starting transfers between devices, swap_y(): lax.ppermute(value, 'noise', noise_pairs(lambda y, x, c: (y ^ by[c], x, c)))  9.17 us
    ppermute x2, starting transfers between devices, swap_x(): lax.ppermute(value, 'noise', noise_pairs(lambda y, x, c: (y, x ^ by[c], c)))  6.59 us
  transfers between devices with their start and end apart: 16, of which 10 were waited for; matrix products, arithmetic and copies ran while one was open for 1% of the time, Pallas kernels for 1%

profile of v12, /device:TPU:1, one launch (start us, length us, event | category | flops | bytes accessed | tf_op | source)
XLA Modules:
  0.0 246.6 jit_solution(8201064011146109280)
XLA Ops:
  7.2 0.0 all-gather.4.cloned.1.call-start
  7.2 5.5 %collective-permute-start.1 = (bf16[128,1024]{1,0:T(8,128)(2,1)}, bf16[128,1024]{1,0:T(8,128)(2,1)S(1)}, u32[]{:S(2)}, u32[]{:S(2)}) collective-permute-start(bf16[128,1024]{1,0:T(8,128)(2,1)} %param.3), channel_id=1, source_target_pairs={{0,128},{16,400},{32,160},{48,432},{64,192},{80,464},{96,224},{112... | collective-permute-start | bytes 786440 | tf_op jit(solution)/shard_map/ppermute | solution.py:44
  12.7 4.4 %collective-permute-start = (bf16[128,1024]{1,0:T(8,128)(2,1)}, bf16[128,1024]{1,0:T(8,128)(2,1)S(1)}, u32[]{:S(2)}, u32[]{:S(2)}) collective-permute-start(bf16[128,1024]{1,0:T(8,128)(2,1)} %param.2), channel_id=1, source_target_pairs={{0,32},{16,112},{32,0},{48,80},{64,96},{80,48},{96,64},{112,16},{1... | collective-permute-start | bytes 786440 | tf_op jit(solution)/shard_map/ppermute | solution.py:40
  17.1 1.0 dynamic_update_slice.14
  18.1 1.0 dynamic_update_slice.12
  19.1 0.0 collective-permute-done.1
  19.1 2.1 collective-permute-done
  21.2 2.2 collective-permute-start.3
  23.5 4.9 %collective-permute-start.2 = (bf16[256,1024]{1,0:T(8,128)(2,1)S(1)}, bf16[256,1024]{1,0:T(8,128)(2,1)S(1)}, u32[]{:S(2)}, u32[]{:S(2)}) collective-permute-start(bf16[256,1024]{1,0:T(8,128)(2,1)S(1)} %constant_dynamic-update-slice_fusion.1.refs_0_), channel_id=1, source_target_pairs={{0,16},{16,0},{32,48},{48,32},{64,80},{80,64},{96,112},{112,96},{1... | collective-permute-start | bytes 1572872 | tf_op jit(solution)/shard_map/ppermute | solution.py:32
  28.4 3.7 %collective-permute-start.5 = (bf16[256,1024]{1,0:T(8,128)(2,1)S(1)}, bf16[256,1024]{1,0:T(8,128)(2,1)S(1)}, u32[]{:S(2)}, u32[]{:S(2)}) collective-permute-start(bf16[256,1024]{1,0:T(8,128)(2,1)S(1)} %constant_dynamic-update-slice_fusion.refs_4_), channel_id=1, source_target_pairs={{0,384},{16,144},{32,416},{48,176},{64,448},{80,208},{96,480},{112... | collective-permute-start | bytes 1572872 | tf_op jit(solution)/shard_map/ppermute | solution.py:44
  32.1 0.0 collective-permute-done.3.refs_1_
  32.1 6.6 %collective-permute-start.4 = (bf16[256,1024]{1,0:T(8,128)(2,1)S(1)}, bf16[256,1024]{1,0:T(8,128)(2,1)S(1)}, u32[]{:S(2)}, u32[]{:S(2)}) collective-permute-start(bf16[256,1024]{1,0:T(8,128)(2,1)S(1)} %collective-permute-done.3.refs_1_), channel_id=1, source_target_pairs={{0,16},{16,0},{32,48},{48,32},{64,80},{80,64},{96,112},{112,96},{1... | collective-permute-start | bytes 1572872 | tf_op jit(solution)/shard_map/ppermute | solution.py:32
  38.7 0.0 collective-permute-done.2.refs_2_
  38.7 0.2 collective-permute-done.5.refs_5_
  38.9 1.3 collective-permute-done.4.refs_3_
  40.2 0.0 all-gather.4.cloned.1.call-update
  40.2 0.0 all-gather.6.cloned.1.call-start
  40.3 0.1 pad_add_fusion.place_ref
  40.4 2.4 shard_map.49
  42.8 8.4 %collective-permute-start.6 = (f32[8,64,512]{2,1,0:T(8,128)S(1)}, f32[8,64,512]{2,1,0:T(8,128)S(1)}, u32[]{:S(2)}, u32[]{:S(2)}) collective-permute-start(f32[8,64,512]{2,1,0:T(8,128)S(1)} %get-tuple-element.32), channel_id=1, source_target_pairs={{0,1},{1,0},{2,3},{3,2},{4,5},{5,4},{6,7},{7,6},{8,9},{9,8},{10,11... | collective-permute-start | bytes 3145736 | tf_op jit(solution)/shard_map/ppermute | solution.py:59
  51.2 12.6 %collective-permute-done.6.got = f32[8,64,512]{2,1,0:T(8,128)S(1)} collective-permute-done((f32[8,64,512]{2,1,0:T(8,128)S(1)}, f32[8,64,512]{2,1,0:T(8,128)S(1)}, u32[]{:S(2)}, u32[]{:S(2)}) %collective-permute-start.6) | collective-permute-done | bytes 1048608 | tf_op jit(solution)/shard_map/ppermute | solution.py:59
  63.8 0.1 shard_map.50
  63.9 3.7 %collective-permute-start.7 = (f32[64,512]{1,0:T(8,128)S(1)}, f32[64,512]{1,0:T(8,128)S(1)}, u32[]{:S(2)}, u32[]{:S(2)}) collective-permute-start(f32[64,512]{1,0:T(8,128)S(1)} %get-tuple-element.34), channel_id=1, source_target_pairs={{0,2},{1,3},{2,4},{3,5},{4,6},{5,7},{6,8},{7,9},{8,10},{9,11},{10,... | collective-permute-start | bytes 393224 | tf_op jit(solution)/shard_map/ppermute | solution.py:59
  67.6 2.5 %collective-permute-start.11 = (f32[64,512]{1,0:T(8,128)S(1)}, f32[64,512]{1,0:T(8,128)S(1)}, u32[]{:S(2)}, u32[]{:S(2)}) collective-permute-start(f32[64,512]{1,0:T(8,128)S(1)} %get-tuple-element.36), channel_id=1, source_target_pairs={{0,14},{1,15},{2,0},{3,1},{4,2},{5,3},{6,4},{7,5},{8,6},{9,7},{10,... | collective-permute-start | bytes 393224 | tf_op jit(solution)/shard_map/ppermute | solution.py:59
  70.1 0.8 collective-permute-done.7
  70.9 4.5 %collective-permute-start.8 = (f32[64,512]{1,0:T(8,128)S(1)}, f32[64,512]{1,0:T(8,128)S(1)}, u32[]{:S(2)}, u32[]{:S(2)}) collective-permute-start(f32[64,512]{1,0:T(8,128)S(1)} %bitcast_add_fusion.4), channel_id=1, source_target_pairs={{0,2},{1,3},{2,4},{3,5},{4,6},{5,7},{6,8},{7,9},{8,10},{9,11},{10,... | collective-permute-start | bytes 393224 | tf_op jit(solution)/shard_map/ppermute | solution.py:59
  75.4 0.1 collective-permute-done.11
  75.5 2.0 collective-permute-start.12
  77.5 0.1 collective-permute-done.8
  77.6 6.0 %collective-permute-start.9 = (f32[64,512]{1,0:T(8,128)S(1)}, f32[64,512]{1,0:T(8,128)S(1)}, u32[]{:S(2)}, u32[]{:S(2)}) collective-permute-start(f32[64,512]{1,0:T(8,128)S(1)} %bitcast_add_fusion.3), channel_id=1, source_target_pairs={{0,2},{1,3},{2,4},{3,5},{4,6},{5,7},{6,8},{7,9},{8,10},{9,11},{10,... | collective-permute-start | bytes 393224 | tf_op jit(solution)/shard_map/ppermute | solution.py:59
  83.7 1.0 collective-permute-done.12
  84.6 1.9 collective-permute-start.13
  86.6 3.2 %collective-permute-done.9 = f32[64,512]{1,0:T(8,128)S(1)} collective-permute-done((f32[64,512]{1,0:T(8,128)S(1)}, f32[64,512]{1,0:T(8,128)S(1)}, u32[]{:S(2)}, u32[]{:S(2)}) %collective-permute-start.9) | collective-permute-done | bytes 131104 | tf_op jit(solution)/shard_map/ppermute | solution.py:59
  89.8 6.1 %collective-permute-start.10 = (f32[64,512]{1,0:T(8,128)S(1)}, f32[64,512]{1,0:T(8,128)S(1)}, u32[]{:S(2)}, u32[]{:S(2)}) collective-permute-start(f32[64,512]{1,0:T(8,128)S(1)} %bitcast_add_fusion.2), channel_id=1, source_target_pairs={{0,2},{1,3},{2,4},{3,5},{4,6},{5,7},{6,8},{7,9},{8,10},{9,11},{10,... | collective-permute-start | bytes 393224 | tf_op jit(solution)/shard_map/ppermute | solution.py:59
  95.9 0.0 collective-permute-done.13
  95.9 5.6 %collective-permute-done.10 = f32[64,512]{1,0:T(8,128)S(1)} collective-permute-done((f32[64,512]{1,0:T(8,128)S(1)}, f32[64,512]{1,0:T(8,128)S(1)}, u32[]{:S(2)}, u32[]{:S(2)}) %collective-permute-start.10) | collective-permute-done | bytes 131104 | tf_op jit(solution)/shard_map/ppermute | solution.py:59
  101.5 0.2 shard_map.51
  101.7 14.4 %all_to_all.35.parts_ref = f32[8,8,640]{2,1,0:T(8,128)S(1)} all-to-all(f32[8,8,640]{2,1,0:T(8,128)S(1)} %shard_map.51), channel_id=1, replica_groups={{0,16,32,48,64,80,96,112},{128,144,160,176,192,208,224,240},{256,272,28..., dimensions={0} | all-to-all | bytes 327680 | tf_op jit(solution)/shard_map/all_to_all | solution.py:300
  116.1 0.7 slice.24
  116.7 0.0 all-gather.4.cloned.1.call-done.y_ref
  116.7 0.0 all-gather.6.cloned.1.call-update
  116.8 0.2 shard_map.52
  116.9 27.2 %all_to_all.36.parts_ref = f32[64,4,128]{2,1,0:T(4,128)S(1)} all-to-all(f32[64,4,128]{2,1,0:T(4,128)S(1)} %shard_map.52), channel_id=1, replica_groups={{0,1,2,3,4,5,6,7,8,9,10,11,12,13,14,15,128,129,130,131,132,133,134,135,..., dimensions={0} | all-to-all | bytes 262144 | tf_op jit(solution)/shard_map/all_to_all | solution.py:386
  144.1 0.3 shard_map.53
  144.4 10.9 %all_to_all.37.parts_ref = f32[8,1,64]{2,1,0:T(1,128)S(1)} all-to-all(f32[8,1,64]{2,1,0:T(1,128)S(1)} %shard_map.53), channel_id=1, replica_groups={{0,16,32,48,64,80,96,112},{128,144,160,176,192,208,224,240},{256,272,28..., dimensions={0} | all-to-all | bytes 4096 | tf_op jit(solution)/shard_map/all_to_all | solution.py:300
  155.3 0.2 shard_map.54
  155.5 21.6 %all_to_all.38.parts_ref = f32[64,4,128]{2,1,0:T(4,128)S(1)} all-to-all(f32[64,4,128]{2,1,0:T(4,128)S(1)} %shard_map.54), channel_id=1, replica_groups={{0,1,2,3,4,5,6,7,8,9,10,11,12,13,14,15,128,129,130,131,132,133,134,135,..., dimensions={0} | all-to-all | bytes 262144 | tf_op jit(solution)/shard_map/all_to_all | solution.py:386
  177.1 0.1 shard_map.55
  177.2 9.6 %all_to_all.39.parts_ref = f32[8,4,128]{2,1,0:T(4,128)S(1)} all-to-all(f32[8,4,128]{2,1,0:T(4,128)S(1)} %shard_map.55), channel_id=1, replica_groups={{0,16,32,48,64,80,96,112},{128,144,160,176,192,208,224,240},{256,272,28..., dimensions={0} | all-to-all | bytes 32768 | tf_op jit(solution)/shard_map/all_to_all | solution.py:300
  186.8 0.0 all-gather.6.cloned.1.call-done
  186.8 0.0 copy-start
  186.8 1.6 copy-done
  188.4 2.6 %shard_map.56 = (f32[128,4096]{1,0:T(8,128)S(1)}, f32[128,128]{1,0:T(8,128)}, f32[32,8,512]{2,1,0:T(8,128)S(1)}) custom-call(f32[16,8,8,512]{3,2,1,0:T(8,128)S(1)} %bitcast.17, f32[8,4,128]{2,1,0:T(4,128)S(1)} %all_to_all.39.parts_ref), custom_call_target="tpu_custom_call" | custom-call | tf_op jit(solution)/shard_map/pallas_call | solution.py:405
  191.0 24.8 %all_to_all.40.parts_ref = f32[32,8,512]{2,1,0:T(8,128)S(1)} all-to-all(f32[32,8,512]{2,1,0:T(8,128)S(1)} %get-tuple-element.40), channel_id=1, replica_groups=mesh['noise'=32,'dp'=16] {'noise'}, dimensions={0} | all-to-all | bytes 1048576 | tf_op jit(solution)/shard_map/all_to_all | solution.py:420
  215.9 2.5 %shard_map.57 = (f32[128,128]{1,0:T(8,128)S(1)}, f32[32,8,512]{2,1,0:T(8,128)S(1)}) custom-call(f32[128,4096]{1,0:T(8,128)S(1)} %get-tuple-element.39.a_ref, f32[32,8,512]{2,1,0:T(8,128)S(1)} %all_to_all.40.parts_ref), custom_call_target="tpu_custom_call" | custom-call | tf_op jit(solution)/shard_map/pallas_call | solution.py:413
  218.3 15.2 %all_to_all.41.parts_ref = f32[32,8,512]{2,1,0:T(8,128)S(1)} all-to-all(f32[32,8,512]{2,1,0:T(8,128)S(1)} %get-tuple-element.42), channel_id=1, replica_groups=mesh['noise'=32,'dp'=16] {'noise'}, dimensions={0} | all-to-all | bytes 1048576 | tf_op jit(solution)/shard_map/all_to_all | solution.py:420
  233.6 6.2 %shard_map.58 = (bf16[128,1024]{1,0:T(8,128)(2,1)}, f32[1,128]{1,0:T(1,128)}, f32[1,256]{1,0:T(1,128)}) custom-call(s32[4]{0:T(128)S(1)} %pad_add_fusion.place_ref, f32[128,4096]{1,0:T(8,128)S(1)} %get-tuple-element.39.a_ref, f32[128,128]{1,0:T(8,128)S(1)} %get-tuple-element.41.u_ref, f32[32,8,512]{2,1,0:T(8,128)S(1)} %all_to_all.41.parts_ref, ...), custom_call_target="tpu_custom_call" | custom-call | tf_op jit(solution)/shard_map/pallas_call | solution.py:423
  (8 shorter events, 0.2 us)
Async XLA Ops:
  7.2 109.6 %all-gather.4.cloned.1.call-start = ((), (), s32[]{:S(2)}) async-start(), calls=%async_computation.7 | async-start | bytes 8650752 | tf_op jit(solution)/shard_map/all_gather | solution.py:309
  7.2 11.9 %collective-permute-start.1 = (bf16[128,1024]{1,0:T(8,128)(2,1)}, bf16[128,1024]{1,0:T(8,128)(2,1)S(1)}, u32[]{:S(2)}, u32[]{:S(2)}) collective-permute-start(bf16[128,1024]{1,0:T(8,128)(2,1)} %param.3), channel_id=1, source_target_pairs={{0,128},{16,400},{32,160},{48,432},{64,192},{80,464},{96,224},{112... | collective-permute-start | bytes 786440 | tf_op jit(solution)/shard_map/ppermute | solution.py:44
  12.7 8.5 %collective-permute-start = (bf16[128,1024]{1,0:T(8,128)(2,1)}, bf16[128,1024]{1,0:T(8,128)(2,1)S(1)}, u32[]{:S(2)}, u32[]{:S(2)}) collective-permute-start(bf16[128,1024]{1,0:T(8,128)(2,1)} %param.2), channel_id=1, source_target_pairs={{0,32},{16,112},{32,0},{48,80},{64,96},{80,48},{96,64},{112,16},{1... | collective-permute-start | bytes 786440 | tf_op jit(solution)/shard_map/ppermute | solution.py:40
  21.2 10.8 %collective-permute-start.3 = (bf16[256,1024]{1,0:T(8,128)(2,1)S(1)}, bf16[256,1024]{1,0:T(8,128)(2,1)S(1)}, u32[]{:S(2)}, u32[]{:S(2)}) collective-permute-start(bf16[256,1024]{1,0:T(8,128)(2,1)S(1)} %constant_dynamic-update-slice_fusion.1.refs_0_), channel_id=1, source_target_pairs={{0,96},{16,48},{32,64},{48,16},{64,32},{80,112},{96,0},{112,80},{1... | collective-permute-start | bytes 1572872 | tf_op jit(solution)/shard_map/ppermute | solution.py:40
  23.5 15.2 %collective-permute-start.2 = (bf16[256,1024]{1,0:T(8,128)(2,1)S(1)}, bf16[256,1024]{1,0:T(8,128)(2,1)S(1)}, u32[]{:S(2)}, u32[]{:S(2)}) collective-permute-start(bf16[256,1024]{1,0:T(8,128)(2,1)S(1)} %constant_dynamic-update-slice_fusion.1.refs_0_), channel_id=1, source_target_pairs={{0,16},{16,0},{32,48},{48,32},{64,80},{80,64},{96,112},{112,96},{1... | collective-permute-start | bytes 1572872 | tf_op jit(solution)/shard_map/ppermute | solution.py:32
  28.4 10.6 %collective-permute-start.5 = (bf16[256,1024]{1,0:T(8,128)(2,1)S(1)}, bf16[256,1024]{1,0:T(8,128)(2,1)S(1)}, u32[]{:S(2)}, u32[]{:S(2)}) collective-permute-start(bf16[256,1024]{1,0:T(8,128)(2,1)S(1)} %constant_dynamic-update-slice_fusion.refs_4_), channel_id=1, source_target_pairs={{0,384},{16,144},{32,416},{48,176},{64,448},{80,208},{96,480},{112... | collective-permute-start | bytes 1572872 | tf_op jit(solution)/shard_map/ppermute | solution.py:44
  32.1 8.1 %collective-permute-start.4 = (bf16[256,1024]{1,0:T(8,128)(2,1)S(1)}, bf16[256,1024]{1,0:T(8,128)(2,1)S(1)}, u32[]{:S(2)}, u32[]{:S(2)}) collective-permute-start(bf16[256,1024]{1,0:T(8,128)(2,1)S(1)} %collective-permute-done.3.refs_1_), channel_id=1, source_target_pairs={{0,16},{16,0},{32,48},{48,32},{64,80},{80,64},{96,112},{112,96},{1... | collective-permute-start | bytes 1572872 | tf_op jit(solution)/shard_map/ppermute | solution.py:32
  40.2 146.6 %all-gather.6.cloned.1.call-start = ((), (), s32[]{:S(2)}) async-start(), calls=%async_computation.8 | async-start | bytes 2228224 | tf_op jit(solution)/shard_map/all_gather | solution.py:363
  42.8 21.0 %collective-permute-start.6 = (f32[8,64,512]{2,1,0:T(8,128)S(1)}, f32[8,64,512]{2,1,0:T(8,128)S(1)}, u32[]{:S(2)}, u32[]{:S(2)}) collective-permute-start(f32[8,64,512]{2,1,0:T(8,128)S(1)} %get-tuple-element.32), channel_id=1, source_target_pairs={{0,1},{1,0},{2,3},{3,2},{4,5},{5,4},{6,7},{7,6},{8,9},{9,8},{10,11... | collective-permute-start | bytes 3145736 | tf_op jit(solution)/shard_map/ppermute | solution.py:59
  63.9 7.0 %collective-permute-start.7 = (f32[64,512]{1,0:T(8,128)S(1)}, f32[64,512]{1,0:T(8,128)S(1)}, u32[]{:S(2)}, u32[]{:S(2)}) collective-permute-start(f32[64,512]{1,0:T(8,128)S(1)} %get-tuple-element.34), channel_id=1, source_target_pairs={{0,2},{1,3},{2,4},{3,5},{4,6},{5,7},{6,8},{7,9},{8,10},{9,11},{10,... | collective-permute-start | bytes 393224 | tf_op jit(solution)/shard_map/ppermute | solution.py:59
  67.6 7.9 %collective-permute-start.11 = (f32[64,512]{1,0:T(8,128)S(1)}, f32[64,512]{1,0:T(8,128)S(1)}, u32[]{:S(2)}, u32[]{:S(2)}) collective-permute-start(f32[64,512]{1,0:T(8,128)S(1)} %get-tuple-element.36), channel_id=1, source_target_pairs={{0,14},{1,15},{2,0},{3,1},{4,2},{5,3},{6,4},{7,5},{8,6},{9,7},{10,... | collective-permute-start | bytes 393224 | tf_op jit(solution)/shard_map/ppermute | solution.py:59
  70.9 6.7 %collective-permute-start.8 = (f32[64,512]{1,0:T(8,128)S(1)}, f32[64,512]{1,0:T(8,128)S(1)}, u32[]{:S(2)}, u32[]{:S(2)}) collective-permute-start(f32[64,512]{1,0:T(8,128)S(1)} %bitcast_add_fusion.4), channel_id=1, source_target_pairs={{0,2},{1,3},{2,4},{3,5},{4,6},{5,7},{6,8},{7,9},{8,10},{9,11},{10,... | collective-permute-start | bytes 393224 | tf_op jit(solution)/shard_map/ppermute | solution.py:59
  75.5 9.1 %collective-permute-start.12 = (f32[64,512]{1,0:T(8,128)S(1)}, f32[64,512]{1,0:T(8,128)S(1)}, u32[]{:S(2)}, u32[]{:S(2)}) collective-permute-start(f32[64,512]{1,0:T(8,128)S(1)} %bitcast_add_fusion.1), channel_id=1, source_target_pairs={{0,14},{1,15},{2,0},{3,1},{4,2},{5,3},{6,4},{7,5},{8,6},{9,7},{10,... | collective-permute-start | bytes 393224 | tf_op jit(solution)/shard_map/ppermute | solution.py:59
  77.6 12.1 %collective-permute-start.9 = (f32[64,512]{1,0:T(8,128)S(1)}, f32[64,512]{1,0:T(8,128)S(1)}, u32[]{:S(2)}, u32[]{:S(2)}) collective-permute-start(f32[64,512]{1,0:T(8,128)S(1)} %bitcast_add_fusion.3), channel_id=1, source_target_pairs={{0,2},{1,3},{2,4},{3,5},{4,6},{5,7},{6,8},{7,9},{8,10},{9,11},{10,... | collective-permute-start | bytes 393224 | tf_op jit(solution)/shard_map/ppermute | solution.py:59
  84.6 11.2 %collective-permute-start.13 = (f32[64,512]{1,0:T(8,128)S(1)}, f32[64,512]{1,0:T(8,128)S(1)}, u32[]{:S(2)}, u32[]{:S(2)}) collective-permute-start(f32[64,512]{1,0:T(8,128)S(1)} %bitcast_add_fusion), channel_id=1, source_target_pairs={{0,14},{1,15},{2,0},{3,1},{4,2},{5,3},{6,4},{7,5},{8,6},{9,7},{10,... | collective-permute-start | bytes 393224 | tf_op jit(solution)/shard_map/ppermute | solution.py:59
  89.8 11.7 %collective-permute-start.10 = (f32[64,512]{1,0:T(8,128)S(1)}, f32[64,512]{1,0:T(8,128)S(1)}, u32[]{:S(2)}, u32[]{:S(2)}) collective-permute-start(f32[64,512]{1,0:T(8,128)S(1)} %bitcast_add_fusion.2), channel_id=1, source_target_pairs={{0,2},{1,3},{2,4},{3,5},{4,6},{5,7},{6,8},{7,9},{8,10},{9,11},{10,... | collective-permute-start | bytes 393224 | tf_op jit(solution)/shard_map/ppermute | solution.py:59
  186.8 1.6 copy-start
Sparse Core Ops, SparseCore 0:
  40.4 68.5 all-gather.3
  116.9 69.3 all-gather.5

commit v13 on v12

--- a/solution.py
+++ b/solution.py
@@ -36,6 +36,9 @@
 PLACES = ((0, 0), FIRST, SECOND, (BOTH, BOTH))
 
 
+ORDERS = ((4, 5, 3, 6), (2, 7, 1, 0))
+
+
 def swap_x(value, by):
     return lax.ppermute(value, "noise", noise_pairs(lambda y, x, c: (y, x ^ by[c], c)))
 
@@ -74,7 +77,7 @@
 
 def partial_kernel(scale, place_ref, *refs):
     here, there, ys = refs[:2], refs[2:4], refs[4:6]
-    keep, give, x_all, y_all, y_squares, chunks = refs[6:]
+    keep, give, (x_all, y_all, y_squares, chunks) = refs[6:8], refs[8:10], refs[10:]
     rows = here[0].shape[0] // 2
     depth = chunks.shape[0]
     high = rows // depth
@@ -111,20 +114,15 @@
         for i in range(4 * depth):
             block = k * 4 + i // depth
             chunks[places[i % depth], block * high : (block + 1) * high, :] = value[i * high : (i + 1) * high]
-    for k in range(depth // 2):
-        keep[k] = chunks[k]
-        give[k] = chunks[depth // 2 + k]
-
-
-def pair_kernel(keep, got, own, ahead, back, ahead_rest, back_rest):
-    own[...] = keep[0] + got[0]
-    middle = keep.shape[0] // 2
-    ahead[...] = keep[middle] + got[middle]
-    back[...] = keep[middle + 1] + got[middle + 1]
-    for k in range(1, middle):
-        ahead_rest[middle - 1 - k] = keep[k] + got[k]
-    for k in range(middle + 2, keep.shape[0]):
-        back_rest[k - middle - 2] = keep[k] + got[k]
+    for part, order in enumerate(ORDERS):
+        for i, k in enumerate(order):
+            keep[part][i] = chunks[k]
+            give[part][i] = chunks[depth // 2 + k]
+
+
+def pair_kernel(keep, got, *outs):
+    for k, out in enumerate(outs):
+        out[...] = keep[k] + got[k]
 
 
 def joined(parts):
@@ -311,11 +309,11 @@
     half = depth // 2
     middle = half // 2
     chunk = (tall // depth, wide)
-    keep, give = pl.pallas_call(
+    *keep, give, give_later = pl.pallas_call(
         functools.partial(partial_kernel, LOG2E / (epsilon * D)),
-        out_shape=[jax.ShapeDtypeStruct((half,) + chunk, f32)] * 2,
+        out_shape=[jax.ShapeDtypeStruct((half // 2,) + chunk, f32)] * 4,
         in_specs=[SMEM] + [VMEM] * 6,
-        out_specs=[VMEM] * 2,
+        out_specs=[VMEM] * 4,
         scratch_shapes=[
             pltpu.VMEM((group * rows, features), jnp.bfloat16),
             pltpu.VMEM((YS * rows, features), jnp.bfloat16),
@@ -325,20 +323,18 @@
         compiler_params=PARAMS,
     )(place, x_near, x_far, x_there, x_far_there, y_near, y_far)
 
-    got = send_z(give, z_partner)
-    own, ahead, back, ahead_rest, back_rest = pl.pallas_call(
-        pair_kernel,
-        out_shape=[
-            jax.ShapeDtypeStruct(chunk, f32),
-            jax.ShapeDtypeStruct(chunk, f32),
-            jax.ShapeDtypeStruct(chunk, f32),
-            jax.ShapeDtypeStruct((middle - 1,) + chunk, f32),
-            jax.ShapeDtypeStruct((middle - 2,) + chunk, f32),
-        ],
-        in_specs=[VMEM] * 2,
-        out_specs=[VMEM] * 5,
-        compiler_params=PARAMS,
-    )(keep, got)
+    sums = {}
+    for part, got in enumerate((send_z(give, z_partner), send_z(give_later, z_partner))):
+        outs = pl.pallas_call(
+            pair_kernel,
+            out_shape=[jax.ShapeDtypeStruct(chunk, f32)] * (half // 2),
+            in_specs=[VMEM] * 2,
+            out_specs=[VMEM] * (half // 2),
+            compiler_params=PARAMS,
+        )(keep[part], got)
+        sums.update(zip(ORDERS[part], outs))
+    own, ahead, back = sums[0], sums[4], sums[5]
+    ahead_rest, back_rest = [sums[3], sums[2], sums[1]], [sums[6], sums[7]]
     for step in range(middle):
         ahead = send_z(ahead, lambda z, c: z + 2 if c == 0 else z - 2)
         if step < middle - 1:

time: 247 us -> 244 us (0.988)
  waiting for transfers between devices: 26.9 us -> 19 us
  starting transfers between devices: 62.5 us -> 65.6 us
    ppermute x8 -> x9, waiting for transfers between devices: 23.3 us -> 14.5 us  [send_z(): return lax.ppermute(value, ('noise', 'dp'), pairs)]
    ppermute x8 -> x9, starting transfers between devices: 35.1 us -> 38.2 us  [send_z(): return lax.ppermute(value, ('noise', 'dp'), pairs)]
    all_to_all x2, blocking collectives: 48.7 us -> 51.8 us  [on_device(): lax.all_to_all(part, ('noise', 'dp'), 0, 0, axis_index_groups=z_groups, t...]
  transfers between devices with their start and end apart: 16 -> 17, of which waited for: 10 -> 10; matrix products, arithmetic and copies ran while one was open for 1% -> 1% of each run, Pallas kernels for 1% -> 1%
where the time goes in v13:
time: 244 us; the launch traced here: 243 us
  blocking collectives  125 us (51%)
  starting transfers between devices  65.6 us (27%)
  waiting for transfers between devices  19 us (8%)
  Pallas kernels  14.7 us (6%)
  between operations  14.3 us (6%)
  local copies, waits for them, and re-layouts  4.28 us (2%)
    all_to_all x2, blocking collectives, on_device(): lax.all_to_all(part, ('noise', 'dp'), 0, 0, axis_index_groups=z_groups, t...  51.8 us
    all_to_all x2, blocking collectives, on_device(): part = lax.all_to_all(part, 'noise', 0, 0, tiled=True)  40.6 us
    ppermute x9, starting transfers between devices, send_z(): return lax.ppermute(value, ('noise', 'dp'), pairs)  38.2 us
    all_to_all x3, blocking collectives, swap(): lax.all_to_all(value, 'noise', 0, 0, axis_index_groups=groups, tiled=True)  32.7 us
    ppermute x9, waiting for transfers between devices, send_z(): return lax.ppermute(value, ('noise', 'dp'), pairs)  14.5 us
    ppermute x2, starting transfers between devices, to_other_core(): lax.ppermute(value, 'noise', noise_pairs(lambda y, x, c: (y, x, 1 - c)))  11.5 us
    ppermute x2, starting transfers between devices, swap_y(): lax.ppermute(value, 'noise', noise_pairs(lambda y, x, c: (y ^ by[c], x, c)))  9.17 us
    ppermute x2, starting transfers between devices, swap_x(): lax.ppermute(value, 'noise', noise_pairs(lambda y, x, c: (y, x ^ by[c], c)))  6.59 us
  transfers between devices with their start and end apart: 17, of which 10 were waited for; matrix products, arithmetic and copies ran while one was open for 1% of the time, Pallas kernels for 1%

profile of v13, /device:TPU:1, one launch (start us, length us, event | category | flops | bytes accessed | tf_op | source)
XLA Modules:
  0.0 243.3 jit_solution(14601791038457762561)
XLA Ops:
  7.2 0.0 all-gather.4.cloned.1.call-start
  7.2 5.5 %collective-permute-start.1 = (bf16[128,1024]{1,0:T(8,128)(2,1)}, bf16[128,1024]{1,0:T(8,128)(2,1)S(1)}, u32[]{:S(2)}, u32[]{:S(2)}) collective-permute-start(bf16[128,1024]{1,0:T(8,128)(2,1)} %param.3), channel_id=1, source_target_pairs={{0,128},{16,400},{32,160},{48,432},{64,192},{80,464},{96,224},{112... | collective-permute-start | bytes 786440 | tf_op jit(solution)/shard_map/ppermute | solution.py:47
  12.7 4.4 %collective-permute-start = (bf16[128,1024]{1,0:T(8,128)(2,1)}, bf16[128,1024]{1,0:T(8,128)(2,1)S(1)}, u32[]{:S(2)}, u32[]{:S(2)}) collective-permute-start(bf16[128,1024]{1,0:T(8,128)(2,1)} %param.2), channel_id=1, source_target_pairs={{0,32},{16,112},{32,0},{48,80},{64,96},{80,48},{96,64},{112,16},{1... | collective-permute-start | bytes 786440 | tf_op jit(solution)/shard_map/ppermute | solution.py:43
  17.1 1.0 dynamic_update_slice.14
  18.1 1.0 dynamic_update_slice.12
  19.1 0.0 collective-permute-done.1
  19.1 2.1 collective-permute-done
  21.2 2.2 collective-permute-start.3
  23.5 4.9 %collective-permute-start.2 = (bf16[256,1024]{1,0:T(8,128)(2,1)S(1)}, bf16[256,1024]{1,0:T(8,128)(2,1)S(1)}, u32[]{:S(2)}, u32[]{:S(2)}) collective-permute-start(bf16[256,1024]{1,0:T(8,128)(2,1)S(1)} %constant_dynamic-update-slice_fusion.1.refs_0_), channel_id=1, source_target_pairs={{0,16},{16,0},{32,48},{48,32},{64,80},{80,64},{96,112},{112,96},{1... | collective-permute-start | bytes 1572872 | tf_op jit(solution)/shard_map/ppermute | solution.py:32
  28.4 3.7 %collective-permute-start.5 = (bf16[256,1024]{1,0:T(8,128)(2,1)S(1)}, bf16[256,1024]{1,0:T(8,128)(2,1)S(1)}, u32[]{:S(2)}, u32[]{:S(2)}) collective-permute-start(bf16[256,1024]{1,0:T(8,128)(2,1)S(1)} %constant_dynamic-update-slice_fusion.refs_4_), channel_id=1, source_target_pairs={{0,384},{16,144},{32,416},{48,176},{64,448},{80,208},{96,480},{112... | collective-permute-start | bytes 1572872 | tf_op jit(solution)/shard_map/ppermute | solution.py:47
  32.1 0.0 collective-permute-done.3.refs_1_
  32.1 6.6 %collective-permute-start.4 = (bf16[256,1024]{1,0:T(8,128)(2,1)S(1)}, bf16[256,1024]{1,0:T(8,128)(2,1)S(1)}, u32[]{:S(2)}, u32[]{:S(2)}) collective-permute-start(bf16[256,1024]{1,0:T(8,128)(2,1)S(1)} %collective-permute-done.3.refs_1_), channel_id=1, source_target_pairs={{0,16},{16,0},{32,48},{48,32},{64,80},{80,64},{96,112},{112,96},{1... | collective-permute-start | bytes 1572872 | tf_op jit(solution)/shard_map/ppermute | solution.py:32
  38.7 0.0 collective-permute-done.2.refs_2_
  38.7 0.2 collective-permute-done.5.refs_5_
  38.9 1.3 collective-permute-done.4.refs_3_
  40.2 0.0 all-gather.4.cloned.1.call-update
  40.2 0.0 all-gather.6.cloned.1.call-start
  40.3 0.1 pad_add_fusion.place_ref
  40.4 2.4 shard_map.49
  42.8 8.4 %collective-permute-start.7 = (f32[4,64,512]{2,1,0:T(8,128)S(1)}, f32[4,64,512]{2,1,0:T(8,128)S(1)}, u32[]{:S(2)}, u32[]{:S(2)}) collective-permute-start(f32[4,64,512]{2,1,0:T(8,128)S(1)} %get-tuple-element.40), channel_id=1, source_target_pairs={{0,1},{1,0},{2,3},{3,2},{4,5},{5,4},{6,7},{7,6},{8,9},{9,8},{10,11... | collective-permute-start | bytes 1572872 | tf_op jit(solution)/shard_map/ppermute | solution.py:62
  51.2 1.9 collective-permute-start.6
  53.1 4.6 %collective-permute-done.7.got = f32[4,64,512]{2,1,0:T(8,128)S(1)} collective-permute-done((f32[4,64,512]{2,1,0:T(8,128)S(1)}, f32[4,64,512]{2,1,0:T(8,128)S(1)}, u32[]{:S(2)}, u32[]{:S(2)}) %collective-permute-start.7) | collective-permute-done | bytes 524320 | tf_op jit(solution)/shard_map/ppermute | solution.py:62
  57.8 0.1 shard_map.51
  57.8 4.1 %collective-permute-start.8 = (f32[64,512]{1,0:T(8,128)S(1)}, f32[64,512]{1,0:T(8,128)S(1)}, u32[]{:S(2)}, u32[]{:S(2)}) collective-permute-start(f32[64,512]{1,0:T(8,128)S(1)} %get-tuple-element.41), channel_id=1, source_target_pairs={{0,2},{1,3},{2,4},{3,5},{4,6},{5,7},{6,8},{7,9},{8,10},{9,11},{10,... | collective-permute-start | bytes 393224 | tf_op jit(solution)/shard_map/ppermute | solution.py:62
  61.9 2.1 collective-permute-start.12
  64.0 1.6 collective-permute-done.8
  65.6 6.0 %collective-permute-start.9 = (f32[64,512]{1,0:T(8,128)S(1)}, f32[64,512]{1,0:T(8,128)S(1)}, u32[]{:S(2)}, u32[]{:S(2)}) collective-permute-start(f32[64,512]{1,0:T(8,128)S(1)} %add.36), channel_id=1, source_target_pairs={{0,2},{1,3},{2,4},{3,5},{4,6},{5,7},{6,8},{7,9},{8,10},{9,11},{10,... | collective-permute-start | bytes 393224 | tf_op jit(solution)/shard_map/ppermute | solution.py:62
  71.6 0.0 collective-permute-done.6.got
  71.7 0.1 shard_map.50
  71.7 0.1 collective-permute-done.12
  71.8 1.9 collective-permute-start.13
  73.7 1.2 collective-permute-done.9
  75.0 5.9 %collective-permute-start.10 = (f32[64,512]{1,0:T(8,128)S(1)}, f32[64,512]{1,0:T(8,128)S(1)}, u32[]{:S(2)}, u32[]{:S(2)}) collective-permute-start(f32[64,512]{1,0:T(8,128)S(1)} %add.37), channel_id=1, source_target_pairs={{0,2},{1,3},{2,4},{3,5},{4,6},{5,7},{6,8},{7,9},{8,10},{9,11},{10,... | collective-permute-start | bytes 393224 | tf_op jit(solution)/shard_map/ppermute | solution.py:62
  80.9 0.0 collective-permute-done.13
  80.9 1.9 collective-permute-start.14
  82.9 2.5 %collective-permute-done.10 = f32[64,512]{1,0:T(8,128)S(1)} collective-permute-done((f32[64,512]{1,0:T(8,128)S(1)}, f32[64,512]{1,0:T(8,128)S(1)}, u32[]{:S(2)}, u32[]{:S(2)}) %collective-permute-start.10) | collective-permute-done | bytes 131104 | tf_op jit(solution)/shard_map/ppermute | solution.py:62
  85.4 5.9 %collective-permute-start.11 = (f32[64,512]{1,0:T(8,128)S(1)}, f32[64,512]{1,0:T(8,128)S(1)}, u32[]{:S(2)}, u32[]{:S(2)}) collective-permute-start(f32[64,512]{1,0:T(8,128)S(1)} %add.38), channel_id=1, source_target_pairs={{0,2},{1,3},{2,4},{3,5},{4,6},{5,7},{6,8},{7,9},{8,10},{9,11},{10,... | collective-permute-start | bytes 393224 | tf_op jit(solution)/shard_map/ppermute | solution.py:62
  91.3 0.0 collective-permute-done.14
  91.3 4.5 %collective-permute-done.11 = f32[64,512]{1,0:T(8,128)S(1)} collective-permute-done((f32[64,512]{1,0:T(8,128)S(1)}, f32[64,512]{1,0:T(8,128)S(1)}, u32[]{:S(2)}, u32[]{:S(2)}) %collective-permute-start.11) | collective-permute-done | bytes 131104 | tf_op jit(solution)/shard_map/ppermute | solution.py:62
  95.8 0.2 shard_map.52
  96.1 14.3 %all_to_all.35.parts_ref = f32[8,8,640]{2,1,0:T(8,128)S(1)} all-to-all(f32[8,8,640]{2,1,0:T(8,128)S(1)} %shard_map.52), channel_id=1, replica_groups={{0,16,32,48,64,80,96,112},{128,144,160,176,192,208,224,240},{256,272,28..., dimensions={0} | all-to-all | bytes 327680 | tf_op jit(solution)/shard_map/all_to_all | solution.py:298
  110.4 0.7 slice.4
  111.0 0.0 all-gather.4.cloned.1.call-done.y_ref
  111.0 0.0 all-gather.6.cloned.1.call-update
  111.1 0.2 shard_map.53
  111.3 29.3 %all_to_all.36.parts_ref = f32[64,4,128]{2,1,0:T(4,128)S(1)} all-to-all(f32[64,4,128]{2,1,0:T(4,128)S(1)} %shard_map.53), channel_id=1, replica_groups={{0,1,2,3,4,5,6,7,8,9,10,11,12,13,14,15,128,129,130,131,132,133,134,135,..., dimensions={0} | all-to-all | bytes 262144 | tf_op jit(solution)/shard_map/all_to_all | solution.py:382
  140.5 0.3 shard_map.54
  140.9 9.3 %all_to_all.37.parts_ref = f32[8,1,64]{2,1,0:T(1,128)S(1)} all-to-all(f32[8,1,64]{2,1,0:T(1,128)S(1)} %shard_map.54), channel_id=1, replica_groups={{0,16,32,48,64,80,96,112},{128,144,160,176,192,208,224,240},{256,272,28..., dimensions={0} | all-to-all | bytes 4096 | tf_op jit(solution)/shard_map/all_to_all | solution.py:298
  150.1 0.2 shard_map.55
  150.3 22.5 %all_to_all.38.parts_ref = f32[64,4,128]{2,1,0:T(4,128)S(1)} all-to-all(f32[64,4,128]{2,1,0:T(4,128)S(1)} %shard_map.55), channel_id=1, replica_groups={{0,1,2,3,4,5,6,7,8,9,10,11,12,13,14,15,128,129,130,131,132,133,134,135,..., dimensions={0} | all-to-all | bytes 262144 | tf_op jit(solution)/shard_map/all_to_all | solution.py:382
  172.8 0.1 shard_map.56
  173.0 9.1 %all_to_all.39.parts_ref = f32[8,4,128]{2,1,0:T(4,128)S(1)} all-to-all(f32[8,4,128]{2,1,0:T(4,128)S(1)} %shard_map.56), channel_id=1, replica_groups={{0,16,32,48,64,80,96,112},{128,144,160,176,192,208,224,240},{256,272,28..., dimensions={0} | all-to-all | bytes 32768 | tf_op jit(solution)/shard_map/all_to_all | solution.py:298
  182.0 0.9 all-gather.6.cloned.1.call-done
  183.0 0.0 copy-start
  183.0 1.6 copy-done
  184.6 2.6 %shard_map.57 = (f32[128,4096]{1,0:T(8,128)S(1)}, f32[128,128]{1,0:T(8,128)}, f32[32,8,512]{2,1,0:T(8,128)S(1)}) custom-call(f32[16,8,8,512]{3,2,1,0:T(8,128)S(1)} %bitcast.7, f32[8,4,128]{2,1,0:T(4,128)S(1)} %all_to_all.39.parts_ref), custom_call_target="tpu_custom_call" | custom-call | tf_op jit(solution)/shard_map/pallas_call | solution.py:401
  187.2 25.4 %all_to_all.40.parts_ref = f32[32,8,512]{2,1,0:T(8,128)S(1)} all-to-all(f32[32,8,512]{2,1,0:T(8,128)S(1)} %get-tuple-element.50), channel_id=1, replica_groups=mesh['noise'=32,'dp'=16] {'noise'}, dimensions={0} | all-to-all | bytes 1048576 | tf_op jit(solution)/shard_map/all_to_all | solution.py:416
  212.6 2.5 %shard_map.58 = (f32[128,128]{1,0:T(8,128)S(1)}, f32[32,8,512]{2,1,0:T(8,128)S(1)}) custom-call(f32[128,4096]{1,0:T(8,128)S(1)} %get-tuple-element.49.a_ref, f32[32,8,512]{2,1,0:T(8,128)S(1)} %all_to_all.40.parts_ref), custom_call_target="tpu_custom_call" | custom-call | tf_op jit(solution)/shard_map/pallas_call | solution.py:409
  215.1 15.2 %all_to_all.41.parts_ref = f32[32,8,512]{2,1,0:T(8,128)S(1)} all-to-all(f32[32,8,512]{2,1,0:T(8,128)S(1)} %get-tuple-element.52), channel_id=1, replica_groups=mesh['noise'=32,'dp'=16] {'noise'}, dimensions={0} | all-to-all | bytes 1048576 | tf_op jit(solution)/shard_map/all_to_all | solution.py:416
  230.3 6.2 %shard_map.59 = (bf16[128,1024]{1,0:T(8,128)(2,1)}, f32[1,128]{1,0:T(1,128)}, f32[1,256]{1,0:T(1,128)}) custom-call(s32[4]{0:T(128)S(1)} %pad_add_fusion.place_ref, f32[128,4096]{1,0:T(8,128)S(1)} %get-tuple-element.49.a_ref, f32[128,128]{1,0:T(8,128)S(1)} %get-tuple-element.51.u_ref, f32[32,8,512]{2,1,0:T(8,128)S(1)} %all_to_all.41.parts_ref, ...), custom_call_target="tpu_custom_call" | custom-call | tf_op jit(solution)/shard_map/pallas_call | solution.py:419
  (8 shorter events, 0.2 us)
Async XLA Ops:
  7.2 103.9 %all-gather.4.cloned.1.call-start = ((), (), s32[]{:S(2)}) async-start(), calls=%async_computation.7 | async-start | bytes 8650752 | tf_op jit(solution)/shard_map/all_gather | solution.py:307
  7.2 11.9 %collective-permute-start.1 = (bf16[128,1024]{1,0:T(8,128)(2,1)}, bf16[128,1024]{1,0:T(8,128)(2,1)S(1)}, u32[]{:S(2)}, u32[]{:S(2)}) collective-permute-start(bf16[128,1024]{1,0:T(8,128)(2,1)} %param.3), channel_id=1, source_target_pairs={{0,128},{16,400},{32,160},{48,432},{64,192},{80,464},{96,224},{112... | collective-permute-start | bytes 786440 | tf_op jit(solution)/shard_map/ppermute | solution.py:47
  12.7 8.5 %collective-permute-start = (bf16[128,1024]{1,0:T(8,128)(2,1)}, bf16[128,1024]{1,0:T(8,128)(2,1)S(1)}, u32[]{:S(2)}, u32[]{:S(2)}) collective-permute-start(bf16[128,1024]{1,0:T(8,128)(2,1)} %param.2), channel_id=1, source_target_pairs={{0,32},{16,112},{32,0},{48,80},{64,96},{80,48},{96,64},{112,16},{1... | collective-permute-start | bytes 786440 | tf_op jit(solution)/shard_map/ppermute | solution.py:43
  21.2 10.8 %collective-permute-start.3 = (bf16[256,1024]{1,0:T(8,128)(2,1)S(1)}, bf16[256,1024]{1,0:T(8,128)(2,1)S(1)}, u32[]{:S(2)}, u32[]{:S(2)}) collective-permute-start(bf16[256,1024]{1,0:T(8,128)(2,1)S(1)} %constant_dynamic-update-slice_fusion.1.refs_0_), channel_id=1, source_target_pairs={{0,96},{16,48},{32,64},{48,16},{64,32},{80,112},{96,0},{112,80},{1... | collective-permute-start | bytes 1572872 | tf_op jit(solution)/shard_map/ppermute | solution.py:43
  23.5 15.2 %collective-permute-start.2 = (bf16[256,1024]{1,0:T(8,128)(2,1)S(1)}, bf16[256,1024]{1,0:T(8,128)(2,1)S(1)}, u32[]{:S(2)}, u32[]{:S(2)}) collective-permute-start(bf16[256,1024]{1,0:T(8,128)(2,1)S(1)} %constant_dynamic-update-slice_fusion.1.refs_0_), channel_id=1, source_target_pairs={{0,16},{16,0},{32,48},{48,32},{64,80},{80,64},{96,112},{112,96},{1... | collective-permute-start | bytes 1572872 | tf_op jit(solution)/shard_map/ppermute | solution.py:32
  28.4 10.6 %collective-permute-start.5 = (bf16[256,1024]{1,0:T(8,128)(2,1)S(1)}, bf16[256,1024]{1,0:T(8,128)(2,1)S(1)}, u32[]{:S(2)}, u32[]{:S(2)}) collective-permute-start(bf16[256,1024]{1,0:T(8,128)(2,1)S(1)} %constant_dynamic-update-slice_fusion.refs_4_), channel_id=1, source_target_pairs={{0,384},{16,144},{32,416},{48,176},{64,448},{80,208},{96,480},{112... | collective-permute-start | bytes 1572872 | tf_op jit(solution)/shard_map/ppermute | solution.py:47
  32.1 8.1 %collective-permute-start.4 = (bf16[256,1024]{1,0:T(8,128)(2,1)S(1)}, bf16[256,1024]{1,0:T(8,128)(2,1)S(1)}, u32[]{:S(2)}, u32[]{:S(2)}) collective-permute-start(bf16[256,1024]{1,0:T(8,128)(2,1)S(1)} %collective-permute-done.3.refs_1_), channel_id=1, source_target_pairs={{0,16},{16,0},{32,48},{48,32},{64,80},{80,64},{96,112},{112,96},{1... | collective-permute-start | bytes 1572872 | tf_op jit(solution)/shard_map/ppermute | solution.py:32
  40.2 142.7 %all-gather.6.cloned.1.call-start = ((), (), s32[]{:S(2)}) async-start(), calls=%async_computation.8 | async-start | bytes 2228224 | tf_op jit(solution)/shard_map/all_gather | solution.py:359
  42.8 15.0 %collective-permute-start.7 = (f32[4,64,512]{2,1,0:T(8,128)S(1)}, f32[4,64,512]{2,1,0:T(8,128)S(1)}, u32[]{:S(2)}, u32[]{:S(2)}) collective-permute-start(f32[4,64,512]{2,1,0:T(8,128)S(1)} %get-tuple-element.40), channel_id=1, source_target_pairs={{0,1},{1,0},{2,3},{3,2},{4,5},{5,4},{6,7},{7,6},{8,9},{9,8},{10,11... | collective-permute-start | bytes 1572872 | tf_op jit(solution)/shard_map/ppermute | solution.py:62
  51.2 20.4 %collective-permute-start.6 = (f32[4,64,512]{2,1,0:T(8,128)S(1)}, f32[4,64,512]{2,1,0:T(8,128)S(1)}, u32[]{:S(2)}, u32[]{:S(2)}) collective-permute-start(f32[4,64,512]{2,1,0:T(8,128)S(1)} %get-tuple-element.37), channel_id=1, source_target_pairs={{0,1},{1,0},{2,3},{3,2},{4,5},{5,4},{6,7},{7,6},{8,9},{9,8},{10,11... | collective-permute-start | bytes 1572872 | tf_op jit(solution)/shard_map/ppermute | solution.py:62
  57.8 7.8 %collective-permute-start.8 = (f32[64,512]{1,0:T(8,128)S(1)}, f32[64,512]{1,0:T(8,128)S(1)}, u32[]{:S(2)}, u32[]{:S(2)}) collective-permute-start(f32[64,512]{1,0:T(8,128)S(1)} %get-tuple-element.41), channel_id=1, source_target_pairs={{0,2},{1,3},{2,4},{3,5},{4,6},{5,7},{6,8},{7,9},{8,10},{9,11},{10,... | collective-permute-start | bytes 393224 | tf_op jit(solution)/shard_map/ppermute | solution.py:62
  61.9 9.8 %collective-permute-start.12 = (f32[64,512]{1,0:T(8,128)S(1)}, f32[64,512]{1,0:T(8,128)S(1)}, u32[]{:S(2)}, u32[]{:S(2)}) collective-permute-start(f32[64,512]{1,0:T(8,128)S(1)} %get-tuple-element.45), channel_id=1, source_target_pairs={{0,14},{1,15},{2,0},{3,1},{4,2},{5,3},{6,4},{7,5},{8,6},{9,7},{10,... | collective-permute-start | bytes 393224 | tf_op jit(solution)/shard_map/ppermute | solution.py:62
  65.6 9.3 %collective-permute-start.9 = (f32[64,512]{1,0:T(8,128)S(1)}, f32[64,512]{1,0:T(8,128)S(1)}, u32[]{:S(2)}, u32[]{:S(2)}) collective-permute-start(f32[64,512]{1,0:T(8,128)S(1)} %add.36), channel_id=1, source_target_pairs={{0,2},{1,3},{2,4},{3,5},{4,6},{5,7},{6,8},{7,9},{8,10},{9,11},{10,... | collective-permute-start | bytes 393224 | tf_op jit(solution)/shard_map/ppermute | solution.py:62
  71.8 9.1 %collective-permute-start.13 = (f32[64,512]{1,0:T(8,128)S(1)}, f32[64,512]{1,0:T(8,128)S(1)}, u32[]{:S(2)}, u32[]{:S(2)}) collective-permute-start(f32[64,512]{1,0:T(8,128)S(1)} %add.40), channel_id=1, source_target_pairs={{0,14},{1,15},{2,0},{3,1},{4,2},{5,3},{6,4},{7,5},{8,6},{9,7},{10,... | collective-permute-start | bytes 393224 | tf_op jit(solution)/shard_map/ppermute | solution.py:62
  75.0 10.4 %collective-permute-start.10 = (f32[64,512]{1,0:T(8,128)S(1)}, f32[64,512]{1,0:T(8,128)S(1)}, u32[]{:S(2)}, u32[]{:S(2)}) collective-permute-start(f32[64,512]{1,0:T(8,128)S(1)} %add.37), channel_id=1, source_target_pairs={{0,2},{1,3},{2,4},{3,5},{4,6},{5,7},{6,8},{7,9},{8,10},{9,11},{10,... | collective-permute-start | bytes 393224 | tf_op jit(solution)/shard_map/ppermute | solution.py:62
  80.9 10.4 %collective-permute-start.14 = (f32[64,512]{1,0:T(8,128)S(1)}, f32[64,512]{1,0:T(8,128)S(1)}, u32[]{:S(2)}, u32[]{:S(2)}) collective-permute-start(f32[64,512]{1,0:T(8,128)S(1)} %add.41), channel_id=1, source_target_pairs={{0,14},{1,15},{2,0},{3,1},{4,2},{5,3},{6,4},{7,5},{8,6},{9,7},{10,... | collective-permute-start | bytes 393224 | tf_op jit(solution)/shard_map/ppermute | solution.py:62
  85.4 10.4 %collective-permute-start.11 = (f32[64,512]{1,0:T(8,128)S(1)}, f32[64,512]{1,0:T(8,128)S(1)}, u32[]{:S(2)}, u32[]{:S(2)}) collective-permute-start(f32[64,512]{1,0:T(8,128)S(1)} %add.38), channel_id=1, source_target_pairs={{0,2},{1,3},{2,4},{3,5},{4,6},{5,7},{6,8},{7,9},{8,10},{9,11},{10,... | collective-permute-start | bytes 393224 | tf_op jit(solution)/shard_map/ppermute | solution.py:62
  183.0 1.6 copy-start
Sparse Core Ops, SparseCore 0:
  40.4 68.5 all-gather.3
  111.6 71.2 all-gather.5

commit v14 on v13

--- a/solution.py
+++ b/solution.py
@@ -36,7 +36,7 @@
 PLACES = ((0, 0), FIRST, SECOND, (BOTH, BOTH))
 
 
-ORDERS = ((4, 5, 3, 6), (2, 7, 1, 0))
+ORDERS = ((4, 5), (3, 6, 2, 7, 1, 0))
 
 
 def swap_x(value, by):
@@ -311,7 +311,7 @@
     chunk = (tall // depth, wide)
     *keep, give, give_later = pl.pallas_call(
         functools.partial(partial_kernel, LOG2E / (epsilon * D)),
-        out_shape=[jax.ShapeDtypeStruct((half // 2,) + chunk, f32)] * 4,
+        out_shape=[jax.ShapeDtypeStruct((len(order),) + chunk, f32) for order in ORDERS * 2],
         in_specs=[SMEM] + [VMEM] * 6,
         out_specs=[VMEM] * 4,
         scratch_shapes=[
@@ -327,9 +327,9 @@
     for part, got in enumerate((send_z(give, z_partner), send_z(give_later, z_partner))):
         outs = pl.pallas_call(
             pair_kernel,
-            out_shape=[jax.ShapeDtypeStruct(chunk, f32)] * (half // 2),
+            out_shape=[jax.ShapeDtypeStruct(chunk, f32)] * len(ORDERS[part]),
             in_specs=[VMEM] * 2,
-            out_specs=[VMEM] * (half // 2),
+            out_specs=[VMEM] * len(ORDERS[part]),
             compiler_params=PARAMS,
         )(keep[part], got)
         sums.update(zip(ORDERS[part], outs))

time: 244 us -> 247 us (1.012)
  waiting for transfers between devices: 19 us -> 24.9 us
    ppermute x9, waiting for transfers between devices: 14.5 us -> 21.2 us  [send_z(): return lax.ppermute(value, ('noise', 'dp'), pairs)]
    all_to_all x2, blocking collectives: 51.8 us -> 48.6 us  [on_device(): lax.all_to_all(part, ('noise', 'dp'), 0, 0, axis_index_groups=z_groups, t...]
where the time goes in v14:
time: 247 us; the launch traced here: 246 us
  blocking collectives  124 us (50%)
  starting transfers between devices  64.4 us (26%)
  waiting for transfers between devices  24.9 us (10%)
  Pallas kernels  14.7 us (6%)
  between operations  14.3 us (6%)
  local copies, waits for them, and re-layouts  4.29 us (2%)
    all_to_all x2, blocking collectives, on_device(): lax.all_to_all(part, ('noise', 'dp'), 0, 0, axis_index_groups=z_groups, t...  48.6 us
    all_to_all x2, blocking collectives, on_device(): part = lax.all_to_all(part, 'noise', 0, 0, tiled=True)  40 us
    ppermute x9, starting transfers between devices, send_z(): return lax.ppermute(value, ('noise', 'dp'), pairs)  37 us
    all_to_all x3, blocking collectives, swap(): lax.all_to_all(value, 'noise', 0, 0, axis_index_groups=groups, tiled=True)  34.9 us
    ppermute x9, waiting for transfers between devices, send_z(): return lax.ppermute(value, ('noise', 'dp'), pairs)  21.2 us
    ppermute x2, starting transfers between devices, to_other_core(): lax.ppermute(value, 'noise', noise_pairs(lambda y, x, c: (y, x, 1 - c)))  11.5 us
    ppermute x2, starting transfers between devices, swap_y(): lax.ppermute(value, 'noise', noise_pairs(lambda y, x, c: (y ^ by[c], x, c)))  9.17 us
    ppermute x2, starting transfers between devices, swap_x(): lax.ppermute(value, 'noise', noise_pairs(lambda y, x, c: (y, x ^ by[c], c)))  6.59 us
  transfers between devices with their start and end apart: 17, of which 10 were waited for; matrix products, arithmetic and copies ran while one was open for 1% of the time, Pallas kernels for 1%

profile of v14, /device:TPU:1, one launch (start us, length us, event | category | flops | bytes accessed | tf_op | source)
XLA Modules:
  0.0 246.4 jit_solution(2957909705410084540)
XLA Ops:
  7.2 0.0 all-gather.4.cloned.1.call-start
  7.2 5.5 %collective-permute-start.1 = (bf16[128,1024]{1,0:T(8,128)(2,1)}, bf16[128,1024]{1,0:T(8,128)(2,1)S(1)}, u32[]{:S(2)}, u32[]{:S(2)}) collective-permute-start(bf16[128,1024]{1,0:T(8,128)(2,1)} %param.3), channel_id=1, source_target_pairs={{0,128},{16,400},{32,160},{48,432},{64,192},{80,464},{96,224},{112... | collective-permute-start | bytes 786440 | tf_op jit(solution)/shard_map/ppermute | solution.py:47
  12.7 4.4 %collective-permute-start = (bf16[128,1024]{1,0:T(8,128)(2,1)}, bf16[128,1024]{1,0:T(8,128)(2,1)S(1)}, u32[]{:S(2)}, u32[]{:S(2)}) collective-permute-start(bf16[128,1024]{1,0:T(8,128)(2,1)} %param.2), channel_id=1, source_target_pairs={{0,32},{16,112},{32,0},{48,80},{64,96},{80,48},{96,64},{112,16},{1... | collective-permute-start | bytes 786440 | tf_op jit(solution)/shard_map/ppermute | solution.py:43
  17.1 1.0 dynamic_update_slice.14
  18.1 1.0 dynamic_update_slice.12
  19.1 0.0 collective-permute-done.1
  19.1 2.1 collective-permute-done
  21.2 2.2 collective-permute-start.3
  23.5 4.9 %collective-permute-start.2 = (bf16[256,1024]{1,0:T(8,128)(2,1)S(1)}, bf16[256,1024]{1,0:T(8,128)(2,1)S(1)}, u32[]{:S(2)}, u32[]{:S(2)}) collective-permute-start(bf16[256,1024]{1,0:T(8,128)(2,1)S(1)} %constant_dynamic-update-slice_fusion.1.refs_0_), channel_id=1, source_target_pairs={{0,16},{16,0},{32,48},{48,32},{64,80},{80,64},{96,112},{112,96},{1... | collective-permute-start | bytes 1572872 | tf_op jit(solution)/shard_map/ppermute | solution.py:32
  28.4 3.7 %collective-permute-start.5 = (bf16[256,1024]{1,0:T(8,128)(2,1)S(1)}, bf16[256,1024]{1,0:T(8,128)(2,1)S(1)}, u32[]{:S(2)}, u32[]{:S(2)}) collective-permute-start(bf16[256,1024]{1,0:T(8,128)(2,1)S(1)} %constant_dynamic-update-slice_fusion.refs_4_), channel_id=1, source_target_pairs={{0,384},{16,144},{32,416},{48,176},{64,448},{80,208},{96,480},{112... | collective-permute-start | bytes 1572872 | tf_op jit(solution)/shard_map/ppermute | solution.py:47
  32.1 0.0 collective-permute-done.3.refs_1_
  32.1 6.6 %collective-permute-start.4 = (bf16[256,1024]{1,0:T(8,128)(2,1)S(1)}, bf16[256,1024]{1,0:T(8,128)(2,1)S(1)}, u32[]{:S(2)}, u32[]{:S(2)}) collective-permute-start(bf16[256,1024]{1,0:T(8,128)(2,1)S(1)} %collective-permute-done.3.refs_1_), channel_id=1, source_target_pairs={{0,16},{16,0},{32,48},{48,32},{64,80},{80,64},{96,112},{112,96},{1... | collective-permute-start | bytes 1572872 | tf_op jit(solution)/shard_map/ppermute | solution.py:32
  38.7 0.0 collective-permute-done.2.refs_2_
  38.7 0.2 collective-permute-done.5.refs_5_
  38.9 1.3 collective-permute-done.4.refs_3_
  40.2 0.0 all-gather.4.cloned.1.call-update
  40.2 0.0 all-gather.6.cloned.1.call-start
  40.3 0.1 pad_add_fusion.place_ref
  40.4 2.4 shard_map.49
  42.8 8.4 %collective-permute-start.6 = (f32[6,64,512]{2,1,0:T(8,128)S(1)}, f32[6,64,512]{2,1,0:T(8,128)S(1)}, u32[]{:S(2)}, u32[]{:S(2)}) collective-permute-start(f32[6,64,512]{2,1,0:T(8,128)S(1)} %get-tuple-element.37), channel_id=1, source_target_pairs={{0,1},{1,0},{2,3},{3,2},{4,5},{5,4},{6,7},{7,6},{8,9},{9,8},{10,11... | collective-permute-start | bytes 2359304 | tf_op jit(solution)/shard_map/ppermute | solution.py:62
  51.2 1.9 collective-permute-start.7
  53.1 10.6 %collective-permute-done.7.got = f32[2,64,512]{2,1,0:T(8,128)S(1)} collective-permute-done((f32[2,64,512]{2,1,0:T(8,128)S(1)}, f32[2,64,512]{2,1,0:T(8,128)S(1)}, u32[]{:S(2)}, u32[]{:S(2)}) %collective-permute-start.7) | collective-permute-done | bytes 262176 | tf_op jit(solution)/shard_map/ppermute | solution.py:62
  63.8 3.7 %collective-permute-start.8 = (f32[64,512]{1,0:T(8,128)S(1)}, f32[64,512]{1,0:T(8,128)S(1)}, u32[]{:S(2)}, u32[]{:S(2)}) collective-permute-start(f32[64,512]{1,0:T(8,128)S(1)} %get-tuple-element.41), channel_id=1, source_target_pairs={{0,2},{1,3},{2,4},{3,5},{4,6},{5,7},{6,8},{7,9},{8,10},{9,11},{10,... | collective-permute-start | bytes 393224 | tf_op jit(solution)/shard_map/ppermute | solution.py:62
  67.5 2.5 %collective-permute-start.12 = (f32[64,512]{1,0:T(8,128)S(1)}, f32[64,512]{1,0:T(8,128)S(1)}, u32[]{:S(2)}, u32[]{:S(2)}) collective-permute-start(f32[64,512]{1,0:T(8,128)S(1)} %get-tuple-element.45), channel_id=1, source_target_pairs={{0,14},{1,15},{2,0},{3,1},{4,2},{5,3},{6,4},{7,5},{8,6},{9,7},{10,... | collective-permute-start | bytes 393224 | tf_op jit(solution)/shard_map/ppermute | solution.py:62
  70.0 0.0 collective-permute-done.6.got
  70.0 0.1 shard_map.50
  70.1 0.7 collective-permute-done.8
  70.8 4.5 %collective-permute-start.9 = (f32[64,512]{1,0:T(8,128)S(1)}, f32[64,512]{1,0:T(8,128)S(1)}, u32[]{:S(2)}, u32[]{:S(2)}) collective-permute-start(f32[64,512]{1,0:T(8,128)S(1)} %add.36), channel_id=1, source_target_pairs={{0,2},{1,3},{2,4},{3,5},{4,6},{5,7},{6,8},{7,9},{8,10},{9,11},{10,... | collective-permute-start | bytes 393224 | tf_op jit(solution)/shard_map/ppermute | solution.py:62
  75.4 0.1 collective-permute-done.12
  75.5 2.0 collective-permute-start.13
  77.4 0.1 collective-permute-done.9
  77.6 6.0 %collective-permute-start.10 = (f32[64,512]{1,0:T(8,128)S(1)}, f32[64,512]{1,0:T(8,128)S(1)}, u32[]{:S(2)}, u32[]{:S(2)}) collective-permute-start(f32[64,512]{1,0:T(8,128)S(1)} %add.37), channel_id=1, source_target_pairs={{0,2},{1,3},{2,4},{3,5},{4,6},{5,7},{6,8},{7,9},{8,10},{9,11},{10,... | collective-permute-start | bytes 393224 | tf_op jit(solution)/shard_map/ppermute | solution.py:62
  83.6 1.0 collective-permute-done.13
  84.6 1.9 collective-permute-start.14
  86.5 3.2 %collective-permute-done.10 = f32[64,512]{1,0:T(8,128)S(1)} collective-permute-done((f32[64,512]{1,0:T(8,128)S(1)}, f32[64,512]{1,0:T(8,128)S(1)}, u32[]{:S(2)}, u32[]{:S(2)}) %collective-permute-start.10) | collective-permute-done | bytes 131104 | tf_op jit(solution)/shard_map/ppermute | solution.py:62
  89.7 6.1 %collective-permute-start.11 = (f32[64,512]{1,0:T(8,128)S(1)}, f32[64,512]{1,0:T(8,128)S(1)}, u32[]{:S(2)}, u32[]{:S(2)}) collective-permute-start(f32[64,512]{1,0:T(8,128)S(1)} %add.38), channel_id=1, source_target_pairs={{0,2},{1,3},{2,4},{3,5},{4,6},{5,7},{6,8},{7,9},{8,10},{9,11},{10,... | collective-permute-start | bytes 393224 | tf_op jit(solution)/shard_map/ppermute | solution.py:62
  95.8 0.0 collective-permute-done.14
  95.8 5.6 %collective-permute-done.11 = f32[64,512]{1,0:T(8,128)S(1)} collective-permute-done((f32[64,512]{1,0:T(8,128)S(1)}, f32[64,512]{1,0:T(8,128)S(1)}, u32[]{:S(2)}, u32[]{:S(2)}) %collective-permute-start.11) | collective-permute-done | bytes 131104 | tf_op jit(solution)/shard_map/ppermute | solution.py:62
  101.4 0.2 shard_map.52
  101.6 14.4 %all_to_all.35.parts_ref = f32[8,8,640]{2,1,0:T(8,128)S(1)} all-to-all(f32[8,8,640]{2,1,0:T(8,128)S(1)} %shard_map.52), channel_id=1, replica_groups={{0,16,32,48,64,80,96,112},{128,144,160,176,192,208,224,240},{256,272,28..., dimensions={0} | all-to-all | bytes 327680 | tf_op jit(solution)/shard_map/all_to_all | solution.py:298
  116.0 0.7 slice.4
  116.7 0.0 all-gather.4.cloned.1.call-done.y_ref
  116.7 0.0 all-gather.6.cloned.1.call-update
  116.7 0.2 shard_map.53
  116.9 27.0 %all_to_all.36.parts_ref = f32[64,4,128]{2,1,0:T(4,128)S(1)} all-to-all(f32[64,4,128]{2,1,0:T(4,128)S(1)} %shard_map.53), channel_id=1, replica_groups={{0,1,2,3,4,5,6,7,8,9,10,11,12,13,14,15,128,129,130,131,132,133,134,135,..., dimensions={0} | all-to-all | bytes 262144 | tf_op jit(solution)/shard_map/all_to_all | solution.py:382
  143.9 0.3 shard_map.54
  144.2 10.9 %all_to_all.37.parts_ref = f32[8,1,64]{2,1,0:T(1,128)S(1)} all-to-all(f32[8,1,64]{2,1,0:T(1,128)S(1)} %shard_map.54), channel_id=1, replica_groups={{0,16,32,48,64,80,96,112},{128,144,160,176,192,208,224,240},{256,272,28..., dimensions={0} | all-to-all | bytes 4096 | tf_op jit(solution)/shard_map/all_to_all | solution.py:298
  155.1 0.2 shard_map.55
  155.3 21.6 %all_to_all.38.parts_ref = f32[64,4,128]{2,1,0:T(4,128)S(1)} all-to-all(f32[64,4,128]{2,1,0:T(4,128)S(1)} %shard_map.55), channel_id=1, replica_groups={{0,1,2,3,4,5,6,7,8,9,10,11,12,13,14,15,128,129,130,131,132,133,134,135,..., dimensions={0} | all-to-all | bytes 262144 | tf_op jit(solution)/shard_map/all_to_all | solution.py:382
  176.9 0.1 shard_map.56
  177.0 9.6 %all_to_all.39.parts_ref = f32[8,4,128]{2,1,0:T(4,128)S(1)} all-to-all(f32[8,4,128]{2,1,0:T(4,128)S(1)} %shard_map.56), channel_id=1, replica_groups={{0,16,32,48,64,80,96,112},{128,144,160,176,192,208,224,240},{256,272,28..., dimensions={0} | all-to-all | bytes 32768 | tf_op jit(solution)/shard_map/all_to_all | solution.py:298
  186.6 0.0 all-gather.6.cloned.1.call-done
  186.6 0.0 copy-start
  186.6 1.6 copy-done
  188.2 2.6 %shard_map.57 = (f32[128,4096]{1,0:T(8,128)S(1)}, f32[128,128]{1,0:T(8,128)}, f32[32,8,512]{2,1,0:T(8,128)S(1)}) custom-call(f32[16,8,8,512]{3,2,1,0:T(8,128)S(1)} %bitcast.7, f32[8,4,128]{2,1,0:T(4,128)S(1)} %all_to_all.39.parts_ref), custom_call_target="tpu_custom_call" | custom-call | tf_op jit(solution)/shard_map/pallas_call | solution.py:401
  190.8 24.8 %all_to_all.40.parts_ref = f32[32,8,512]{2,1,0:T(8,128)S(1)} all-to-all(f32[32,8,512]{2,1,0:T(8,128)S(1)} %get-tuple-element.50), channel_id=1, replica_groups=mesh['noise'=32,'dp'=16] {'noise'}, dimensions={0} | all-to-all | bytes 1048576 | tf_op jit(solution)/shard_map/all_to_all | solution.py:416
  215.7 2.5 %shard_map.58 = (f32[128,128]{1,0:T(8,128)S(1)}, f32[32,8,512]{2,1,0:T(8,128)S(1)}) custom-call(f32[128,4096]{1,0:T(8,128)S(1)} %get-tuple-element.49.a_ref, f32[32,8,512]{2,1,0:T(8,128)S(1)} %all_to_all.40.parts_ref), custom_call_target="tpu_custom_call" | custom-call | tf_op jit(solution)/shard_map/pallas_call | solution.py:409
  218.1 15.2 %all_to_all.41.parts_ref = f32[32,8,512]{2,1,0:T(8,128)S(1)} all-to-all(f32[32,8,512]{2,1,0:T(8,128)S(1)} %get-tuple-element.52), channel_id=1, replica_groups=mesh['noise'=32,'dp'=16] {'noise'}, dimensions={0} | all-to-all | bytes 1048576 | tf_op jit(solution)/shard_map/all_to_all | solution.py:416
  233.4 6.2 %shard_map.59 = (bf16[128,1024]{1,0:T(8,128)(2,1)}, f32[1,128]{1,0:T(1,128)}, f32[1,256]{1,0:T(1,128)}) custom-call(s32[4]{0:T(128)S(1)} %pad_add_fusion.place_ref, f32[128,4096]{1,0:T(8,128)S(1)} %get-tuple-element.49.a_ref, f32[128,128]{1,0:T(8,128)S(1)} %get-tuple-element.51.u_ref, f32[32,8,512]{2,1,0:T(8,128)S(1)} %all_to_all.41.parts_ref, ...), custom_call_target="tpu_custom_call" | custom-call | tf_op jit(solution)/shard_map/pallas_call | solution.py:419
  (9 shorter events, 0.2 us)
Async XLA Ops:
  7.2 109.5 %all-gather.4.cloned.1.call-start = ((), (), s32[]{:S(2)}) async-start(), calls=%async_computation.7 | async-start | bytes 8650752 | tf_op jit(solution)/shard_map/all_gather | solution.py:307
  7.2 11.9 %collective-permute-start.1 = (bf16[128,1024]{1,0:T(8,128)(2,1)}, bf16[128,1024]{1,0:T(8,128)(2,1)S(1)}, u32[]{:S(2)}, u32[]{:S(2)}) collective-permute-start(bf16[128,1024]{1,0:T(8,128)(2,1)} %param.3), channel_id=1, source_target_pairs={{0,128},{16,400},{32,160},{48,432},{64,192},{80,464},{96,224},{112... | collective-permute-start | bytes 786440 | tf_op jit(solution)/shard_map/ppermute | solution.py:47
  12.7 8.5 %collective-permute-start = (bf16[128,1024]{1,0:T(8,128)(2,1)}, bf16[128,1024]{1,0:T(8,128)(2,1)S(1)}, u32[]{:S(2)}, u32[]{:S(2)}) collective-permute-start(bf16[128,1024]{1,0:T(8,128)(2,1)} %param.2), channel_id=1, source_target_pairs={{0,32},{16,112},{32,0},{48,80},{64,96},{80,48},{96,64},{112,16},{1... | collective-permute-start | bytes 786440 | tf_op jit(solution)/shard_map/ppermute | solution.py:43
  21.2 10.8 %collective-permute-start.3 = (bf16[256,1024]{1,0:T(8,128)(2,1)S(1)}, bf16[256,1024]{1,0:T(8,128)(2,1)S(1)}, u32[]{:S(2)}, u32[]{:S(2)}) collective-permute-start(bf16[256,1024]{1,0:T(8,128)(2,1)S(1)} %constant_dynamic-update-slice_fusion.1.refs_0_), channel_id=1, source_target_pairs={{0,96},{16,48},{32,64},{48,16},{64,32},{80,112},{96,0},{112,80},{1... | collective-permute-start | bytes 1572872 | tf_op jit(solution)/shard_map/ppermute | solution.py:43
  23.5 15.2 %collective-permute-start.2 = (bf16[256,1024]{1,0:T(8,128)(2,1)S(1)}, bf16[256,1024]{1,0:T(8,128)(2,1)S(1)}, u32[]{:S(2)}, u32[]{:S(2)}) collective-permute-start(bf16[256,1024]{1,0:T(8,128)(2,1)S(1)} %constant_dynamic-update-slice_fusion.1.refs_0_), channel_id=1, source_target_pairs={{0,16},{16,0},{32,48},{48,32},{64,80},{80,64},{96,112},{112,96},{1... | collective-permute-start | bytes 1572872 | tf_op jit(solution)/shard_map/ppermute | solution.py:32
  28.4 10.6 %collective-permute-start.5 = (bf16[256,1024]{1,0:T(8,128)(2,1)S(1)}, bf16[256,1024]{1,0:T(8,128)(2,1)S(1)}, u32[]{:S(2)}, u32[]{:S(2)}) collective-permute-start(bf16[256,1024]{1,0:T(8,128)(2,1)S(1)} %constant_dynamic-update-slice_fusion.refs_4_), channel_id=1, source_target_pairs={{0,384},{16,144},{32,416},{48,176},{64,448},{80,208},{96,480},{112... | collective-permute-start | bytes 1572872 | tf_op jit(solution)/shard_map/ppermute | solution.py:47
  32.1 8.1 %collective-permute-start.4 = (bf16[256,1024]{1,0:T(8,128)(2,1)S(1)}, bf16[256,1024]{1,0:T(8,128)(2,1)S(1)}, u32[]{:S(2)}, u32[]{:S(2)}) collective-permute-start(bf16[256,1024]{1,0:T(8,128)(2,1)S(1)} %collective-permute-done.3.refs_1_), channel_id=1, source_target_pairs={{0,16},{16,0},{32,48},{48,32},{64,80},{80,64},{96,112},{112,96},{1... | collective-permute-start | bytes 1572872 | tf_op jit(solution)/shard_map/ppermute | solution.py:32
  40.2 146.4 %all-gather.6.cloned.1.call-start = ((), (), s32[]{:S(2)}) async-start(), calls=%async_computation.8 | async-start | bytes 2228224 | tf_op jit(solution)/shard_map/all_gather | solution.py:359
  42.8 27.2 %collective-permute-start.6 = (f32[6,64,512]{2,1,0:T(8,128)S(1)}, f32[6,64,512]{2,1,0:T(8,128)S(1)}, u32[]{:S(2)}, u32[]{:S(2)}) collective-permute-start(f32[6,64,512]{2,1,0:T(8,128)S(1)} %get-tuple-element.37), channel_id=1, source_target_pairs={{0,1},{1,0},{2,3},{3,2},{4,5},{5,4},{6,7},{7,6},{8,9},{9,8},{10,11... | collective-permute-start | bytes 2359304 | tf_op jit(solution)/shard_map/ppermute | solution.py:62
  51.2 12.6 %collective-permute-start.7 = (f32[2,64,512]{2,1,0:T(8,128)S(1)}, f32[2,64,512]{2,1,0:T(8,128)S(1)}, u32[]{:S(2)}, u32[]{:S(2)}) collective-permute-start(f32[2,64,512]{2,1,0:T(8,128)S(1)} %get-tuple-element.40), channel_id=1, source_target_pairs={{0,1},{1,0},{2,3},{3,2},{4,5},{5,4},{6,7},{7,6},{8,9},{9,8},{10,11... | collective-permute-start | bytes 786440 | tf_op jit(solution)/shard_map/ppermute | solution.py:62
  63.8 7.0 %collective-permute-start.8 = (f32[64,512]{1,0:T(8,128)S(1)}, f32[64,512]{1,0:T(8,128)S(1)}, u32[]{:S(2)}, u32[]{:S(2)}) collective-permute-start(f32[64,512]{1,0:T(8,128)S(1)} %get-tuple-element.41), channel_id=1, source_target_pairs={{0,2},{1,3},{2,4},{3,5},{4,6},{5,7},{6,8},{7,9},{8,10},{9,11},{10,... | collective-permute-start | bytes 393224 | tf_op jit(solution)/shard_map/ppermute | solution.py:62
  67.5 7.9 %collective-permute-start.12 = (f32[64,512]{1,0:T(8,128)S(1)}, f32[64,512]{1,0:T(8,128)S(1)}, u32[]{:S(2)}, u32[]{:S(2)}) collective-permute-start(f32[64,512]{1,0:T(8,128)S(1)} %get-tuple-element.45), channel_id=1, source_target_pairs={{0,14},{1,15},{2,0},{3,1},{4,2},{5,3},{6,4},{7,5},{8,6},{9,7},{10,... | collective-permute-start | bytes 393224 | tf_op jit(solution)/shard_map/ppermute | solution.py:62
  70.8 6.7 %collective-permute-start.9 = (f32[64,512]{1,0:T(8,128)S(1)}, f32[64,512]{1,0:T(8,128)S(1)}, u32[]{:S(2)}, u32[]{:S(2)}) collective-permute-start(f32[64,512]{1,0:T(8,128)S(1)} %add.36), channel_id=1, source_target_pairs={{0,2},{1,3},{2,4},{3,5},{4,6},{5,7},{6,8},{7,9},{8,10},{9,11},{10,... | collective-permute-start | bytes 393224 | tf_op jit(solution)/shard_map/ppermute | solution.py:62
  75.5 9.1 %collective-permute-start.13 = (f32[64,512]{1,0:T(8,128)S(1)}, f32[64,512]{1,0:T(8,128)S(1)}, u32[]{:S(2)}, u32[]{:S(2)}) collective-permute-start(f32[64,512]{1,0:T(8,128)S(1)} %add.40), channel_id=1, source_target_pairs={{0,14},{1,15},{2,0},{3,1},{4,2},{5,3},{6,4},{7,5},{8,6},{9,7},{10,... | collective-permute-start | bytes 393224 | tf_op jit(solution)/shard_map/ppermute | solution.py:62
  77.6 12.1 %collective-permute-start.10 = (f32[64,512]{1,0:T(8,128)S(1)}, f32[64,512]{1,0:T(8,128)S(1)}, u32[]{:S(2)}, u32[]{:S(2)}) collective-permute-start(f32[64,512]{1,0:T(8,128)S(1)} %add.37), channel_id=1, source_target_pairs={{0,2},{1,3},{2,4},{3,5},{4,6},{5,7},{6,8},{7,9},{8,10},{9,11},{10,... | collective-permute-start | bytes 393224 | tf_op jit(solution)/shard_map/ppermute | solution.py:62
  84.6 11.2 %collective-permute-start.14 = (f32[64,512]{1,0:T(8,128)S(1)}, f32[64,512]{1,0:T(8,128)S(1)}, u32[]{:S(2)}, u32[]{:S(2)}) collective-permute-start(f32[64,512]{1,0:T(8,128)S(1)} %add.41), channel_id=1, source_target_pairs={{0,14},{1,15},{2,0},{3,1},{4,2},{5,3},{6,4},{7,5},{8,6},{9,7},{10,... | collective-permute-start | bytes 393224 | tf_op jit(solution)/shard_map/ppermute | solution.py:62
  89.7 11.7 %collective-permute-start.11 = (f32[64,512]{1,0:T(8,128)S(1)}, f32[64,512]{1,0:T(8,128)S(1)}, u32[]{:S(2)}, u32[]{:S(2)}) collective-permute-start(f32[64,512]{1,0:T(8,128)S(1)} %add.38), channel_id=1, source_target_pairs={{0,2},{1,3},{2,4},{3,5},{4,6},{5,7},{6,8},{7,9},{8,10},{9,11},{10,... | collective-permute-start | bytes 393224 | tf_op jit(solution)/shard_map/ppermute | solution.py:62
  186.6 1.6 copy-start
Sparse Core Ops, SparseCore 0:
  40.4 68.5 all-gather.3
  116.8 69.2 all-gather.5
